TPU v7x, 32 devices: a whole 2x2x4 slice. The times are simulated.
32 devices in a mesh: groups: 2 (over x), blk: 4 (over y, core), tsplit: 4 (over z).
Axes of the slice: x: 2, y: 2, z: 4, core: 2. Of those that a mesh axis runs over, the one named last changes fastest.
Arguments:
- sources: bfloat16 [2048, 512], P(('groups', 'blk')), parts along dimension 0, may hold values from -4 to 4
- targets: bfloat16 [32768, 512], P(('groups', 'blk', 'tsplit')), parts along dimension 0, may hold values from -4 to 4
- tgt_potential: float32 [32768], P(('groups', 'blk', 'tsplit')), parts along dimension 0, may hold values from -1 to 1
- src_logmass: float32 [2048], P(('groups', 'blk')), parts along dimension 0, may hold values from -9.5 to -7.5
- tgt_logmass: float32 [32768], P(('groups', 'blk', 'tsplit')), parts along dimension 0, may hold values from -12 to -10
- src_exponent: float32 [2048], P(('groups', 'blk')), parts along dimension 0, may hold values from 0.4 to 0.95
- tgt_exponent: float32 [32768], P(('groups', 'blk', 'tsplit')), parts along dimension 0, may hold values from 0.4 to 0.95
Outputs:
- src_potential: float32 [2048], P(('groups', 'blk')), parts along dimension 0
- tgt_update: float32 [32768], P(('groups', 'blk', 'tsplit')), parts along dimension 0
There are 2 independent parts, one for each index of `groups`. A program takes and returns all parts, laid end to end along the dimension named above; each array names one. Nothing has to cross between parts.
All inputs are finite; a program needn't handle non-finite values.
Results may differ from a plain program's by a relative error of at most 0.0003.
Values may be sent and summed in bfloat16 or wider, within the bound.
No kernel may reach another device: no remote copies, remote signals or barrier semaphores. Data moves between devices by JAX's collectives and lax.ppermute only.
A program may use at most 64 MiB of HBM per device.

v0:
```python
import jax
import jax.numpy as jnp
from jax import lax
from jax.sharding import PartitionSpec as P

EPSILON = 0.5
LOGIT_SCALE = 2.0 / EPSILON


def absorb(state_pair, key_rows, offsets, anchors):
    running_peak, running_mass = state_pair
    logits = (
        LOGIT_SCALE * jnp.dot(anchors, key_rows.T, preferred_element_type=jnp.float32)
        + offsets[None, :]
    )
    new_peak = jnp.maximum(running_peak, jnp.max(logits, axis=1))
    running_mass = running_mass * jnp.exp(running_peak - new_peak) + jnp.sum(
        jnp.exp(logits - new_peak[:, None]), axis=1
    )
    return (new_peak, running_mass)


def absorb_blocked(state_pair, key_rows, offsets, anchors):
    row_count = key_rows.shape[0]
    block_count = row_count // 512

    def advance(inner_pair, pieces):
        return (absorb(inner_pair, pieces[0], pieces[1], anchors), None)

    shaped = (
        key_rows.reshape(block_count, 512, key_rows.shape[1]),
        offsets.reshape(block_count, 512),
    )
    state_pair, _ = lax.scan(advance, state_pair, shaped)
    return state_pair


def partial_columns(key_rows, anchors, offsets):
    logits = (
        LOGIT_SCALE * jnp.dot(key_rows, anchors.T, preferred_element_type=jnp.float32)
        + offsets[None, :]
    )
    column_peak = jnp.max(logits, axis=1)
    column_mass = jnp.sum(jnp.exp(logits - column_peak[:, None]), axis=1)
    return (column_peak, column_mass)


def columns_blocked(key_rows, anchors, offsets):
    row_count = key_rows.shape[0]
    block_count = row_count // 512
    shaped = key_rows.reshape(block_count, 512, key_rows.shape[1])
    peak_part, mass_part = lax.map(
        lambda block_rows: partial_columns(block_rows, anchors, offsets), shaped
    )
    return (peak_part.reshape(row_count), mass_part.reshape(row_count))


def fold_home(peak_home, mass_home, slab_total, tgt_count):
    peak_home = peak_home.reshape(slab_total, tgt_count)
    mass_home = mass_home.reshape(slab_total, tgt_count)
    column_peak = jnp.max(peak_home, axis=0)
    column_mass = jnp.sum(mass_home * jnp.exp(peak_home - column_peak[None, :]), axis=0)
    return (column_peak, column_mass)


def shards(sources, targets, tgt_potential, src_logmass, tgt_logmass, src_exponent, tgt_exponent):
    src_count = sources.shape[0]
    tgt_count = targets.shape[0]
    slab_total = lax.axis_size("blk")
    src_sq = jnp.sum(jnp.square(sources.astype(jnp.float32)), axis=1) / EPSILON
    tgt_sq = jnp.sum(jnp.square(targets.astype(jnp.float32)), axis=1) / EPSILON
    tgt_offset = tgt_potential + tgt_logmass - tgt_sq
    all_tgt_offset = lax.all_gather(tgt_offset, "blk", axis=0, tiled=True)
    start_peak = jnp.full((src_count,), -jnp.inf, jnp.float32)
    start_mass = jnp.zeros((src_count,), jnp.float32)
    start_all = (start_peak, start_mass)
    folded = absorb_blocked(
        (start_all[0], start_all[1]),
        lax.all_gather(targets, "blk", axis=0, tiled=True),
        all_tgt_offset,
        sources,
    )
    row_peak, row_mass = (folded[0], folded[1])
    global_peak = lax.pmax(row_peak, "tsplit")
    row_mass = lax.psum(row_mass * jnp.exp(row_peak - global_peak), "tsplit")
    row_peak = global_peak
    row_lse = row_peak + jnp.log(row_mass) - src_sq
    src_potential = src_exponent * (src_logmass - row_lse)
    src_offset = src_potential + src_logmass - src_sq
    peak_part, mass_part = columns_blocked(
        lax.all_gather(targets, "blk", axis=0, tiled=True), sources, src_offset
    )
    peak_all = peak_part
    mass_all = mass_part
    peak_all, mass_all = (peak_all, mass_all)
    peak_home, mass_home = (
        lax.all_to_all(peak_all, "blk", split_axis=0, concat_axis=0, tiled=True),
        lax.all_to_all(mass_all, "blk", split_axis=0, concat_axis=0, tiled=True),
    )
    column_peak, column_mass = fold_home(peak_home, mass_home, slab_total, tgt_count)
    column_lse = column_peak + jnp.log(column_mass) - tgt_sq
    tgt_update = tgt_exponent * (tgt_logmass - column_lse)
    return (src_potential, tgt_update)


def solution(mesh):
    placed = (
        P(("groups", "blk"), None),
        P(("groups", "blk", "tsplit"), None),
        P(("groups", "blk", "tsplit")),
        P(("groups", "blk")),
        P(("groups", "blk", "tsplit")),
        P(("groups", "blk")),
        P(("groups", "blk", "tsplit")),
    )
    return jax.shard_map(
        shards,
        mesh=mesh,
        in_specs=placed,
        out_specs=(P(("groups", "blk")), P(("groups", "blk", "tsplit"))),
        check_vma=False,
    )
```

profile of v0, /device:TPU:0, one launch (start us, length us, event | category | flops | bytes accessed | tf_op | source)
XLA Modules:
  0.0 116.8 jit_solution(7091084052989492332)
XLA Ops:
  7.9 1.5 %multiply_reduce_fusion = f32[1024]{0:T(1024)S(1)} fusion(bf16[1024,512]{1,0:T(8,128)(2,1)} %param.12), kind=kLoop, calls=%fused_computation.17 | loop fusion | flops 1571840 | bytes 1052672 | tf_op jit(solution)/shard_map/reduce_sum | solution.py:71
  10.1 6.2 %all_gather.8 = f32[4096]{0:T(1024)S(1)} all-gather(f32[1024]{0:T(1024)S(1)} %add_subtract_fusion), channel_id=1, replica_groups=mesh['groups'=2,'blk'=4,'tsplit'=4] {'blk'}, dimensions={0}, use_global_device_ids=true | all-gather | bytes 20480 | tf_op jit(solution)/shard_map/all_gather | solution.py:73
  17.4 29.3 %all-gather.2.cloned.1.call-done = bf16[4096,512]{1,0:T(8,128)(2,1)} async-done(((bf16[1024,512]{1,0:T(8,128)(2,1)}), bf16[4096,512]{1,0:T(8,128)(2,1)}) %all-gather.2.cloned.1.call-update) | async-done | bytes 4194320 | tf_op jit(solution)/shard_map/all_gather | solution.py:79
  46.8 13.2 %while.26 = (s32[]{:T(128)}, f32[256]{0:T(256)S(1)}, f32[256]{0:T(256)S(1)}, bf16[8,512,512]{2,1,0:T(8,128)(2,1)}, bf16[256,512]{1,0:T(8,128)(2,1)}, /*index=5*/f32[8,512]{1,0:T(8,128)S(1)}, s32[]{:T(128)}, s32[]{:T(128)}) while((s32[]{:T(128)}, f32[256]{0:T(256)S(1)}, f32[256]{0:T(256)S(1)}, bf16[8,512,512]{2,1,0:T(8,128)(2,1)}, ...), condition=%wide.region_4.5_spmd.clone, body=%wide.region_1.4_spmd.clone.sunk | while | flops 134874368 | bytes 1855076 | solution.py:34
  46.8 1.5 %fusion.26 = (f32[256]{0:T(256)S(1)}, f32[512,256]{1,0:T(8,128)S(1)}) fusion(f32[512]{0:T(512)S(1)} %bitcast.42, bf16[256,512]{1,0:T(8,128)(2,1)} %get-tuple-element.225, bf16[8,512,512]{2,1,0:T(8,128)(2,1)} %get-tuple-element.224, s32[]{:T(128)} %get-tuple-element.213), kind=kOutput, calls=%fused_computation.29.clone.1 | convolution fusion | flops 134610688 | bytes 1314304 | tf_op jit(solution)/shard_map/while/body/eval_jaxpr/dot_general | solution.py:13
  50.1 1.5 %fusion.26 = (f32[256]{0:T(256)S(1)}, f32[512,256]{1,0:T(8,128)S(1)}) fusion(f32[512]{0:T(512)S(1)} %bitcast.42, bf16[256,512]{1,0:T(8,128)(2,1)} %get-tuple-element.225, bf16[8,512,512]{2,1,0:T(8,128)(2,1)} %get-tuple-element.224, s32[]{:T(128)} %get-tuple-element.213), kind=kOutput, calls=%fused_computation.29.clone.1 | convolution fusion | flops 134610688 | bytes 1314304 | tf_op jit(solution)/shard_map/while/body/eval_jaxpr/dot_general | solution.py:13
  51.8 1.5 %fusion.26 = (f32[256]{0:T(256)S(1)}, f32[512,256]{1,0:T(8,128)S(1)}) fusion(f32[512]{0:T(512)S(1)} %bitcast.42, bf16[256,512]{1,0:T(8,128)(2,1)} %get-tuple-element.225, bf16[8,512,512]{2,1,0:T(8,128)(2,1)} %get-tuple-element.224, s32[]{:T(128)} %get-tuple-element.213), kind=kOutput, calls=%fused_computation.29.clone.1 | convolution fusion | flops 134610688 | bytes 1314304 | tf_op jit(solution)/shard_map/while/body/eval_jaxpr/dot_general | solution.py:13
  53.4 1.5 %fusion.26 = (f32[256]{0:T(256)S(1)}, f32[512,256]{1,0:T(8,128)S(1)}) fusion(f32[512]{0:T(512)S(1)} %bitcast.42, bf16[256,512]{1,0:T(8,128)(2,1)} %get-tuple-element.225, bf16[8,512,512]{2,1,0:T(8,128)(2,1)} %get-tuple-element.224, s32[]{:T(128)} %get-tuple-element.213), kind=kOutput, calls=%fused_computation.29.clone.1 | convolution fusion | flops 134610688 | bytes 1314304 | tf_op jit(solution)/shard_map/while/body/eval_jaxpr/dot_general | solution.py:13
  58.4 1.5 %fusion.26 = (f32[256]{0:T(256)S(1)}, f32[512,256]{1,0:T(8,128)S(1)}) fusion(f32[512]{0:T(512)S(1)} %bitcast.42, bf16[256,512]{1,0:T(8,128)(2,1)} %get-tuple-element.225, bf16[8,512,512]{2,1,0:T(8,128)(2,1)} %get-tuple-element.224, s32[]{:T(128)} %get-tuple-element.213), kind=kOutput, calls=%fused_computation.29.clone.1 | convolution fusion | flops 134610688 | bytes 1314304 | tf_op jit(solution)/shard_map/while/body/eval_jaxpr/dot_general | solution.py:13
  60.0 11.7 %pmax.7 = f32[256]{0:T(256)S(1)} all-reduce(f32[256]{0:T(256)S(1)} %get-tuple-element.68), channel_id=1, replica_groups=mesh['groups'=2,'blk'=4,'tsplit'=4] {'tsplit'}, use_global_device_ids=true, to_apply=%region_5.6 | all-reduce | flops 256 | bytes 2048 | tf_op jit(solution)/shard_map/pmax | solution.py:84
  71.7 8.4 %psum.7 = f32[256]{0:T(256)S(1)} all-reduce(f32[256]{0:T(256)S(1)} %exponential_multiply_fusion), channel_id=1, replica_groups=mesh['groups'=2,'blk'=4,'tsplit'=4] {'tsplit'}, use_global_device_ids=true, to_apply=%region_6.7 | all-reduce | flops 256 | bytes 2048 | tf_op jit(solution)/shard_map/psum | solution.py:85
  80.7 13.8 %while.25 = (s32[]{:T(128)}, f32[8,512]{1,0:T(8,128)S(1)}, f32[8,512]{1,0:T(8,128)S(1)}, bf16[8,512,512]{2,1,0:T(8,128)(2,1)}, bf16[256,512]{1,0:T(8,128)(2,1)}, /*index=5*/f32[256]{0:T(256)S(1)}, s32[]{:T(128)}, s32[]{:T(128)}) while((s32[]{:T(128)}, f32[8,512]{1,0:T(8,128)S(1)}, f32[8,512]{1,0:T(8,128)S(1)}, ...), condition=%wide.region_11.12_spmd, body=%wide.region_8.11_spmd.sunk | while | flops 134872064 | bytes 1850973 | solution.py:52
  80.7 1.5 %fusion.24 = (f32[512]{0:T(512)S(1)}, f32[512,256]{0,1:T(8,128)S(1)}) fusion(f32[256]{0:T(256)S(1)} %get-tuple-element.250, bf16[256,512]{1,0:T(8,128)(2,1)} %get-tuple-element.249, bf16[8,512,512]{2,1,0:T(8,128)(2,1)} %get-tuple-element.248, s32[]{:T(128)} %get-tuple-element.237), kind=kOutput, calls=%fused_computation.28.clone.1 | convolution fusion | flops 134610432 | bytes 1314304 | tf_op jit(solution)/shard_map/while/body/eval_jaxpr/dot_general | solution.py:40
  82.4 1.5 %fusion.24 = (f32[512]{0:T(512)S(1)}, f32[512,256]{0,1:T(8,128)S(1)}) fusion(f32[256]{0:T(256)S(1)} %get-tuple-element.250, bf16[256,512]{1,0:T(8,128)(2,1)} %get-tuple-element.249, bf16[8,512,512]{2,1,0:T(8,128)(2,1)} %get-tuple-element.248, s32[]{:T(128)} %get-tuple-element.237), kind=kOutput, calls=%fused_computation.28.clone.1 | convolution fusion | flops 134610432 | bytes 1314304 | tf_op jit(solution)/shard_map/while/body/eval_jaxpr/dot_general | solution.py:40
  84.2 1.5 %fusion.24 = (f32[512]{0:T(512)S(1)}, f32[512,256]{0,1:T(8,128)S(1)}) fusion(f32[256]{0:T(256)S(1)} %get-tuple-element.250, bf16[256,512]{1,0:T(8,128)(2,1)} %get-tuple-element.249, bf16[8,512,512]{2,1,0:T(8,128)(2,1)} %get-tuple-element.248, s32[]{:T(128)} %get-tuple-element.237), kind=kOutput, calls=%fused_computation.28.clone.1 | convolution fusion | flops 134610432 | bytes 1314304 | tf_op jit(solution)/shard_map/while/body/eval_jaxpr/dot_general | solution.py:40
  85.9 1.5 %fusion.24 = (f32[512]{0:T(512)S(1)}, f32[512,256]{0,1:T(8,128)S(1)}) fusion(f32[256]{0:T(256)S(1)} %get-tuple-element.250, bf16[256,512]{1,0:T(8,128)(2,1)} %get-tuple-element.249, bf16[8,512,512]{2,1,0:T(8,128)(2,1)} %get-tuple-element.248, s32[]{:T(128)} %get-tuple-element.237), kind=kOutput, calls=%fused_computation.28.clone.1 | convolution fusion | flops 134610432 | bytes 1314304 | tf_op jit(solution)/shard_map/while/body/eval_jaxpr/dot_general | solution.py:40
  87.6 1.5 %fusion.24 = (f32[512]{0:T(512)S(1)}, f32[512,256]{0,1:T(8,128)S(1)}) fusion(f32[256]{0:T(256)S(1)} %get-tuple-element.250, bf16[256,512]{1,0:T(8,128)(2,1)} %get-tuple-element.249, bf16[8,512,512]{2,1,0:T(8,128)(2,1)} %get-tuple-element.248, s32[]{:T(128)} %get-tuple-element.237), kind=kOutput, calls=%fused_computation.28.clone.1 | convolution fusion | flops 134610432 | bytes 1314304 | tf_op jit(solution)/shard_map/while/body/eval_jaxpr/dot_general | solution.py:40
  89.3 1.5 %fusion.24 = (f32[512]{0:T(512)S(1)}, f32[512,256]{0,1:T(8,128)S(1)}) fusion(f32[256]{0:T(256)S(1)} %get-tuple-element.250, bf16[256,512]{1,0:T(8,128)(2,1)} %get-tuple-element.249, bf16[8,512,512]{2,1,0:T(8,128)(2,1)} %get-tuple-element.248, s32[]{:T(128)} %get-tuple-element.237), kind=kOutput, calls=%fused_computation.28.clone.1 | convolution fusion | flops 134610432 | bytes 1314304 | tf_op jit(solution)/shard_map/while/body/eval_jaxpr/dot_general | solution.py:40
  91.0 1.5 %fusion.24 = (f32[512]{0:T(512)S(1)}, f32[512,256]{0,1:T(8,128)S(1)}) fusion(f32[256]{0:T(256)S(1)} %get-tuple-element.250, bf16[256,512]{1,0:T(8,128)(2,1)} %get-tuple-element.249, bf16[8,512,512]{2,1,0:T(8,128)(2,1)} %get-tuple-element.248, s32[]{:T(128)} %get-tuple-element.237), kind=kOutput, calls=%fused_computation.28.clone.1 | convolution fusion | flops 134610432 | bytes 1314304 | tf_op jit(solution)/shard_map/while/body/eval_jaxpr/dot_general | solution.py:40
  92.8 1.5 %fusion.24 = (f32[512]{0:T(512)S(1)}, f32[512,256]{0,1:T(8,128)S(1)}) fusion(f32[256]{0:T(256)S(1)} %get-tuple-element.250, bf16[256,512]{1,0:T(8,128)(2,1)} %get-tuple-element.249, bf16[8,512,512]{2,1,0:T(8,128)(2,1)} %get-tuple-element.248, s32[]{:T(128)} %get-tuple-element.237), kind=kOutput, calls=%fused_computation.28.clone.1 | convolution fusion | flops 134610432 | bytes 1314304 | tf_op jit(solution)/shard_map/while/body/eval_jaxpr/dot_general | solution.py:40
  95.1 3.2 %all-to-all-start = ((f32[4,1024,1]{1,2,0:T(1,128)}), f32[4,1024,1]{1,2,0:T(1,128)S(1)}, u32[]{:S(2)}, u32[]{:S(2)}) async-start(f32[4,1024,1]{1,2,0:T(1,128)} %all_to_all.12), calls=%async_computation | async-start | bytes 32768 | tf_op jit(solution)/shard_map/all_to_all | solution.py:97
  99.0 3.2 %all-to-all-done = f32[4,1024,1]{1,2,0:T(1,128)S(1)} async-done(((f32[4,1024,1]{1,2,0:T(1,128)}), f32[4,1024,1]{1,2,0:T(1,128)S(1)}, u32[]{:S(2)}, u32[]{:S(2)}) %all-to-all-start) | async-done | bytes 16416 | tf_op jit(solution)/shard_map/all_to_all | solution.py:97
  102.2 3.2 %all-to-all-start.1 = ((f32[4,1024,1]{1,2,0:T(1,128)}), f32[4,1024,1]{1,2,0:T(1,128)S(1)}, u32[]{:S(2)}, u32[]{:S(2)}) async-start(f32[4,1024,1]{1,2,0:T(1,128)} %all_to_all.14), calls=%async_computation.1 | async-start | bytes 32768 | tf_op jit(solution)/shard_map/all_to_all | solution.py:98
  105.5 3.8 %all-to-all-done.1 = f32[4,1024,1]{1,2,0:T(1,128)S(1)} async-done(((f32[4,1024,1]{1,2,0:T(1,128)}), f32[4,1024,1]{1,2,0:T(1,128)S(1)}, u32[]{:S(2)}, u32[]{:S(2)}) %all-to-all-start.1) | async-done | bytes 16416 | tf_op jit(solution)/shard_map/all_to_all | solution.py:98
  (91 shorter events, 12.5 us)
Async XLA Ops:
  7.2 39.6 %all-gather.2.cloned.1.call-start = ((), (), s32[]{:S(2)}) async-start(), calls=%async_computation.2 | async-start | bytes 5242880 | tf_op jit(solution)/shard_map/all_gather | solution.py:79
  46.8 33.3 %copy-start.2 = (f32[256]{0:T(256)S(1)}, f32[256]{0:T(256)}, u32[]{:S(2)}) copy-start(f32[256]{0:T(256)} %param.14) | copy-start | bytes 3076
  46.8 33.3 %copy-start.3 = (f32[256]{0:T(256)S(1)}, f32[256]{0:T(256)}, u32[]{:S(2)}) copy-start(f32[256]{0:T(256)} %param.16) | copy-start | bytes 3076
  80.7 28.6 %copy-start = (f32[1024]{0:T(1024)S(1)}, f32[1024]{0:T(1024)}, u32[]{:S(2)}) copy-start(f32[1024]{0:T(1024)} %param.15) | copy-start | bytes 12292
  80.7 28.6 %copy-start.1 = (f32[1024]{0:T(1024)S(1)}, f32[1024]{0:T(1024)}, u32[]{:S(2)}) copy-start(f32[1024]{0:T(1024)} %param.17) | copy-start | bytes 12292
  95.1 7.1 %all-to-all-start = ((f32[4,1024,1]{1,2,0:T(1,128)}), f32[4,1024,1]{1,2,0:T(1,128)S(1)}, u32[]{:S(2)}, u32[]{:S(2)}) async-start(f32[4,1024,1]{1,2,0:T(1,128)} %all_to_all.12), calls=%async_computation | async-start | bytes 32768 | tf_op jit(solution)/shard_map/all_to_all | solution.py:97
  102.2 7.1 %all-to-all-start.1 = ((f32[4,1024,1]{1,2,0:T(1,128)}), f32[4,1024,1]{1,2,0:T(1,128)S(1)}, u32[]{:S(2)}, u32[]{:S(2)}) async-start(f32[4,1024,1]{1,2,0:T(1,128)} %all_to_all.14), calls=%async_computation.1 | async-start | bytes 32768 | tf_op jit(solution)/shard_map/all_to_all | solution.py:98
Sparse Core Ops, SparseCore 0:
  9.6 37.1 all-gather.1
where the time goes:
time: 118 us; the launch traced here: 117 us
  waiting for transfers between devices  37 us (31%)
  blocking collectives  26.3 us (22%)
  matrix products  23.4 us (20%)
  between operations  14.1 us (12%)
  other arithmetic  6.6 us (6%)
  starting transfers between devices  6.52 us (6%)
  local copies, waits for them, and re-layouts  2.26 us (2%)
    all_gather x1, waiting for transfers between devices, shards(): lax.all_gather(targets, 'blk', axis=0, tiled=True)  29.3 us
    dot_general x8, matrix products, partial_columns(): jnp.dot(key_rows, anchors.T, preferred_element_type=jnp.float32)  11.7 us
    pmax x1, blocking collectives, shards(): global_peak = lax.pmax(row_peak, 'tsplit')  11.7 us
    dot_general x8, matrix products, absorb(): jnp.dot(anchors, key_rows.T, preferred_element_type=jnp.float32)  11.7 us
    psum x1, blocking collectives, shards(): row_mass = lax.psum(row_mass * jnp.exp(row_peak - global_peak), 'tsplit')  8.39 us
    all_gather x1, blocking collectives, shards(): all_tgt_offset = lax.all_gather(tgt_offset, 'blk', axis=0, tiled=True)  6.2 us
    all_to_all x1, waiting for transfers between devices, shards(): lax.all_to_all(mass_all, 'blk', split_axis=0, concat_axis=0, tiled=True)  3.79 us
    all_to_all x1, starting transfers between devices, shards(): lax.all_to_all(peak_all, 'blk', split_axis=0, concat_axis=0, tiled=True)  3.25 us
  transfers between devices with their start and end apart: 3, of which 3 were waited for; matrix products, arithmetic and copies ran while one was open for 3% of the time, Pallas kernels for 0%

commit v1 on v0

v1 whole, which is shorter than its diff:
```python
import functools

import jax
import jax.numpy as jnp
from jax import lax
from jax.experimental import pallas as pl
from jax.experimental.pallas import tpu as pltpu
from jax.sharding import PartitionSpec as P

EPSILON = 0.5
LOGIT_SCALE = 2.0 / EPSILON
LANES = 128
CHUNK = 256
VMEM = pl.BlockSpec(memory_space=pltpu.VMEM)
SMEM = pl.BlockSpec(memory_space=pltpu.SMEM)
NT_DIMS = (((1,), (1,)), ((), ()))


def diagonal():
    rows = lax.broadcasted_iota(jnp.int32, (LANES, LANES), 0)
    cols = lax.broadcasted_iota(jnp.int32, (LANES, LANES), 1)
    return rows == cols


def to_lanes(column, eye):
    return jnp.sum(jnp.where(eye, column, 0.0), axis=0, keepdims=True)


def to_column(lanes, eye):
    return jnp.sum(jnp.where(eye, lanes, 0.0), axis=1, keepdims=True)


def fold_rows(value, op):
    return op(value.reshape(value.shape[0] // 8, 8, value.shape[1]), axis=0)


def row_block(rows_ref, tgt_ref, offset_ref, logit_ref, slot):
    tgt_count = tgt_ref.shape[0]
    rows = rows_ref[...]
    peak = None
    for at in range(0, tgt_count, CHUNK):
        part = pl.ds(at, CHUNK)
        logits = LOGIT_SCALE * lax.dot_general(tgt_ref[part, :], rows, NT_DIMS, preferred_element_type=jnp.float32)
        logit_ref[slot, part, :] = logits
        high = fold_rows(logits + offset_ref[part, :1], jnp.max)
        peak = high if peak is None else jnp.maximum(peak, high)
    peak = jnp.max(peak, axis=0, keepdims=True)
    mass = None
    for at in range(0, tgt_count, CHUNK):
        part = pl.ds(at, CHUNK)
        term = jnp.exp(logit_ref[slot, part, :] + (offset_ref[part, :1] - peak))
        term = fold_rows(term, jnp.sum)
        mass = term if mass is None else mass + term
    mass = jnp.sum(mass, axis=0, keepdims=True)
    return peak + jnp.log(mass)


def near_kernel(own_ref, pair_ref, tgt_ref, pot_ref, mass_ref, logit_ref, lse_ref, offset_ref, tsq_ref, ssq_ref):
    eye = diagonal()
    tgt_count = tgt_ref.shape[0]
    for group in range(tgt_count // LANES):
        part = pl.ds(group * LANES, LANES)
        rows = tgt_ref[part, :].astype(jnp.float32)
        square = jnp.sum(rows * rows, axis=1, keepdims=True) / EPSILON
        offset = to_column(pot_ref[group : group + 1, :] + mass_ref[group : group + 1, :], eye) - square
        offset_ref[part, :] = jnp.broadcast_to(offset, (LANES, LANES))
        tsq_ref[group : group + 1, :] = to_lanes(square, eye)
    for group in range(own_ref.shape[0] // LANES):
        rows = own_ref[pl.ds(group * LANES, LANES), :].astype(jnp.float32)
        square = jnp.sum(rows * rows, axis=1, keepdims=True) / EPSILON
        ssq_ref[group : group + 1, :] = to_lanes(square, eye)
    lse_ref[0:1, :] = row_block(own_ref, tgt_ref, offset_ref, logit_ref, 0)
    lse_ref[1:2, :] = row_block(pair_ref, tgt_ref, offset_ref, logit_ref, 1)


def far_kernel(count, *refs):
    blocks = refs[:count]
    tgt_ref, offset_ref, logit_ref, lse_ref = refs[count:]
    for slot in range(count):
        lse_ref[slot : slot + 1, :] = row_block(blocks[slot], tgt_ref, offset_ref, logit_ref, slot)


def column_kernel(order_ref, near_ref, far_ref, srcoff_ref, tsq_ref, mass_ref, expo_ref, out_ref, off_ref):
    eye = diagonal()
    near = near_ref.shape[0]
    far = far_ref.shape[0]
    src_count = near_ref.shape[2]
    tgt_count = near_ref.shape[1]
    for slot in range(near + far):
        off_ref[slot : slot + 1, :] = srcoff_ref[pl.ds(order_ref[slot], 1), :]

    def logits(slot, part):
        held = near_ref[slot, part, :] if slot < near else far_ref[slot - near, part, :]
        return held + off_ref[slot : slot + 1, :]

    def fold_lanes(value, op):
        out = value[:, :LANES]
        for at in range(LANES, src_count, LANES):
            out = op(out, value[:, at : at + LANES])
        return out

    for group in range(tgt_count // LANES):
        part = pl.ds(group * LANES, LANES)
        peak = None
        for slot in range(near + far):
            high = fold_lanes(logits(slot, part), jnp.maximum)
            peak = high if peak is None else jnp.maximum(peak, high)
        peak = jnp.max(peak, axis=1, keepdims=True)
        mass = None
        for slot in range(near + far):
            term = fold_lanes(jnp.exp(logits(slot, part) - peak), jnp.add)
            mass = term if mass is None else mass + term
        mass = jnp.sum(mass, axis=1, keepdims=True)
        row = slice(group, group + 1)
        lse = to_lanes(peak, eye) + jnp.log(to_lanes(mass, eye)) - tsq_ref[row, :]
        out_ref[row, :] = expo_ref[row, :] * (mass_ref[row, :] - lse)


def f32(*shape):
    return jax.ShapeDtypeStruct(shape, jnp.float32)


def params():
    return pltpu.CompilerParams(vmem_limit_bytes=48 * 1024 * 1024)


def shards(sources, targets, tgt_potential, src_logmass, tgt_logmass, src_exponent, tgt_exponent):
    src_count, width = sources.shape
    tgt_count = targets.shape[0]
    slabs = lax.axis_size("blk")
    sets = lax.axis_size("tsplit")
    chips = slabs // 2
    groups = tgt_count // LANES
    me = lax.axis_index("blk")

    pair_way = [(i, i ^ 1) for i in range(slabs)]
    pair = lax.ppermute(sources, "blk", pair_way)
    straight = [
        lax.ppermute(sources, "blk", [(i, (i + 2 * step) % slabs) for i in range(slabs)]) for step in range(1, chips)
    ]
    crossed = [lax.ppermute(block, "blk", pair_way) for block in straight]
    far_blocks = straight + crossed
    origin = [(me + slabs - 2 * step) % slabs for step in range(1, chips)]
    order = jnp.stack([me, me ^ 1] + origin + [at ^ 1 for at in origin]).astype(jnp.int32)

    potential = tgt_potential.reshape(groups, LANES)
    logmass = tgt_logmass.reshape(groups, LANES)
    exponent = tgt_exponent.reshape(groups, LANES)

    pair_flops = 2 * src_count * tgt_count * width
    near_logits, near_lse, offset, tgt_sq, src_sq = pl.pallas_call(
        near_kernel,
        out_shape=(
            f32(2, tgt_count, src_count),
            f32(2, src_count),
            f32(tgt_count, LANES),
            f32(groups, LANES),
            f32(src_count // LANES, LANES),
        ),
        in_specs=[VMEM] * 5,
        out_specs=(VMEM,) * 5,
        compiler_params=params(),
        cost_estimate=pl.CostEstimate(
            flops=2 * pair_flops, bytes_accessed=4 * 2**20, transcendentals=2 * src_count * tgt_count
        ),
        name="near_rows",
    )(sources, pair, targets, potential, logmass)
    far = len(far_blocks)
    far_logits, far_lse = pl.pallas_call(
        functools.partial(far_kernel, far),
        out_shape=(f32(far, tgt_count, src_count), f32(far, src_count)),
        in_specs=[VMEM] * (far + 2),
        out_specs=(VMEM,) * 2,
        compiler_params=params(),
        cost_estimate=pl.CostEstimate(
            flops=far * pair_flops, bytes_accessed=4 * 2**20, transcendentals=far * src_count * tgt_count
        ),
        name="far_rows",
    )(*far_blocks, targets, offset)

    own_sq = src_sq.reshape(src_count)
    partial_lse = jnp.concatenate([near_lse, far_lse])
    placed = order[None, :, None] == jnp.arange(slabs, dtype=jnp.int32)[:, None, None]
    partial_lse = jnp.sum(jnp.where(placed, partial_lse[None], 0.0), axis=1).reshape(-1)
    shift = src_exponent * (src_logmass + own_sq) + src_logmass - own_sq
    payload = jnp.concatenate([partial_lse, src_exponent, shift])
    everyone = lax.all_gather(payload, ("blk", "tsplit"), axis=0, tiled=False)
    total = slabs * src_count
    lses = everyone[:, :total]
    peak = jnp.max(lses, axis=0)
    lse = peak + jnp.log(jnp.sum(jnp.exp(lses - peak[None, :]), axis=0))
    homes = everyone.reshape(slabs, sets, -1)[:, 0, total:]
    slopes = homes[:, :src_count].reshape(total)
    shifts = homes[:, src_count:].reshape(total)
    src_offset = (shifts - slopes * lse).reshape(slabs, src_count)
    own_lse = lax.dynamic_slice_in_dim(lse, me * src_count, src_count) - own_sq
    src_potential = src_exponent * (src_logmass - own_lse)

    tgt_update = pl.pallas_call(
        column_kernel,
        out_shape=f32(groups, LANES),
        in_specs=[SMEM] + [VMEM] * 6,
        out_specs=VMEM,
        scratch_shapes=[pltpu.VMEM((slabs, src_count), jnp.float32)],
        compiler_params=params(),
        name="columns",
    )(order, near_logits, far_logits, src_offset, tgt_sq, logmass, exponent)
    return (src_potential, tgt_update.reshape(tgt_count))


def solution(mesh):
    placed = (
        P(("groups", "blk"), None),
        P(("groups", "blk", "tsplit"), None),
        P(("groups", "blk", "tsplit")),
        P(("groups", "blk")),
        P(("groups", "blk", "tsplit")),
        P(("groups", "blk")),
        P(("groups", "blk", "tsplit")),
    )
    return jax.shard_map(
        shards,
        mesh=mesh,
        in_specs=placed,
        out_specs=(P(("groups", "blk")), P(("groups", "blk", "tsplit"))),
        check_vma=False,
    )
```

time: 118 us -> 58.5 us (0.50)
  waiting for transfers between devices: 37 us -> 7.03 us
  matrix products: 23.4 us -> 0 us
  between operations: 14.1 us -> 0.79 us
  blocking collectives: 26.3 us -> 34.1 us
  Pallas kernels: 0 us -> 4.82 us
  other arithmetic: 6.6 us -> 1.83 us
  local copies, waits for them, and re-layouts: 2.26 us -> 6.55 us
  starting transfers between devices: 6.52 us -> 3.12 us
    all_gather x1 -> x0, waiting for transfers between devices: 29.3 us -> none  [shards(): lax.all_gather(targets, 'blk', axis=0, tiled=True)]
    all_gather x1, blocking collectives: 6.2 us -> 34.1 us  [shards(): everyone = lax.all_gather(payload, ('blk', 'tsplit'), axis=0, tiled=False)]
    dot_general x16 -> x0, matrix products: 23.4 us -> none  [the longest x8 11.7 us: partial_columns(): jnp.dot(key_rows, anchors.T, preferred_element_type=jnp.float32)]
    pmax x1 -> x0, blocking collectives: 11.7 us -> none  [shards(): global_peak = lax.pmax(row_peak, 'tsplit')]
    psum x1 -> x0, blocking collectives: 8.39 us -> none  [shards(): row_mass = lax.psum(row_mass * jnp.exp(row_peak - global_peak), 'tsplit')]
    ppermute x0 -> x3, waiting for transfers between devices: none -> 7.03 us  [the longest x1 7.02 us: shards(): lax.ppermute(sources, 'blk', [(i, (i + 2 * step) % slabs) for i in range(...]
    all_to_all x2 -> x0, waiting for transfers between devices: 6.99 us -> none  [the longest x1 3.79 us: shards(): lax.all_to_all(mass_all, 'blk', split_axis=0, concat_axis=0, tiled=True)]
    unnamed x8 -> x26, local copies, waits for them, and re-layouts: 0.01 us -> 6.5 us
  transfers between devices with their start and end apart: 3 -> 3, of which waited for: 3 -> 1; matrix products, arithmetic and copies ran while one was open for 3% -> 1% of each run, Pallas kernels for 0% -> 2%
where the time goes in v1:
time: 58.5 us; the launch traced here: 58.2 us
  blocking collectives  34.1 us (58%)
  waiting for transfers between devices  7.03 us (12%)
  local copies, waits for them, and re-layouts  6.55 us (11%)
  Pallas kernels  4.82 us (8%)
  starting transfers between devices  3.12 us (5%)
  other arithmetic  1.83 us (3%)
  between operations  0.79 us (1%)
    all_gather x1, blocking collectives, shards(): everyone = lax.all_gather(payload, ('blk', 'tsplit'), axis=0, tiled=False)  34.1 us
    ppermute x1, waiting for transfers between devices, shards(): lax.ppermute(sources, 'blk', [(i, (i + 2 * step) % slabs) for i in range(...  7.02 us
    unnamed x26, local copies, waits for them, and re-layouts  6.5 us
    ppermute x1, starting transfers between devices, shards(): lax.ppermute(sources, 'blk', [(i, (i + 2 * step) % slabs) for i in range(...  2.59 us
    pallas_call x1, Pallas kernels, shards(): pl.pallas_call(column_kernel, out_shape=f32(groups, LANES), in_specs=[SME...  2.34 us
    pallas_call x1, Pallas kernels, shards(): pl.pallas_call(near_kernel, out_shape=(f32(2, tgt_count, src_count), f32(...  1.29 us
    pallas_call x1, Pallas kernels, shards(): pl.pallas_call(functools.partial(far_kernel, far), out_shape=(f32(far, tg...  1.19 us
  transfers between devices with their start and end apart: 3, of which 1 were waited for; matrix products, arithmetic and copies ran while one was open for 1% of the time, Pallas kernels for 2%

profile of v1, /device:TPU:0, one launch (start us, length us, event | category | flops | bytes accessed | tf_op | source)
XLA Modules:
  0.0 58.2 jit_solution(10990565816351011549)
XLA Ops:
  0.6 0.0 copy-start.9
  0.6 0.5 collective-permute-start
  1.2 2.6 %collective-permute-start.1 = (bf16[256,512]{1,0:T(8,128)(2,1)}, bf16[256,512]{1,0:T(8,128)(2,1)S(1)}, u32[]{:S(2)}, u32[]{:S(2)}) collective-permute-start(bf16[256,512]{1,0:T(8,128)(2,1)} %own_ref.1), channel_id=1, source_target_pairs={{0,8},{4,12},{8,0},{12,4},{1,9},{5,13},{9,1},{13,5},{2,10},{6,14},... | collective-permute-start | bytes 786440 | tf_op jit(solution)/shard_map/ppermute | solution.py:139
  3.8 0.1 pad_add_fusion.order_ref
  3.8 7.0 %collective-permute-done.1.refs_0_ = bf16[256,512]{1,0:T(8,128)(2,1)S(1)} collective-permute-done((bf16[256,512]{1,0:T(8,128)(2,1)}, bf16[256,512]{1,0:T(8,128)(2,1)S(1)}, u32[]{:S(2)}, u32[]{:S(2)}) %collective-permute-start.1) | collective-permute-done | bytes 262176 | tf_op jit(solution)/shard_map/ppermute | solution.py:139
  10.9 0.0 collective-permute-start.2
  10.9 0.0 collective-permute-done.pair_ref
  10.9 1.2 %copy-done.2 = bf16[1024,512]{1,0:T(8,128)(2,1)S(1)} copy-done((bf16[1024,512]{1,0:T(8,128)(2,1)S(1)}, bf16[1024,512]{1,0:T(8,128)(2,1)}, u32[]{:S(2)}) %copy-start.2) | copy-done | bytes 1048600
  12.1 0.7 %copy-done.4 = f32[1024]{0:T(1024)S(1)} copy-done((f32[1024]{0:T(1024)S(1)}, f32[1024]{0:T(1024)}, u32[]{:S(2)}) %copy-start.4) | copy-done | bytes 4120
  12.8 0.9 %copy-done.7 = bf16[256,512]{1,0:T(8,128)(2,1)S(1)} copy-done((bf16[256,512]{1,0:T(8,128)(2,1)S(1)}, bf16[256,512]{1,0:T(8,128)(2,1)}, u32[]{:S(2)}) %copy-start.7) | copy-done | bytes 262168
  13.7 0.7 %copy-done.8 = f32[1024]{0:T(1024)S(1)} copy-done((f32[1024]{0:T(1024)S(1)}, f32[1024]{0:T(1024)}, u32[]{:S(2)}) %copy-start.8) | copy-done | bytes 4120
  14.4 1.3 %near_rows.1 = (f32[2,1024,256]{2,1,0:T(8,128)S(1)}, f32[2,256]{1,0:T(2,128)S(1)}, f32[1024,128]{1,0:T(8,128)S(1)}, f32[8,128]{1,0:T(8,128)S(1)}, f32[2,128]{1,0:T(2,128)S(1)}) custom-call(bf16[256,512]{1,0:T(8,128)(2,1)S(1)} %copy-done.7, bf16[256,512]{1,0:T(8,128)(2,1)S(1)} %collective-permute-done.pair_ref, bf16[1024,512]{1,0:T(8,128)(2,1)S(1)} %copy-done.2, ...), custom_call_target="tpu_custom_call" | custom-call | flops 536870912 | bytes 4194304 | tf_op jit(solution)/shard_map/near_rows/pallas_call | solution.py:151
  15.7 0.7 %bitcast_subtract_fusion.1 = f32[256]{0:T(256)S(1)} fusion(f32[2,128]{1,0:T(2,128)S(1)} %get-tuple-element.12, f32[256]{0:T(256)} %param.10, f32[256]{0:T(256)} %param.12), kind=kLoop, calls=%fused_computation.12 | loop fusion | flops 1024 | bytes 4096 | tf_op jit(solution)/shard_map/sub | solution.py:185
  16.4 0.0 collective-permute-done.2.refs_1_
  16.4 1.2 %far_rows.1 = (f32[2,1024,256]{2,1,0:T(8,128)S(1)}, f32[2,256]{1,0:T(2,128)S(1)}) custom-call(bf16[256,512]{1,0:T(8,128)(2,1)S(1)} %collective-permute-done.1.refs_0_, bf16[256,512]{1,0:T(8,128)(2,1)S(1)} %collective-permute-done.2.refs_1_, bf16[1024,512]{1,0:T(8,128)(2,1)S(1)} %copy-done.3, f32[1024,128]{1,0:T(8,128)S(1)} %get-tuple-element.10.refs_3_), custom_call_target="tpu_custom_call" | custom-call | flops 536870912 | bytes 4194304 | tf_op jit(solution)/shard_map/far_rows/pallas_call | solution.py:169
  17.6 0.0 copy-start
  17.6 1.3 %copy-done = f32[2,1024,256]{2,1,0:T(8,128)} copy-done((f32[2,1024,256]{2,1,0:T(8,128)}, f32[2,1024,256]{2,1,0:T(8,128)S(1)}, u32[]{:S(2)}) %copy-start) | copy-done | bytes 2097176
  19.0 0.1 select_reduce_fusion
  19.1 0.0 copy-done.9
  19.1 34.1 %all-gather.1 = f32[16,1,1536]{2,1,0:T(1,128)S(1)} all-gather(f32[1,1,1536]{2,1,0:T(1,128)S(1)} %reshape.65), channel_id=2, replica_groups=mesh['groups'=2,'blk'=4,'tsplit'=4] {'blk','tsplit'}, dimensions={0}, use_global_device_ids=true | all-gather | bytes 104448 | tf_op jit(solution)/shard_map/all_gather | solution.py:187
  53.3 0.6 %fusion.4 = f32[256]{0:T(256)} fusion(f32[256]{0:T(256)S(1)} %copy-done.9, f32[256]{0:T(256)S(1)} %copy-done.10, f32[2,128]{1,0:T(2,128)S(1)} %get-tuple-element.12, f32[1024]{0:T(1024)S(1)} %log_add_fusion, s32[]{:T(128)S(6)} %select_n.16), kind=kLoop, calls=%fused_computation.17 | loop fusion | flops 768 | bytes 5124 | tf_op jit(solution)/shard_map/mul | solution.py:197
  53.9 0.2 reduce
  54.3 1.6 %copy-done.1 = f32[2,1024,256]{2,1,0:T(8,128)S(1)} copy-done((f32[2,1024,256]{2,1,0:T(8,128)S(1)}, f32[2,1024,256]{2,1,0:T(8,128)}, u32[]{:S(2)}) %copy-start.1) | copy-done | bytes 2097176
  55.9 2.3 %columns.1 = f32[8,128]{1,0:T(8,128)} custom-call(s32[4]{0:T(128)S(1)} %pad_add_fusion.order_ref, f32[2,1024,256]{2,1,0:T(8,128)S(1)} %get-tuple-element.13.near_ref, f32[2,1024,256]{2,1,0:T(8,128)S(1)} %copy-done.1, f32[4,256]{1,0:T(4,128)S(1)} %fusion.srcoff_ref, f32[8,128]{1,0:T(8,128)S(1)} %get-tuple-element.15.tsq_ref, f32[8,128]{1,0:T(8,128)S(1)} %bitcast.31, ...), custom_call_target="tpu_custom_call" | custom-call | tf_op jit(solution)/shard_map/columns/pallas_call | solution.py:199
  (27 shorter events, 0.2 us)
Async XLA Ops:
  0.6 18.4 %copy-start.9 = (f32[256]{0:T(256)S(1)}, f32[256]{0:T(256)}, u32[]{:S(2)}) copy-start(f32[256]{0:T(256)} %param.12) | copy-start | bytes 3076
  0.6 10.2 %collective-permute-start = (bf16[256,512]{1,0:T(8,128)(2,1)}, bf16[256,512]{1,0:T(8,128)(2,1)S(1)}, u32[]{:S(2)}, u32[]{:S(2)}) collective-permute-start(bf16[256,512]{1,0:T(8,128)(2,1)} %own_ref.1), channel_id=1, source_target_pairs={{0,4},{4,0},{8,12},{12,8},{1,5},{5,1},{9,13},{13,9},{2,6},{6,2},{1... | collective-permute-start | bytes 786440 | tf_op jit(solution)/shard_map/ppermute | solution.py:137
  1.2 9.7 %collective-permute-start.1 = (bf16[256,512]{1,0:T(8,128)(2,1)}, bf16[256,512]{1,0:T(8,128)(2,1)S(1)}, u32[]{:S(2)}, u32[]{:S(2)}) collective-permute-start(bf16[256,512]{1,0:T(8,128)(2,1)} %own_ref.1), channel_id=1, source_target_pairs={{0,8},{4,12},{8,0},{12,4},{1,9},{5,13},{9,1},{13,5},{2,10},{6,14},... | collective-permute-start | bytes 786440 | tf_op jit(solution)/shard_map/ppermute | solution.py:139
  10.9 5.6 %collective-permute-start.2 = (bf16[256,512]{1,0:T(8,128)(2,1)S(1)}, bf16[256,512]{1,0:T(8,128)(2,1)S(1)}, u32[]{:S(2)}, u32[]{:S(2)}) collective-permute-start(bf16[256,512]{1,0:T(8,128)(2,1)S(1)} %collective-permute-done.1.refs_0_), channel_id=1, source_target_pairs={{0,4},{4,0},{8,12},{12,8},{1,5},{5,1},{9,13},{13,9},{2,6},{6,2},{1... | collective-permute-start | bytes 786440 | tf_op jit(solution)/shard_map/ppermute | solution.py:141
  10.9 1.2 %copy-start.2 = (bf16[1024,512]{1,0:T(8,128)(2,1)S(1)}, bf16[1024,512]{1,0:T(8,128)(2,1)}, u32[]{:S(2)}) copy-start(bf16[1024,512]{1,0:T(8,128)(2,1)} %refs_2_.1) | copy-start | bytes 3145732
  12.1 0.7 %copy-start.4 = (f32[1024]{0:T(1024)S(1)}, f32[1024]{0:T(1024)}, u32[]{:S(2)}) copy-start(f32[1024]{0:T(1024)} %param.11) | copy-start | bytes 12292
  12.8 0.9 %copy-start.7 = (bf16[256,512]{1,0:T(8,128)(2,1)S(1)}, bf16[256,512]{1,0:T(8,128)(2,1)}, u32[]{:S(2)}) copy-start(bf16[256,512]{1,0:T(8,128)(2,1)} %own_ref.1) | copy-start | bytes 786436
  13.7 0.7 %copy-start.8 = (f32[1024]{0:T(1024)S(1)}, f32[1024]{0:T(1024)}, u32[]{:S(2)}) copy-start(f32[1024]{0:T(1024)} %param.9) | copy-start | bytes 12292
  14.4 2.0 %copy-start.3 = (bf16[1024,512]{1,0:T(8,128)(2,1)S(1)}, bf16[1024,512]{1,0:T(8,128)(2,1)}, u32[]{:S(2)}) copy-start(bf16[1024,512]{1,0:T(8,128)(2,1)} %refs_2_.1) | copy-start | bytes 3145732
  14.4 38.9 %copy-start.10 = (f32[256]{0:T(256)S(1)}, f32[256]{0:T(256)}, u32[]{:S(2)}) copy-start(f32[256]{0:T(256)} %param.10) | copy-start | bytes 3076
  14.4 39.8 %copy-start.5 = (f32[1024]{0:T(1024)S(1)}, f32[1024]{0:T(1024)}, u32[]{:S(2)}) copy-start(f32[1024]{0:T(1024)} %param.11) | copy-start | bytes 12292
  14.4 39.8 %copy-start.6 = (f32[1024]{0:T(1024)S(1)}, f32[1024]{0:T(1024)}, u32[]{:S(2)}) copy-start(f32[1024]{0:T(1024)} %param.13) | copy-start | bytes 12292
  17.6 1.3 %copy-start = (f32[2,1024,256]{2,1,0:T(8,128)}, f32[2,1024,256]{2,1,0:T(8,128)S(1)}, u32[]{:S(2)}) copy-start(f32[2,1024,256]{2,1,0:T(8,128)S(1)} %get-tuple-element.14.far_ref) | copy-start | bytes 6291460
  54.3 1.6 %copy-start.1 = (f32[2,1024,256]{2,1,0:T(8,128)S(1)}, f32[2,1024,256]{2,1,0:T(8,128)}, u32[]{:S(2)}) copy-start(f32[2,1024,256]{2,1,0:T(8,128)} %copy-done) | copy-start | bytes 6291460

commit v2 on v1

v2 whole, which is shorter than its diff:
```python
import functools

import jax
import jax.numpy as jnp
from jax import lax
from jax.experimental import pallas as pl
from jax.experimental.pallas import tpu as pltpu
from jax.sharding import PartitionSpec as P

EPSILON = 0.5
LOGIT_SCALE = 2.0 / EPSILON
LANES = 128
CHUNK = 256
VMEM = pl.BlockSpec(memory_space=pltpu.VMEM)
NT_DIMS = (((1,), (1,)), ((), ()))


def diagonal():
    rows = lax.broadcasted_iota(jnp.int32, (LANES, LANES), 0)
    cols = lax.broadcasted_iota(jnp.int32, (LANES, LANES), 1)
    return rows == cols


def to_lanes(column, eye):
    return jnp.sum(jnp.where(eye, column, 0.0), axis=0, keepdims=True)


def to_column(lanes, eye):
    return jnp.sum(jnp.where(eye, lanes, 0.0), axis=1, keepdims=True)


def fold_rows(value, op):
    return op(value.reshape(value.shape[0] // 8, 8, value.shape[1]), axis=0)


def row_block(rows_ref, tgt_refs, offset_ref, z_at, lse_at, eye):
    rows = rows_ref[...] * LOGIT_SCALE
    src_count = rows.shape[0]
    tgt_count = tgt_refs[0].shape[0]
    peak = None
    for half, tgt_ref in enumerate(tgt_refs):
        for at in range(0, tgt_count, CHUNK):
            cols = slice(half * tgt_count + at, half * tgt_count + at + CHUNK)
            dots = lax.dot_general(rows, tgt_ref[at : at + CHUNK, :], NT_DIMS, preferred_element_type=jnp.float32)
            z = dots + offset_ref[:, cols]
            z_at[:, cols] = z
            for lane in range(0, CHUNK, LANES):
                part = z[:, lane : lane + LANES]
                peak = part if peak is None else jnp.maximum(peak, part)
    peak = jnp.max(peak, axis=1, keepdims=True)
    mass = None
    for at in range(0, len(tgt_refs) * tgt_count, LANES):
        term = jnp.exp(z_at[:, at : at + LANES] - peak)
        mass = term if mass is None else mass + term
    mass = jnp.sum(mass, axis=1, keepdims=True)
    for at in range(0, src_count, LANES):
        part = slice(at, at + LANES)
        lse_at[:, part] = to_lanes(peak[part], eye) + jnp.log(to_lanes(mass[part], eye))


def near_kernel(src_ref, own_ref, pair_ref, own_base_ref, pair_base_ref, z_ref, lse_ref, offset_ref):
    eye = diagonal()
    tgt_count = own_ref.shape[0]
    for half, (tgt_ref, base_ref) in enumerate(((own_ref, own_base_ref), (pair_ref, pair_base_ref))):
        for group in range(tgt_count // LANES):
            rows = tgt_ref[group * LANES : (group + 1) * LANES, :].astype(jnp.float32)
            square = jnp.sum(rows * rows, axis=1, keepdims=True) / EPSILON
            at = half * tgt_count + group * LANES
            offset_ref[:, at : at + LANES] = base_ref[group : group + 1, :] - to_lanes(square, eye)
    row_block(src_ref, (own_ref, pair_ref), offset_ref, z_ref, lse_ref, eye)


def far_kernel(count, *refs):
    eye = diagonal()
    blocks = refs[:count]
    own_ref, pair_ref, offset_ref, z_ref, lse_ref = refs[count:]
    for slot in range(count):
        row_block(
            blocks[slot], (own_ref, pair_ref), offset_ref, z_ref.at[slot], lse_ref.at[slot], eye
        )


def column_kernel(
    near_ref, far_ref, lse_ref, slope_ref, shift_ref, mass_ref, sq_ref, own_ref, pair_ref, potential_ref, off_ref
):
    eye = diagonal()
    slots, src_count = lse_ref.shape
    tgt_count = near_ref.shape[1] // 2
    lse = lse_ref[...]
    potential_ref[...] = slope_ref[0:1, :] * (mass_ref[...] - (lse[0:1, :] - sq_ref[...]))
    offset = shift_ref[...] - slope_ref[...] * lse
    for slot in range(slots):
        for at in range(0, src_count, LANES):
            column = to_column(offset[slot : slot + 1, at : at + LANES], eye)
            off_ref[slot, at : at + LANES, :] = jnp.broadcast_to(column, (LANES, LANES))

    def held(slot, cols):
        z = near_ref[:, cols] if slot == 0 else far_ref[slot - 1, :, cols]
        return z + off_ref[slot]

    for at in range(0, 2 * tgt_count, LANES):
        cols = slice(at, at + LANES)
        peak = None
        for slot in range(slots):
            high = fold_rows(held(slot, cols), jnp.max)
            peak = high if peak is None else jnp.maximum(peak, high)
        peak = jnp.max(peak, axis=0, keepdims=True)
        mass = None
        for slot in range(slots):
            term = fold_rows(jnp.exp(held(slot, cols) - peak), jnp.sum)
            mass = term if mass is None else mass + term
        mass = jnp.sum(mass, axis=0, keepdims=True)
        group = at // LANES
        if at < tgt_count:
            own_ref[group : group + 1, :] = peak + jnp.log(mass)
        else:
            group -= tgt_count // LANES
            pair_ref[group : group + 1, :] = peak + jnp.log(mass)


def f32(*shape):
    return jax.ShapeDtypeStruct(shape, jnp.float32)


def params():
    return pltpu.CompilerParams(vmem_limit_bytes=32 * 1024 * 1024)


def merge(left, right):
    peak = jnp.maximum(left, right)
    return peak + jnp.log(jnp.exp(left - peak) + jnp.exp(right - peak))


def shards(sources, targets, tgt_potential, src_logmass, tgt_logmass, src_exponent, tgt_exponent):
    src_count, width = sources.shape
    tgt_count = targets.shape[0]
    slabs = lax.axis_size("blk")
    sets = lax.axis_size("tsplit")
    chips = slabs // 2
    groups = tgt_count // LANES
    assert chips & (chips - 1) == 0 and sets & (sets - 1) == 0

    def pair(value):
        return lax.ppermute(value, "blk", [(i, i ^ 1) for i in range(slabs)])

    def across(value, chip):
        return lax.ppermute(value, "blk", [(i, i ^ (2 * chip)) for i in range(slabs)])

    def along(value, step):
        return lax.ppermute(value, "tsplit", [(i, i ^ step) for i in range(sets)])

    far_blocks = [across(sources, chip) for chip in range(1, chips)]
    pair_targets = pair(targets)
    base = (tgt_potential + tgt_logmass).reshape(groups, LANES)
    pair_base = pair(base)
    own_sq = jnp.sum(jnp.square(sources.astype(jnp.float32)), axis=1) / EPSILON
    shift = src_exponent * (src_logmass + own_sq) + src_logmass - own_sq
    line = jnp.stack([src_exponent, shift])
    lines = jnp.stack([line] + [across(line, chip) for chip in range(1, chips)])

    block_pairs = src_count * 2 * tgt_count

    def cost(blocks):
        return pl.CostEstimate(
            flops=2 * blocks * block_pairs * width, bytes_accessed=2 * 2**20, transcendentals=blocks * block_pairs
        )

    near_z, near_lse, offset = pl.pallas_call(
        near_kernel,
        out_shape=(f32(src_count, 2 * tgt_count), f32(1, src_count), f32(1, 2 * tgt_count)),
        in_specs=[VMEM] * 5,
        out_specs=(VMEM,) * 3,
        compiler_params=params(),
        cost_estimate=cost(1),
        name="near_rows",
    )(sources, targets, pair_targets, base, pair_base)
    far = chips - 1
    far_z, far_lse = pl.pallas_call(
        functools.partial(far_kernel, far),
        out_shape=(f32(far, src_count, 2 * tgt_count), f32(far, 1, src_count)),
        in_specs=[VMEM] * (far + 3),
        out_specs=(VMEM,) * 2,
        compiler_params=params(),
        cost_estimate=cost(far),
        name="far_rows",
    )(*far_blocks, targets, pair_targets, offset)

    lse = jnp.concatenate([near_lse, far_lse.reshape(far, src_count)])
    chip = 1
    while chip < chips:
        other = across(lse, chip)
        lse = merge(lse, jnp.stack([other[slot ^ chip] for slot in range(chips)]))
        chip *= 2
    step = 1
    while step < sets:
        lse = merge(lse, along(lse, step))
        step *= 2

    own_part, pair_part, src_potential = pl.pallas_call(
        column_kernel,
        out_shape=(f32(groups, LANES), f32(groups, LANES), f32(1, src_count)),
        in_specs=[VMEM] * 7,
        out_specs=(VMEM,) * 3,
        scratch_shapes=[pltpu.VMEM((chips, src_count, LANES), jnp.float32)],
        compiler_params=params(),
        cost_estimate=cost(chips),
        name="columns",
    )(near_z, far_z, lse, lines[:, 0], lines[:, 1], src_logmass.reshape(1, -1), own_sq.reshape(1, -1))
    columns = merge(own_part, pair(pair_part)).reshape(tgt_count)
    tgt_update = tgt_exponent * (2.0 * tgt_logmass + tgt_potential - columns)
    return (src_potential.reshape(src_count), tgt_update)


def solution(mesh):
    placed = (
        P(("groups", "blk"), None),
        P(("groups", "blk", "tsplit"), None),
        P(("groups", "blk", "tsplit")),
        P(("groups", "blk")),
        P(("groups", "blk", "tsplit")),
        P(("groups", "blk")),
        P(("groups", "blk", "tsplit")),
    )
    return jax.shard_map(
        shards,
        mesh=mesh,
        in_specs=placed,
        out_specs=(P(("groups", "blk")), P(("groups", "blk", "tsplit"))),
        check_vma=False,
    )
```

time: 58.5 us -> 28.3 us (0.48)
  blocking collectives: 34.1 us -> 0 us
  starting transfers between devices: 3.12 us -> 10.4 us
  local copies, waits for them, and re-layouts: 6.55 us -> 2.21 us
  other arithmetic: 1.83 us -> 3.28 us
  Pallas kernels: 4.82 us -> 4.03 us
    all_gather x1 -> x0, blocking collectives: 34.1 us -> none  [shards(): everyone = lax.all_gather(payload, ('blk', 'tsplit'), axis=0, tiled=False)]
    ppermute x3 -> x8, starting transfers between devices: 3.12 us -> 10.4 us  [the longest x3 5.12 us: across(): return lax.ppermute(value, 'blk', [(i, i ^ 2 * chip) for i in range(slabs)])]
    unnamed x26 -> x16, local copies, waits for them, and re-layouts: 6.5 us -> 2.2 us
    reduce_sum x2 -> x1, other arithmetic: 0.12 us -> 1.11 us  [shards(): own_sq = jnp.sum(jnp.square(sources.astype(jnp.float32)), axis=1) / EPSILON]
    pallas_call x3, Pallas kernels: 4.82 us -> 4.03 us  [the longest x1 1.53 us: shards(): pl.pallas_call(column_kernel, out_shape=(f32(groups, LANES), f32(groups,...]
    div x0 -> x1, other arithmetic: none -> 0.75 us  [shards(): own_sq = jnp.sum(jnp.square(sources.astype(jnp.float32)), axis=1) / EPSILON]
    sub x2 -> x0, other arithmetic: 0.71 us -> none  [the longest x1 0.7 us: shards(): shift = src_exponent * (src_logmass + own_sq) + src_logmass - own_sq]
    reshape x0 -> x1, other arithmetic: none -> 0.71 us  [shards(): base = (tgt_potential + tgt_logmass).reshape(groups, LANES)]
  transfers between devices with their start and end apart: 3 -> 8, of which waited for: 1 -> 5; matrix products, arithmetic and copies ran while one was open for 1% -> 9% of each run, Pallas kernels for 2% -> 5%
where the time goes in v2:
time: 28.3 us; the launch traced here: 28 us
  starting transfers between devices  10.4 us (37%)
  waiting for transfers between devices  7.35 us (26%)
  Pallas kernels  4.03 us (14%)
  other arithmetic  3.28 us (12%)
  local copies, waits for them, and re-layouts  2.21 us (8%)
  between operations  0.73 us (3%)
    ppermute x3, starting transfers between devices, across(): return lax.ppermute(value, 'blk', [(i, i ^ 2 * chip) for i in range(slabs)])  5.12 us
    ppermute x2, starting transfers between devices, along(): return lax.ppermute(value, 'tsplit', [(i, i ^ step) for i in range(sets)])  4.74 us
    ppermute x2, waiting for transfers between devices, along(): return lax.ppermute(value, 'tsplit', [(i, i ^ step) for i in range(sets)])  3.44 us
    ppermute x3, waiting for transfers between devices, across(): return lax.ppermute(value, 'blk', [(i, i ^ 2 * chip) for i in range(slabs)])  2.74 us
    unnamed x16, local copies, waits for them, and re-layouts  2.2 us
    pallas_call x1, Pallas kernels, shards(): pl.pallas_call(column_kernel, out_shape=(f32(groups, LANES), f32(groups,...  1.53 us
    pallas_call x1, Pallas kernels, shards(): pl.pallas_call(near_kernel, out_shape=(f32(src_count, 2 * tgt_count), f32...  1.36 us
    ppermute x3, waiting for transfers between devices, pair(): return lax.ppermute(value, 'blk', [(i, i ^ 1) for i in range(slabs)])  1.17 us
  transfers between devices with their start and end apart: 8, of which 5 were waited for; matrix products, arithmetic and copies ran while one was open for 9% of the time, Pallas kernels for 5%

profile of v2, /device:TPU:0, one launch (start us, length us, event | category | flops | bytes accessed | tf_op | source)
XLA Modules:
  0.0 28.0 jit_solution(15747035544913888872)
XLA Ops:
  0.6 0.5 %collective-permute-start = (bf16[1024,512]{1,0:T(8,128)(2,1)}, bf16[1024,512]{1,0:T(8,128)(2,1)S(1)}, u32[]{:S(2)}, u32[]{:S(2)}) collective-permute-start(bf16[1024,512]{1,0:T(8,128)(2,1)} %refs_1_.1), channel_id=1, source_target_pairs={{0,4},{4,0},{8,12},{12,8},{1,5},{5,1},{9,13},{13,9},{2,6},{6,2},{1... | collective-permute-start | bytes 3145736 | tf_op jit(solution)/shard_map/ppermute | solution.py:144
  1.1 0.7 %add_bitcast_fusion.own_base_ref = f32[8,128]{1,0:T(8,128)S(1)} fusion(f32[1024]{0:T(1024)} %param.9, f32[1024]{0:T(1024)} %param.11), kind=kLoop, calls=%fused_computation.7 | loop fusion | flops 1024 | bytes 12288 | tf_op jit(solution)/shard_map/reshape | solution.py:154
  1.9 0.1 collective-permute-start.1
  1.9 3.0 %collective-permute-start.2 = (bf16[256,512]{1,0:T(8,128)(2,1)}, bf16[256,512]{1,0:T(8,128)(2,1)S(1)}, u32[]{:S(2)}, u32[]{:S(2)}) collective-permute-start(bf16[256,512]{1,0:T(8,128)(2,1)} %src_ref.1), channel_id=1, source_target_pairs={{0,8},{4,12},{8,0},{12,4},{1,9},{5,13},{9,1},{13,5},{2,10},{6,14},... | collective-permute-start | bytes 786440 | tf_op jit(solution)/shard_map/ppermute | solution.py:147
  4.9 1.1 %multiply_reduce_fusion = f32[256]{0:T(256)S(1)} fusion(bf16[256,512]{1,0:T(8,128)(2,1)} %src_ref.1), kind=kLoop, calls=%fused_computation | loop fusion | flops 392960 | bytes 263168 | tf_op jit(solution)/shard_map/reduce_sum | solution.py:156
  6.0 0.0 copy-start.3
  6.0 0.8 %broadcast_multiply_fusion = (f32[256]{0:T(256)S(1)}, f32[256]{0:T(256)S(1)}) fusion(f32[256]{0:T(256)S(1)} %multiply_reduce_fusion, f32[256]{0:T(256)} %param.10, f32[256]{0:T(256)} %param.12), kind=kLoop, calls=%fused_computation.25 | loop fusion | flops 1280 | bytes 5120 | tf_op jit(solution)/shard_map/div | solution.py:156
  6.8 1.2 %copy-done = bf16[1024,512]{1,0:T(8,128)(2,1)S(1)} copy-done((bf16[1024,512]{1,0:T(8,128)(2,1)S(1)}, bf16[1024,512]{1,0:T(8,128)(2,1)}, u32[]{:S(2)}) %copy-start) | copy-done | bytes 1048600
  8.0 0.9 %copy-done.2 = bf16[256,512]{1,0:T(8,128)(2,1)S(1)} copy-done((bf16[256,512]{1,0:T(8,128)(2,1)S(1)}, bf16[256,512]{1,0:T(8,128)(2,1)}, u32[]{:S(2)}) %copy-start.2) | copy-done | bytes 262168
  9.0 1.4 %near_rows.1 = (f32[256,2048]{1,0:T(8,128)S(1)}, f32[1,256]{1,0:T(1,128)S(1)}, f32[1,2048]{1,0:T(1,128)S(1)}) custom-call(bf16[256,512]{1,0:T(8,128)(2,1)S(1)} %copy-done.2, bf16[1024,512]{1,0:T(8,128)(2,1)S(1)} %copy-done, bf16[1024,512]{1,0:T(8,128)(2,1)S(1)} %collective-permute-done.pair_ref.refs_2_, f32[8,128]{1,0:T(8,128)S(1)} %add_bitcast_fusion.own_base_ref, ...), custom_call_target="tpu_custom_call" | custom-call | flops 536870912 | bytes 2097152 | tf_op jit(solution)/shard_map/near_rows/pallas_call | solution.py:168
  10.3 1.3 %collective-permute-done.2.refs_0_ = bf16[256,512]{1,0:T(8,128)(2,1)S(1)} collective-permute-done((bf16[256,512]{1,0:T(8,128)(2,1)}, bf16[256,512]{1,0:T(8,128)(2,1)S(1)}, u32[]{:S(2)}, u32[]{:S(2)}) %collective-permute-start.2) | collective-permute-done | bytes 262176 | tf_op jit(solution)/shard_map/ppermute | solution.py:147
  11.6 1.1 %far_rows.1 = (f32[1,256,2048]{2,1,0:T(8,128)S(1)}, f32[1,1,256]{2,1,0:T(1,128)S(1)}) custom-call(bf16[256,512]{1,0:T(8,128)(2,1)S(1)} %collective-permute-done.2.refs_0_, bf16[1024,512]{1,0:T(8,128)(2,1)S(1)} %copy-done.1, bf16[1024,512]{1,0:T(8,128)(2,1)S(1)} %collective-permute-done.pair_ref.refs_2_, f32[1,2048]{1,0:T(1,128)S(1)} %get-tuple-element.11.refs_3_), custom_call_target="tpu_custom_call" | custom-call | flops 536870912 | bytes 2097152 | tf_op jit(solution)/shard_map/far_rows/pallas_call | solution.py:178
  12.7 1.8 %collective-permute-start.3 = (f32[2,256]{1,0:T(2,128)S(1)}, f32[2,256]{1,0:T(2,128)S(1)}, u32[]{:S(2)}, u32[]{:S(2)}) collective-permute-start(f32[2,256]{1,0:T(2,128)S(1)} %pad_maximum_fusion.1), channel_id=1, source_target_pairs={{0,8},{4,12},{8,0},{12,4},{1,9},{5,13},{9,1},{13,5},{2,10},{6,14},... | collective-permute-start | bytes 6152 | tf_op jit(solution)/shard_map/ppermute | solution.py:147
  14.6 0.3 %collective-permute-start.6 = (f32[2,256]{1,0:T(2,128)S(1)}, f32[2,256]{1,0:T(2,128)S(1)}, u32[]{:S(2)}, u32[]{:S(2)}) collective-permute-start(f32[2,256]{1,0:T(2,128)S(1)} %get-tuple-element.20), channel_id=1, source_target_pairs={{0,8},{4,12},{8,0},{12,4},{1,9},{5,13},{9,1},{13,5},{2,10},{6,14},... | collective-permute-start | bytes 6152 | tf_op jit(solution)/shard_map/ppermute | solution.py:147
  14.9 1.5 %collective-permute-done.3 = f32[2,256]{1,0:T(2,128)S(1)} collective-permute-done((f32[2,256]{1,0:T(2,128)S(1)}, f32[2,256]{1,0:T(2,128)S(1)}, u32[]{:S(2)}, u32[]{:S(2)}) %collective-permute-start.3) | collective-permute-done | bytes 2080 | tf_op jit(solution)/shard_map/ppermute | solution.py:147
  16.4 1.9 %collective-permute-start.4 = (f32[2,256]{1,0:T(2,128)S(1)}, f32[2,256]{1,0:T(2,128)S(1)}, u32[]{:S(2)}, u32[]{:S(2)}) collective-permute-start(f32[2,256]{1,0:T(2,128)S(1)} %log_add_fusion.2), channel_id=1, source_target_pairs={{0,1},{1,0},{2,3},{3,2},{4,5},{5,4},{6,7},{7,6},{8,9},{9,8},{10,11... | collective-permute-start | bytes 6152 | tf_op jit(solution)/shard_map/ppermute | solution.py:150
  18.3 1.8 %collective-permute-done.4 = f32[2,256]{1,0:T(2,128)S(1)} collective-permute-done((f32[2,256]{1,0:T(2,128)S(1)}, f32[2,256]{1,0:T(2,128)S(1)}, u32[]{:S(2)}, u32[]{:S(2)}) %collective-permute-start.4) | collective-permute-done | bytes 2080 | tf_op jit(solution)/shard_map/ppermute | solution.py:150
  20.1 2.9 %collective-permute-start.5 = (f32[2,256]{1,0:T(2,128)S(1)}, f32[2,256]{1,0:T(2,128)S(1)}, u32[]{:S(2)}, u32[]{:S(2)}) collective-permute-start(f32[2,256]{1,0:T(2,128)S(1)} %log_add_fusion.1), channel_id=1, source_target_pairs={{0,2},{1,3},{2,0},{3,1},{4,6},{5,7},{6,4},{7,5},{8,10},{9,11},{10,... | collective-permute-start | bytes 6152 | tf_op jit(solution)/shard_map/ppermute | solution.py:150
  23.0 1.7 %collective-permute-done.5 = f32[2,256]{1,0:T(2,128)S(1)} collective-permute-done((f32[2,256]{1,0:T(2,128)S(1)}, f32[2,256]{1,0:T(2,128)S(1)}, u32[]{:S(2)}, u32[]{:S(2)}) %collective-permute-start.5) | collective-permute-done | bytes 2080 | tf_op jit(solution)/shard_map/ppermute | solution.py:150
  24.7 0.0 copy-start.5
  24.7 0.0 copy-start.7
  24.7 1.5 %columns.1 = (f32[8,128]{1,0:T(8,128)S(1)}, f32[8,128]{1,0:T(8,128)S(1)}, f32[1,256]{1,0:T(1,128)}) custom-call(f32[256,2048]{1,0:T(8,128)S(1)} %get-tuple-element.10.near_ref, f32[1,256,2048]{2,1,0:T(8,128)S(1)} %get-tuple-element.12.far_ref, f32[2,256]{1,0:T(2,128)S(1)} %log_add_fusion.lse_ref, f32[2,256]{1,0:T(2,128)S(1)} %get-tuple-element.19.slope_ref, ...), custom_call_target="tpu_custom_call" | custom-call | flops 1073741824 | bytes 2097152 | tf_op jit(solution)/shard_map/columns/pallas_call | solution.py:199
  26.2 1.2 %collective-permute-done.7 = f32[8,128]{1,0:T(8,128)S(1)} collective-permute-done((f32[8,128]{1,0:T(8,128)S(1)}, f32[8,128]{1,0:T(8,128)S(1)}, u32[]{:S(2)}, u32[]{:S(2)}) %collective-permute-start.7) | collective-permute-done | bytes 4128 | tf_op jit(solution)/shard_map/ppermute | solution.py:144
  27.4 0.6 %fusion = f32[1024]{0:T(1024)} fusion(f32[1024]{0:T(1024)S(1)} %copy-done.7, f32[8,128]{1,0:T(8,128)S(1)} %collective-permute-done.7, f32[8,128]{1,0:T(8,128)S(1)} %get-tuple-element.16, f32[1024]{0:T(1024)S(1)} %copy-done.4, f32[1024]{0:T(1024)S(1)} %copy-done.5), kind=kLoop, calls=%fused_computation.4 | loop fusion | flops 9216 | bytes 24576 | tf_op jit(solution)/shard_map/mul | solution.py:210
  (24 shorter events, 0.1 us)
Async XLA Ops:
  0.6 6.1 %collective-permute-start = (bf16[1024,512]{1,0:T(8,128)(2,1)}, bf16[1024,512]{1,0:T(8,128)(2,1)S(1)}, u32[]{:S(2)}, u32[]{:S(2)}) collective-permute-start(bf16[1024,512]{1,0:T(8,128)(2,1)} %refs_1_.1), channel_id=1, source_target_pairs={{0,4},{4,0},{8,12},{12,8},{1,5},{5,1},{9,13},{13,9},{2,6},{6,2},{1... | collective-permute-start | bytes 3145736 | tf_op jit(solution)/shard_map/ppermute | solution.py:144
  1.9 4.9 %collective-permute-start.1 = (f32[8,128]{1,0:T(8,128)S(1)}, f32[8,128]{1,0:T(8,128)S(1)}, u32[]{:S(2)}, u32[]{:S(2)}) collective-permute-start(f32[8,128]{1,0:T(8,128)S(1)} %add_bitcast_fusion.own_base_ref), channel_id=1, source_target_pairs={{0,4},{4,0},{8,12},{12,8},{1,5},{5,1},{9,13},{13,9},{2,6},{6,2},{1... | collective-permute-start | bytes 12296 | tf_op jit(solution)/shard_map/ppermute | solution.py:144
  1.9 9.7 %collective-permute-start.2 = (bf16[256,512]{1,0:T(8,128)(2,1)}, bf16[256,512]{1,0:T(8,128)(2,1)S(1)}, u32[]{:S(2)}, u32[]{:S(2)}) collective-permute-start(bf16[256,512]{1,0:T(8,128)(2,1)} %src_ref.1), channel_id=1, source_target_pairs={{0,8},{4,12},{8,0},{12,4},{1,9},{5,13},{9,1},{13,5},{2,10},{6,14},... | collective-permute-start | bytes 786440 | tf_op jit(solution)/shard_map/ppermute | solution.py:147
  6.0 8.6 %copy-start.6 = (f32[256]{0:T(256)S(1)}, f32[256]{0:T(256)}, u32[]{:S(2)}) copy-start(f32[256]{0:T(256)} %param.12) | copy-start | bytes 3076
  6.0 18.7 %copy-start.3 = (f32[256]{0:T(256)S(1)}, f32[256]{0:T(256)}, u32[]{:S(2)}) copy-start(f32[256]{0:T(256)} %param.10) | copy-start | bytes 3076
  6.8 1.2 %copy-start = (bf16[1024,512]{1,0:T(8,128)(2,1)S(1)}, bf16[1024,512]{1,0:T(8,128)(2,1)}, u32[]{:S(2)}) copy-start(bf16[1024,512]{1,0:T(8,128)(2,1)} %refs_1_.1) | copy-start | bytes 3145732
  8.0 0.9 %copy-start.2 = (bf16[256,512]{1,0:T(8,128)(2,1)S(1)}, bf16[256,512]{1,0:T(8,128)(2,1)}, u32[]{:S(2)}) copy-start(bf16[256,512]{1,0:T(8,128)(2,1)} %src_ref.1) | copy-start | bytes 786436
  9.0 2.6 %copy-start.1 = (bf16[1024,512]{1,0:T(8,128)(2,1)S(1)}, bf16[1024,512]{1,0:T(8,128)(2,1)}, u32[]{:S(2)}) copy-start(bf16[1024,512]{1,0:T(8,128)(2,1)} %refs_1_.1) | copy-start | bytes 3145732
  12.7 3.7 %collective-permute-start.3 = (f32[2,256]{1,0:T(2,128)S(1)}, f32[2,256]{1,0:T(2,128)S(1)}, u32[]{:S(2)}, u32[]{:S(2)}) collective-permute-start(f32[2,256]{1,0:T(2,128)S(1)} %pad_maximum_fusion.1), channel_id=1, source_target_pairs={{0,8},{4,12},{8,0},{12,4},{1,9},{5,13},{9,1},{13,5},{2,10},{6,14},... | collective-permute-start | bytes 6152 | tf_op jit(solution)/shard_map/ppermute | solution.py:147
  14.6 3.7 %collective-permute-start.6 = (f32[2,256]{1,0:T(2,128)S(1)}, f32[2,256]{1,0:T(2,128)S(1)}, u32[]{:S(2)}, u32[]{:S(2)}) collective-permute-start(f32[2,256]{1,0:T(2,128)S(1)} %get-tuple-element.20), channel_id=1, source_target_pairs={{0,8},{4,12},{8,0},{12,4},{1,9},{5,13},{9,1},{13,5},{2,10},{6,14},... | collective-permute-start | bytes 6152 | tf_op jit(solution)/shard_map/ppermute | solution.py:147
  16.4 3.7 %collective-permute-start.4 = (f32[2,256]{1,0:T(2,128)S(1)}, f32[2,256]{1,0:T(2,128)S(1)}, u32[]{:S(2)}, u32[]{:S(2)}) collective-permute-start(f32[2,256]{1,0:T(2,128)S(1)} %log_add_fusion.2), channel_id=1, source_target_pairs={{0,1},{1,0},{2,3},{3,2},{4,5},{5,4},{6,7},{7,6},{8,9},{9,8},{10,11... | collective-permute-start | bytes 6152 | tf_op jit(solution)/shard_map/ppermute | solution.py:150
  20.1 4.5 %collective-permute-start.5 = (f32[2,256]{1,0:T(2,128)S(1)}, f32[2,256]{1,0:T(2,128)S(1)}, u32[]{:S(2)}, u32[]{:S(2)}) collective-permute-start(f32[2,256]{1,0:T(2,128)S(1)} %log_add_fusion.1), channel_id=1, source_target_pairs={{0,2},{1,3},{2,0},{3,1},{4,6},{5,7},{6,4},{7,5},{8,10},{9,11},{10,... | collective-permute-start | bytes 6152 | tf_op jit(solution)/shard_map/ppermute | solution.py:150
  24.7 2.7 %copy-start.4 = (f32[1024]{0:T(1024)S(1)}, f32[1024]{0:T(1024)}, u32[]{:S(2)}) copy-start(f32[1024]{0:T(1024)} %param.9) | copy-start | bytes 12292
  24.7 2.7 %copy-start.5 = (f32[1024]{0:T(1024)S(1)}, f32[1024]{0:T(1024)}, u32[]{:S(2)}) copy-start(f32[1024]{0:T(1024)} %param.11) | copy-start | bytes 12292
  24.7 2.7 %copy-start.7 = (f32[1024]{0:T(1024)S(1)}, f32[1024]{0:T(1024)}, u32[]{:S(2)}) copy-start(f32[1024]{0:T(1024)} %param.13) | copy-start | bytes 12292
  26.2 1.2 %collective-permute-start.7 = (f32[8,128]{1,0:T(8,128)S(1)}, f32[8,128]{1,0:T(8,128)S(1)}, u32[]{:S(2)}, u32[]{:S(2)}) collective-permute-start(f32[8,128]{1,0:T(8,128)S(1)} %get-tuple-element.17), channel_id=1, source_target_pairs={{0,4},{4,0},{8,12},{12,8},{1,5},{5,1},{9,13},{13,9},{2,6},{6,2},{1... | collective-permute-start | bytes 12296 | tf_op jit(solution)/shard_map/ppermute | solution.py:144

commit v3 on v2

v3 whole, which is shorter than its diff:
```python
import functools

import jax
import jax.numpy as jnp
from jax import lax
from jax.experimental import pallas as pl
from jax.experimental.pallas import tpu as pltpu
from jax.sharding import PartitionSpec as P

EPSILON = 0.5
LOGIT_SCALE = 2.0 / EPSILON
LANES = 128
CHUNK = 256
VMEM = pl.BlockSpec(memory_space=pltpu.VMEM)
SMEM = pl.BlockSpec(memory_space=pltpu.SMEM)
HBM = pl.BlockSpec(memory_space=pltpu.HBM)
NT_DIMS = (((1,), (1,)), ((), ()))


def diagonal():
    rows = lax.broadcasted_iota(jnp.int32, (LANES, LANES), 0)
    cols = lax.broadcasted_iota(jnp.int32, (LANES, LANES), 1)
    return rows == cols


def to_lanes(column, eye):
    return jnp.sum(jnp.where(eye, column, 0.0), axis=0, keepdims=True)


def to_column(lanes, eye):
    return jnp.sum(jnp.where(eye, lanes, 0.0), axis=1, keepdims=True)


def fold_rows(value, op):
    return op(value.reshape(value.shape[0] // 8, 8, value.shape[1]), axis=0)


def squares(rows_ref, at):
    rows = rows_ref[at : at + LANES, :].astype(jnp.float32)
    return jnp.sum(rows * rows, axis=1, keepdims=True) / EPSILON


def row_block(rows_ref, tgt_ref, offset_ref, z_ref, eye):
    rows = rows_ref[...] * LOGIT_SCALE
    src_count = rows.shape[0]
    tgt_count = tgt_ref.shape[0]
    peak = None
    for at in range(0, tgt_count, CHUNK):
        cols = slice(at, at + CHUNK)
        dots = lax.dot_general(rows, tgt_ref[cols, :], NT_DIMS, preferred_element_type=jnp.float32)
        z = dots + offset_ref[:, cols]
        z_ref[:, cols] = z
        for lane in range(0, CHUNK, LANES):
            part = z[:, lane : lane + LANES]
            peak = part if peak is None else jnp.maximum(peak, part)
    peak = jnp.max(peak, axis=1, keepdims=True)
    mass = None
    for at in range(0, tgt_count, LANES):
        term = jnp.exp(z_ref[:, at : at + LANES] - peak)
        mass = term if mass is None else mass + term
    mass = jnp.sum(mass, axis=1, keepdims=True)
    parts = [slice(at, at + LANES) for at in range(0, src_count, LANES)]
    return jnp.concatenate([to_lanes(peak[p], eye) + jnp.log(to_lanes(mass[p], eye)) for p in parts], axis=1)


def put_row(held, value, row):
    return jnp.where(lax.broadcasted_iota(jnp.int32, held.shape, 0) == row, value, held)


def prepare_kernel(
    core_ref, src_hbm, tgt_hbm, pot_hbm, mass_hbm, tgt_ref, offset_ref, z_ref, lse_ref, src_ref, pot_ref, mass_ref, sems
):
    copies = [
        pltpu.make_async_copy(source, target, sems.at[at])
        for at, (source, target) in enumerate(
            ((tgt_hbm, tgt_ref), (src_hbm, src_ref), (pot_hbm, pot_ref), (mass_hbm, mass_ref))
        )
    ]
    for copy in copies:
        copy.start()
    for copy in copies:
        copy.wait()
    eye = diagonal()
    for group in range(tgt_ref.shape[0] // LANES):
        at = group * LANES
        base = pot_ref[group : group + 1, :] + mass_ref[group : group + 1, :]
        offset_ref[:, at : at + LANES] = base - to_lanes(squares(tgt_ref, at), eye)
    lse = row_block(src_ref, tgt_ref, offset_ref, z_ref, eye)
    lse_ref[...] = put_row(jnp.zeros(lse_ref.shape, jnp.float32), lse, core_ref[0])


def block_kernel(slot, core_ref, rows_ref, tgt_ref, offset_ref, held_ref, z_ref, lse_ref):
    lse = row_block(rows_ref, tgt_ref, offset_ref, z_ref, diagonal())
    lse_ref[...] = put_row(held_ref[...], lse, slot ^ core_ref[0])


def squares_kernel(count, core_ref, *refs):
    eye = diagonal()
    blocks, out_ref = refs[:count], refs[count]
    out = jnp.zeros(out_ref.shape, jnp.float32)
    for slot, rows_ref in enumerate(blocks):
        row = [to_lanes(squares(rows_ref, at), eye) for at in range(0, rows_ref.shape[0], LANES)]
        out = put_row(out, jnp.concatenate(row, axis=1), slot ^ core_ref[0])
    out_ref[...] = out


def column_kernel(slots, core_ref, *refs):
    eye = diagonal()
    z_refs = refs[:slots]
    lse_ref, slope_ref, logmass_ref, sq_ref, pot_ref, mass_ref, expo_ref, potential_ref, out_ref, off_ref = refs[slots:]
    core = core_ref[0]
    src_count, tgt_count = z_refs[0].shape
    potential = slope_ref[...] * (logmass_ref[...] - (lse_ref[...] - sq_ref[...]))
    mine = lax.broadcasted_iota(jnp.int32, potential.shape, 0) == core
    potential_ref[...] = jnp.sum(jnp.where(mine, potential, 0.0), axis=0, keepdims=True)
    offset = potential + logmass_ref[...] - sq_ref[...]
    for slot in range(slots):
        row = jnp.where(core == 0, offset[slot : slot + 1, :], offset[slot ^ 1 : (slot ^ 1) + 1, :])
        for at in range(0, src_count, LANES):
            column = to_column(row[:, at : at + LANES], eye)
            off_ref[slot, at : at + LANES, :] = jnp.broadcast_to(column, (LANES, LANES))

    for at in range(0, tgt_count, LANES):
        cols = slice(at, at + LANES)
        peak = None
        for slot in range(slots):
            high = fold_rows(z_refs[slot][:, cols] + off_ref[slot], jnp.max)
            peak = high if peak is None else jnp.maximum(peak, high)
        peak = jnp.max(peak, axis=0, keepdims=True)
        mass = None
        for slot in range(slots):
            term = fold_rows(jnp.exp(z_refs[slot][:, cols] + off_ref[slot] - peak), jnp.sum)
            mass = term if mass is None else mass + term
        mass = jnp.sum(mass, axis=0, keepdims=True)
        row = slice(at // LANES, at // LANES + 1)
        out_ref[row, :] = expo_ref[row, :] * (2.0 * mass_ref[row, :] + pot_ref[row, :] - (peak + jnp.log(mass)))


def f32(*shape):
    return jax.ShapeDtypeStruct(shape, jnp.float32)


def params(mebibytes):
    return pltpu.CompilerParams(vmem_limit_bytes=mebibytes * 1024 * 1024)


def merge(*parts):
    peak = functools.reduce(jnp.maximum, parts)
    return peak + jnp.log(sum(jnp.exp(part - peak) for part in parts))


def shards(sources, targets, tgt_potential, src_logmass, tgt_logmass, src_exponent, tgt_exponent):
    src_count, width = sources.shape
    tgt_count = targets.shape[0]
    slabs = lax.axis_size("blk")
    sets = lax.axis_size("tsplit")
    chips = slabs // 2
    groups = tgt_count // LANES
    core = lax.axis_index("blk") & 1
    core_word = core.astype(jnp.int32).reshape(1)
    assert chips > 1 and sets > 1 and chips & (chips - 1) == 0 and sets & (sets - 1) == 0

    def blk(value, flip):
        return lax.ppermute(value, "blk", [(i, i ^ flip) for i in range(slabs)])

    def route(value, parity, flip, step):
        pairs = [
            (b * sets + z, (b ^ flip) * sets + (z ^ step)) for b in range(parity, slabs, 2) for z in range(sets)
        ]
        return lax.ppermute(value, ("blk", "tsplit"), pairs)

    def mirror(value, chip):
        parts = value.reshape(chips, 2, src_count)
        return jnp.concatenate([parts[k ^ chip] for k in range(chips)], axis=0)

    straight = [blk(sources, 2 * chip) for chip in range(1, chips)]
    paired = blk(sources, 1)
    blocks = [sources, paired]
    potential = tgt_potential.reshape(groups, LANES)
    logmass = tgt_logmass.reshape(groups, LANES)
    exponent = tgt_exponent.reshape(groups, LANES)
    block_pairs = src_count * tgt_count
    cost = pl.CostEstimate(flops=2 * block_pairs * width, bytes_accessed=2**20, transcendentals=block_pairs)

    held, offset, z, lse = pl.pallas_call(
        prepare_kernel,
        out_shape=(
            jax.ShapeDtypeStruct(targets.shape, targets.dtype),
            f32(1, tgt_count),
            f32(src_count, tgt_count),
            f32(slabs, src_count),
        ),
        in_specs=[SMEM] + [HBM] * 4,
        out_specs=(VMEM,) * 4,
        scratch_shapes=[
            pltpu.VMEM(sources.shape, sources.dtype),
            pltpu.VMEM((groups, LANES), jnp.float32),
            pltpu.VMEM((groups, LANES), jnp.float32),
            pltpu.SemaphoreType.DMA((4,)),
        ],
        compiler_params=params(12),
        cost_estimate=cost,
        name="prepare",
    )(core_word, *[pltpu.with_memory_space_constraint(x, pltpu.HBM) for x in (sources, targets, potential, logmass)])
    zs = [z]
    lse, src_slope, src_mass = lax.optimization_barrier((lse, src_exponent, src_logmass))
    line = jnp.stack([src_slope, src_mass])
    line = jnp.where(core == 0, jnp.stack([line, blk(line, 1)]), jnp.stack([blk(line, 1), line]))
    lines = jnp.concatenate([line] + [blk(line, 2 * chip) for chip in range(1, chips)])
    for slot in range(1, slabs):
        if slot == slabs - 1:
            lse, lines = lax.optimization_barrier((lse, lines))
        z, lse = pl.pallas_call(
            functools.partial(block_kernel, slot),
            out_shape=(f32(src_count, tgt_count), f32(slabs, src_count)),
            in_specs=[SMEM] + [VMEM] * 4,
            out_specs=(VMEM,) * 2,
            compiler_params=params(12),
            cost_estimate=cost,
            name=f"rows_{slot}",
        )(core_word, blocks[slot], held, offset, lse)
        zs.append(z)
        if slot == 1:
            lse, *straight = lax.optimization_barrier((lse, *straight))
            for block in straight:
                blocks += [block, blk(block, 1)]
    src_sq = pl.pallas_call(
        functools.partial(squares_kernel, slabs),
        out_shape=f32(slabs, src_count),
        in_specs=[SMEM] + [VMEM] * slabs,
        out_specs=VMEM,
        compiler_params=params(12),
        cost_estimate=pl.CostEstimate(flops=slabs * src_count * width, bytes_accessed=2**20, transcendentals=0),
        name="source_squares",
    )(core_word, *blocks)

    lse = merge(lse, route(lse, 0, 1, 0), mirror(route(lse, 1, 2, 0), 1), mirror(route(lse, 0, 3, 0), 1))
    chip = 2
    while chip < chips:
        lse = merge(lse, mirror(route(lse, 1, 2 * chip, 0), chip))
        chip *= 2
    step = 1
    while 2 * step < sets:
        lse = merge(lse, route(lse, 1, 0, step))
        step *= 2
    here, there, direct = route(lse, 1, 1, 0), route(lse, 1, 1, step), route(lse, 1, 0, step)
    lse = merge(jnp.where(core == 0, here, lse), jnp.where(core == 0, there, direct))

    src_potential, tgt_update = pl.pallas_call(
        functools.partial(column_kernel, slabs),
        out_shape=(f32(1, src_count), f32(groups, LANES)),
        in_specs=[SMEM] + [VMEM] * (slabs + 7),
        out_specs=(VMEM,) * 2,
        scratch_shapes=[pltpu.VMEM((slabs, src_count, LANES), jnp.float32)],
        compiler_params=params(8 + 2 * slabs),
        cost_estimate=pl.CostEstimate(
            flops=6 * slabs * block_pairs, bytes_accessed=2**20, transcendentals=slabs * block_pairs
        ),
        name="columns",
    )(core_word, *zs, lse, lines[:, 0], lines[:, 1], src_sq, potential, logmass, exponent)
    return (src_potential.reshape(src_count), tgt_update.reshape(tgt_count))


def solution(mesh):
    placed = (
        P(("groups", "blk"), None),
        P(("groups", "blk", "tsplit"), None),
        P(("groups", "blk", "tsplit")),
        P(("groups", "blk")),
        P(("groups", "blk", "tsplit")),
        P(("groups", "blk")),
        P(("groups", "blk", "tsplit")),
    )
    return jax.shard_map(
        shards,
        mesh=mesh,
        in_specs=placed,
        out_specs=(P(("groups", "blk")), P(("groups", "blk", "tsplit"))),
        check_vma=False,
    )
```

time: 28.3 us -> 41.9 us (1.48)
  waiting for transfers between devices: 7.35 us -> 14.7 us
  Pallas kernels: 4.03 us -> 9.09 us
  starting transfers between devices: 10.4 us -> 15.1 us
  other arithmetic: 3.28 us -> 0.09 us
  local copies, waits for them, and re-layouts: 2.21 us -> 1.4 us
    ppermute x8 -> x12, waiting for transfers between devices: 7.35 us -> 14.7 us  [the longest x7 7.62 us: route(): return lax.ppermute(value, ('blk', 'tsplit'), pairs)]
    pallas_call x3 -> x6, Pallas kernels: 4.03 us -> 9.09 us  [the longest x3 4.08 us: shards(): pl.pallas_call(functools.partial(block_kernel, slot), out_shape=(f32(src_...]
    ppermute x8 -> x12, starting transfers between devices: 10.4 us -> 15.1 us  [the longest x7 9.68 us: route(): return lax.ppermute(value, ('blk', 'tsplit'), pairs)]
    reduce_sum x1 -> x0, other arithmetic: 1.11 us -> none  [shards(): own_sq = jnp.sum(jnp.square(sources.astype(jnp.float32)), axis=1) / EPSILON]
    unnamed x16 -> x12, local copies, waits for them, and re-layouts: 2.2 us -> 1.39 us
    div x1 -> x0, other arithmetic: 0.75 us -> none  [shards(): own_sq = jnp.sum(jnp.square(sources.astype(jnp.float32)), axis=1) / EPSILON]
    reshape x1 -> x0, other arithmetic: 0.71 us -> none  [shards(): base = (tgt_potential + tgt_logmass).reshape(groups, LANES)]
    mul x1 -> x0, other arithmetic: 0.62 us -> none  [shards(): tgt_update = tgt_exponent * (2.0 * tgt_logmass + tgt_potential - columns)]
  transfers between devices with their start and end apart: 8 -> 12, of which waited for: 5 -> 6; matrix products, arithmetic and copies ran while one was open for 9% -> 0% of each run, Pallas kernels for 5% -> 14%
where the time goes in v3:
time: 41.9 us; the launch traced here: 41.2 us
  starting transfers between devices  15.1 us (36%)
  waiting for transfers between devices  14.7 us (35%)
  Pallas kernels  9.09 us (22%)
  local copies, waits for them, and re-layouts  1.4 us (3%)
  between operations  0.84 us (2%)
    ppermute x7, starting transfers between devices, route(): return lax.ppermute(value, ('blk', 'tsplit'), pairs)  9.68 us
    ppermute x7, waiting for transfers between devices, route(): return lax.ppermute(value, ('blk', 'tsplit'), pairs)  7.62 us
    ppermute x5, waiting for transfers between devices, blk(): return lax.ppermute(value, 'blk', [(i, i ^ flip) for i in range(slabs)])  7.04 us
    ppermute x5, starting transfers between devices, blk(): return lax.ppermute(value, 'blk', [(i, i ^ flip) for i in range(slabs)])  5.44 us
    pallas_call x3, Pallas kernels, shards(): pl.pallas_call(functools.partial(block_kernel, slot), out_shape=(f32(src_...  4.08 us
    pallas_call x1, Pallas kernels, shards(): pl.pallas_call(prepare_kernel, out_shape=(jax.ShapeDtypeStruct(targets.sh...  2.09 us
    pallas_call x1, Pallas kernels, shards(): pl.pallas_call(functools.partial(column_kernel, slabs), out_shape=(f32(1,...  1.61 us
    unnamed x12, local copies, waits for them, and re-layouts  1.39 us
  transfers between devices with their start and end apart: 12, of which 6 were waited for; matrix products, arithmetic and copies ran while one was open for 0% of the time, Pallas kernels for 14%

profile of v3, /device:TPU:0, one launch (start us, length us, event | category | flops | bytes accessed | tf_op | source)
XLA Modules:
  0.0 41.2 jit_solution(9521273561629288560)
XLA Ops:
  0.6 0.5 %collective-permute-start = (bf16[256,512]{1,0:T(8,128)(2,1)}, bf16[256,512]{1,0:T(8,128)(2,1)S(1)}, u32[]{:S(2)}, u32[]{:S(2)}) collective-permute-start(bf16[256,512]{1,0:T(8,128)(2,1)} %refs_0_.1), channel_id=1, source_target_pairs={{0,4},{4,0},{8,12},{12,8},{1,5},{5,1},{9,13},{13,9},{2,6},{6,2},{1... | collective-permute-start | bytes 786440 | tf_op jit(solution)/shard_map/ppermute | solution.py:164
  1.1 2.6 %collective-permute-start.1 = (bf16[256,512]{1,0:T(8,128)(2,1)}, bf16[256,512]{1,0:T(8,128)(2,1)}, u32[]{:S(2)}, u32[]{:S(2)}) collective-permute-start(bf16[256,512]{1,0:T(8,128)(2,1)} %refs_0_.1), channel_id=1, source_target_pairs={{0,8},{4,12},{8,0},{12,4},{1,9},{5,13},{9,1},{13,5},{2,10},{6,14},... | collective-permute-start | bytes 786440 | tf_op jit(solution)/shard_map/ppermute | solution.py:164
  3.7 2.1 %prepare.1 = (bf16[1024,512]{1,0:T(8,128)(2,1)S(1)}, f32[1,1024]{1,0:T(1,128)S(1)}, f32[256,1024]{1,0:T(8,128)S(1)}, f32[4,256]{1,0:T(4,128)S(1)}) custom-call(s32[1]{0:T(128)} %bitcast.core_ref, bf16[256,512]{1,0:T(8,128)(2,1)} %refs_0_.1, bf16[1024,512]{1,0:T(8,128)(2,1)} %tgt_hbm.1, f32[8,128]{1,0:T(8,128)} %bitcast.12, f32[8,128]{1,0:T(8,128)} %bitcast.14), custom_call_target="tpu_custom_call" | custom-call | flops 268435456 | bytes 1048576 | tf_op jit(solution)/shard_map/prepare/pallas_call | solution.py:185
  5.9 0.7 %rows_1.1 = (f32[256,1024]{1,0:T(8,128)S(1)}, f32[4,256]{1,0:T(4,128)S(1)}) custom-call(s32[1]{0:T(128)} %bitcast.core_ref, bf16[256,512]{1,0:T(8,128)(2,1)S(1)} %collective-permute-done.rows_ref.refs_1_, bf16[1024,512]{1,0:T(8,128)(2,1)S(1)} %get-tuple-element.22.tgt_ref, f32[1,1024]{1,0:T(1,128)S(1)} %get-tuple-element.23.offset_ref, ...), custom_call_target="tpu_custom_call" | custom-call | flops 268435456 | bytes 1048576 | tf_op jit(solution)/shard_map/rows_1/pallas_call | solution.py:213
  6.6 4.4 %collective-permute-done.1.rows_ref.refs_2_ = bf16[256,512]{1,0:T(8,128)(2,1)} collective-permute-done((bf16[256,512]{1,0:T(8,128)(2,1)}, bf16[256,512]{1,0:T(8,128)(2,1)}, u32[]{:S(2)}, u32[]{:S(2)}) %collective-permute-start.1) | collective-permute-done | bytes 262176 | tf_op jit(solution)/shard_map/ppermute | solution.py:164
  11.0 0.7 %copy-done.4 = f32[256]{0:T(256)S(1)} copy-done((f32[256]{0:T(256)S(1)}, f32[256]{0:T(256)}, u32[]{:S(2)}) %copy-start.4) | copy-done | bytes 1048
  12.2 0.8 %collective-permute-done.3 = f32[2,256]{1,0:T(2,128)S(1)} collective-permute-done((f32[2,256]{1,0:T(2,128)S(1)}, f32[2,256]{1,0:T(2,128)S(1)}, u32[]{:S(2)}, u32[]{:S(2)}) %collective-permute-start.3) | collective-permute-done | bytes 2080 | tf_op jit(solution)/shard_map/ppermute | solution.py:164
  13.0 1.8 %collective-permute-start.4 = (f32[2,2,256]{2,0,1:T(2,128)S(1)}, f32[2,2,256]{2,0,1:T(2,128)S(1)}, u32[]{:S(2)}, u32[]{:S(2)}) collective-permute-start(f32[2,2,256]{2,0,1:T(2,128)S(1)} %maximum_select_fusion), channel_id=1, source_target_pairs={{0,8},{4,12},{8,0},{12,4},{1,9},{5,13},{9,1},{13,5},{2,10},{6,14},... | collective-permute-start | bytes 12296 | tf_op jit(solution)/shard_map/ppermute | solution.py:164
  14.8 1.8 %collective-permute-done.4 = f32[2,2,256]{2,0,1:T(2,128)S(1)} collective-permute-done((f32[2,2,256]{2,0,1:T(2,128)S(1)}, f32[2,2,256]{2,0,1:T(2,128)S(1)}, u32[]{:S(2)}, u32[]{:S(2)}) %collective-permute-start.4) | collective-permute-done | bytes 4128 | tf_op jit(solution)/shard_map/ppermute | solution.py:164
  16.7 1.7 %rows_2.1 = (f32[256,1024]{1,0:T(8,128)S(1)}, f32[4,256]{1,0:T(4,128)S(1)}) custom-call(s32[1]{0:T(128)} %bitcast.core_ref, bf16[256,512]{1,0:T(8,128)(2,1)} %collective-permute-done.1.rows_ref.refs_2_, bf16[1024,512]{1,0:T(8,128)(2,1)S(1)} %get-tuple-element.22.tgt_ref, f32[1,1024]{1,0:T(1,128)S(1)} %get-tuple-element.23.offset_ref, ...), custom_call_target="tpu_custom_call" | custom-call | flops 268435456 | bytes 1048576 | tf_op jit(solution)/shard_map/rows_2/pallas_call | solution.py:213
  18.4 1.7 %rows_3.1 = (f32[256,1024]{1,0:T(8,128)S(1)}, f32[4,256]{1,0:T(4,128)S(1)}) custom-call(s32[1]{0:T(128)} %bitcast.core_ref, bf16[256,512]{1,0:T(8,128)(2,1)} %collective-permute-done.2.rows_ref.refs_3_, bf16[1024,512]{1,0:T(8,128)(2,1)S(1)} %get-tuple-element.22.tgt_ref, f32[1,1024]{1,0:T(1,128)S(1)} %get-tuple-element.23.offset_ref, ...), custom_call_target="tpu_custom_call" | custom-call | flops 268435456 | bytes 1048576 | tf_op jit(solution)/shard_map/rows_3/pallas_call | solution.py:213
  20.1 2.5 %collective-permute-start.7 = (f32[4,256]{1,0:T(4,128)S(1)}, f32[4,256]{1,0:T(4,128)S(1)}, u32[]{:S(2)}, u32[]{:S(2)}) collective-permute-start(f32[4,256]{1,0:T(4,128)S(1)} %get-tuple-element.36), channel_id=1, source_target_pairs={{0,12},{1,13},{2,14},{3,15},{8,4},{9,5},{10,6},{11,7},{16,28},{17,... | collective-permute-start | bytes 12296 | tf_op jit(solution)/shard_map/ppermute | solution.py:170
  22.5 0.7 %collective-permute-start.6 = (f32[4,256]{1,0:T(4,128)S(1)}, f32[4,256]{1,0:T(4,128)S(1)}, u32[]{:S(2)}, u32[]{:S(2)}) collective-permute-start(f32[4,256]{1,0:T(4,128)S(1)} %get-tuple-element.36), channel_id=1, source_target_pairs={{4,12},{5,13},{6,14},{7,15},{12,4},{13,5},{14,6},{15,7},{20,28},{2... | collective-permute-start | bytes 12296 | tf_op jit(solution)/shard_map/ppermute | solution.py:170
  23.2 2.7 %collective-permute-start.5 = (f32[4,256]{1,0:T(4,128)S(1)}, f32[4,256]{1,0:T(4,128)S(1)}, u32[]{:S(2)}, u32[]{:S(2)}) collective-permute-start(f32[4,256]{1,0:T(4,128)S(1)} %get-tuple-element.36), channel_id=1, source_target_pairs={{0,4},{1,5},{2,6},{3,7},{8,12},{9,13},{10,14},{11,15},{16,20},{17,... | collective-permute-start | bytes 12296 | tf_op jit(solution)/shard_map/ppermute | solution.py:170
  25.9 0.8 %collective-permute-done.5 = f32[4,256]{1,0:T(4,128)S(1)} collective-permute-done((f32[4,256]{1,0:T(4,128)S(1)}, f32[4,256]{1,0:T(4,128)S(1)}, u32[]{:S(2)}, u32[]{:S(2)}) %collective-permute-start.5) | collective-permute-done | bytes 4128 | tf_op jit(solution)/shard_map/ppermute | solution.py:170
  26.7 0.7 %collective-permute-start.8 = (f32[4,256]{1,0:T(4,128)S(1)}, f32[4,256]{1,0:T(4,128)S(1)}, u32[]{:S(2)}, u32[]{:S(2)}) collective-permute-start(f32[4,256]{1,0:T(4,128)S(1)} %log_add_fusion.2), channel_id=1, source_target_pairs={{4,5},{5,4},{6,7},{7,6},{12,13},{13,12},{14,15},{15,14},{20,21},{2... | collective-permute-start | bytes 12296 | tf_op jit(solution)/shard_map/ppermute | solution.py:170
  27.4 0.7 %collective-permute-start.11 = (f32[4,256]{1,0:T(4,128)S(1)}, f32[4,256]{1,0:T(4,128)S(1)}, u32[]{:S(2)}, u32[]{:S(2)}) collective-permute-start(f32[4,256]{1,0:T(4,128)S(1)} %log_add_fusion.1), channel_id=1, source_target_pairs={{4,6},{5,7},{6,4},{7,5},{12,14},{13,15},{14,12},{15,13},{20,22},{2... | collective-permute-start | bytes 12296 | tf_op jit(solution)/shard_map/ppermute | solution.py:170
  28.1 1.3 %collective-permute-start.10 = (f32[4,256]{1,0:T(4,128)S(1)}, f32[4,256]{1,0:T(4,128)S(1)}, u32[]{:S(2)}, u32[]{:S(2)}) collective-permute-start(f32[4,256]{1,0:T(4,128)S(1)} %log_add_fusion.1), channel_id=1, source_target_pairs={{4,2},{5,3},{6,0},{7,1},{12,10},{13,11},{14,8},{15,9},{20,18},{21,... | collective-permute-start | bytes 12296 | tf_op jit(solution)/shard_map/ppermute | solution.py:170
  29.4 1.3 %collective-permute-start.9 = (f32[4,256]{1,0:T(4,128)S(1)}, f32[4,256]{1,0:T(4,128)S(1)}, u32[]{:S(2)}, u32[]{:S(2)}) collective-permute-start(f32[4,256]{1,0:T(4,128)S(1)} %log_add_fusion.1), channel_id=1, source_target_pairs={{4,0},{5,1},{6,2},{7,3},{12,8},{13,9},{14,10},{15,11},{20,16},{21,... | collective-permute-start | bytes 12296 | tf_op jit(solution)/shard_map/ppermute | solution.py:170
  30.7 1.3 %source_squares.1.refs_7_ = f32[4,256]{1,0:T(4,128)S(1)} custom-call(s32[1]{0:T(128)} %bitcast.core_ref, bf16[256,512]{1,0:T(8,128)(2,1)S(1)} %copy-done, bf16[256,512]{1,0:T(8,128)(2,1)S(1)} %collective-permute-done.rows_ref.refs_1_, bf16[256,512]{1,0:T(8,128)(2,1)} %collective-permute-done.1.rows_ref.refs_2_, ...), custom_call_target="tpu_custom_call" | custom-call | flops 524288 | bytes 1048576 | tf_op jit(solution)/shard_map/source_squares/pallas_call | solution.py:227
  32.0 6.1 %collective-permute-done.10 = f32[4,256]{1,0:T(4,128)S(1)} collective-permute-done((f32[4,256]{1,0:T(4,128)S(1)}, f32[4,256]{1,0:T(4,128)S(1)}, u32[]{:S(2)}, u32[]{:S(2)}) %collective-permute-start.10) | collective-permute-done | bytes 4128 | tf_op jit(solution)/shard_map/ppermute | solution.py:170
  38.1 0.7 %collective-permute-done.9 = f32[4,256]{1,0:T(4,128)S(1)} collective-permute-done((f32[4,256]{1,0:T(4,128)S(1)}, f32[4,256]{1,0:T(4,128)S(1)}, u32[]{:S(2)}, u32[]{:S(2)}) %collective-permute-start.9) | collective-permute-done | bytes 4128 | tf_op jit(solution)/shard_map/ppermute | solution.py:170
  38.9 0.7 %copy-done.3 = f32[1024]{0:T(1024)S(1)} copy-done((f32[1024]{0:T(1024)S(1)}, f32[1024]{0:T(1024)}, u32[]{:S(2)}) %copy-start.3) | copy-done | bytes 4120
  39.6 1.6 %columns.1 = (f32[1,256]{1,0:T(1,128)}, f32[8,128]{1,0:T(8,128)}) custom-call(s32[1]{0:T(128)} %bitcast.core_ref, f32[256,1024]{1,0:T(8,128)S(1)} %get-tuple-element.21.refs_0_, f32[256,1024]{1,0:T(8,128)S(1)} %get-tuple-element.26.refs_1_, f32[256,1024]{1,0:T(8,128)S(1)} %get-tuple-element.30.refs_2_, f32[256,1024]{1,0:T(8,128)S(1)} %get-tuple-element.35.refs_3_, ...), custom_call_target="tpu_custom_call" | custom-call | flops 6291456 | bytes 1048576 | tf_op jit(solution)/shard_map/columns/pallas_call | solution.py:249
  (29 shorter events, 0.7 us)
Async XLA Ops:
  0.6 5.2 %collective-permute-start = (bf16[256,512]{1,0:T(8,128)(2,1)}, bf16[256,512]{1,0:T(8,128)(2,1)S(1)}, u32[]{:S(2)}, u32[]{:S(2)}) collective-permute-start(bf16[256,512]{1,0:T(8,128)(2,1)} %refs_0_.1), channel_id=1, source_target_pairs={{0,4},{4,0},{8,12},{12,8},{1,5},{5,1},{9,13},{13,9},{2,6},{6,2},{1... | collective-permute-start | bytes 786440 | tf_op jit(solution)/shard_map/ppermute | solution.py:164
  1.1 9.8 %collective-permute-start.1 = (bf16[256,512]{1,0:T(8,128)(2,1)}, bf16[256,512]{1,0:T(8,128)(2,1)}, u32[]{:S(2)}, u32[]{:S(2)}) collective-permute-start(bf16[256,512]{1,0:T(8,128)(2,1)} %refs_0_.1), channel_id=1, source_target_pairs={{0,8},{4,12},{8,0},{12,4},{1,9},{5,13},{9,1},{13,5},{2,10},{6,14},... | collective-permute-start | bytes 786440 | tf_op jit(solution)/shard_map/ppermute | solution.py:164
  5.9 5.1 %copy-start.5 = (f32[256]{0:T(256)S(1)}, f32[256]{0:T(256)}, u32[]{:S(2)}) copy-start(f32[256]{0:T(256)} %param.12) | copy-start | bytes 3076
  11.0 7.4 %collective-permute-start.2 = (bf16[256,512]{1,0:T(8,128)(2,1)}, bf16[256,512]{1,0:T(8,128)(2,1)}, u32[]{:S(2)}, u32[]{:S(2)}) collective-permute-start(bf16[256,512]{1,0:T(8,128)(2,1)} %collective-permute-done.1.rows_ref.refs_2_), channel_id=1, source_target_pairs={{0,4},{4,0},{8,12},{12,8},{1,5},{5,1},{9,13},{13,9},{2,6},{6,2},{1... | collective-permute-start | bytes 786440 | tf_op jit(solution)/shard_map/ppermute | solution.py:164
  11.0 0.7 %copy-start.4 = (f32[256]{0:T(256)S(1)}, f32[256]{0:T(256)}, u32[]{:S(2)}) copy-start(f32[256]{0:T(256)} %param.10) | copy-start | bytes 3076
  11.6 1.3 %collective-permute-start.3 = (f32[2,256]{1,0:T(2,128)S(1)}, f32[2,256]{1,0:T(2,128)S(1)}, u32[]{:S(2)}, u32[]{:S(2)}) collective-permute-start(f32[2,256]{1,0:T(2,128)S(1)} %pad_maximum_fusion.3), channel_id=1, source_target_pairs={{0,4},{4,0},{8,12},{12,8},{1,5},{5,1},{9,13},{13,9},{2,6},{6,2},{1... | collective-permute-start | bytes 6152 | tf_op jit(solution)/shard_map/ppermute | solution.py:164
  13.0 3.7 %collective-permute-start.4 = (f32[2,2,256]{2,0,1:T(2,128)S(1)}, f32[2,2,256]{2,0,1:T(2,128)S(1)}, u32[]{:S(2)}, u32[]{:S(2)}) collective-permute-start(f32[2,2,256]{2,0,1:T(2,128)S(1)} %maximum_select_fusion), channel_id=1, source_target_pairs={{0,8},{4,12},{8,0},{12,4},{1,9},{5,13},{9,1},{13,5},{2,10},{6,14},... | collective-permute-start | bytes 12296 | tf_op jit(solution)/shard_map/ppermute | solution.py:164
  18.3 12.3 %copy-start = (bf16[256,512]{1,0:T(8,128)(2,1)S(1)}, bf16[256,512]{1,0:T(8,128)(2,1)}, u32[]{:S(2)}) copy-start(bf16[256,512]{1,0:T(8,128)(2,1)} %refs_0_.1) | copy-start | bytes 786436
  20.1 5.8 %collective-permute-start.7 = (f32[4,256]{1,0:T(4,128)S(1)}, f32[4,256]{1,0:T(4,128)S(1)}, u32[]{:S(2)}, u32[]{:S(2)}) collective-permute-start(f32[4,256]{1,0:T(4,128)S(1)} %get-tuple-element.36), channel_id=1, source_target_pairs={{0,12},{1,13},{2,14},{3,15},{8,4},{9,5},{10,6},{11,7},{16,28},{17,... | collective-permute-start | bytes 12296 | tf_op jit(solution)/shard_map/ppermute | solution.py:170
  22.5 3.4 %collective-permute-start.6 = (f32[4,256]{1,0:T(4,128)S(1)}, f32[4,256]{1,0:T(4,128)S(1)}, u32[]{:S(2)}, u32[]{:S(2)}) collective-permute-start(f32[4,256]{1,0:T(4,128)S(1)} %get-tuple-element.36), channel_id=1, source_target_pairs={{4,12},{5,13},{6,14},{7,15},{12,4},{13,5},{14,6},{15,7},{20,28},{2... | collective-permute-start | bytes 12296 | tf_op jit(solution)/shard_map/ppermute | solution.py:170
  23.2 3.5 %collective-permute-start.5 = (f32[4,256]{1,0:T(4,128)S(1)}, f32[4,256]{1,0:T(4,128)S(1)}, u32[]{:S(2)}, u32[]{:S(2)}) collective-permute-start(f32[4,256]{1,0:T(4,128)S(1)} %get-tuple-element.36), channel_id=1, source_target_pairs={{0,4},{1,5},{2,6},{3,7},{8,12},{9,13},{10,14},{11,15},{16,20},{17,... | collective-permute-start | bytes 12296 | tf_op jit(solution)/shard_map/ppermute | solution.py:170
  26.7 0.7 %collective-permute-start.8 = (f32[4,256]{1,0:T(4,128)S(1)}, f32[4,256]{1,0:T(4,128)S(1)}, u32[]{:S(2)}, u32[]{:S(2)}) collective-permute-start(f32[4,256]{1,0:T(4,128)S(1)} %log_add_fusion.2), channel_id=1, source_target_pairs={{4,5},{5,4},{6,7},{7,6},{12,13},{13,12},{14,15},{15,14},{20,21},{2... | collective-permute-start | bytes 12296 | tf_op jit(solution)/shard_map/ppermute | solution.py:170
  27.4 4.6 %collective-permute-start.11 = (f32[4,256]{1,0:T(4,128)S(1)}, f32[4,256]{1,0:T(4,128)S(1)}, u32[]{:S(2)}, u32[]{:S(2)}) collective-permute-start(f32[4,256]{1,0:T(4,128)S(1)} %log_add_fusion.1), channel_id=1, source_target_pairs={{4,6},{5,7},{6,4},{7,5},{12,14},{13,15},{14,12},{15,13},{20,22},{2... | collective-permute-start | bytes 12296 | tf_op jit(solution)/shard_map/ppermute | solution.py:170
  28.1 10.1 %collective-permute-start.10 = (f32[4,256]{1,0:T(4,128)S(1)}, f32[4,256]{1,0:T(4,128)S(1)}, u32[]{:S(2)}, u32[]{:S(2)}) collective-permute-start(f32[4,256]{1,0:T(4,128)S(1)} %log_add_fusion.1), channel_id=1, source_target_pairs={{4,2},{5,3},{6,0},{7,1},{12,10},{13,11},{14,8},{15,9},{20,18},{21,... | collective-permute-start | bytes 12296 | tf_op jit(solution)/shard_map/ppermute | solution.py:170
  29.4 9.5 %collective-permute-start.9 = (f32[4,256]{1,0:T(4,128)S(1)}, f32[4,256]{1,0:T(4,128)S(1)}, u32[]{:S(2)}, u32[]{:S(2)}) collective-permute-start(f32[4,256]{1,0:T(4,128)S(1)} %log_add_fusion.1), channel_id=1, source_target_pairs={{4,0},{5,1},{6,2},{7,3},{12,8},{13,9},{14,10},{15,11},{20,16},{21,... | collective-permute-start | bytes 12296 | tf_op jit(solution)/shard_map/ppermute | solution.py:170
  38.9 0.7 %copy-start.3 = (f32[1024]{0:T(1024)S(1)}, f32[1024]{0:T(1024)}, u32[]{:S(2)}) copy-start(f32[1024]{0:T(1024)} %param.13) | copy-start | bytes 12292
  38.9 0.7 %copy-start.2 = (f32[1024]{0:T(1024)S(1)}, f32[1024]{0:T(1024)}, u32[]{:S(2)}) copy-start(f32[1024]{0:T(1024)} %param.11) | copy-start | bytes 12292
  38.9 0.7 %copy-start.1 = (f32[1024]{0:T(1024)S(1)}, f32[1024]{0:T(1024)}, u32[]{:S(2)}) copy-start(f32[1024]{0:T(1024)} %param.9) | copy-start | bytes 12292

commit v4 on v2

v4 whole, which is shorter than its diff:
```python
import functools

import jax
import jax.numpy as jnp
from jax import lax
from jax.experimental import pallas as pl
from jax.experimental.pallas import tpu as pltpu
from jax.sharding import PartitionSpec as P

EPSILON = 0.5
LOGIT_SCALE = 2.0 / EPSILON
LANES = 128
CHUNK = 256
VMEM = pl.BlockSpec(memory_space=pltpu.VMEM)
HBM = pl.BlockSpec(memory_space=pltpu.HBM)
NT_DIMS = (((1,), (1,)), ((), ()))


def diagonal():
    rows = lax.broadcasted_iota(jnp.int32, (LANES, LANES), 0)
    cols = lax.broadcasted_iota(jnp.int32, (LANES, LANES), 1)
    return rows == cols


def to_lanes(column, eye):
    return jnp.sum(jnp.where(eye, column, 0.0), axis=0, keepdims=True)


def to_column(lanes, eye):
    return jnp.sum(jnp.where(eye, lanes, 0.0), axis=1, keepdims=True)


def fold_rows(value, op):
    return op(value.reshape(value.shape[0] // 8, 8, value.shape[1]), axis=0)


def merge(*parts):
    peak = functools.reduce(jnp.maximum, parts)
    return peak + jnp.log(sum(jnp.exp(part - peak) for part in parts))


def squares(rows_ref, at):
    rows = rows_ref[at : at + LANES, :].astype(jnp.float32)
    return jnp.sum(rows * rows, axis=1, keepdims=True) / EPSILON


def row_block(rows_ref, sides, eye):
    rows = rows_ref[...] * LOGIT_SCALE
    src_count = rows.shape[0]
    peak = None
    for tgt_ref, offset_ref, z_ref in sides:
        for at in range(0, tgt_ref.shape[0], CHUNK):
            cols = slice(at, at + CHUNK)
            dots = lax.dot_general(rows, tgt_ref[cols, :], NT_DIMS, preferred_element_type=jnp.float32)
            z = dots + offset_ref[:, cols]
            z_ref[:, cols] = z
            for lane in range(0, CHUNK, LANES):
                part = z[:, lane : lane + LANES]
                peak = part if peak is None else jnp.maximum(peak, part)
    peak = jnp.max(peak, axis=1, keepdims=True)
    mass = None
    for _, _, z_ref in sides:
        for at in range(0, z_ref.shape[1], LANES):
            term = jnp.exp(z_ref[:, at : at + LANES] - peak)
            mass = term if mass is None else mass + term
    mass = jnp.sum(mass, axis=1, keepdims=True)
    parts = [slice(at, at + LANES) for at in range(0, src_count, LANES)]
    return jnp.concatenate([to_lanes(peak[p], eye) + jnp.log(to_lanes(mass[p], eye)) for p in parts], axis=1)


def prepare_kernel(
    src_hbm, tgt_hbm, pot_hbm, mass_hbm, slope_hbm, logmass_hbm,
    tgt_ref, offset_ref, z_ref, lse_ref, line_ref, sq_ref,
    src_ref, pot_ref, mass_ref, slope_ref, logmass_ref, sems,
):
    pairs = (
        (tgt_hbm, tgt_ref), (src_hbm, src_ref), (pot_hbm, pot_ref),
        (mass_hbm, mass_ref), (slope_hbm, slope_ref), (logmass_hbm, logmass_ref),
    )
    copies = [pltpu.make_async_copy(source, target, sems.at[at]) for at, (source, target) in enumerate(pairs)]
    for copy in copies:
        copy.start()
    for copy in copies[1:]:
        copy.wait()
    eye = diagonal()
    for group in range(src_ref.shape[0] // LANES):
        cols = slice(group * LANES, (group + 1) * LANES)
        square = to_lanes(squares(src_ref, group * LANES), eye)
        slope = slope_ref[group : group + 1, :]
        logmass = logmass_ref[group : group + 1, :]
        sq_ref[:, cols] = logmass + square
        line_ref[0:1, cols] = slope
        line_ref[1:2, cols] = slope * (logmass + square) + (logmass - square)
    copies[0].wait()
    for group in range(tgt_ref.shape[0] // LANES):
        at = group * LANES
        base = pot_ref[group : group + 1, :] + mass_ref[group : group + 1, :]
        offset_ref[:, at : at + LANES] = base - to_lanes(squares(tgt_ref, at), eye)
    lse_ref[...] = row_block(src_ref, ((tgt_ref, offset_ref, z_ref),), eye)


def near_kernel(rows_ref, tgt_ref, offset_ref, held_ref, z_ref, lse_ref):
    lse_ref[...] = merge(held_ref[...], row_block(rows_ref, ((tgt_ref, offset_ref, z_ref),), diagonal()))


def far_kernel(count, *refs):
    eye = diagonal()
    blocks = refs[:count]
    own_ref, own_offset_ref, pair_ref, pair_offset_ref, own_z_ref, pair_z_ref, lse_ref = refs[count:]
    for slot in range(count):
        sides = ((own_ref, own_offset_ref, own_z_ref.at[slot]), (pair_ref, pair_offset_ref, pair_z_ref.at[slot]))
        lse_ref[slot] = row_block(blocks[slot], sides, eye)


def column_kernel(near_ref, far_ref, lse_ref, lines_ref, out_ref, off_ref):
    eye = diagonal()
    slots, src_count = lse_ref.shape
    for slot in range(slots):
        offset = lines_ref[slot, 1:2, :] - lines_ref[slot, 0:1, :] * lse_ref[slot : slot + 1, :]
        for at in range(0, src_count, LANES):
            column = to_column(offset[:, at : at + LANES], eye)
            off_ref[slot, at : at + LANES, :] = jnp.broadcast_to(column, (LANES, LANES))

    def shifted(slot, cols):
        z = near_ref[:, cols] if slot == 0 else far_ref[slot - 1, :, cols]
        return z + off_ref[slot]

    for group in range(out_ref.shape[0]):
        cols = slice(group * LANES, (group + 1) * LANES)
        peak = None
        for slot in range(slots):
            high = fold_rows(shifted(slot, cols), jnp.max)
            peak = high if peak is None else jnp.maximum(peak, high)
        peak = jnp.max(peak, axis=0, keepdims=True)
        mass = None
        for slot in range(slots):
            term = fold_rows(jnp.exp(shifted(slot, cols) - peak), jnp.sum)
            mass = term if mass is None else mass + term
        mass = jnp.sum(mass, axis=0, keepdims=True)
        out_ref[group : group + 1, :] = peak + jnp.log(mass)


def f32(*shape):
    return jax.ShapeDtypeStruct(shape, jnp.float32)


def params(mebibytes):
    return pltpu.CompilerParams(vmem_limit_bytes=mebibytes * 1024 * 1024)


def shards(sources, targets, tgt_potential, src_logmass, tgt_logmass, src_exponent, tgt_exponent):
    src_count, width = sources.shape
    tgt_count = targets.shape[0]
    slabs = lax.axis_size("blk")
    sets = lax.axis_size("tsplit")
    chips = slabs // 2
    far = chips - 1
    groups = tgt_count // LANES
    src_groups = src_count // LANES
    assert chips > 1 and chips & (chips - 1) == 0 and sets & (sets - 1) == 0

    def pair(value):
        return lax.ppermute(value, "blk", [(i, i ^ 1) for i in range(slabs)])

    def across(value, chip):
        return lax.ppermute(value, "blk", [(i, i ^ (2 * chip)) for i in range(slabs)])

    def along(value, step):
        return lax.ppermute(value, "tsplit", [(i, i ^ step) for i in range(sets)])

    def cost(blocks):
        pairs = blocks * src_count * tgt_count
        return pl.CostEstimate(flops=2 * pairs * width, bytes_accessed=2**20, transcendentals=pairs)

    far_blocks = [across(sources, chip) for chip in range(1, chips)]
    pair_targets = pair(targets)
    inputs = (
        sources,
        targets,
        tgt_potential.reshape(groups, LANES),
        tgt_logmass.reshape(groups, LANES),
        src_exponent.reshape(src_groups, LANES),
        src_logmass.reshape(src_groups, LANES),
    )
    held, offset, own_z, lse, line, src_shift = pl.pallas_call(
        prepare_kernel,
        out_shape=(
            jax.ShapeDtypeStruct(targets.shape, targets.dtype),
            f32(1, tgt_count),
            f32(src_count, tgt_count),
            f32(1, src_count),
            f32(2, src_count),
            f32(1, src_count),
        ),
        in_specs=[HBM] * 6,
        out_specs=(VMEM,) * 6,
        scratch_shapes=[pltpu.VMEM(x.shape, x.dtype) for x in (inputs[0],) + inputs[2:]]
        + [pltpu.SemaphoreType.DMA((6,))],
        compiler_params=params(12),
        cost_estimate=cost(1),
        name="prepare",
    )(*[pltpu.with_memory_space_constraint(x, pltpu.HBM) for x in inputs])
    pair_offset = pair(offset)
    lines = jnp.stack([line] + [across(line, chip) for chip in range(1, chips)])
    pair_z, lse = pl.pallas_call(
        near_kernel,
        out_shape=(f32(src_count, tgt_count), f32(1, src_count)),
        in_specs=[VMEM] * 4,
        out_specs=(VMEM,) * 2,
        compiler_params=params(12),
        cost_estimate=cost(1),
        name="near_rows",
    )(sources, pair_targets, pair_offset, lse)
    lse, lines, *far_blocks = lax.optimization_barrier((lse, lines, *far_blocks))
    own_far_z, pair_far_z, far_lse = pl.pallas_call(
        functools.partial(far_kernel, far),
        out_shape=(f32(far, src_count, tgt_count), f32(far, src_count, tgt_count), f32(far, 1, src_count)),
        in_specs=[VMEM] * (far + 4),
        out_specs=(VMEM,) * 3,
        compiler_params=params(8 + 3 * far),
        cost_estimate=cost(2 * far),
        name="far_rows",
    )(*far_blocks, held, offset, pair_targets, pair_offset)

    lse = jnp.concatenate([lse, far_lse.reshape(far, src_count)])
    chip = 1
    while chip < chips:
        other = across(lse, chip)
        lse = merge(lse, jnp.stack([other[slot ^ chip] for slot in range(chips)]))
        chip *= 2
    lse = merge(lse, *[along(lse, step) for step in range(1, sets)])

    def columns(near_z, far_z, lse):
        return pl.pallas_call(
            column_kernel,
            out_shape=f32(groups, LANES),
            in_specs=[VMEM] * 4,
            out_specs=VMEM,
            scratch_shapes=[pltpu.VMEM((chips, src_count, LANES), jnp.float32)],
            compiler_params=params(8 + 2 * chips),
            cost_estimate=pl.CostEstimate(
                flops=6 * chips * src_count * tgt_count,
                bytes_accessed=2**20,
                transcendentals=chips * src_count * tgt_count,
            ),
            name="columns",
        )(near_z, far_z, lse, lines)

    pair_part = columns(pair_z, pair_far_z, lse)
    lse, pair_part = lax.optimization_barrier((lse, pair_part))
    home = pair(pair_part)
    total = merge(columns(own_z, own_far_z, lse), home).reshape(tgt_count)
    tgt_update = tgt_exponent * (2.0 * tgt_logmass + tgt_potential - total)
    src_potential = src_exponent * (src_shift - lse[0:1]).reshape(src_count)
    return (src_potential, tgt_update)


def solution(mesh):
    placed = (
        P(("groups", "blk"), None),
        P(("groups", "blk", "tsplit"), None),
        P(("groups", "blk", "tsplit")),
        P(("groups", "blk")),
        P(("groups", "blk", "tsplit")),
        P(("groups", "blk")),
        P(("groups", "blk", "tsplit")),
    )
    return jax.shard_map(
        shards,
        mesh=mesh,
        in_specs=placed,
        out_specs=(P(("groups", "blk")), P(("groups", "blk", "tsplit"))),
        check_vma=False,
    )
```

time: 28.3 us -> 28.3 us (level)
  waiting for transfers between devices: 7.35 us -> 10.2 us
  other arithmetic: 3.28 us -> 1.27 us
  local copies, waits for them, and re-layouts: 2.21 us -> 0.84 us
  Pallas kernels: 4.03 us -> 5.27 us
  starting transfers between devices: 10.4 us -> 9.78 us
    ppermute x3, waiting for transfers between devices: 2.74 us -> 6.37 us  [across(): return lax.ppermute(value, 'blk', [(i, i ^ 2 * chip) for i in range(slabs)])]
    unnamed x16 -> x10, local copies, waits for them, and re-layouts: 2.2 us -> 0.84 us
    pallas_call x2 -> x4, Pallas kernels: 2.89 us -> 4.13 us  [the longest x1 2.29 us: shards(): pl.pallas_call(prepare_kernel, out_shape=(jax.ShapeDtypeStruct(targets.sh...]
    ppermute x3, waiting for transfers between devices: 1.17 us -> 0.01 us  [pair(): return lax.ppermute(value, 'blk', [(i, i ^ 1) for i in range(slabs)])]
    reduce_sum x1 -> x0, other arithmetic: 1.11 us -> none  [shards(): own_sq = jnp.sum(jnp.square(sources.astype(jnp.float32)), axis=1) / EPSILON]
    div x1 -> x0, other arithmetic: 0.75 us -> none  [shards(): own_sq = jnp.sum(jnp.square(sources.astype(jnp.float32)), axis=1) / EPSILON]
    reshape x1 -> x0, other arithmetic: 0.71 us -> none  [shards(): base = (tgt_potential + tgt_logmass).reshape(groups, LANES)]
    ppermute x3, starting transfers between devices: 5.12 us -> 4.5 us  [across(): return lax.ppermute(value, 'blk', [(i, i ^ 2 * chip) for i in range(slabs)])]
  transfers between devices with their start and end apart: 8 -> 9, of which waited for: 5 -> 4; matrix products, arithmetic and copies ran while one was open for 9% -> 2% of each run, Pallas kernels for 5% -> 13%
where the time goes in v4:
time: 28.3 us; the launch traced here: 28.1 us
  waiting for transfers between devices  10.2 us (36%)
  starting transfers between devices  9.78 us (35%)
  Pallas kernels  5.27 us (19%)
  other arithmetic  1.27 us (4%)
  local copies, waits for them, and re-layouts  0.84 us (3%)
  between operations  0.73 us (3%)
    ppermute x3, waiting for transfers between devices, across(): return lax.ppermute(value, 'blk', [(i, i ^ 2 * chip) for i in range(slabs)])  6.37 us
    ppermute x3, starting transfers between devices, across(): return lax.ppermute(value, 'blk', [(i, i ^ 2 * chip) for i in range(slabs)])  4.5 us
    ppermute x3, starting transfers between devices, along(): return lax.ppermute(value, 'tsplit', [(i, i ^ step) for i in range(sets)])  4.47 us
    ppermute x3, waiting for transfers between devices, along(): return lax.ppermute(value, 'tsplit', [(i, i ^ step) for i in range(sets)])  3.81 us
    pallas_call x1, Pallas kernels, shards(): pl.pallas_call(prepare_kernel, out_shape=(jax.ShapeDtypeStruct(targets.sh...  2.29 us
    pallas_call x1, Pallas kernels, shards(): pl.pallas_call(functools.partial(far_kernel, far), out_shape=(f32(far, sr...  1.15 us
    pallas_call x2, Pallas kernels, columns(): pl.pallas_call(column_kernel, out_shape=f32(groups, LANES), in_specs=[VME...  1.11 us
    unnamed x10, local copies, waits for them, and re-layouts  0.84 us
  transfers between devices with their start and end apart: 9, of which 4 were waited for; matrix products, arithmetic and copies ran while one was open for 2% of the time, Pallas kernels for 13%

profile of v4, /device:TPU:0, one launch (start us, length us, event | category | flops | bytes accessed | tf_op | source)
XLA Modules:
  0.0 28.1 jit_solution(9358132743640373453)
XLA Ops:
  0.6 0.5 %collective-permute-start = (bf16[1024,512]{1,0:T(8,128)(2,1)}, bf16[1024,512]{1,0:T(8,128)(2,1)S(1)}, u32[]{:S(2)}, u32[]{:S(2)}) collective-permute-start(bf16[1024,512]{1,0:T(8,128)(2,1)} %tgt_hbm.1), channel_id=1, source_target_pairs={{0,4},{4,0},{8,12},{12,8},{1,5},{5,1},{9,13},{13,9},{2,6},{6,2},{1... | collective-permute-start | bytes 3145736 | tf_op jit(solution)/shard_map/ppermute | solution.py:163
  1.1 2.6 %collective-permute-start.3 = (bf16[256,512]{1,0:T(8,128)(2,1)}, bf16[256,512]{1,0:T(8,128)(2,1)S(1)}, u32[]{:S(2)}, u32[]{:S(2)}) collective-permute-start(bf16[256,512]{1,0:T(8,128)(2,1)} %rows_ref.1), channel_id=1, source_target_pairs={{0,8},{4,12},{8,0},{12,4},{1,9},{5,13},{9,1},{13,5},{2,10},{6,14},... | collective-permute-start | bytes 786440 | tf_op jit(solution)/shard_map/ppermute | solution.py:166
  3.7 2.3 %prepare.1 = (bf16[1024,512]{1,0:T(8,128)(2,1)S(1)}, f32[1,1024]{1,0:T(1,128)S(1)}, f32[256,1024]{1,0:T(8,128)S(1)}, f32[1,256]{1,0:T(1,128)S(1)}, f32[2,256]{1,0:T(2,128)S(1)}, /*index=5*/f32[1,256]{1,0:T(1,128)S(1)}) custom-call(bf16[256,512]{1,0:T(8,128)(2,1)} %rows_ref.1, bf16[1024,512]{1,0:T(8,128)(2,1)} %tgt_hbm.1, f32[8,128]{1,0:T(8,128)} %bitcast.16, ...), custom_call_target="tpu_custom_call" | custom-call | flops 268435456 | bytes 1048576 | tf_op jit(solution)/shard_map/prepare/pallas_call | solution.py:185
  6.0 0.1 collective-permute-start.2
  6.1 0.2 collective-permute-start.1
  6.3 4.5 %collective-permute-done.2 = f32[2,256]{1,0:T(2,128)S(1)} collective-permute-done((f32[2,256]{1,0:T(2,128)S(1)}, f32[2,256]{1,0:T(2,128)S(1)}, u32[]{:S(2)}, u32[]{:S(2)}) %collective-permute-start.2) | collective-permute-done | bytes 2080 | tf_op jit(solution)/shard_map/ppermute | solution.py:166
  10.9 0.7 %near_rows.1 = (f32[256,1024]{1,0:T(8,128)S(1)}, f32[1,256]{1,0:T(1,128)S(1)}) custom-call(bf16[256,512]{1,0:T(8,128)(2,1)S(1)} %copy-done, bf16[1024,512]{1,0:T(8,128)(2,1)S(1)} %collective-permute-done.tgt_ref.refs_3_, f32[1,1024]{1,0:T(1,128)S(1)} %collective-permute-done.1.offset_ref.refs_4_, f32[1,256]{1,0:T(1,128)S(1)} %get-tuple-element.20.held_ref), custom_call_target="tpu_custom_call" | custom-call | flops 268435456 | bytes 1048576 | tf_op jit(solution)/shard_map/near_rows/pallas_call | solution.py:205
  11.7 1.1 %far_rows.1 = (f32[1,256,1024]{2,1,0:T(8,128)S(1)}, f32[1,256,1024]{2,1,0:T(8,128)S(1)}, f32[1,1,256]{2,1,0:T(1,128)S(1)}) custom-call(bf16[256,512]{1,0:T(8,128)(2,1)S(1)} %collective-permute-done.3.refs_0_, bf16[1024,512]{1,0:T(8,128)(2,1)S(1)} %get-tuple-element.25.refs_1_, f32[1,1024]{1,0:T(1,128)S(1)} %get-tuple-element.19.refs_2_, ...), custom_call_target="tpu_custom_call" | custom-call | flops 536870912 | bytes 1048576 | tf_op jit(solution)/shard_map/far_rows/pallas_call | solution.py:215
  12.8 1.8 %collective-permute-start.4 = (f32[2,256]{1,0:T(2,128)S(1)}, f32[2,256]{1,0:T(2,128)S(1)}, u32[]{:S(2)}, u32[]{:S(2)}) collective-permute-start(f32[2,256]{1,0:T(2,128)S(1)} %pad_maximum_fusion.1), channel_id=1, source_target_pairs={{0,8},{4,12},{8,0},{12,4},{1,9},{5,13},{9,1},{13,5},{2,10},{6,14},... | collective-permute-start | bytes 6152 | tf_op jit(solution)/shard_map/ppermute | solution.py:166
  14.7 1.8 %collective-permute-done.4 = f32[2,256]{1,0:T(2,128)S(1)} collective-permute-done((f32[2,256]{1,0:T(2,128)S(1)}, f32[2,256]{1,0:T(2,128)S(1)}, u32[]{:S(2)}, u32[]{:S(2)}) %collective-permute-start.4) | collective-permute-done | bytes 2080 | tf_op jit(solution)/shard_map/ppermute | solution.py:166
  16.5 2.9 %collective-permute-start.6 = (f32[2,256]{1,0:T(2,128)S(1)}, f32[2,256]{1,0:T(2,128)S(1)}, u32[]{:S(2)}, u32[]{:S(2)}) collective-permute-start(f32[2,256]{1,0:T(2,128)S(1)} %log_add_fusion.1), channel_id=1, source_target_pairs={{0,2},{1,3},{2,0},{3,1},{4,6},{5,7},{6,4},{7,5},{8,10},{9,11},{10,... | collective-permute-start | bytes 6152 | tf_op jit(solution)/shard_map/ppermute | solution.py:169
  19.4 1.3 %collective-permute-start.7 = (f32[2,256]{1,0:T(2,128)S(1)}, f32[2,256]{1,0:T(2,128)S(1)}, u32[]{:S(2)}, u32[]{:S(2)}) collective-permute-start(f32[2,256]{1,0:T(2,128)S(1)} %log_add_fusion.1), channel_id=1, source_target_pairs={{0,3},{1,2},{2,1},{3,0},{4,7},{5,6},{6,5},{7,4},{8,11},{9,10},{10,... | collective-permute-start | bytes 6152 | tf_op jit(solution)/shard_map/ppermute | solution.py:169
  20.8 0.2 collective-permute-start.5
  21.0 0.1 collective-permute-done.6
  21.1 3.7 %collective-permute-done.7 = f32[2,256]{1,0:T(2,128)S(1)} collective-permute-done((f32[2,256]{1,0:T(2,128)S(1)}, f32[2,256]{1,0:T(2,128)S(1)}, u32[]{:S(2)}, u32[]{:S(2)}) %collective-permute-start.7) | collective-permute-done | bytes 2080 | tf_op jit(solution)/shard_map/ppermute | solution.py:169
  24.9 0.6 %columns.2 = f32[8,128]{1,0:T(8,128)S(1)} custom-call(f32[256,1024]{1,0:T(8,128)S(1)} %get-tuple-element.27.near_ref, f32[1,256,1024]{2,1,0:T(8,128)S(1)} %get-tuple-element.28.far_ref, f32[2,256]{1,0:T(2,128)S(1)} %log_add_fusion.lse_ref, f32[2,2,256]{2,1,0:T(2,128)S(1)} %pad_maximum_fusion.lines_ref), custom_call_target="tpu_custom_call" | custom-call | flops 3145728 | bytes 1048576 | tf_op jit(solution)/shard_map/columns/pallas_call | solution.py:234
  25.4 0.1 collective-permute-start.8
  25.5 0.7 %copy-done.3 = f32[256]{0:T(256)S(1)} copy-done((f32[256]{0:T(256)S(1)}, f32[256]{0:T(256)}, u32[]{:S(2)}) %copy-start.3) | copy-done | bytes 1048
  26.2 0.6 %mul.12 = f32[256]{0:T(256)} multiply(f32[256]{0:T(256)S(1)} %copy-done.3, f32[256]{0:T(256)S(1)} %bitcast.19) | non-fusion elementwise | flops 256 | bytes 3072 | tf_op jit(solution)/shard_map/mul | solution.py:254
  26.8 0.5 %columns.3 = f32[8,128]{1,0:T(8,128)S(1)} custom-call(f32[256,1024]{1,0:T(8,128)S(1)} %get-tuple-element.31.near_ref, f32[1,256,1024]{2,1,0:T(8,128)S(1)} %get-tuple-element.32.far_ref, f32[2,256]{1,0:T(2,128)S(1)} %log_add_fusion.lse_ref, f32[2,2,256]{2,1,0:T(2,128)S(1)} %pad_maximum_fusion.lines_ref), custom_call_target="tpu_custom_call" | custom-call | flops 3145728 | bytes 1048576 | tf_op jit(solution)/shard_map/columns/pallas_call | solution.py:234
  27.3 0.1 copy-done.1
  27.4 0.0 copy-done.2
  27.5 0.0 copy-done.4
  27.5 0.6 %fusion = f32[1024]{0:T(1024)} fusion(f32[1024]{0:T(1024)S(1)} %copy-done.4, f32[8,128]{1,0:T(8,128)S(1)} %collective-permute-done.8, f32[8,128]{1,0:T(8,128)S(1)} %columns.3, f32[1024]{0:T(1024)S(1)} %copy-done.1, f32[1024]{0:T(1024)S(1)} %copy-done.2), kind=kLoop, calls=%fused_computation.2 | loop fusion | flops 9216 | bytes 24576 | tf_op jit(solution)/shard_map/mul | solution.py:253
  (17 shorter events, 0.1 us)
Async XLA Ops:
  0.6 10.3 %collective-permute-start = (bf16[1024,512]{1,0:T(8,128)(2,1)}, bf16[1024,512]{1,0:T(8,128)(2,1)S(1)}, u32[]{:S(2)}, u32[]{:S(2)}) collective-permute-start(bf16[1024,512]{1,0:T(8,128)(2,1)} %tgt_hbm.1), channel_id=1, source_target_pairs={{0,4},{4,0},{8,12},{12,8},{1,5},{5,1},{9,13},{13,9},{2,6},{6,2},{1... | collective-permute-start | bytes 3145736 | tf_op jit(solution)/shard_map/ppermute | solution.py:163
  1.1 10.5 %collective-permute-start.3 = (bf16[256,512]{1,0:T(8,128)(2,1)}, bf16[256,512]{1,0:T(8,128)(2,1)S(1)}, u32[]{:S(2)}, u32[]{:S(2)}) collective-permute-start(bf16[256,512]{1,0:T(8,128)(2,1)} %rows_ref.1), channel_id=1, source_target_pairs={{0,8},{4,12},{8,0},{12,4},{1,9},{5,13},{9,1},{13,5},{2,10},{6,14},... | collective-permute-start | bytes 786440 | tf_op jit(solution)/shard_map/ppermute | solution.py:166
  3.7 7.2 %copy-start = (bf16[256,512]{1,0:T(8,128)(2,1)S(1)}, bf16[256,512]{1,0:T(8,128)(2,1)}, u32[]{:S(2)}) copy-start(bf16[256,512]{1,0:T(8,128)(2,1)} %rows_ref.1) | copy-start | bytes 786436
  6.0 4.9 %collective-permute-start.2 = (f32[2,256]{1,0:T(2,128)S(1)}, f32[2,256]{1,0:T(2,128)S(1)}, u32[]{:S(2)}, u32[]{:S(2)}) collective-permute-start(f32[2,256]{1,0:T(2,128)S(1)} %get-tuple-element.22), channel_id=1, source_target_pairs={{0,8},{4,12},{8,0},{12,4},{1,9},{5,13},{9,1},{13,5},{2,10},{6,14},... | collective-permute-start | bytes 6152 | tf_op jit(solution)/shard_map/ppermute | solution.py:166
  6.1 4.8 %collective-permute-start.1 = (f32[1,1024]{1,0:T(1,128)S(1)}, f32[1,1024]{1,0:T(1,128)S(1)}, u32[]{:S(2)}, u32[]{:S(2)}) collective-permute-start(f32[1,1024]{1,0:T(1,128)S(1)} %get-tuple-element.19.refs_2_), channel_id=1, source_target_pairs={{0,4},{4,0},{8,12},{12,8},{1,5},{5,1},{9,13},{13,9},{2,6},{6,2},{1... | collective-permute-start | bytes 12296 | tf_op jit(solution)/shard_map/ppermute | solution.py:163
  12.8 3.7 %collective-permute-start.4 = (f32[2,256]{1,0:T(2,128)S(1)}, f32[2,256]{1,0:T(2,128)S(1)}, u32[]{:S(2)}, u32[]{:S(2)}) collective-permute-start(f32[2,256]{1,0:T(2,128)S(1)} %pad_maximum_fusion.1), channel_id=1, source_target_pairs={{0,8},{4,12},{8,0},{12,4},{1,9},{5,13},{9,1},{13,5},{2,10},{6,14},... | collective-permute-start | bytes 6152 | tf_op jit(solution)/shard_map/ppermute | solution.py:166
  16.5 4.5 %collective-permute-start.6 = (f32[2,256]{1,0:T(2,128)S(1)}, f32[2,256]{1,0:T(2,128)S(1)}, u32[]{:S(2)}, u32[]{:S(2)}) collective-permute-start(f32[2,256]{1,0:T(2,128)S(1)} %log_add_fusion.1), channel_id=1, source_target_pairs={{0,2},{1,3},{2,0},{3,1},{4,6},{5,7},{6,4},{7,5},{8,10},{9,11},{10,... | collective-permute-start | bytes 6152 | tf_op jit(solution)/shard_map/ppermute | solution.py:169
  19.4 5.4 %collective-permute-start.7 = (f32[2,256]{1,0:T(2,128)S(1)}, f32[2,256]{1,0:T(2,128)S(1)}, u32[]{:S(2)}, u32[]{:S(2)}) collective-permute-start(f32[2,256]{1,0:T(2,128)S(1)} %log_add_fusion.1), channel_id=1, source_target_pairs={{0,3},{1,2},{2,1},{3,0},{4,7},{5,6},{6,5},{7,4},{8,11},{9,10},{10,... | collective-permute-start | bytes 6152 | tf_op jit(solution)/shard_map/ppermute | solution.py:169
  20.8 4.0 %collective-permute-start.5 = (f32[2,256]{1,0:T(2,128)S(1)}, f32[2,256]{1,0:T(2,128)S(1)}, u32[]{:S(2)}, u32[]{:S(2)}) collective-permute-start(f32[2,256]{1,0:T(2,128)S(1)} %log_add_fusion.1), channel_id=1, source_target_pairs={{0,1},{1,0},{2,3},{3,2},{4,5},{5,4},{6,7},{7,6},{8,9},{9,8},{10,11... | collective-permute-start | bytes 6152 | tf_op jit(solution)/shard_map/ppermute | solution.py:169
  25.4 1.9 %collective-permute-start.8 = (f32[8,128]{1,0:T(8,128)S(1)}, f32[8,128]{1,0:T(8,128)S(1)}, u32[]{:S(2)}, u32[]{:S(2)}) collective-permute-start(f32[8,128]{1,0:T(8,128)S(1)} %columns.2), channel_id=1, source_target_pairs={{0,4},{4,0},{8,12},{12,8},{1,5},{5,1},{9,13},{13,9},{2,6},{6,2},{1... | collective-permute-start | bytes 12296 | tf_op jit(solution)/shard_map/ppermute | solution.py:163
  25.5 0.7 %copy-start.3 = (f32[256]{0:T(256)S(1)}, f32[256]{0:T(256)}, u32[]{:S(2)}) copy-start(f32[256]{0:T(256)} %param.12) | copy-start | bytes 3076
  26.7 0.7 %copy-start.1 = (f32[1024]{0:T(1024)S(1)}, f32[1024]{0:T(1024)}, u32[]{:S(2)}) copy-start(f32[1024]{0:T(1024)} %param.9) | copy-start | bytes 12292
  26.8 0.7 %copy-start.2 = (f32[1024]{0:T(1024)S(1)}, f32[1024]{0:T(1024)}, u32[]{:S(2)}) copy-start(f32[1024]{0:T(1024)} %param.11) | copy-start | bytes 12292
  26.8 0.7 %copy-start.4 = (f32[1024]{0:T(1024)S(1)}, f32[1024]{0:T(1024)}, u32[]{:S(2)}) copy-start(f32[1024]{0:T(1024)} %param.13) | copy-start | bytes 12292

commit v5 on v4

--- a/solution.py
+++ b/solution.py
@@ -12,6 +12,7 @@
 LANES = 128
 CHUNK = 256
 VMEM = pl.BlockSpec(memory_space=pltpu.VMEM)
+SMEM = pl.BlockSpec(memory_space=pltpu.SMEM)
 HBM = pl.BlockSpec(memory_space=pltpu.HBM)
 NT_DIMS = (((1,), (1,)), ((), ()))
 
@@ -44,8 +45,8 @@
     return jnp.sum(rows * rows, axis=1, keepdims=True) / EPSILON
 
 
-def row_block(rows_ref, sides, eye):
-    rows = rows_ref[...] * LOGIT_SCALE
+def row_block(rows, sides, eye):
+    rows = rows * LOGIT_SCALE
     src_count = rows.shape[0]
     peak = None
     for tgt_ref, offset_ref, z_ref in sides:
@@ -70,7 +71,7 @@
 
 def prepare_kernel(
     src_hbm, tgt_hbm, pot_hbm, mass_hbm, slope_hbm, logmass_hbm,
-    tgt_ref, offset_ref, z_ref, lse_ref, line_ref, sq_ref,
+    tgt_ref, offset_ref, z_ref, lse_ref, line_ref, sum_ref,
     src_ref, pot_ref, mass_ref, slope_ref, logmass_ref, sems,
 ):
     pairs = (
@@ -88,7 +89,7 @@
         square = to_lanes(squares(src_ref, group * LANES), eye)
         slope = slope_ref[group : group + 1, :]
         logmass = logmass_ref[group : group + 1, :]
-        sq_ref[:, cols] = logmass + square
+        sum_ref[:, cols] = logmass + square
         line_ref[0:1, cols] = slope
         line_ref[1:2, cols] = slope * (logmass + square) + (logmass - square)
     copies[0].wait()
@@ -96,29 +97,33 @@
         at = group * LANES
         base = pot_ref[group : group + 1, :] + mass_ref[group : group + 1, :]
         offset_ref[:, at : at + LANES] = base - to_lanes(squares(tgt_ref, at), eye)
-    lse_ref[...] = row_block(src_ref, ((tgt_ref, offset_ref, z_ref),), eye)
+    lse_ref[...] = row_block(src_ref[...], ((tgt_ref, offset_ref, z_ref),), eye)
 
 
 def near_kernel(rows_ref, tgt_ref, offset_ref, held_ref, z_ref, lse_ref):
-    lse_ref[...] = merge(held_ref[...], row_block(rows_ref, ((tgt_ref, offset_ref, z_ref),), diagonal()))
-
-
-def far_kernel(count, *refs):
+    lse_ref[...] = merge(held_ref[...], row_block(rows_ref[...], ((tgt_ref, offset_ref, z_ref),), diagonal()))
+
+
+def far_kernel(count, core_ref, *refs):
     eye = diagonal()
-    blocks = refs[:count]
-    own_ref, own_offset_ref, pair_ref, pair_offset_ref, own_z_ref, pair_z_ref, lse_ref = refs[count:]
+    early, late = refs[:count], refs[count : 2 * count]
+    own_ref, own_offset_ref, pair_ref, pair_offset_ref, held_ref, line_ref = refs[2 * count : 2 * count + 6]
+    own_z_ref, pair_z_ref, out_ref = refs[2 * count + 6 :]
+    slots = count + 1
+    out_ref[0:1, :] = held_ref[...]
+    out_ref[slots : slots + 2, :] = line_ref[...]
     for slot in range(count):
+        rows = jnp.where(core_ref[0] == 0, early[slot][...], late[slot][...])
         sides = ((own_ref, own_offset_ref, own_z_ref.at[slot]), (pair_ref, pair_offset_ref, pair_z_ref.at[slot]))
-        lse_ref[slot] = row_block(blocks[slot], sides, eye)
-
-
-def column_kernel(near_ref, far_ref, lse_ref, lines_ref, out_ref, off_ref):
+        out_ref[slot + 1 : slot + 2, :] = row_block(rows, sides, eye)
+
+
+def sum_columns(near_ref, far_ref, offset, off_ref, out_ref):
     eye = diagonal()
-    slots, src_count = lse_ref.shape
+    slots, src_count = offset.shape
     for slot in range(slots):
-        offset = lines_ref[slot, 1:2, :] - lines_ref[slot, 0:1, :] * lse_ref[slot : slot + 1, :]
         for at in range(0, src_count, LANES):
-            column = to_column(offset[:, at : at + LANES], eye)
+            column = to_column(offset[slot : slot + 1, at : at + LANES], eye)
             off_ref[slot, at : at + LANES, :] = jnp.broadcast_to(column, (LANES, LANES))
 
     def shifted(slot, cols):
@@ -140,6 +145,16 @@
         out_ref[group : group + 1, :] = peak + jnp.log(mass)
 
 
+def pair_kernel(near_ref, far_ref, lse_ref, slope_ref, shift_ref, out_ref, off_ref):
+    sum_columns(near_ref, far_ref, shift_ref[...] - slope_ref[...] * lse_ref[...], off_ref, out_ref)
+
+
+def own_kernel(near_ref, far_ref, lse_ref, slope_ref, shift_ref, sum_ref, out_ref, potential_ref, off_ref):
+    lse, slope = lse_ref[...], slope_ref[...]
+    potential_ref[...] = slope[0:1, :] * (sum_ref[...] - lse[0:1, :])
+    sum_columns(near_ref, far_ref, shift_ref[...] - slope * lse, off_ref, out_ref)
+
+
 def f32(*shape):
     return jax.ShapeDtypeStruct(shape, jnp.float32)
 
@@ -172,7 +187,13 @@
         pairs = blocks * src_count * tgt_count
         return pl.CostEstimate(flops=2 * pairs * width, bytes_accessed=2**20, transcendentals=pairs)
 
-    far_blocks = [across(sources, chip) for chip in range(1, chips)]
+    core = lax.axis_index("blk") & 1
+    core_word = core.astype(jnp.int32).reshape(1)
+
+    def across_one(value, chip, parity):
+        return lax.ppermute(value, "blk", [(i, i ^ (2 * chip) if i & 1 == parity else i) for i in range(slabs)])
+
+    early = [across_one(sources, chip, 0) for chip in range(1, chips)]
     pair_targets = pair(targets)
     inputs = (
         sources,
@@ -182,7 +203,7 @@
         src_exponent.reshape(src_groups, LANES),
         src_logmass.reshape(src_groups, LANES),
     )
-    held, offset, own_z, lse, line, src_shift = pl.pallas_call(
+    held, offset, own_z, lse, line, src_sum = pl.pallas_call(
         prepare_kernel,
         out_shape=(
             jax.ShapeDtypeStruct(targets.shape, targets.dtype),
@@ -200,8 +221,10 @@
         cost_estimate=cost(1),
         name="prepare",
     )(*[pltpu.with_memory_space_constraint(x, pltpu.HBM) for x in inputs])
+    lse, late_sources = lax.optimization_barrier((lse, sources))
+    late = [across_one(late_sources, chip, 1) for chip in range(1, chips)]
     pair_offset = pair(offset)
-    lines = jnp.stack([line] + [across(line, chip) for chip in range(1, chips)])
+    lse, *early = lax.optimization_barrier((lse, *early))
     pair_z, lse = pl.pallas_call(
         near_kernel,
         out_shape=(f32(src_count, tgt_count), f32(1, src_count)),
@@ -211,31 +234,38 @@
         cost_estimate=cost(1),
         name="near_rows",
     )(sources, pair_targets, pair_offset, lse)
-    lse, lines, *far_blocks = lax.optimization_barrier((lse, lines, *far_blocks))
-    own_far_z, pair_far_z, far_lse = pl.pallas_call(
+    far_lines = [across(line, chip) for chip in range(2, chips)]
+    lse, *moved = lax.optimization_barrier((lse, *early, *late, *far_lines))
+    own_far_z, pair_far_z, payload = pl.pallas_call(
         functools.partial(far_kernel, far),
-        out_shape=(f32(far, src_count, tgt_count), f32(far, src_count, tgt_count), f32(far, 1, src_count)),
-        in_specs=[VMEM] * (far + 4),
+        out_shape=(f32(far, src_count, tgt_count), f32(far, src_count, tgt_count), f32(chips + 2, src_count)),
+        in_specs=[SMEM] + [VMEM] * (2 * far + 6),
         out_specs=(VMEM,) * 3,
         compiler_params=params(8 + 3 * far),
         cost_estimate=cost(2 * far),
         name="far_rows",
-    )(*far_blocks, held, offset, pair_targets, pair_offset)
-
-    lse = jnp.concatenate([lse, far_lse.reshape(far, src_count)])
-    chip = 1
+    )(core_word, *moved[: 2 * far], held, offset, pair_targets, pair_offset, lse, line)
+
+    other = across(payload, 1)
+    lines = jnp.stack([line, other[chips:]] + moved[2 * far :], axis=1)
+    lse = merge(payload[:chips], jnp.stack([other[slot ^ 1] for slot in range(chips)]))
+    chip = 2
     while chip < chips:
         other = across(lse, chip)
         lse = merge(lse, jnp.stack([other[slot ^ chip] for slot in range(chips)]))
         chip *= 2
-    lse = merge(lse, *[along(lse, step) for step in range(1, sets)])
-
-    def columns(near_z, far_z, lse):
+    step = 1
+    while step < sets:
+        lse = merge(lse, along(lse, step))
+        step *= 2
+
+    def columns(kernel, near_z, far_z, *more):
+        outs = (f32(groups, LANES), f32(1, src_count))[: 1 + len(more)]
         return pl.pallas_call(
-            column_kernel,
-            out_shape=f32(groups, LANES),
-            in_specs=[VMEM] * 4,
-            out_specs=VMEM,
+            kernel,
+            out_shape=outs,
+            in_specs=[VMEM] * (5 + len(more)),
+            out_specs=(VMEM,) * len(outs),
             scratch_shapes=[pltpu.VMEM((chips, src_count, LANES), jnp.float32)],
             compiler_params=params(8 + 2 * chips),
             cost_estimate=pl.CostEstimate(
@@ -244,15 +274,15 @@
                 transcendentals=chips * src_count * tgt_count,
             ),
             name="columns",
-        )(near_z, far_z, lse, lines)
-
-    pair_part = columns(pair_z, pair_far_z, lse)
+        )(near_z, far_z, lse, lines[0], lines[1], *more)
+
+    (pair_part,) = columns(pair_kernel, pair_z, pair_far_z)
     lse, pair_part = lax.optimization_barrier((lse, pair_part))
     home = pair(pair_part)
-    total = merge(columns(own_z, own_far_z, lse), home).reshape(tgt_count)
+    own_part, src_potential = columns(own_kernel, own_z, own_far_z, src_sum)
+    total = merge(own_part, home).reshape(tgt_count)
     tgt_update = tgt_exponent * (2.0 * tgt_logmass + tgt_potential - total)
-    src_potential = src_exponent * (src_shift - lse[0:1]).reshape(src_count)
-    return (src_potential, tgt_update)
+    return (src_potential.reshape(src_count), tgt_update)
 
 
 def solution(mesh):

time: 28.3 us -> 30.2 us (1.067)
  starting transfers between devices: 9.78 us -> 13.5 us
  waiting for transfers between devices: 10.2 us -> 8.05 us
  Pallas kernels: 5.27 us -> 6.83 us
  local copies, waits for them, and re-layouts: 0.84 us -> 0.04 us
  other arithmetic: 1.27 us -> 0.69 us
    ppermute x0 -> x2, starting transfers between devices: none -> 5.78 us  [across_one(): lax.ppermute(value, 'blk', [(i, i ^ 2 * chip if i & 1 == parity else i) f...]
    ppermute x3 -> x1, starting transfers between devices: 4.5 us -> 0.36 us  [across(): return lax.ppermute(value, 'blk', [(i, i ^ 2 * chip) for i in range(slabs)])]
    ppermute x3 -> x1, waiting for transfers between devices: 6.37 us -> 3.31 us  [across(): return lax.ppermute(value, 'blk', [(i, i ^ 2 * chip) for i in range(slabs)])]
    ppermute x3, starting transfers between devices: 0.81 us -> 3.1 us  [pair(): return lax.ppermute(value, 'blk', [(i, i ^ 1) for i in range(slabs)])]
    pallas_call x1, Pallas kernels: 1.15 us -> 2.18 us  [shards(): pl.pallas_call(functools.partial(far_kernel, far), out_shape=(f32(far, sr...]
    ppermute x3, waiting for transfers between devices: 0.01 us -> 0.86 us  [pair(): return lax.ppermute(value, 'blk', [(i, i ^ 1) for i in range(slabs)])]
    unnamed x10 -> x8, local copies, waits for them, and re-layouts: 0.84 us -> 0.02 us
    mul x1 -> x0, other arithmetic: 0.56 us -> none  [shards(): src_potential = src_exponent * (src_shift - lse[0:1]).reshape(src_count)]
  transfers between devices with their start and end apart: 9 -> 8, of which waited for: 4 -> 4; matrix products, arithmetic and copies ran while one was open for 2% -> 0% of each run, Pallas kernels for 13% -> 14%
where the time goes in v5:
time: 30.2 us; the launch traced here: 29.9 us
  starting transfers between devices  13.5 us (45%)
  waiting for transfers between devices  8.05 us (27%)
  Pallas kernels  6.83 us (23%)
  between operations  0.74 us (2%)
  other arithmetic  0.69 us (2%)
    ppermute x2, starting transfers between devices, across_one(): lax.ppermute(value, 'blk', [(i, i ^ 2 * chip if i & 1 == parity else i) f...  5.78 us
    ppermute x2, starting transfers between devices, along(): return lax.ppermute(value, 'tsplit', [(i, i ^ step) for i in range(sets)])  4.3 us
    ppermute x2, waiting for transfers between devices, along(): return lax.ppermute(value, 'tsplit', [(i, i ^ step) for i in range(sets)])  3.87 us
    ppermute x1, waiting for transfers between devices, across(): return lax.ppermute(value, 'blk', [(i, i ^ 2 * chip) for i in range(slabs)])  3.31 us
    ppermute x3, starting transfers between devices, pair(): return lax.ppermute(value, 'blk', [(i, i ^ 1) for i in range(slabs)])  3.1 us
    pallas_call x1, Pallas kernels, shards(): pl.pallas_call(prepare_kernel, out_shape=(jax.ShapeDtypeStruct(targets.sh...  2.29 us
    pallas_call x1, Pallas kernels, shards(): pl.pallas_call(functools.partial(far_kernel, far), out_shape=(f32(far, sr...  2.18 us
    pallas_call x2, Pallas kernels, columns(): pl.pallas_call(kernel, out_shape=outs, in_specs=[VMEM] * (5 + len(more)),...  1.63 us
  transfers between devices with their start and end apart: 8, of which 4 were waited for; matrix products, arithmetic and copies ran while one was open for 0% of the time, Pallas kernels for 14%

profile of v5, /device:TPU:0, one launch (start us, length us, event | category | flops | bytes accessed | tf_op | source)
XLA Modules:
  0.0 29.9 jit_solution(17126739306629801439)
XLA Ops:
  0.6 0.5 %collective-permute-start = (bf16[1024,512]{1,0:T(8,128)(2,1)}, bf16[1024,512]{1,0:T(8,128)(2,1)S(1)}, u32[]{:S(2)}, u32[]{:S(2)}) collective-permute-start(bf16[1024,512]{1,0:T(8,128)(2,1)} %tgt_hbm.1), channel_id=1, source_target_pairs={{0,4},{4,0},{8,12},{12,8},{1,5},{5,1},{9,13},{13,9},{2,6},{6,2},{1... | collective-permute-start | bytes 3145736 | tf_op jit(solution)/shard_map/ppermute | solution.py:178
  1.1 4.4 %collective-permute-start.2 = (bf16[256,512]{1,0:T(8,128)(2,1)}, bf16[256,512]{1,0:T(8,128)(2,1)}, u32[]{:S(2)}, u32[]{:S(2)}) collective-permute-start(bf16[256,512]{1,0:T(8,128)(2,1)} %rows_ref.1), channel_id=1, source_target_pairs={{0,8},{4,4},{8,0},{12,12},{1,9},{5,5},{9,1},{13,13},{2,10},{6,6},{... | collective-permute-start | bytes 786440 | tf_op jit(solution)/shard_map/ppermute | solution.py:194
  5.6 2.3 %prepare.1 = (bf16[1024,512]{1,0:T(8,128)(2,1)S(1)}, f32[1,1024]{1,0:T(1,128)S(1)}, f32[256,1024]{1,0:T(8,128)S(1)}, f32[1,256]{1,0:T(1,128)S(1)}, f32[2,256]{1,0:T(2,128)S(1)}, /*index=5*/f32[1,256]{1,0:T(1,128)S(1)}) custom-call(bf16[256,512]{1,0:T(8,128)(2,1)} %rows_ref.1, bf16[1024,512]{1,0:T(8,128)(2,1)} %tgt_hbm.1, f32[8,128]{1,0:T(8,128)} %bitcast.14, ...), custom_call_target="tpu_custom_call" | custom-call | flops 268435456 | bytes 1048576 | tf_op jit(solution)/shard_map/prepare/pallas_call | solution.py:206
  7.9 1.3 %collective-permute-start.3 = (bf16[256,512]{1,0:T(8,128)(2,1)S(1)}, bf16[256,512]{1,0:T(8,128)(2,1)}, u32[]{:S(2)}, u32[]{:S(2)}) collective-permute-start(bf16[256,512]{1,0:T(8,128)(2,1)S(1)} %copy-done), channel_id=1, source_target_pairs={{0,0},{4,12},{8,8},{12,4},{1,1},{5,13},{9,9},{13,5},{2,2},{6,14},{... | collective-permute-start | bytes 786440 | tf_op jit(solution)/shard_map/ppermute | solution.py:194
  9.3 2.5 %collective-permute-start.1 = (f32[1,1024]{1,0:T(1,128)S(1)}, f32[1,1024]{1,0:T(1,128)S(1)}, u32[]{:S(2)}, u32[]{:S(2)}) collective-permute-start(f32[1,1024]{1,0:T(1,128)S(1)} %get-tuple-element.25.refs_3_), channel_id=1, source_target_pairs={{0,4},{4,0},{8,12},{12,8},{1,5},{5,1},{9,13},{13,9},{2,6},{6,2},{1... | collective-permute-start | bytes 12296 | tf_op jit(solution)/shard_map/ppermute | solution.py:178
  11.8 0.0 collective-permute-done.2.refs_0_
  11.8 0.8 %collective-permute-done.1.offset_ref.refs_5_ = f32[1,1024]{1,0:T(1,128)S(1)} collective-permute-done((f32[1,1024]{1,0:T(1,128)S(1)}, f32[1,1024]{1,0:T(1,128)S(1)}, u32[]{:S(2)}, u32[]{:S(2)}) %collective-permute-start.1) | collective-permute-done | bytes 4128 | tf_op jit(solution)/shard_map/ppermute | solution.py:178
  12.6 0.7 %near_rows.1 = (f32[256,1024]{1,0:T(8,128)S(1)}, f32[1,256]{1,0:T(1,128)S(1)}) custom-call(bf16[256,512]{1,0:T(8,128)(2,1)S(1)} %copy-done, bf16[1024,512]{1,0:T(8,128)(2,1)S(1)} %collective-permute-done.tgt_ref.refs_4_, f32[1,1024]{1,0:T(1,128)S(1)} %collective-permute-done.1.offset_ref.refs_5_, f32[1,256]{1,0:T(1,128)S(1)} %get-tuple-element.28.held_ref), custom_call_target="tpu_custom_call" | custom-call | flops 268435456 | bytes 1048576 | tf_op jit(solution)/shard_map/near_rows/pallas_call | solution.py:228
  13.3 0.0 collective-permute-done.3.refs_1_
  13.3 2.2 %far_rows.1 = (f32[1,256,1024]{2,1,0:T(8,128)S(1)}, f32[1,256,1024]{2,1,0:T(8,128)S(1)}, f32[4,256]{1,0:T(4,128)S(1)}) custom-call(s32[1]{0:T(128)} %bitcast.4.core_ref, bf16[256,512]{1,0:T(8,128)(2,1)} %collective-permute-done.2.refs_0_, bf16[256,512]{1,0:T(8,128)(2,1)} %collective-permute-done.3.refs_1_, bf16[1024,512]{1,0:T(8,128)(2,1)S(1)} %get-tuple-element.34.refs_2_, ...), custom_call_target="tpu_custom_call" | custom-call | flops 536870912 | bytes 1048576 | tf_op jit(solution)/shard_map/far_rows/pallas_call | solution.py:239
  15.5 0.4 %collective-permute-start.4 = (f32[4,256]{1,0:T(4,128)S(1)}, f32[4,256]{1,0:T(4,128)S(1)}, u32[]{:S(2)}, u32[]{:S(2)}) collective-permute-start(f32[4,256]{1,0:T(4,128)S(1)} %get-tuple-element.38), channel_id=1, source_target_pairs={{0,8},{4,12},{8,0},{12,4},{1,9},{5,13},{9,1},{13,5},{2,10},{6,14},... | collective-permute-start | bytes 12296 | tf_op jit(solution)/shard_map/ppermute | solution.py:181
  15.9 3.3 %collective-permute-done.4 = f32[4,256]{1,0:T(4,128)S(1)} collective-permute-done((f32[4,256]{1,0:T(4,128)S(1)}, f32[4,256]{1,0:T(4,128)S(1)}, u32[]{:S(2)}, u32[]{:S(2)}) %collective-permute-start.4) | collective-permute-done | bytes 4128 | tf_op jit(solution)/shard_map/ppermute | solution.py:181
  19.2 1.6 %collective-permute-start.5 = (f32[2,256]{1,0:T(2,128)S(1)}, f32[2,256]{1,0:T(2,128)S(1)}, u32[]{:S(2)}, u32[]{:S(2)}) collective-permute-start(f32[2,256]{1,0:T(2,128)S(1)} %log_add_fusion.2), channel_id=1, source_target_pairs={{0,1},{1,0},{2,3},{3,2},{4,5},{5,4},{6,7},{7,6},{8,9},{9,8},{10,11... | collective-permute-start | bytes 6152 | tf_op jit(solution)/shard_map/ppermute | solution.py:184
  20.9 2.0 %collective-permute-done.5 = f32[2,256]{1,0:T(2,128)S(1)} collective-permute-done((f32[2,256]{1,0:T(2,128)S(1)}, f32[2,256]{1,0:T(2,128)S(1)}, u32[]{:S(2)}, u32[]{:S(2)}) %collective-permute-start.5) | collective-permute-done | bytes 2080 | tf_op jit(solution)/shard_map/ppermute | solution.py:184
  22.9 2.7 %collective-permute-start.6 = (f32[2,256]{1,0:T(2,128)S(1)}, f32[2,256]{1,0:T(2,128)S(1)}, u32[]{:S(2)}, u32[]{:S(2)}) collective-permute-start(f32[2,256]{1,0:T(2,128)S(1)} %log_add_fusion.1), channel_id=1, source_target_pairs={{0,2},{1,3},{2,0},{3,1},{4,6},{5,7},{6,4},{7,5},{8,10},{9,11},{10,... | collective-permute-start | bytes 6152 | tf_op jit(solution)/shard_map/ppermute | solution.py:184
  25.6 1.9 %collective-permute-done.6 = f32[2,256]{1,0:T(2,128)S(1)} collective-permute-done((f32[2,256]{1,0:T(2,128)S(1)}, f32[2,256]{1,0:T(2,128)S(1)}, u32[]{:S(2)}, u32[]{:S(2)}) %collective-permute-start.6) | collective-permute-done | bytes 2080 | tf_op jit(solution)/shard_map/ppermute | solution.py:184
  27.5 0.6 %columns.2 = f32[8,128]{1,0:T(8,128)S(1)} custom-call(f32[256,1024]{1,0:T(8,128)S(1)} %get-tuple-element.39.near_ref, f32[1,256,1024]{2,1,0:T(8,128)S(1)} %get-tuple-element.40.far_ref, f32[2,256]{1,0:T(2,128)S(1)} %log_add_fusion.lse_ref, f32[2,256]{1,0:T(2,128)S(1)} %get-tuple-element.47.slope_ref, f32[2,256]{1,0:T(2,128)S(1)} %get-tuple-element.46.shift_ref), custom_call_target="tpu_custom_call" | custom-call | flops 3145728 | bytes 1048576 | tf_op jit(solution)/shard_map/columns/pallas_call | solution.py:264
  28.0 0.1 collective-permute-start.7
  28.1 0.0 copy-start.1
  28.1 0.0 copy-start.2
  28.1 0.0 copy-start.3
  28.1 1.1 %columns.3 = (f32[8,128]{1,0:T(8,128)S(1)}, f32[1,256]{1,0:T(1,128)}) custom-call(f32[256,1024]{1,0:T(8,128)S(1)} %get-tuple-element.24.near_ref, f32[1,256,1024]{2,1,0:T(8,128)S(1)} %get-tuple-element.37.far_ref, f32[2,256]{1,0:T(2,128)S(1)} %log_add_fusion.lse_ref, f32[2,256]{1,0:T(2,128)S(1)} %get-tuple-element.47.slope_ref, ...), custom_call_target="tpu_custom_call" | custom-call | flops 3145728 | bytes 1048576 | tf_op jit(solution)/shard_map/columns/pallas_call | solution.py:264
  29.2 0.0 collective-permute-done.7
  29.3 0.6 %fusion = f32[1024]{0:T(1024)} fusion(f32[1024]{0:T(1024)S(1)} %copy-done.3, f32[8,128]{1,0:T(8,128)S(1)} %collective-permute-done.7, f32[8,128]{1,0:T(8,128)S(1)} %get-tuple-element.44, f32[1024]{0:T(1024)S(1)} %copy-done.1, f32[1024]{0:T(1024)S(1)} %copy-done.2), kind=kLoop, calls=%fused_computation.3 | loop fusion | flops 9216 | bytes 24576 | tf_op jit(solution)/shard_map/mul | solution.py:284
  (14 shorter events, 0.1 us)
Async XLA Ops:
  0.6 12.0 %collective-permute-start = (bf16[1024,512]{1,0:T(8,128)(2,1)}, bf16[1024,512]{1,0:T(8,128)(2,1)S(1)}, u32[]{:S(2)}, u32[]{:S(2)}) collective-permute-start(bf16[1024,512]{1,0:T(8,128)(2,1)} %tgt_hbm.1), channel_id=1, source_target_pairs={{0,4},{4,0},{8,12},{12,8},{1,5},{5,1},{9,13},{13,9},{2,6},{6,2},{1... | collective-permute-start | bytes 3145736 | tf_op jit(solution)/shard_map/ppermute | solution.py:178
  1.1 10.6 %collective-permute-start.2 = (bf16[256,512]{1,0:T(8,128)(2,1)}, bf16[256,512]{1,0:T(8,128)(2,1)}, u32[]{:S(2)}, u32[]{:S(2)}) collective-permute-start(bf16[256,512]{1,0:T(8,128)(2,1)} %rows_ref.1), channel_id=1, source_target_pairs={{0,8},{4,4},{8,0},{12,12},{1,9},{5,5},{9,1},{13,13},{2,10},{6,6},{... | collective-permute-start | bytes 786440 | tf_op jit(solution)/shard_map/ppermute | solution.py:194
  5.6 2.3 %copy-start = (bf16[256,512]{1,0:T(8,128)(2,1)S(1)}, bf16[256,512]{1,0:T(8,128)(2,1)}, u32[]{:S(2)}) copy-start(bf16[256,512]{1,0:T(8,128)(2,1)} %rows_ref.1) | copy-start | bytes 786436
  7.9 5.4 %collective-permute-start.3 = (bf16[256,512]{1,0:T(8,128)(2,1)S(1)}, bf16[256,512]{1,0:T(8,128)(2,1)}, u32[]{:S(2)}, u32[]{:S(2)}) collective-permute-start(bf16[256,512]{1,0:T(8,128)(2,1)S(1)} %copy-done), channel_id=1, source_target_pairs={{0,0},{4,12},{8,8},{12,4},{1,1},{5,13},{9,9},{13,5},{2,2},{6,14},{... | collective-permute-start | bytes 786440 | tf_op jit(solution)/shard_map/ppermute | solution.py:194
  9.3 3.3 %collective-permute-start.1 = (f32[1,1024]{1,0:T(1,128)S(1)}, f32[1,1024]{1,0:T(1,128)S(1)}, u32[]{:S(2)}, u32[]{:S(2)}) collective-permute-start(f32[1,1024]{1,0:T(1,128)S(1)} %get-tuple-element.25.refs_3_), channel_id=1, source_target_pairs={{0,4},{4,0},{8,12},{12,8},{1,5},{5,1},{9,13},{13,9},{2,6},{6,2},{1... | collective-permute-start | bytes 12296 | tf_op jit(solution)/shard_map/ppermute | solution.py:178
  15.5 3.7 %collective-permute-start.4 = (f32[4,256]{1,0:T(4,128)S(1)}, f32[4,256]{1,0:T(4,128)S(1)}, u32[]{:S(2)}, u32[]{:S(2)}) collective-permute-start(f32[4,256]{1,0:T(4,128)S(1)} %get-tuple-element.38), channel_id=1, source_target_pairs={{0,8},{4,12},{8,0},{12,4},{1,9},{5,13},{9,1},{13,5},{2,10},{6,14},... | collective-permute-start | bytes 12296 | tf_op jit(solution)/shard_map/ppermute | solution.py:181
  19.2 3.7 %collective-permute-start.5 = (f32[2,256]{1,0:T(2,128)S(1)}, f32[2,256]{1,0:T(2,128)S(1)}, u32[]{:S(2)}, u32[]{:S(2)}) collective-permute-start(f32[2,256]{1,0:T(2,128)S(1)} %log_add_fusion.2), channel_id=1, source_target_pairs={{0,1},{1,0},{2,3},{3,2},{4,5},{5,4},{6,7},{7,6},{8,9},{9,8},{10,11... | collective-permute-start | bytes 6152 | tf_op jit(solution)/shard_map/ppermute | solution.py:184
  22.9 4.5 %collective-permute-start.6 = (f32[2,256]{1,0:T(2,128)S(1)}, f32[2,256]{1,0:T(2,128)S(1)}, u32[]{:S(2)}, u32[]{:S(2)}) collective-permute-start(f32[2,256]{1,0:T(2,128)S(1)} %log_add_fusion.1), channel_id=1, source_target_pairs={{0,2},{1,3},{2,0},{3,1},{4,6},{5,7},{6,4},{7,5},{8,10},{9,11},{10,... | collective-permute-start | bytes 6152 | tf_op jit(solution)/shard_map/ppermute | solution.py:184
  28.0 1.2 %collective-permute-start.7 = (f32[8,128]{1,0:T(8,128)S(1)}, f32[8,128]{1,0:T(8,128)S(1)}, u32[]{:S(2)}, u32[]{:S(2)}) collective-permute-start(f32[8,128]{1,0:T(8,128)S(1)} %columns.2), channel_id=1, source_target_pairs={{0,4},{4,0},{8,12},{12,8},{1,5},{5,1},{9,13},{13,9},{2,6},{6,2},{1... | collective-permute-start | bytes 12296 | tf_op jit(solution)/shard_map/ppermute | solution.py:178
  28.1 1.2 %copy-start.1 = (f32[1024]{0:T(1024)S(1)}, f32[1024]{0:T(1024)}, u32[]{:S(2)}) copy-start(f32[1024]{0:T(1024)} %param.9) | copy-start | bytes 12292
  28.1 1.1 %copy-start.2 = (f32[1024]{0:T(1024)S(1)}, f32[1024]{0:T(1024)}, u32[]{:S(2)}) copy-start(f32[1024]{0:T(1024)} %param.11) | copy-start | bytes 12292
  28.1 1.1 %copy-start.3 = (f32[1024]{0:T(1024)S(1)}, f32[1024]{0:T(1024)}, u32[]{:S(2)}) copy-start(f32[1024]{0:T(1024)} %param.13) | copy-start | bytes 12292

commit v6 on v5

--- a/solution.py
+++ b/solution.py
@@ -12,7 +12,6 @@
 LANES = 128
 CHUNK = 256
 VMEM = pl.BlockSpec(memory_space=pltpu.VMEM)
-SMEM = pl.BlockSpec(memory_space=pltpu.SMEM)
 HBM = pl.BlockSpec(memory_space=pltpu.HBM)
 NT_DIMS = (((1,), (1,)), ((), ()))
 
@@ -104,18 +103,16 @@
     lse_ref[...] = merge(held_ref[...], row_block(rows_ref[...], ((tgt_ref, offset_ref, z_ref),), diagonal()))
 
 
-def far_kernel(count, core_ref, *refs):
+def far_kernel(count, *refs):
     eye = diagonal()
-    early, late = refs[:count], refs[count : 2 * count]
-    own_ref, own_offset_ref, pair_ref, pair_offset_ref, held_ref, line_ref = refs[2 * count : 2 * count + 6]
-    own_z_ref, pair_z_ref, out_ref = refs[2 * count + 6 :]
+    own_ref, own_offset_ref, pair_ref, pair_offset_ref, held_ref, line_ref = refs[count : count + 6]
+    own_z_ref, pair_z_ref, out_ref = refs[count + 6 :]
     slots = count + 1
     out_ref[0:1, :] = held_ref[...]
     out_ref[slots : slots + 2, :] = line_ref[...]
     for slot in range(count):
-        rows = jnp.where(core_ref[0] == 0, early[slot][...], late[slot][...])
         sides = ((own_ref, own_offset_ref, own_z_ref.at[slot]), (pair_ref, pair_offset_ref, pair_z_ref.at[slot]))
-        out_ref[slot + 1 : slot + 2, :] = row_block(rows, sides, eye)
+        out_ref[slot + 1 : slot + 2, :] = row_block(refs[slot][...], sides, eye)
 
 
 def sum_columns(near_ref, far_ref, offset, off_ref, out_ref):
@@ -187,13 +184,7 @@
         pairs = blocks * src_count * tgt_count
         return pl.CostEstimate(flops=2 * pairs * width, bytes_accessed=2**20, transcendentals=pairs)
 
-    core = lax.axis_index("blk") & 1
-    core_word = core.astype(jnp.int32).reshape(1)
-
-    def across_one(value, chip, parity):
-        return lax.ppermute(value, "blk", [(i, i ^ (2 * chip) if i & 1 == parity else i) for i in range(slabs)])
-
-    early = [across_one(sources, chip, 0) for chip in range(1, chips)]
+    far_blocks = [across(sources, chip) for chip in range(1, chips)]
     pair_targets = pair(targets)
     inputs = (
         sources,
@@ -221,10 +212,7 @@
         cost_estimate=cost(1),
         name="prepare",
     )(*[pltpu.with_memory_space_constraint(x, pltpu.HBM) for x in inputs])
-    lse, late_sources = lax.optimization_barrier((lse, sources))
-    late = [across_one(late_sources, chip, 1) for chip in range(1, chips)]
     pair_offset = pair(offset)
-    lse, *early = lax.optimization_barrier((lse, *early))
     pair_z, lse = pl.pallas_call(
         near_kernel,
         out_shape=(f32(src_count, tgt_count), f32(1, src_count)),
@@ -235,19 +223,19 @@
         name="near_rows",
     )(sources, pair_targets, pair_offset, lse)
     far_lines = [across(line, chip) for chip in range(2, chips)]
-    lse, *moved = lax.optimization_barrier((lse, *early, *late, *far_lines))
+    lse, *moved = lax.optimization_barrier((lse, *far_blocks, *far_lines))
     own_far_z, pair_far_z, payload = pl.pallas_call(
         functools.partial(far_kernel, far),
         out_shape=(f32(far, src_count, tgt_count), f32(far, src_count, tgt_count), f32(chips + 2, src_count)),
-        in_specs=[SMEM] + [VMEM] * (2 * far + 6),
+        in_specs=[VMEM] * (far + 6),
         out_specs=(VMEM,) * 3,
         compiler_params=params(8 + 3 * far),
         cost_estimate=cost(2 * far),
         name="far_rows",
-    )(core_word, *moved[: 2 * far], held, offset, pair_targets, pair_offset, lse, line)
+    )(*moved[:far], held, offset, pair_targets, pair_offset, lse, line)
 
     other = across(payload, 1)
-    lines = jnp.stack([line, other[chips:]] + moved[2 * far :], axis=1)
+    lines = jnp.stack([line, other[chips:]] + moved[far:], axis=1)
     lse = merge(payload[:chips], jnp.stack([other[slot ^ 1] for slot in range(chips)]))
     chip = 2
     while chip < chips:

time: 30.2 us -> 26.5 us (0.88)
  starting transfers between devices: 13.5 us -> 10 us
  waiting for transfers between devices: 8.05 us -> 9.13 us
  Pallas kernels: 6.83 us -> 5.79 us
    ppermute x2 -> x0, starting transfers between devices: 5.78 us -> none  [across_one(): lax.ppermute(value, 'blk', [(i, i ^ 2 * chip if i & 1 == parity else i) f...]
    ppermute x1 -> x2, starting transfers between devices: 0.36 us -> 4.41 us  [across(): return lax.ppermute(value, 'blk', [(i, i ^ 2 * chip) for i in range(slabs)])]
    ppermute x3, starting transfers between devices: 3.1 us -> 0.82 us  [pair(): return lax.ppermute(value, 'blk', [(i, i ^ 1) for i in range(slabs)])]
    ppermute x1 -> x2, waiting for transfers between devices: 3.31 us -> 4.69 us  [across(): return lax.ppermute(value, 'blk', [(i, i ^ 2 * chip) for i in range(slabs)])]
    pallas_call x1, Pallas kernels: 2.18 us -> 1.14 us  [shards(): pl.pallas_call(functools.partial(far_kernel, far), out_shape=(f32(far, sr...]
    ppermute x2, starting transfers between devices: 4.3 us -> 4.78 us  [along(): return lax.ppermute(value, 'tsplit', [(i, i ^ step) for i in range(sets)])]
    ppermute x2, waiting for transfers between devices: 3.87 us -> 3.39 us  [along(): return lax.ppermute(value, 'tsplit', [(i, i ^ step) for i in range(sets)])]
  transfers between devices with their start and end apart: 8 -> 7, of which waited for: 4 -> 5; matrix products, arithmetic and copies ran while one was open for 0% -> 0% of each run, Pallas kernels for 14% -> 15%
where the time goes in v6:
time: 26.5 us; the launch traced here: 26.4 us
  starting transfers between devices  10 us (38%)
  waiting for transfers between devices  9.13 us (34%)
  Pallas kernels  5.79 us (22%)
  between operations  0.7 us (3%)
  other arithmetic  0.69 us (3%)
    ppermute x2, starting transfers between devices, along(): return lax.ppermute(value, 'tsplit', [(i, i ^ step) for i in range(sets)])  4.78 us
    ppermute x2, waiting for transfers between devices, across(): return lax.ppermute(value, 'blk', [(i, i ^ 2 * chip) for i in range(slabs)])  4.69 us
    ppermute x2, starting transfers between devices, across(): return lax.ppermute(value, 'blk', [(i, i ^ 2 * chip) for i in range(slabs)])  4.41 us
    ppermute x2, waiting for transfers between devices, along(): return lax.ppermute(value, 'tsplit', [(i, i ^ step) for i in range(sets)])  3.39 us
    pallas_call x1, Pallas kernels, shards(): pl.pallas_call(prepare_kernel, out_shape=(jax.ShapeDtypeStruct(targets.sh...  2.29 us
    pallas_call x2, Pallas kernels, columns(): pl.pallas_call(kernel, out_shape=outs, in_specs=[VMEM] * (5 + len(more)),...  1.63 us
    pallas_call x1, Pallas kernels, shards(): pl.pallas_call(functools.partial(far_kernel, far), out_shape=(f32(far, sr...  1.14 us
    ppermute x3, waiting for transfers between devices, pair(): return lax.ppermute(value, 'blk', [(i, i ^ 1) for i in range(slabs)])  1.04 us
  transfers between devices with their start and end apart: 7, of which 5 were waited for; matrix products, arithmetic and copies ran while one was open for 0% of the time, Pallas kernels for 15%

profile of v6, /device:TPU:0, one launch (start us, length us, event | category | flops | bytes accessed | tf_op | source)
XLA Modules:
  0.0 26.4 jit_solution(16491628787862702800)
XLA Ops:
  0.6 0.5 %collective-permute-start = (bf16[1024,512]{1,0:T(8,128)(2,1)}, bf16[1024,512]{1,0:T(8,128)(2,1)S(1)}, u32[]{:S(2)}, u32[]{:S(2)}) collective-permute-start(bf16[1024,512]{1,0:T(8,128)(2,1)} %tgt_hbm.1), channel_id=1, source_target_pairs={{0,4},{4,0},{8,12},{12,8},{1,5},{5,1},{9,13},{13,9},{2,6},{6,2},{1... | collective-permute-start | bytes 3145736 | tf_op jit(solution)/shard_map/ppermute | solution.py:175
  1.1 2.6 %collective-permute-start.2 = (bf16[256,512]{1,0:T(8,128)(2,1)}, bf16[256,512]{1,0:T(8,128)(2,1)S(1)}, u32[]{:S(2)}, u32[]{:S(2)}) collective-permute-start(bf16[256,512]{1,0:T(8,128)(2,1)} %rows_ref.1), channel_id=1, source_target_pairs={{0,8},{4,12},{8,0},{12,4},{1,9},{5,13},{9,1},{13,5},{2,10},{6,14},... | collective-permute-start | bytes 786440 | tf_op jit(solution)/shard_map/ppermute | solution.py:178
  3.7 2.3 %prepare.1 = (bf16[1024,512]{1,0:T(8,128)(2,1)S(1)}, f32[1,1024]{1,0:T(1,128)S(1)}, f32[256,1024]{1,0:T(8,128)S(1)}, f32[1,256]{1,0:T(1,128)S(1)}, f32[2,256]{1,0:T(2,128)S(1)}, /*index=5*/f32[1,256]{1,0:T(1,128)S(1)}) custom-call(bf16[256,512]{1,0:T(8,128)(2,1)} %rows_ref.1, bf16[1024,512]{1,0:T(8,128)(2,1)} %tgt_hbm.1, f32[8,128]{1,0:T(8,128)} %bitcast.13, ...), custom_call_target="tpu_custom_call" | custom-call | flops 268435456 | bytes 1048576 | tf_op jit(solution)/shard_map/prepare/pallas_call | solution.py:197
  6.0 0.2 collective-permute-start.1
  6.3 1.0 %collective-permute-done.1.offset_ref.refs_4_ = f32[1,1024]{1,0:T(1,128)S(1)} collective-permute-done((f32[1,1024]{1,0:T(1,128)S(1)}, f32[1,1024]{1,0:T(1,128)S(1)}, u32[]{:S(2)}, u32[]{:S(2)}) %collective-permute-start.1) | collective-permute-done | bytes 4128 | tf_op jit(solution)/shard_map/ppermute | solution.py:175
  7.3 0.0 collective-permute-done.tgt_ref.refs_3_
  7.3 0.7 %near_rows.1 = (f32[256,1024]{1,0:T(8,128)S(1)}, f32[1,256]{1,0:T(1,128)S(1)}) custom-call(bf16[256,512]{1,0:T(8,128)(2,1)S(1)} %copy-done, bf16[1024,512]{1,0:T(8,128)(2,1)S(1)} %collective-permute-done.tgt_ref.refs_3_, f32[1,1024]{1,0:T(1,128)S(1)} %collective-permute-done.1.offset_ref.refs_4_, f32[1,256]{1,0:T(1,128)S(1)} %get-tuple-element.21.held_ref), custom_call_target="tpu_custom_call" | custom-call | flops 268435456 | bytes 1048576 | tf_op jit(solution)/shard_map/near_rows/pallas_call | solution.py:216
  8.0 2.8 %collective-permute-done.2.refs_0_ = bf16[256,512]{1,0:T(8,128)(2,1)S(1)} collective-permute-done((bf16[256,512]{1,0:T(8,128)(2,1)}, bf16[256,512]{1,0:T(8,128)(2,1)S(1)}, u32[]{:S(2)}, u32[]{:S(2)}) %collective-permute-start.2) | collective-permute-done | bytes 262176 | tf_op jit(solution)/shard_map/ppermute | solution.py:178
  10.9 1.1 %far_rows.1 = (f32[1,256,1024]{2,1,0:T(8,128)S(1)}, f32[1,256,1024]{2,1,0:T(8,128)S(1)}, f32[4,256]{1,0:T(4,128)S(1)}) custom-call(bf16[256,512]{1,0:T(8,128)(2,1)S(1)} %collective-permute-done.2.refs_0_, bf16[1024,512]{1,0:T(8,128)(2,1)S(1)} %get-tuple-element.24.refs_1_, f32[1,1024]{1,0:T(1,128)S(1)} %get-tuple-element.20.refs_2_, ...), custom_call_target="tpu_custom_call" | custom-call | flops 536870912 | bytes 1048576 | tf_op jit(solution)/shard_map/far_rows/pallas_call | solution.py:227
  12.0 1.8 %collective-permute-start.3 = (f32[4,256]{1,0:T(4,128)S(1)}, f32[4,256]{1,0:T(4,128)S(1)}, u32[]{:S(2)}, u32[]{:S(2)}) collective-permute-start(f32[4,256]{1,0:T(4,128)S(1)} %get-tuple-element.28), channel_id=1, source_target_pairs={{0,8},{4,12},{8,0},{12,4},{1,9},{5,13},{9,1},{13,5},{2,10},{6,14},... | collective-permute-start | bytes 12296 | tf_op jit(solution)/shard_map/ppermute | solution.py:178
  13.8 1.9 %collective-permute-done.3 = f32[4,256]{1,0:T(4,128)S(1)} collective-permute-done((f32[4,256]{1,0:T(4,128)S(1)}, f32[4,256]{1,0:T(4,128)S(1)}, u32[]{:S(2)}, u32[]{:S(2)}) %collective-permute-start.3) | collective-permute-done | bytes 4128 | tf_op jit(solution)/shard_map/ppermute | solution.py:178
  15.7 1.9 %collective-permute-start.4 = (f32[2,256]{1,0:T(2,128)S(1)}, f32[2,256]{1,0:T(2,128)S(1)}, u32[]{:S(2)}, u32[]{:S(2)}) collective-permute-start(f32[2,256]{1,0:T(2,128)S(1)} %log_add_fusion.2), channel_id=1, source_target_pairs={{0,1},{1,0},{2,3},{3,2},{4,5},{5,4},{6,7},{7,6},{8,9},{9,8},{10,11... | collective-permute-start | bytes 6152 | tf_op jit(solution)/shard_map/ppermute | solution.py:181
  17.6 1.7 %collective-permute-done.4 = f32[2,256]{1,0:T(2,128)S(1)} collective-permute-done((f32[2,256]{1,0:T(2,128)S(1)}, f32[2,256]{1,0:T(2,128)S(1)}, u32[]{:S(2)}, u32[]{:S(2)}) %collective-permute-start.4) | collective-permute-done | bytes 2080 | tf_op jit(solution)/shard_map/ppermute | solution.py:181
  19.4 2.9 %collective-permute-start.5 = (f32[2,256]{1,0:T(2,128)S(1)}, f32[2,256]{1,0:T(2,128)S(1)}, u32[]{:S(2)}, u32[]{:S(2)}) collective-permute-start(f32[2,256]{1,0:T(2,128)S(1)} %log_add_fusion.1), channel_id=1, source_target_pairs={{0,2},{1,3},{2,0},{3,1},{4,6},{5,7},{6,4},{7,5},{8,10},{9,11},{10,... | collective-permute-start | bytes 6152 | tf_op jit(solution)/shard_map/ppermute | solution.py:181
  22.3 1.6 %collective-permute-done.5 = f32[2,256]{1,0:T(2,128)S(1)} collective-permute-done((f32[2,256]{1,0:T(2,128)S(1)}, f32[2,256]{1,0:T(2,128)S(1)}, u32[]{:S(2)}, u32[]{:S(2)}) %collective-permute-start.5) | collective-permute-done | bytes 2080 | tf_op jit(solution)/shard_map/ppermute | solution.py:181
  23.9 0.6 %columns.2 = f32[8,128]{1,0:T(8,128)S(1)} custom-call(f32[256,1024]{1,0:T(8,128)S(1)} %get-tuple-element.29.near_ref, f32[1,256,1024]{2,1,0:T(8,128)S(1)} %get-tuple-element.30.far_ref, f32[2,256]{1,0:T(2,128)S(1)} %log_add_fusion.lse_ref, f32[2,256]{1,0:T(2,128)S(1)} %get-tuple-element.37.slope_ref, f32[2,256]{1,0:T(2,128)S(1)} %get-tuple-element.36.shift_ref), custom_call_target="tpu_custom_call" | custom-call | flops 3145728 | bytes 1048576 | tf_op jit(solution)/shard_map/columns/pallas_call | solution.py:252
  24.5 0.1 collective-permute-start.6
  24.6 0.0 copy-start.1
  24.6 0.0 copy-start.2
  24.6 0.0 copy-start.3
  24.6 1.1 %columns.3 = (f32[8,128]{1,0:T(8,128)S(1)}, f32[1,256]{1,0:T(1,128)}) custom-call(f32[256,1024]{1,0:T(8,128)S(1)} %get-tuple-element.19.near_ref, f32[1,256,1024]{2,1,0:T(8,128)S(1)} %get-tuple-element.27.far_ref, f32[2,256]{1,0:T(2,128)S(1)} %log_add_fusion.lse_ref, f32[2,256]{1,0:T(2,128)S(1)} %get-tuple-element.37.slope_ref, ...), custom_call_target="tpu_custom_call" | custom-call | flops 3145728 | bytes 1048576 | tf_op jit(solution)/shard_map/columns/pallas_call | solution.py:252
  25.7 0.0 collective-permute-done.6
  25.7 0.0 copy-done.3
  25.7 0.6 %fusion = f32[1024]{0:T(1024)} fusion(f32[1024]{0:T(1024)S(1)} %copy-done.3, f32[8,128]{1,0:T(8,128)S(1)} %collective-permute-done.6, f32[8,128]{1,0:T(8,128)S(1)} %get-tuple-element.34, f32[1024]{0:T(1024)S(1)} %copy-done.1, f32[1024]{0:T(1024)S(1)} %copy-done.2), kind=kLoop, calls=%fused_computation.3 | loop fusion | flops 9216 | bytes 24576 | tf_op jit(solution)/shard_map/mul | solution.py:272
  (12 shorter events, 0.1 us)
Async XLA Ops:
  0.6 6.6 %collective-permute-start = (bf16[1024,512]{1,0:T(8,128)(2,1)}, bf16[1024,512]{1,0:T(8,128)(2,1)S(1)}, u32[]{:S(2)}, u32[]{:S(2)}) collective-permute-start(bf16[1024,512]{1,0:T(8,128)(2,1)} %tgt_hbm.1), channel_id=1, source_target_pairs={{0,4},{4,0},{8,12},{12,8},{1,5},{5,1},{9,13},{13,9},{2,6},{6,2},{1... | collective-permute-start | bytes 3145736 | tf_op jit(solution)/shard_map/ppermute | solution.py:175
  1.1 9.7 %collective-permute-start.2 = (bf16[256,512]{1,0:T(8,128)(2,1)}, bf16[256,512]{1,0:T(8,128)(2,1)S(1)}, u32[]{:S(2)}, u32[]{:S(2)}) collective-permute-start(bf16[256,512]{1,0:T(8,128)(2,1)} %rows_ref.1), channel_id=1, source_target_pairs={{0,8},{4,12},{8,0},{12,4},{1,9},{5,13},{9,1},{13,5},{2,10},{6,14},... | collective-permute-start | bytes 786440 | tf_op jit(solution)/shard_map/ppermute | solution.py:178
  3.7 3.5 %copy-start = (bf16[256,512]{1,0:T(8,128)(2,1)S(1)}, bf16[256,512]{1,0:T(8,128)(2,1)}, u32[]{:S(2)}) copy-start(bf16[256,512]{1,0:T(8,128)(2,1)} %rows_ref.1) | copy-start | bytes 786436
  6.0 1.2 %collective-permute-start.1 = (f32[1,1024]{1,0:T(1,128)S(1)}, f32[1,1024]{1,0:T(1,128)S(1)}, u32[]{:S(2)}, u32[]{:S(2)}) collective-permute-start(f32[1,1024]{1,0:T(1,128)S(1)} %get-tuple-element.20.refs_2_), channel_id=1, source_target_pairs={{0,4},{4,0},{8,12},{12,8},{1,5},{5,1},{9,13},{13,9},{2,6},{6,2},{1... | collective-permute-start | bytes 12296 | tf_op jit(solution)/shard_map/ppermute | solution.py:175
  12.0 3.7 %collective-permute-start.3 = (f32[4,256]{1,0:T(4,128)S(1)}, f32[4,256]{1,0:T(4,128)S(1)}, u32[]{:S(2)}, u32[]{:S(2)}) collective-permute-start(f32[4,256]{1,0:T(4,128)S(1)} %get-tuple-element.28), channel_id=1, source_target_pairs={{0,8},{4,12},{8,0},{12,4},{1,9},{5,13},{9,1},{13,5},{2,10},{6,14},... | collective-permute-start | bytes 12296 | tf_op jit(solution)/shard_map/ppermute | solution.py:178
  15.7 3.7 %collective-permute-start.4 = (f32[2,256]{1,0:T(2,128)S(1)}, f32[2,256]{1,0:T(2,128)S(1)}, u32[]{:S(2)}, u32[]{:S(2)}) collective-permute-start(f32[2,256]{1,0:T(2,128)S(1)} %log_add_fusion.2), channel_id=1, source_target_pairs={{0,1},{1,0},{2,3},{3,2},{4,5},{5,4},{6,7},{7,6},{8,9},{9,8},{10,11... | collective-permute-start | bytes 6152 | tf_op jit(solution)/shard_map/ppermute | solution.py:181
  19.4 4.5 %collective-permute-start.5 = (f32[2,256]{1,0:T(2,128)S(1)}, f32[2,256]{1,0:T(2,128)S(1)}, u32[]{:S(2)}, u32[]{:S(2)}) collective-permute-start(f32[2,256]{1,0:T(2,128)S(1)} %log_add_fusion.1), channel_id=1, source_target_pairs={{0,2},{1,3},{2,0},{3,1},{4,6},{5,7},{6,4},{7,5},{8,10},{9,11},{10,... | collective-permute-start | bytes 6152 | tf_op jit(solution)/shard_map/ppermute | solution.py:181
  24.5 1.2 %collective-permute-start.6 = (f32[8,128]{1,0:T(8,128)S(1)}, f32[8,128]{1,0:T(8,128)S(1)}, u32[]{:S(2)}, u32[]{:S(2)}) collective-permute-start(f32[8,128]{1,0:T(8,128)S(1)} %columns.2), channel_id=1, source_target_pairs={{0,4},{4,0},{8,12},{12,8},{1,5},{5,1},{9,13},{13,9},{2,6},{6,2},{1... | collective-permute-start | bytes 12296 | tf_op jit(solution)/shard_map/ppermute | solution.py:175
  24.6 1.2 %copy-start.1 = (f32[1024]{0:T(1024)S(1)}, f32[1024]{0:T(1024)}, u32[]{:S(2)}) copy-start(f32[1024]{0:T(1024)} %param.9) | copy-start | bytes 12292
  24.6 1.1 %copy-start.2 = (f32[1024]{0:T(1024)S(1)}, f32[1024]{0:T(1024)}, u32[]{:S(2)}) copy-start(f32[1024]{0:T(1024)} %param.11) | copy-start | bytes 12292
  24.6 1.1 %copy-start.3 = (f32[1024]{0:T(1024)S(1)}, f32[1024]{0:T(1024)}, u32[]{:S(2)}) copy-start(f32[1024]{0:T(1024)} %param.13) | copy-start | bytes 12292

commit v7 on v6

--- a/solution.py
+++ b/solution.py
@@ -12,6 +12,7 @@
 LANES = 128
 CHUNK = 256
 VMEM = pl.BlockSpec(memory_space=pltpu.VMEM)
+SMEM = pl.BlockSpec(memory_space=pltpu.SMEM)
 HBM = pl.BlockSpec(memory_space=pltpu.HBM)
 NT_DIMS = (((1,), (1,)), ((), ()))
 
@@ -68,7 +69,24 @@
     return jnp.concatenate([to_lanes(peak[p], eye) + jnp.log(to_lanes(mass[p], eye)) for p in parts], axis=1)
 
 
-def prepare_kernel(
+def prepare_kernel(turn, core_ref, *refs):
+    inputs, refs = refs[:6], refs[6:]
+    earlier, refs = refs[: 6 * (1 - turn)], refs[6 * (1 - turn) :]
+    outs, scratch = refs[:6], refs[6:]
+
+    @pl.when(core_ref[0] == turn)
+    def work():
+        prepare(*inputs, *outs, *scratch)
+
+    if earlier:
+
+        @pl.when(core_ref[0] != turn)
+        def hand_on():
+            for source, target in zip(earlier, outs):
+                target[...] = source[...]
+
+
+def prepare(
     src_hbm, tgt_hbm, pot_hbm, mass_hbm, slope_hbm, logmass_hbm,
     tgt_ref, offset_ref, z_ref, lse_ref, line_ref, sum_ref,
     src_ref, pot_ref, mass_ref, slope_ref, logmass_ref, sems,
@@ -184,7 +202,8 @@
         pairs = blocks * src_count * tgt_count
         return pl.CostEstimate(flops=2 * pairs * width, bytes_accessed=2**20, transcendentals=pairs)
 
-    far_blocks = [across(sources, chip) for chip in range(1, chips)]
+    core = lax.axis_index("blk") & 1
+    core_word = core.astype(jnp.int32).reshape(1)
     pair_targets = pair(targets)
     inputs = (
         sources,
@@ -194,24 +213,32 @@
         src_exponent.reshape(src_groups, LANES),
         src_logmass.reshape(src_groups, LANES),
     )
-    held, offset, own_z, lse, line, src_sum = pl.pallas_call(
-        prepare_kernel,
-        out_shape=(
-            jax.ShapeDtypeStruct(targets.shape, targets.dtype),
-            f32(1, tgt_count),
-            f32(src_count, tgt_count),
-            f32(1, src_count),
-            f32(2, src_count),
-            f32(1, src_count),
-        ),
-        in_specs=[HBM] * 6,
-        out_specs=(VMEM,) * 6,
-        scratch_shapes=[pltpu.VMEM(x.shape, x.dtype) for x in (inputs[0],) + inputs[2:]]
-        + [pltpu.SemaphoreType.DMA((6,))],
-        compiler_params=params(12),
-        cost_estimate=cost(1),
-        name="prepare",
-    )(*[pltpu.with_memory_space_constraint(x, pltpu.HBM) for x in inputs])
+    inputs = [pltpu.with_memory_space_constraint(x, pltpu.HBM) for x in inputs]
+
+    def prepare_on(turn, *earlier):
+        return pl.pallas_call(
+            functools.partial(prepare_kernel, turn),
+            out_shape=(
+                jax.ShapeDtypeStruct(targets.shape, targets.dtype),
+                f32(1, tgt_count),
+                f32(src_count, tgt_count),
+                f32(1, src_count),
+                f32(2, src_count),
+                f32(1, src_count),
+            ),
+            in_specs=[SMEM] + [HBM] * 6 + [VMEM] * len(earlier),
+            out_specs=(VMEM,) * 6,
+            scratch_shapes=[pltpu.VMEM(x.shape, x.dtype) for x in (inputs[0], *inputs[2:])]
+            + [pltpu.SemaphoreType.DMA((6,))],
+            compiler_params=params(12),
+            cost_estimate=cost(1),
+            name=f"prepare_{turn}",
+        )(core_word, *inputs, *earlier)
+
+    earlier = prepare_on(1)
+    first, sent = lax.optimization_barrier((earlier[5], sources))
+    far_blocks = [across(sent, chip) for chip in range(1, chips)]
+    held, offset, own_z, lse, line, src_sum = prepare_on(0, *earlier[:5], first)
     pair_offset = pair(offset)
     pair_z, lse = pl.pallas_call(
         near_kernel,

time: 26.5 us -> 25.3 us (0.955)
  waiting for transfers between devices: 9.13 us -> 5.71 us
  starting transfers between devices: 10 us -> 11.2 us
  Pallas kernels: 5.79 us -> 6.76 us
    ppermute x2, waiting for transfers between devices: 4.69 us -> 1.73 us  [across(): return lax.ppermute(value, 'blk', [(i, i ^ 2 * chip) for i in range(slabs)])]
    pallas_call x1, Pallas kernels: 0.73 us -> 1.68 us  [shards(): pl.pallas_call(near_kernel, out_shape=(f32(src_count, tgt_count), f32(1,...]
    ppermute x2, starting transfers between devices: 4.41 us -> 4.98 us  [across(): return lax.ppermute(value, 'blk', [(i, i ^ 2 * chip) for i in range(slabs)])]
    ppermute x2, starting transfers between devices: 4.78 us -> 5.24 us  [along(): return lax.ppermute(value, 'tsplit', [(i, i ^ step) for i in range(sets)])]
    ppermute x2, waiting for transfers between devices: 3.39 us -> 3.11 us  [along(): return lax.ppermute(value, 'tsplit', [(i, i ^ step) for i in range(sets)])]
    pallas_call x1 -> x2, Pallas kernels: 2.29 us -> 2.3 us  [prepare_on(): pl.pallas_call(functools.partial(prepare_kernel, turn), out_shape=(jax.Sh...]
  transfers between devices with their start and end apart: 7 -> 7, of which waited for: 5 -> 5; matrix products, arithmetic and copies ran while one was open for 0% -> 0% of each run, Pallas kernels for 15% -> 20%
where the time goes in v7:
time: 25.3 us; the launch traced here: 25.1 us
  starting transfers between devices  11.2 us (44%)
  Pallas kernels  6.76 us (27%)
  waiting for transfers between devices  5.71 us (23%)
  between operations  0.71 us (3%)
  other arithmetic  0.69 us (3%)
    ppermute x2, starting transfers between devices, along(): return lax.ppermute(value, 'tsplit', [(i, i ^ step) for i in range(sets)])  5.24 us
    ppermute x2, starting transfers between devices, across(): return lax.ppermute(value, 'blk', [(i, i ^ 2 * chip) for i in range(slabs)])  4.98 us
    ppermute x2, waiting for transfers between devices, along(): return lax.ppermute(value, 'tsplit', [(i, i ^ step) for i in range(sets)])  3.11 us
    pallas_call x2, Pallas kernels, prepare_on(): pl.pallas_call(functools.partial(prepare_kernel, turn), out_shape=(jax.Sh...  2.3 us
    ppermute x2, waiting for transfers between devices, across(): return lax.ppermute(value, 'blk', [(i, i ^ 2 * chip) for i in range(slabs)])  1.73 us
    pallas_call x1, Pallas kernels, shards(): pl.pallas_call(near_kernel, out_shape=(f32(src_count, tgt_count), f32(1,...  1.68 us
    pallas_call x2, Pallas kernels, columns(): pl.pallas_call(kernel, out_shape=outs, in_specs=[VMEM] * (5 + len(more)),...  1.63 us
    pallas_call x1, Pallas kernels, shards(): pl.pallas_call(functools.partial(far_kernel, far), out_shape=(f32(far, sr...  1.14 us
  transfers between devices with their start and end apart: 7, of which 5 were waited for; matrix products, arithmetic and copies ran while one was open for 0% of the time, Pallas kernels for 20%

profile of v7, /device:TPU:0, one launch (start us, length us, event | category | flops | bytes accessed | tf_op | source)
XLA Modules:
  0.0 25.1 jit_solution(2346878099390252464)
XLA Ops:
  0.6 0.5 %collective-permute-start = (bf16[1024,512]{1,0:T(8,128)(2,1)}, bf16[1024,512]{1,0:T(8,128)(2,1)S(1)}, u32[]{:S(2)}, u32[]{:S(2)}) collective-permute-start(bf16[1024,512]{1,0:T(8,128)(2,1)} %refs_1_.3), channel_id=1, source_target_pairs={{0,4},{4,0},{8,12},{12,8},{1,5},{5,1},{9,13},{13,9},{2,6},{6,2},{1... | collective-permute-start | bytes 3145736 | tf_op jit(solution)/shard_map/ppermute | solution.py:193
  1.1 0.1 prepare_1.1
  1.2 2.6 %collective-permute-start.2 = (bf16[256,512]{1,0:T(8,128)(2,1)}, bf16[256,512]{1,0:T(8,128)(2,1)S(1)}, u32[]{:S(2)}, u32[]{:S(2)}) collective-permute-start(bf16[256,512]{1,0:T(8,128)(2,1)} %rows_ref.1), channel_id=1, source_target_pairs={{0,8},{4,12},{8,0},{12,4},{1,9},{5,13},{9,1},{13,5},{2,10},{6,14},... | collective-permute-start | bytes 786440 | tf_op jit(solution)/shard_map/ppermute | solution.py:196
  3.8 2.2 %prepare_0.1 = (bf16[1024,512]{1,0:T(8,128)(2,1)S(1)}, f32[1,1024]{1,0:T(1,128)S(1)}, f32[256,1024]{1,0:T(8,128)S(1)}, f32[1,256]{1,0:T(1,128)S(1)}, f32[2,256]{1,0:T(2,128)S(1)}, /*index=5*/f32[1,256]{1,0:T(1,128)S(1)}) custom-call(s32[1]{0:T(128)} %bitcast.core_ref, bf16[256,512]{1,0:T(8,128)(2,1)} %rows_ref.1, bf16[1024,512]{1,0:T(8,128)(2,1)} %refs_1_.3, ...), custom_call_target="tpu_custom_call" | custom-call | flops 268435456 | bytes 1048576 | tf_op jit(solution)/shard_map/prepare_0/pallas_call | solution.py:219
  6.1 0.4 %collective-permute-start.1 = (f32[1,1024]{1,0:T(1,128)S(1)}, f32[1,1024]{1,0:T(1,128)S(1)}, u32[]{:S(2)}, u32[]{:S(2)}) collective-permute-start(f32[1,1024]{1,0:T(1,128)S(1)} %get-tuple-element.35.refs_2_), channel_id=1, source_target_pairs={{0,4},{4,0},{8,12},{12,8},{1,5},{5,1},{9,13},{13,9},{2,6},{6,2},{1... | collective-permute-start | bytes 12296 | tf_op jit(solution)/shard_map/ppermute | solution.py:193
  6.5 0.8 %collective-permute-done.1.offset_ref.refs_4_ = f32[1,1024]{1,0:T(1,128)S(1)} collective-permute-done((f32[1,1024]{1,0:T(1,128)S(1)}, f32[1,1024]{1,0:T(1,128)S(1)}, u32[]{:S(2)}, u32[]{:S(2)}) %collective-permute-start.1) | collective-permute-done | bytes 4128 | tf_op jit(solution)/shard_map/ppermute | solution.py:193
  7.3 0.0 collective-permute-done.tgt_ref.refs_3_
  7.3 1.7 %near_rows.1 = (f32[256,1024]{1,0:T(8,128)S(1)}, f32[1,256]{1,0:T(1,128)S(1)}) custom-call(bf16[256,512]{1,0:T(8,128)(2,1)} %rows_ref.1, bf16[1024,512]{1,0:T(8,128)(2,1)S(1)} %collective-permute-done.tgt_ref.refs_3_, f32[1,1024]{1,0:T(1,128)S(1)} %collective-permute-done.1.offset_ref.refs_4_, f32[1,256]{1,0:T(1,128)S(1)} %get-tuple-element.36.held_ref), custom_call_target="tpu_custom_call" | custom-call | flops 268435456 | bytes 1048576 | tf_op jit(solution)/shard_map/near_rows/pallas_call | solution.py:243
  9.0 0.1 collective-permute-done.2.refs_0_
  9.1 1.1 %far_rows.1 = (f32[1,256,1024]{2,1,0:T(8,128)S(1)}, f32[1,256,1024]{2,1,0:T(8,128)S(1)}, f32[4,256]{1,0:T(4,128)S(1)}) custom-call(bf16[256,512]{1,0:T(8,128)(2,1)S(1)} %collective-permute-done.2.refs_0_, bf16[1024,512]{1,0:T(8,128)(2,1)S(1)} %get-tuple-element.40.refs_1_, f32[1,1024]{1,0:T(1,128)S(1)} %get-tuple-element.35.refs_2_, ...), custom_call_target="tpu_custom_call" | custom-call | flops 536870912 | bytes 1048576 | tf_op jit(solution)/shard_map/far_rows/pallas_call | solution.py:254
  10.3 2.4 %collective-permute-start.3 = (f32[4,256]{1,0:T(4,128)S(1)}, f32[4,256]{1,0:T(4,128)S(1)}, u32[]{:S(2)}, u32[]{:S(2)}) collective-permute-start(f32[4,256]{1,0:T(4,128)S(1)} %get-tuple-element.44), channel_id=1, source_target_pairs={{0,8},{4,12},{8,0},{12,4},{1,9},{5,13},{9,1},{13,5},{2,10},{6,14},... | collective-permute-start | bytes 12296 | tf_op jit(solution)/shard_map/ppermute | solution.py:196
  12.7 1.6 %collective-permute-done.3 = f32[4,256]{1,0:T(4,128)S(1)} collective-permute-done((f32[4,256]{1,0:T(4,128)S(1)}, f32[4,256]{1,0:T(4,128)S(1)}, u32[]{:S(2)}, u32[]{:S(2)}) %collective-permute-start.3) | collective-permute-done | bytes 4128 | tf_op jit(solution)/shard_map/ppermute | solution.py:196
  14.3 2.1 %collective-permute-start.4 = (f32[2,256]{1,0:T(2,128)S(1)}, f32[2,256]{1,0:T(2,128)S(1)}, u32[]{:S(2)}, u32[]{:S(2)}) collective-permute-start(f32[2,256]{1,0:T(2,128)S(1)} %log_add_fusion.2), channel_id=1, source_target_pairs={{0,1},{1,0},{2,3},{3,2},{4,5},{5,4},{6,7},{7,6},{8,9},{9,8},{10,11... | collective-permute-start | bytes 6152 | tf_op jit(solution)/shard_map/ppermute | solution.py:199
  16.4 1.6 %collective-permute-done.4 = f32[2,256]{1,0:T(2,128)S(1)} collective-permute-done((f32[2,256]{1,0:T(2,128)S(1)}, f32[2,256]{1,0:T(2,128)S(1)}, u32[]{:S(2)}, u32[]{:S(2)}) %collective-permute-start.4) | collective-permute-done | bytes 2080 | tf_op jit(solution)/shard_map/ppermute | solution.py:199
  18.0 3.1 %collective-permute-start.5 = (f32[2,256]{1,0:T(2,128)S(1)}, f32[2,256]{1,0:T(2,128)S(1)}, u32[]{:S(2)}, u32[]{:S(2)}) collective-permute-start(f32[2,256]{1,0:T(2,128)S(1)} %log_add_fusion.1), channel_id=1, source_target_pairs={{0,2},{1,3},{2,0},{3,1},{4,6},{5,7},{6,4},{7,5},{8,10},{9,11},{10,... | collective-permute-start | bytes 6152 | tf_op jit(solution)/shard_map/ppermute | solution.py:199
  21.1 1.6 %collective-permute-done.5 = f32[2,256]{1,0:T(2,128)S(1)} collective-permute-done((f32[2,256]{1,0:T(2,128)S(1)}, f32[2,256]{1,0:T(2,128)S(1)}, u32[]{:S(2)}, u32[]{:S(2)}) %collective-permute-start.5) | collective-permute-done | bytes 2080 | tf_op jit(solution)/shard_map/ppermute | solution.py:199
  22.7 0.6 %columns.2 = f32[8,128]{1,0:T(8,128)S(1)} custom-call(f32[256,1024]{1,0:T(8,128)S(1)} %get-tuple-element.45.near_ref, f32[1,256,1024]{2,1,0:T(8,128)S(1)} %get-tuple-element.46.far_ref, f32[2,256]{1,0:T(2,128)S(1)} %log_add_fusion.lse_ref, f32[2,256]{1,0:T(2,128)S(1)} %get-tuple-element.53.slope_ref, f32[2,256]{1,0:T(2,128)S(1)} %get-tuple-element.52.shift_ref), custom_call_target="tpu_custom_call" | custom-call | flops 3145728 | bytes 1048576 | tf_op jit(solution)/shard_map/columns/pallas_call | solution.py:279
  23.3 0.1 collective-permute-start.6
  23.3 0.0 copy-start
  23.4 0.0 copy-start.1
  23.4 0.0 copy-start.2
  23.4 1.1 %columns.3 = (f32[8,128]{1,0:T(8,128)S(1)}, f32[1,256]{1,0:T(1,128)}) custom-call(f32[256,1024]{1,0:T(8,128)S(1)} %get-tuple-element.34.near_ref, f32[1,256,1024]{2,1,0:T(8,128)S(1)} %get-tuple-element.43.far_ref, f32[2,256]{1,0:T(2,128)S(1)} %log_add_fusion.lse_ref, f32[2,256]{1,0:T(2,128)S(1)} %get-tuple-element.53.slope_ref, ...), custom_call_target="tpu_custom_call" | custom-call | flops 3145728 | bytes 1048576 | tf_op jit(solution)/shard_map/columns/pallas_call | solution.py:279
  24.5 0.0 collective-permute-done.6
  24.5 0.6 %fusion = f32[1024]{0:T(1024)} fusion(f32[1024]{0:T(1024)S(1)} %copy-done.2, f32[8,128]{1,0:T(8,128)S(1)} %collective-permute-done.6, f32[8,128]{1,0:T(8,128)S(1)} %get-tuple-element.50, f32[1024]{0:T(1024)S(1)} %copy-done, f32[1024]{0:T(1024)S(1)} %copy-done.1), kind=kLoop, calls=%fused_computation.3 | loop fusion | flops 9216 | bytes 24576 | tf_op jit(solution)/shard_map/mul | solution.py:299
  (11 shorter events, 0.1 us)
Async XLA Ops:
  0.6 6.7 %collective-permute-start = (bf16[1024,512]{1,0:T(8,128)(2,1)}, bf16[1024,512]{1,0:T(8,128)(2,1)S(1)}, u32[]{:S(2)}, u32[]{:S(2)}) collective-permute-start(bf16[1024,512]{1,0:T(8,128)(2,1)} %refs_1_.3), channel_id=1, source_target_pairs={{0,4},{4,0},{8,12},{12,8},{1,5},{5,1},{9,13},{13,9},{2,6},{6,2},{1... | collective-permute-start | bytes 3145736 | tf_op jit(solution)/shard_map/ppermute | solution.py:193
  1.2 7.9 %collective-permute-start.2 = (bf16[256,512]{1,0:T(8,128)(2,1)}, bf16[256,512]{1,0:T(8,128)(2,1)S(1)}, u32[]{:S(2)}, u32[]{:S(2)}) collective-permute-start(bf16[256,512]{1,0:T(8,128)(2,1)} %rows_ref.1), channel_id=1, source_target_pairs={{0,8},{4,12},{8,0},{12,4},{1,9},{5,13},{9,1},{13,5},{2,10},{6,14},... | collective-permute-start | bytes 786440 | tf_op jit(solution)/shard_map/ppermute | solution.py:196
  6.1 1.2 %collective-permute-start.1 = (f32[1,1024]{1,0:T(1,128)S(1)}, f32[1,1024]{1,0:T(1,128)S(1)}, u32[]{:S(2)}, u32[]{:S(2)}) collective-permute-start(f32[1,1024]{1,0:T(1,128)S(1)} %get-tuple-element.35.refs_2_), channel_id=1, source_target_pairs={{0,4},{4,0},{8,12},{12,8},{1,5},{5,1},{9,13},{13,9},{2,6},{6,2},{1... | collective-permute-start | bytes 12296 | tf_op jit(solution)/shard_map/ppermute | solution.py:193
  10.3 4.0 %collective-permute-start.3 = (f32[4,256]{1,0:T(4,128)S(1)}, f32[4,256]{1,0:T(4,128)S(1)}, u32[]{:S(2)}, u32[]{:S(2)}) collective-permute-start(f32[4,256]{1,0:T(4,128)S(1)} %get-tuple-element.44), channel_id=1, source_target_pairs={{0,8},{4,12},{8,0},{12,4},{1,9},{5,13},{9,1},{13,5},{2,10},{6,14},... | collective-permute-start | bytes 12296 | tf_op jit(solution)/shard_map/ppermute | solution.py:196
  14.3 3.7 %collective-permute-start.4 = (f32[2,256]{1,0:T(2,128)S(1)}, f32[2,256]{1,0:T(2,128)S(1)}, u32[]{:S(2)}, u32[]{:S(2)}) collective-permute-start(f32[2,256]{1,0:T(2,128)S(1)} %log_add_fusion.2), channel_id=1, source_target_pairs={{0,1},{1,0},{2,3},{3,2},{4,5},{5,4},{6,7},{7,6},{8,9},{9,8},{10,11... | collective-permute-start | bytes 6152 | tf_op jit(solution)/shard_map/ppermute | solution.py:199
  18.0 4.7 %collective-permute-start.5 = (f32[2,256]{1,0:T(2,128)S(1)}, f32[2,256]{1,0:T(2,128)S(1)}, u32[]{:S(2)}, u32[]{:S(2)}) collective-permute-start(f32[2,256]{1,0:T(2,128)S(1)} %log_add_fusion.1), channel_id=1, source_target_pairs={{0,2},{1,3},{2,0},{3,1},{4,6},{5,7},{6,4},{7,5},{8,10},{9,11},{10,... | collective-permute-start | bytes 6152 | tf_op jit(solution)/shard_map/ppermute | solution.py:199
  23.3 1.2 %collective-permute-start.6 = (f32[8,128]{1,0:T(8,128)S(1)}, f32[8,128]{1,0:T(8,128)S(1)}, u32[]{:S(2)}, u32[]{:S(2)}) collective-permute-start(f32[8,128]{1,0:T(8,128)S(1)} %columns.2), channel_id=1, source_target_pairs={{0,4},{4,0},{8,12},{12,8},{1,5},{5,1},{9,13},{13,9},{2,6},{6,2},{1... | collective-permute-start | bytes 12296 | tf_op jit(solution)/shard_map/ppermute | solution.py:193
  23.3 1.2 %copy-start = (f32[1024]{0:T(1024)S(1)}, f32[1024]{0:T(1024)}, u32[]{:S(2)}) copy-start(f32[1024]{0:T(1024)} %param.9) | copy-start | bytes 12292
  23.4 1.1 %copy-start.1 = (f32[1024]{0:T(1024)S(1)}, f32[1024]{0:T(1024)}, u32[]{:S(2)}) copy-start(f32[1024]{0:T(1024)} %param.11) | copy-start | bytes 12292
  23.4 1.1 %copy-start.2 = (f32[1024]{0:T(1024)S(1)}, f32[1024]{0:T(1024)}, u32[]{:S(2)}) copy-start(f32[1024]{0:T(1024)} %param.13) | copy-start | bytes 12292

commit v8 on v7

--- a/solution.py
+++ b/solution.py
@@ -71,8 +71,8 @@
 
 def prepare_kernel(turn, core_ref, *refs):
     inputs, refs = refs[:6], refs[6:]
-    earlier, refs = refs[: 6 * (1 - turn)], refs[6 * (1 - turn) :]
-    outs, scratch = refs[:6], refs[6:]
+    earlier, refs = refs[: 7 * (1 - turn)], refs[7 * (1 - turn) :]
+    outs, scratch = refs[:7], refs[7:]
 
     @pl.when(core_ref[0] == turn)
     def work():
@@ -88,8 +88,8 @@
 
 def prepare(
     src_hbm, tgt_hbm, pot_hbm, mass_hbm, slope_hbm, logmass_hbm,
-    tgt_ref, offset_ref, z_ref, lse_ref, line_ref, sum_ref,
-    src_ref, pot_ref, mass_ref, slope_ref, logmass_ref, sems,
+    tgt_ref, src_ref, offset_ref, z_ref, lse_ref, line_ref, sum_ref,
+    pot_ref, mass_ref, slope_ref, logmass_ref, sems,
 ):
     pairs = (
         (tgt_hbm, tgt_ref), (src_hbm, src_ref), (pot_hbm, pot_ref),
@@ -220,6 +220,7 @@
             functools.partial(prepare_kernel, turn),
             out_shape=(
                 jax.ShapeDtypeStruct(targets.shape, targets.dtype),
+                jax.ShapeDtypeStruct(sources.shape, sources.dtype),
                 f32(1, tgt_count),
                 f32(src_count, tgt_count),
                 f32(1, src_count),
@@ -227,8 +228,8 @@
                 f32(1, src_count),
             ),
             in_specs=[SMEM] + [HBM] * 6 + [VMEM] * len(earlier),
-            out_specs=(VMEM,) * 6,
-            scratch_shapes=[pltpu.VMEM(x.shape, x.dtype) for x in (inputs[0], *inputs[2:])]
+            out_specs=(VMEM,) * 7,
+            scratch_shapes=[pltpu.VMEM(x.shape, x.dtype) for x in inputs[2:]]
             + [pltpu.SemaphoreType.DMA((6,))],
             compiler_params=params(12),
             cost_estimate=cost(1),
@@ -236,9 +237,9 @@
         )(core_word, *inputs, *earlier)
 
     earlier = prepare_on(1)
-    first, sent = lax.optimization_barrier((earlier[5], sources))
+    first, sent = lax.optimization_barrier((earlier[6], sources))
     far_blocks = [across(sent, chip) for chip in range(1, chips)]
-    held, offset, own_z, lse, line, src_sum = prepare_on(0, *earlier[:5], first)
+    held, held_sources, offset, own_z, lse, line, src_sum = prepare_on(0, *earlier[:6], first)
     pair_offset = pair(offset)
     pair_z, lse = pl.pallas_call(
         near_kernel,
@@ -248,7 +249,7 @@
         compiler_params=params(12),
         cost_estimate=cost(1),
         name="near_rows",
-    )(sources, pair_targets, pair_offset, lse)
+    )(held_sources, pair_targets, pair_offset, lse)
     far_lines = [across(line, chip) for chip in range(2, chips)]
     lse, *moved = lax.optimization_barrier((lse, *far_blocks, *far_lines))
     own_far_z, pair_far_z, payload = pl.pallas_call(
@@ -269,10 +270,8 @@
         other = across(lse, chip)
         lse = merge(lse, jnp.stack([other[slot ^ chip] for slot in range(chips)]))
         chip *= 2
-    step = 1
-    while step < sets:
-        lse = merge(lse, along(lse, step))
-        step *= 2
+    around = lax.all_gather(lse, "tsplit")
+    lse = merge(*[around[z] for z in range(sets)])
 
     def columns(kernel, near_z, far_z, *more):
         outs = (f32(groups, LANES), f32(1, src_count))[: 1 + len(more)]

time: 25.3 us -> 30.9 us (1.22)
  blocking collectives: 0 us -> 12.6 us
  starting transfers between devices: 11.2 us -> 5.61 us
  waiting for transfers between devices: 5.71 us -> 4.47 us
  Pallas kernels: 6.76 us -> 5.79 us
  local copies, waits for them, and re-layouts: 0.03 us -> 0.92 us
    all_gather x0 -> x1, blocking collectives: none -> 12.6 us  [shards(): around = lax.all_gather(lse, 'tsplit')]
    ppermute x2 -> x0, starting transfers between devices: 5.24 us -> none  [along(): return lax.ppermute(value, 'tsplit', [(i, i ^ step) for i in range(sets)])]
    ppermute x2 -> x0, waiting for transfers between devices: 3.11 us -> none  [along(): return lax.ppermute(value, 'tsplit', [(i, i ^ step) for i in range(sets)])]
    ppermute x2, waiting for transfers between devices: 1.73 us -> 3.27 us  [across(): return lax.ppermute(value, 'blk', [(i, i ^ 2 * chip) for i in range(slabs)])]
    pallas_call x1, Pallas kernels: 1.68 us -> 0.73 us  [shards(): pl.pallas_call(near_kernel, out_shape=(f32(src_count, tgt_count), f32(1,...]
    unnamed x6 -> x8, local copies, waits for them, and re-layouts: 0.02 us -> 0.91 us
    ppermute x3, starting transfers between devices: 0.99 us -> 0.66 us  [pair(): return lax.ppermute(value, 'blk', [(i, i ^ 1) for i in range(slabs)])]
    ppermute x3, waiting for transfers between devices: 0.87 us -> 1.2 us  [pair(): return lax.ppermute(value, 'blk', [(i, i ^ 1) for i in range(slabs)])]
  transfers between devices with their start and end apart: 7 -> 5, of which waited for: 5 -> 3; matrix products, arithmetic and copies ran while one was open for 0% -> 0% of each run, Pallas kernels for 20% -> 13%
where the time goes in v8:
time: 30.9 us; the launch traced here: 30.8 us
  blocking collectives  12.6 us (41%)
  Pallas kernels  5.79 us (19%)
  starting transfers between devices  5.61 us (18%)
  waiting for transfers between devices  4.47 us (14%)
  local copies, waits for them, and re-layouts  0.92 us (3%)
  between operations  0.72 us (2%)
  other arithmetic  0.67 us (2%)
    all_gather x1, blocking collectives, shards(): around = lax.all_gather(lse, 'tsplit')  12.6 us
    ppermute x2, starting transfers between devices, across(): return lax.ppermute(value, 'blk', [(i, i ^ 2 * chip) for i in range(slabs)])  4.95 us
    ppermute x2, waiting for transfers between devices, across(): return lax.ppermute(value, 'blk', [(i, i ^ 2 * chip) for i in range(slabs)])  3.27 us
    pallas_call x2, Pallas kernels, prepare_on(): pl.pallas_call(functools.partial(prepare_kernel, turn), out_shape=(jax.Sh...  2.3 us
    pallas_call x2, Pallas kernels, columns(): pl.pallas_call(kernel, out_shape=outs, in_specs=[VMEM] * (5 + len(more)),...  1.63 us
    ppermute x3, waiting for transfers between devices, pair(): return lax.ppermute(value, 'blk', [(i, i ^ 1) for i in range(slabs)])  1.2 us
    pallas_call x1, Pallas kernels, shards(): pl.pallas_call(functools.partial(far_kernel, far), out_shape=(f32(far, sr...  1.14 us
    unnamed x8, local copies, waits for them, and re-layouts  0.91 us
  transfers between devices with their start and end apart: 5, of which 3 were waited for; matrix products, arithmetic and copies ran while one was open for 0% of the time, Pallas kernels for 13%

profile of v8, /device:TPU:0, one launch (start us, length us, event | category | flops | bytes accessed | tf_op | source)
XLA Modules:
  0.0 30.8 jit_solution(9054765190013879018)
XLA Ops:
  0.6 0.5 %collective-permute-start = (bf16[1024,512]{1,0:T(8,128)(2,1)}, bf16[1024,512]{1,0:T(8,128)(2,1)S(1)}, u32[]{:S(2)}, u32[]{:S(2)}) collective-permute-start(bf16[1024,512]{1,0:T(8,128)(2,1)} %refs_1_.3), channel_id=1, source_target_pairs={{0,4},{4,0},{8,12},{12,8},{1,5},{5,1},{9,13},{13,9},{2,6},{6,2},{1... | collective-permute-start | bytes 3145736 | tf_op jit(solution)/shard_map/ppermute | solution.py:193
  1.1 0.1 prepare_1.1
  1.2 0.9 %copy-done = bf16[256,512]{1,0:T(8,128)(2,1)S(1)} copy-done((bf16[256,512]{1,0:T(8,128)(2,1)S(1)}, bf16[256,512]{1,0:T(8,128)(2,1)}, u32[]{:S(2)}) %copy-start) | copy-done | bytes 262168
  2.1 2.5 %collective-permute-start.2 = (bf16[256,512]{1,0:T(8,128)(2,1)S(1)}, bf16[256,512]{1,0:T(8,128)(2,1)S(1)}, u32[]{:S(2)}, u32[]{:S(2)}) collective-permute-start(bf16[256,512]{1,0:T(8,128)(2,1)S(1)} %copy-done), channel_id=1, source_target_pairs={{0,8},{4,12},{8,0},{12,4},{1,9},{5,13},{9,1},{13,5},{2,10},{6,14},... | collective-permute-start | bytes 786440 | tf_op jit(solution)/shard_map/ppermute | solution.py:196
  4.6 2.2 %prepare_0.1 = (bf16[1024,512]{1,0:T(8,128)(2,1)S(1)}, bf16[256,512]{1,0:T(8,128)(2,1)S(1)}, f32[1,1024]{1,0:T(1,128)S(1)}, f32[256,1024]{1,0:T(8,128)S(1)}, f32...) custom-call(s32[1]{0:T(128)} %bitcast.core_ref, bf16[256,512]{1,0:T(8,128)(2,1)} %refs_0_.3, ...), custom_call_target="tpu_custom_call" | custom-call | flops 268435456 | bytes 1048576 | tf_op jit(solution)/shard_map/prepare_0/pallas_call | solution.py:219
  6.9 0.1 collective-permute-start.1
  7.0 1.2 %collective-permute-done.1.offset_ref.refs_4_ = f32[1,1024]{1,0:T(1,128)S(1)} collective-permute-done((f32[1,1024]{1,0:T(1,128)S(1)}, f32[1,1024]{1,0:T(1,128)S(1)}, u32[]{:S(2)}, u32[]{:S(2)}) %collective-permute-start.1) | collective-permute-done | bytes 4128 | tf_op jit(solution)/shard_map/ppermute | solution.py:193
  8.1 0.0 collective-permute-done.tgt_ref.refs_3_
  8.1 0.7 %near_rows.1 = (f32[256,1024]{1,0:T(8,128)S(1)}, f32[1,256]{1,0:T(1,128)S(1)}) custom-call(bf16[256,512]{1,0:T(8,128)(2,1)S(1)} %get-tuple-element.38.rows_ref, bf16[1024,512]{1,0:T(8,128)(2,1)S(1)} %collective-permute-done.tgt_ref.refs_3_, f32[1,1024]{1,0:T(1,128)S(1)} %collective-permute-done.1.offset_ref.refs_4_, f32[1,256]{1,0:T(1,128)S(1)} %get-tuple-element.40.held_ref), custom_call_target="tpu_custom_call" | custom-call | flops 268435456 | bytes 1048576 | tf_op jit(solution)/shard_map/near_rows/pallas_call | solution.py:244
  8.9 1.7 %collective-permute-done.2.refs_0_ = bf16[256,512]{1,0:T(8,128)(2,1)S(1)} collective-permute-done((bf16[256,512]{1,0:T(8,128)(2,1)S(1)}, bf16[256,512]{1,0:T(8,128)(2,1)S(1)}, u32[]{:S(2)}, u32[]{:S(2)}) %collective-permute-start.2) | collective-permute-done | bytes 262176 | tf_op jit(solution)/shard_map/ppermute | solution.py:196
  10.5 1.1 %far_rows.1 = (f32[1,256,1024]{2,1,0:T(8,128)S(1)}, f32[1,256,1024]{2,1,0:T(8,128)S(1)}, f32[4,256]{1,0:T(4,128)S(1)}) custom-call(bf16[256,512]{1,0:T(8,128)(2,1)S(1)} %collective-permute-done.2.refs_0_, bf16[1024,512]{1,0:T(8,128)(2,1)S(1)} %get-tuple-element.44.refs_1_, f32[1,1024]{1,0:T(1,128)S(1)} %get-tuple-element.39.refs_2_, ...), custom_call_target="tpu_custom_call" | custom-call | flops 536870912 | bytes 1048576 | tf_op jit(solution)/shard_map/far_rows/pallas_call | solution.py:255
  11.7 2.4 %collective-permute-start.3 = (f32[4,256]{1,0:T(4,128)S(1)}, f32[4,256]{1,0:T(4,128)S(1)}, u32[]{:S(2)}, u32[]{:S(2)}) collective-permute-start(f32[4,256]{1,0:T(4,128)S(1)} %get-tuple-element.48), channel_id=1, source_target_pairs={{0,8},{4,12},{8,0},{12,4},{1,9},{5,13},{9,1},{13,5},{2,10},{6,14},... | collective-permute-start | bytes 12296 | tf_op jit(solution)/shard_map/ppermute | solution.py:196
  14.1 1.6 %collective-permute-done.3 = f32[4,256]{1,0:T(4,128)S(1)} collective-permute-done((f32[4,256]{1,0:T(4,128)S(1)}, f32[4,256]{1,0:T(4,128)S(1)}, u32[]{:S(2)}, u32[]{:S(2)}) %collective-permute-start.3) | collective-permute-done | bytes 4128 | tf_op jit(solution)/shard_map/ppermute | solution.py:196
  15.7 12.6 %all-gather.1 = f32[4,2,256]{2,1,0:T(2,128)S(1)} all-gather(f32[1,2,256]{2,1,0:T(2,128)S(1)} %add_bitcast_fusion), channel_id=2, replica_groups=mesh['groups'=2,'blk'=4,'tsplit'=4] {'tsplit'}, dimensions={0}, use_global_device_ids=true | all-gather | bytes 10240 | tf_op jit(solution)/shard_map/all_gather | solution.py:273
  28.4 0.6 %columns.2 = f32[8,128]{1,0:T(8,128)S(1)} custom-call(f32[256,1024]{1,0:T(8,128)S(1)} %get-tuple-element.49.near_ref, f32[1,256,1024]{2,1,0:T(8,128)S(1)} %get-tuple-element.50.far_ref, f32[2,256]{1,0:T(2,128)S(1)} %log_add_fusion.lse_ref, f32[2,256]{1,0:T(2,128)S(1)} %get-tuple-element.57.slope_ref, f32[2,256]{1,0:T(2,128)S(1)} %get-tuple-element.56.shift_ref), custom_call_target="tpu_custom_call" | custom-call | flops 3145728 | bytes 1048576 | tf_op jit(solution)/shard_map/columns/pallas_call | solution.py:278
  28.9 0.1 collective-permute-start.4
  29.0 0.0 copy-start.1
  29.0 0.0 copy-start.2
  29.0 0.0 copy-start.3
  29.0 1.1 %columns.3 = (f32[8,128]{1,0:T(8,128)S(1)}, f32[1,256]{1,0:T(1,128)}) custom-call(f32[256,1024]{1,0:T(8,128)S(1)} %get-tuple-element.37.near_ref, f32[1,256,1024]{2,1,0:T(8,128)S(1)} %get-tuple-element.47.far_ref, f32[2,256]{1,0:T(2,128)S(1)} %log_add_fusion.lse_ref, f32[2,256]{1,0:T(2,128)S(1)} %get-tuple-element.57.slope_ref, ...), custom_call_target="tpu_custom_call" | custom-call | flops 3145728 | bytes 1048576 | tf_op jit(solution)/shard_map/columns/pallas_call | solution.py:278
  30.1 0.0 collective-permute-done.4
  30.1 0.0 copy-done.1
  30.1 0.0 copy-done.3
  30.2 0.6 %fusion = f32[1024]{0:T(1024)} fusion(f32[1024]{0:T(1024)S(1)} %copy-done.3, f32[8,128]{1,0:T(8,128)S(1)} %collective-permute-done.4, f32[8,128]{1,0:T(8,128)S(1)} %get-tuple-element.54, f32[1024]{0:T(1024)S(1)} %copy-done.1, f32[1024]{0:T(1024)S(1)} %copy-done.2), kind=kLoop, calls=%fused_computation.3 | loop fusion | flops 9216 | bytes 24576 | tf_op jit(solution)/shard_map/mul | solution.py:298
  (9 shorter events, 0.1 us)
Async XLA Ops:
  0.6 7.5 %collective-permute-start = (bf16[1024,512]{1,0:T(8,128)(2,1)}, bf16[1024,512]{1,0:T(8,128)(2,1)S(1)}, u32[]{:S(2)}, u32[]{:S(2)}) collective-permute-start(bf16[1024,512]{1,0:T(8,128)(2,1)} %refs_1_.3), channel_id=1, source_target_pairs={{0,4},{4,0},{8,12},{12,8},{1,5},{5,1},{9,13},{13,9},{2,6},{6,2},{1... | collective-permute-start | bytes 3145736 | tf_op jit(solution)/shard_map/ppermute | solution.py:193
  1.1 0.9 %copy-start = (bf16[256,512]{1,0:T(8,128)(2,1)S(1)}, bf16[256,512]{1,0:T(8,128)(2,1)}, u32[]{:S(2)}) copy-start(bf16[256,512]{1,0:T(8,128)(2,1)} %refs_0_.3) | copy-start | bytes 786436
  2.1 8.4 %collective-permute-start.2 = (bf16[256,512]{1,0:T(8,128)(2,1)S(1)}, bf16[256,512]{1,0:T(8,128)(2,1)S(1)}, u32[]{:S(2)}, u32[]{:S(2)}) collective-permute-start(bf16[256,512]{1,0:T(8,128)(2,1)S(1)} %copy-done), channel_id=1, source_target_pairs={{0,8},{4,12},{8,0},{12,4},{1,9},{5,13},{9,1},{13,5},{2,10},{6,14},... | collective-permute-start | bytes 786440 | tf_op jit(solution)/shard_map/ppermute | solution.py:196
  6.9 1.2 %collective-permute-start.1 = (f32[1,1024]{1,0:T(1,128)S(1)}, f32[1,1024]{1,0:T(1,128)S(1)}, u32[]{:S(2)}, u32[]{:S(2)}) collective-permute-start(f32[1,1024]{1,0:T(1,128)S(1)} %get-tuple-element.39.refs_2_), channel_id=1, source_target_pairs={{0,4},{4,0},{8,12},{12,8},{1,5},{5,1},{9,13},{13,9},{2,6},{6,2},{1... | collective-permute-start | bytes 12296 | tf_op jit(solution)/shard_map/ppermute | solution.py:193
  11.7 4.0 %collective-permute-start.3 = (f32[4,256]{1,0:T(4,128)S(1)}, f32[4,256]{1,0:T(4,128)S(1)}, u32[]{:S(2)}, u32[]{:S(2)}) collective-permute-start(f32[4,256]{1,0:T(4,128)S(1)} %get-tuple-element.48), channel_id=1, source_target_pairs={{0,8},{4,12},{8,0},{12,4},{1,9},{5,13},{9,1},{13,5},{2,10},{6,14},... | collective-permute-start | bytes 12296 | tf_op jit(solution)/shard_map/ppermute | solution.py:196
  28.9 1.2 %collective-permute-start.4 = (f32[8,128]{1,0:T(8,128)S(1)}, f32[8,128]{1,0:T(8,128)S(1)}, u32[]{:S(2)}, u32[]{:S(2)}) collective-permute-start(f32[8,128]{1,0:T(8,128)S(1)} %columns.2), channel_id=1, source_target_pairs={{0,4},{4,0},{8,12},{12,8},{1,5},{5,1},{9,13},{13,9},{2,6},{6,2},{1... | collective-permute-start | bytes 12296 | tf_op jit(solution)/shard_map/ppermute | solution.py:193
  29.0 1.2 %copy-start.1 = (f32[1024]{0:T(1024)S(1)}, f32[1024]{0:T(1024)}, u32[]{:S(2)}) copy-start(f32[1024]{0:T(1024)} %param.9) | copy-start | bytes 12292
  29.0 1.1 %copy-start.2 = (f32[1024]{0:T(1024)S(1)}, f32[1024]{0:T(1024)}, u32[]{:S(2)}) copy-start(f32[1024]{0:T(1024)} %param.11) | copy-start | bytes 12292
  29.0 1.1 %copy-start.3 = (f32[1024]{0:T(1024)S(1)}, f32[1024]{0:T(1024)}, u32[]{:S(2)}) copy-start(f32[1024]{0:T(1024)} %param.13) | copy-start | bytes 12292

commit v9 on v7

--- a/solution.py
+++ b/solution.py
@@ -269,10 +269,7 @@
         other = across(lse, chip)
         lse = merge(lse, jnp.stack([other[slot ^ chip] for slot in range(chips)]))
         chip *= 2
-    step = 1
-    while step < sets:
-        lse = merge(lse, along(lse, step))
-        step *= 2
+    lse = merge(lse, *[along(lse, step) for step in range(sets - 1, 0, -1)])
 
     def columns(kernel, near_z, far_z, *more):
         outs = (f32(groups, LANES), f32(1, src_count))[: 1 + len(more)]

time: 25.3 us -> 25.6 us (1.012)
  waiting for transfers between devices: 5.71 us -> 6.42 us
  starting transfers between devices: 11.2 us -> 10.8 us
    ppermute x2 -> x3, waiting for transfers between devices: 3.11 us -> 3.82 us  [along(): return lax.ppermute(value, 'tsplit', [(i, i ^ step) for i in range(sets)])]
    ppermute x2 -> x3, starting transfers between devices: 5.24 us -> 4.8 us  [along(): return lax.ppermute(value, 'tsplit', [(i, i ^ step) for i in range(sets)])]
  transfers between devices with their start and end apart: 7 -> 8, of which waited for: 5 -> 5; matrix products, arithmetic and copies ran while one was open for 0% -> 0% of each run, Pallas kernels for 20% -> 20%
where the time goes in v9:
time: 25.6 us; the launch traced here: 25.4 us
  starting transfers between devices  10.8 us (42%)
  Pallas kernels  6.75 us (26%)
  waiting for transfers between devices  6.42 us (25%)
  between operations  0.71 us (3%)
  other arithmetic  0.69 us (3%)
    ppermute x2, starting transfers between devices, across(): return lax.ppermute(value, 'blk', [(i, i ^ 2 * chip) for i in range(slabs)])  4.98 us
    ppermute x3, starting transfers between devices, along(): return lax.ppermute(value, 'tsplit', [(i, i ^ step) for i in range(sets)])  4.8 us
    ppermute x3, waiting for transfers between devices, along(): return lax.ppermute(value, 'tsplit', [(i, i ^ step) for i in range(sets)])  3.82 us
    pallas_call x2, Pallas kernels, prepare_on(): pl.pallas_call(functools.partial(prepare_kernel, turn), out_shape=(jax.Sh...  2.3 us
    ppermute x2, waiting for transfers between devices, across(): return lax.ppermute(value, 'blk', [(i, i ^ 2 * chip) for i in range(slabs)])  1.73 us
    pallas_call x1, Pallas kernels, shards(): pl.pallas_call(near_kernel, out_shape=(f32(src_count, tgt_count), f32(1,...  1.68 us
    pallas_call x2, Pallas kernels, columns(): pl.pallas_call(kernel, out_shape=outs, in_specs=[VMEM] * (5 + len(more)),...  1.63 us
    pallas_call x1, Pallas kernels, shards(): pl.pallas_call(functools.partial(far_kernel, far), out_shape=(f32(far, sr...  1.14 us
  transfers between devices with their start and end apart: 8, of which 5 were waited for; matrix products, arithmetic and copies ran while one was open for 0% of the time, Pallas kernels for 20%

profile of v9, /device:TPU:0, one launch (start us, length us, event | category | flops | bytes accessed | tf_op | source)
XLA Modules:
  0.0 25.4 jit_solution(6922628646592522801)
XLA Ops:
  0.6 0.5 %collective-permute-start = (bf16[1024,512]{1,0:T(8,128)(2,1)}, bf16[1024,512]{1,0:T(8,128)(2,1)S(1)}, u32[]{:S(2)}, u32[]{:S(2)}) collective-permute-start(bf16[1024,512]{1,0:T(8,128)(2,1)} %refs_1_.3), channel_id=1, source_target_pairs={{0,4},{4,0},{8,12},{12,8},{1,5},{5,1},{9,13},{13,9},{2,6},{6,2},{1... | collective-permute-start | bytes 3145736 | tf_op jit(solution)/shard_map/ppermute | solution.py:193
  1.1 0.1 prepare_1.1
  1.2 2.6 %collective-permute-start.2 = (bf16[256,512]{1,0:T(8,128)(2,1)}, bf16[256,512]{1,0:T(8,128)(2,1)S(1)}, u32[]{:S(2)}, u32[]{:S(2)}) collective-permute-start(bf16[256,512]{1,0:T(8,128)(2,1)} %rows_ref.1), channel_id=1, source_target_pairs={{0,8},{4,12},{8,0},{12,4},{1,9},{5,13},{9,1},{13,5},{2,10},{6,14},... | collective-permute-start | bytes 786440 | tf_op jit(solution)/shard_map/ppermute | solution.py:196
  3.8 2.2 %prepare_0.1 = (bf16[1024,512]{1,0:T(8,128)(2,1)S(1)}, f32[1,1024]{1,0:T(1,128)S(1)}, f32[256,1024]{1,0:T(8,128)S(1)}, f32[1,256]{1,0:T(1,128)S(1)}, f32[2,256]{1,0:T(2,128)S(1)}, /*index=5*/f32[1,256]{1,0:T(1,128)S(1)}) custom-call(s32[1]{0:T(128)} %bitcast.core_ref, bf16[256,512]{1,0:T(8,128)(2,1)} %rows_ref.1, bf16[1024,512]{1,0:T(8,128)(2,1)} %refs_1_.3, ...), custom_call_target="tpu_custom_call" | custom-call | flops 268435456 | bytes 1048576 | tf_op jit(solution)/shard_map/prepare_0/pallas_call | solution.py:219
  6.1 0.4 %collective-permute-start.1 = (f32[1,1024]{1,0:T(1,128)S(1)}, f32[1,1024]{1,0:T(1,128)S(1)}, u32[]{:S(2)}, u32[]{:S(2)}) collective-permute-start(f32[1,1024]{1,0:T(1,128)S(1)} %get-tuple-element.35.refs_2_), channel_id=1, source_target_pairs={{0,4},{4,0},{8,12},{12,8},{1,5},{5,1},{9,13},{13,9},{2,6},{6,2},{1... | collective-permute-start | bytes 12296 | tf_op jit(solution)/shard_map/ppermute | solution.py:193
  6.5 0.8 %collective-permute-done.1.offset_ref.refs_4_ = f32[1,1024]{1,0:T(1,128)S(1)} collective-permute-done((f32[1,1024]{1,0:T(1,128)S(1)}, f32[1,1024]{1,0:T(1,128)S(1)}, u32[]{:S(2)}, u32[]{:S(2)}) %collective-permute-start.1) | collective-permute-done | bytes 4128 | tf_op jit(solution)/shard_map/ppermute | solution.py:193
  7.3 0.0 collective-permute-done.tgt_ref.refs_3_
  7.3 1.7 %near_rows.1 = (f32[256,1024]{1,0:T(8,128)S(1)}, f32[1,256]{1,0:T(1,128)S(1)}) custom-call(bf16[256,512]{1,0:T(8,128)(2,1)} %rows_ref.1, bf16[1024,512]{1,0:T(8,128)(2,1)S(1)} %collective-permute-done.tgt_ref.refs_3_, f32[1,1024]{1,0:T(1,128)S(1)} %collective-permute-done.1.offset_ref.refs_4_, f32[1,256]{1,0:T(1,128)S(1)} %get-tuple-element.36.held_ref), custom_call_target="tpu_custom_call" | custom-call | flops 268435456 | bytes 1048576 | tf_op jit(solution)/shard_map/near_rows/pallas_call | solution.py:243
  9.0 0.1 collective-permute-done.2.refs_0_
  9.1 1.1 %far_rows.1 = (f32[1,256,1024]{2,1,0:T(8,128)S(1)}, f32[1,256,1024]{2,1,0:T(8,128)S(1)}, f32[4,256]{1,0:T(4,128)S(1)}) custom-call(bf16[256,512]{1,0:T(8,128)(2,1)S(1)} %collective-permute-done.2.refs_0_, bf16[1024,512]{1,0:T(8,128)(2,1)S(1)} %get-tuple-element.40.refs_1_, f32[1,1024]{1,0:T(1,128)S(1)} %get-tuple-element.35.refs_2_, ...), custom_call_target="tpu_custom_call" | custom-call | flops 536870912 | bytes 1048576 | tf_op jit(solution)/shard_map/far_rows/pallas_call | solution.py:254
  10.3 2.4 %collective-permute-start.3 = (f32[4,256]{1,0:T(4,128)S(1)}, f32[4,256]{1,0:T(4,128)S(1)}, u32[]{:S(2)}, u32[]{:S(2)}) collective-permute-start(f32[4,256]{1,0:T(4,128)S(1)} %get-tuple-element.44), channel_id=1, source_target_pairs={{0,8},{4,12},{8,0},{12,4},{1,9},{5,13},{9,1},{13,5},{2,10},{6,14},... | collective-permute-start | bytes 12296 | tf_op jit(solution)/shard_map/ppermute | solution.py:196
  12.7 1.6 %collective-permute-done.3 = f32[4,256]{1,0:T(4,128)S(1)} collective-permute-done((f32[4,256]{1,0:T(4,128)S(1)}, f32[4,256]{1,0:T(4,128)S(1)}, u32[]{:S(2)}, u32[]{:S(2)}) %collective-permute-start.3) | collective-permute-done | bytes 4128 | tf_op jit(solution)/shard_map/ppermute | solution.py:196
  14.3 4.2 %collective-permute-start.4 = (f32[2,256]{1,0:T(2,128)S(1)}, f32[2,256]{1,0:T(2,128)S(1)}, u32[]{:S(2)}, u32[]{:S(2)}) collective-permute-start(f32[2,256]{1,0:T(2,128)S(1)} %log_add_fusion.1), channel_id=1, source_target_pairs={{0,3},{1,2},{2,1},{3,0},{4,7},{5,6},{6,5},{7,4},{8,11},{9,10},{10,... | collective-permute-start | bytes 6152 | tf_op jit(solution)/shard_map/ppermute | solution.py:199
  18.4 0.6 %collective-permute-start.6 = (f32[2,256]{1,0:T(2,128)S(1)}, f32[2,256]{1,0:T(2,128)S(1)}, u32[]{:S(2)}, u32[]{:S(2)}) collective-permute-start(f32[2,256]{1,0:T(2,128)S(1)} %log_add_fusion.1), channel_id=1, source_target_pairs={{0,1},{1,0},{2,3},{3,2},{4,5},{5,4},{6,7},{7,6},{8,9},{9,8},{10,11... | collective-permute-start | bytes 6152 | tf_op jit(solution)/shard_map/ppermute | solution.py:199
  19.1 0.9 %collective-permute-done.4 = f32[2,256]{1,0:T(2,128)S(1)} collective-permute-done((f32[2,256]{1,0:T(2,128)S(1)}, f32[2,256]{1,0:T(2,128)S(1)}, u32[]{:S(2)}, u32[]{:S(2)}) %collective-permute-start.4) | collective-permute-done | bytes 2080 | tf_op jit(solution)/shard_map/ppermute | solution.py:199
  20.0 2.9 %collective-permute-done.5 = f32[2,256]{1,0:T(2,128)S(1)} collective-permute-done((f32[2,256]{1,0:T(2,128)S(1)}, f32[2,256]{1,0:T(2,128)S(1)}, u32[]{:S(2)}, u32[]{:S(2)}) %collective-permute-start.5) | collective-permute-done | bytes 2080 | tf_op jit(solution)/shard_map/ppermute | solution.py:199
  23.0 0.6 %columns.2 = f32[8,128]{1,0:T(8,128)S(1)} custom-call(f32[256,1024]{1,0:T(8,128)S(1)} %get-tuple-element.45.near_ref, f32[1,256,1024]{2,1,0:T(8,128)S(1)} %get-tuple-element.46.far_ref, f32[2,256]{1,0:T(2,128)S(1)} %log_add_fusion.lse_ref, f32[2,256]{1,0:T(2,128)S(1)} %get-tuple-element.53.slope_ref, f32[2,256]{1,0:T(2,128)S(1)} %get-tuple-element.52.shift_ref), custom_call_target="tpu_custom_call" | custom-call | flops 3145728 | bytes 1048576 | tf_op jit(solution)/shard_map/columns/pallas_call | solution.py:276
  23.5 0.1 collective-permute-start.7
  23.6 0.0 copy-start
  23.6 0.0 copy-start.1
  23.6 0.0 copy-start.2
  23.6 1.1 %columns.3 = (f32[8,128]{1,0:T(8,128)S(1)}, f32[1,256]{1,0:T(1,128)}) custom-call(f32[256,1024]{1,0:T(8,128)S(1)} %get-tuple-element.34.near_ref, f32[1,256,1024]{2,1,0:T(8,128)S(1)} %get-tuple-element.43.far_ref, f32[2,256]{1,0:T(2,128)S(1)} %log_add_fusion.lse_ref, f32[2,256]{1,0:T(2,128)S(1)} %get-tuple-element.53.slope_ref, ...), custom_call_target="tpu_custom_call" | custom-call | flops 3145728 | bytes 1048576 | tf_op jit(solution)/shard_map/columns/pallas_call | solution.py:276
  24.7 0.0 collective-permute-done.7
  24.8 0.6 %fusion = f32[1024]{0:T(1024)} fusion(f32[1024]{0:T(1024)S(1)} %copy-done.2, f32[8,128]{1,0:T(8,128)S(1)} %collective-permute-done.7, f32[8,128]{1,0:T(8,128)S(1)} %get-tuple-element.50, f32[1024]{0:T(1024)S(1)} %copy-done, f32[1024]{0:T(1024)S(1)} %copy-done.1), kind=kLoop, calls=%fused_computation.3 | loop fusion | flops 9216 | bytes 24576 | tf_op jit(solution)/shard_map/mul | solution.py:296
  (12 shorter events, 0.1 us)
Async XLA Ops:
  0.6 6.7 %collective-permute-start = (bf16[1024,512]{1,0:T(8,128)(2,1)}, bf16[1024,512]{1,0:T(8,128)(2,1)S(1)}, u32[]{:S(2)}, u32[]{:S(2)}) collective-permute-start(bf16[1024,512]{1,0:T(8,128)(2,1)} %refs_1_.3), channel_id=1, source_target_pairs={{0,4},{4,0},{8,12},{12,8},{1,5},{5,1},{9,13},{13,9},{2,6},{6,2},{1... | collective-permute-start | bytes 3145736 | tf_op jit(solution)/shard_map/ppermute | solution.py:193
  1.2 7.9 %collective-permute-start.2 = (bf16[256,512]{1,0:T(8,128)(2,1)}, bf16[256,512]{1,0:T(8,128)(2,1)S(1)}, u32[]{:S(2)}, u32[]{:S(2)}) collective-permute-start(bf16[256,512]{1,0:T(8,128)(2,1)} %rows_ref.1), channel_id=1, source_target_pairs={{0,8},{4,12},{8,0},{12,4},{1,9},{5,13},{9,1},{13,5},{2,10},{6,14},... | collective-permute-start | bytes 786440 | tf_op jit(solution)/shard_map/ppermute | solution.py:196
  6.1 1.2 %collective-permute-start.1 = (f32[1,1024]{1,0:T(1,128)S(1)}, f32[1,1024]{1,0:T(1,128)S(1)}, u32[]{:S(2)}, u32[]{:S(2)}) collective-permute-start(f32[1,1024]{1,0:T(1,128)S(1)} %get-tuple-element.35.refs_2_), channel_id=1, source_target_pairs={{0,4},{4,0},{8,12},{12,8},{1,5},{5,1},{9,13},{13,9},{2,6},{6,2},{1... | collective-permute-start | bytes 12296 | tf_op jit(solution)/shard_map/ppermute | solution.py:193
  10.3 4.0 %collective-permute-start.3 = (f32[4,256]{1,0:T(4,128)S(1)}, f32[4,256]{1,0:T(4,128)S(1)}, u32[]{:S(2)}, u32[]{:S(2)}) collective-permute-start(f32[4,256]{1,0:T(4,128)S(1)} %get-tuple-element.44), channel_id=1, source_target_pairs={{0,8},{4,12},{8,0},{12,4},{1,9},{5,13},{9,1},{13,5},{2,10},{6,14},... | collective-permute-start | bytes 12296 | tf_op jit(solution)/shard_map/ppermute | solution.py:196
  14.3 5.7 %collective-permute-start.4 = (f32[2,256]{1,0:T(2,128)S(1)}, f32[2,256]{1,0:T(2,128)S(1)}, u32[]{:S(2)}, u32[]{:S(2)}) collective-permute-start(f32[2,256]{1,0:T(2,128)S(1)} %log_add_fusion.1), channel_id=1, source_target_pairs={{0,3},{1,2},{2,1},{3,0},{4,7},{5,6},{6,5},{7,4},{8,11},{9,10},{10,... | collective-permute-start | bytes 6152 | tf_op jit(solution)/shard_map/ppermute | solution.py:199
  18.4 4.5 %collective-permute-start.5 = (f32[2,256]{1,0:T(2,128)S(1)}, f32[2,256]{1,0:T(2,128)S(1)}, u32[]{:S(2)}, u32[]{:S(2)}) collective-permute-start(f32[2,256]{1,0:T(2,128)S(1)} %log_add_fusion.1), channel_id=1, source_target_pairs={{0,2},{1,3},{2,0},{3,1},{4,6},{5,7},{6,4},{7,5},{8,10},{9,11},{10,... | collective-permute-start | bytes 6152 | tf_op jit(solution)/shard_map/ppermute | solution.py:199
  18.4 4.5 %collective-permute-start.6 = (f32[2,256]{1,0:T(2,128)S(1)}, f32[2,256]{1,0:T(2,128)S(1)}, u32[]{:S(2)}, u32[]{:S(2)}) collective-permute-start(f32[2,256]{1,0:T(2,128)S(1)} %log_add_fusion.1), channel_id=1, source_target_pairs={{0,1},{1,0},{2,3},{3,2},{4,5},{5,4},{6,7},{7,6},{8,9},{9,8},{10,11... | collective-permute-start | bytes 6152 | tf_op jit(solution)/shard_map/ppermute | solution.py:199
  23.5 1.2 %collective-permute-start.7 = (f32[8,128]{1,0:T(8,128)S(1)}, f32[8,128]{1,0:T(8,128)S(1)}, u32[]{:S(2)}, u32[]{:S(2)}) collective-permute-start(f32[8,128]{1,0:T(8,128)S(1)} %columns.2), channel_id=1, source_target_pairs={{0,4},{4,0},{8,12},{12,8},{1,5},{5,1},{9,13},{13,9},{2,6},{6,2},{1... | collective-permute-start | bytes 12296 | tf_op jit(solution)/shard_map/ppermute | solution.py:193
  23.6 1.2 %copy-start = (f32[1024]{0:T(1024)S(1)}, f32[1024]{0:T(1024)}, u32[]{:S(2)}) copy-start(f32[1024]{0:T(1024)} %param.9) | copy-start | bytes 12292
  23.6 1.1 %copy-start.1 = (f32[1024]{0:T(1024)S(1)}, f32[1024]{0:T(1024)}, u32[]{:S(2)}) copy-start(f32[1024]{0:T(1024)} %param.11) | copy-start | bytes 12292
  23.6 1.1 %copy-start.2 = (f32[1024]{0:T(1024)S(1)}, f32[1024]{0:T(1024)}, u32[]{:S(2)}) copy-start(f32[1024]{0:T(1024)} %param.13) | copy-start | bytes 12292

commit v10 on v7

--- a/solution.py
+++ b/solution.py
@@ -1,4 +1,5 @@
 import functools
+import math
 
 import jax
 import jax.numpy as jnp
@@ -9,6 +10,8 @@
 
 EPSILON = 0.5
 LOGIT_SCALE = 2.0 / EPSILON
+LOG2_E = math.log2(math.e)
+LOG_2 = math.log(2.0)
 LANES = 128
 CHUNK = 256
 VMEM = pl.BlockSpec(memory_space=pltpu.VMEM)
@@ -31,10 +34,6 @@
     return jnp.sum(jnp.where(eye, lanes, 0.0), axis=1, keepdims=True)
 
 
-def fold_rows(value, op):
-    return op(value.reshape(value.shape[0] // 8, 8, value.shape[1]), axis=0)
-
-
 def merge(*parts):
     peak = functools.reduce(jnp.maximum, parts)
     return peak + jnp.log(sum(jnp.exp(part - peak) for part in parts))
@@ -48,25 +47,42 @@
 def row_block(rows, sides, eye):
     rows = rows * LOGIT_SCALE
     src_count = rows.shape[0]
-    peak = None
-    for tgt_ref, offset_ref, z_ref in sides:
-        for at in range(0, tgt_ref.shape[0], CHUNK):
-            cols = slice(at, at + CHUNK)
-            dots = lax.dot_general(rows, tgt_ref[cols, :], NT_DIMS, preferred_element_type=jnp.float32)
-            z = dots + offset_ref[:, cols]
-            z_ref[:, cols] = z
-            for lane in range(0, CHUNK, LANES):
-                part = z[:, lane : lane + LANES]
-                peak = part if peak is None else jnp.maximum(peak, part)
-    peak = jnp.max(peak, axis=1, keepdims=True)
-    mass = None
-    for _, _, z_ref in sides:
-        for at in range(0, z_ref.shape[1], LANES):
-            term = jnp.exp(z_ref[:, at : at + LANES] - peak)
-            mass = term if mass is None else mass + term
+
+    def product(side, at):
+        tgt_ref, offset_ref, z_ref = sides[side]
+        cols = slice(at, at + CHUNK)
+        dots = lax.dot_general(rows, tgt_ref[cols, :], NT_DIMS, preferred_element_type=jnp.float32)
+        z = (dots + offset_ref[:, cols]) * LOG2_E
+        z_ref[:, cols] = z
+        high = z[:, :LANES]
+        for lane in range(LANES, CHUNK, LANES):
+            high = jnp.maximum(high, z[:, lane : lane + LANES])
+        return high
+
+    def raise_to(side, at, peak):
+        z_ref = sides[side][2]
+        return sum(jnp.exp2(z_ref[:, lane : lane + LANES] - peak) for lane in range(at, at + CHUNK, LANES))
+
+    steps = range(0, sides[0][0].shape[0], CHUNK)
+    peaks, masses = [], []
+    for side in range(len(sides) + 1):
+        peak = mass = None
+        for at in steps:
+            if side < len(sides):
+                high = product(side, at)
+                peak = high if peak is None else jnp.maximum(peak, high)
+            if side > 0:
+                term = raise_to(side - 1, at, peaks[-1])
+                mass = term if mass is None else mass + term
+        if side < len(sides):
+            peaks.append(peak)
+        if side > 0:
+            masses.append(mass)
+    peak = jnp.max(functools.reduce(jnp.maximum, peaks), axis=1, keepdims=True)
+    mass = sum(mass * jnp.exp2(high - peak) for high, mass in zip(peaks, masses))
     mass = jnp.sum(mass, axis=1, keepdims=True)
     parts = [slice(at, at + LANES) for at in range(0, src_count, LANES)]
-    return jnp.concatenate([to_lanes(peak[p], eye) + jnp.log(to_lanes(mass[p], eye)) for p in parts], axis=1)
+    return jnp.concatenate([to_lanes(peak[p], eye) * LOG_2 + jnp.log(to_lanes(mass[p], eye)) for p in parts], axis=1)
 
 
 def prepare_kernel(turn, core_ref, *refs):
@@ -138,26 +154,21 @@
     slots, src_count = offset.shape
     for slot in range(slots):
         for at in range(0, src_count, LANES):
-            column = to_column(offset[slot : slot + 1, at : at + LANES], eye)
+            column = to_column(offset[slot : slot + 1, at : at + LANES] * LOG2_E, eye)
             off_ref[slot, at : at + LANES, :] = jnp.broadcast_to(column, (LANES, LANES))
-
-    def shifted(slot, cols):
-        z = near_ref[:, cols] if slot == 0 else far_ref[slot - 1, :, cols]
-        return z + off_ref[slot]
 
     for group in range(out_ref.shape[0]):
         cols = slice(group * LANES, (group + 1) * LANES)
-        peak = None
+        peaks, masses = [], []
         for slot in range(slots):
-            high = fold_rows(shifted(slot, cols), jnp.max)
-            peak = high if peak is None else jnp.maximum(peak, high)
-        peak = jnp.max(peak, axis=0, keepdims=True)
-        mass = None
-        for slot in range(slots):
-            term = fold_rows(jnp.exp(shifted(slot, cols) - peak), jnp.sum)
-            mass = term if mass is None else mass + term
+            z = near_ref[:, cols] if slot == 0 else far_ref[slot - 1, :, cols]
+            z = (z + off_ref[slot]).reshape(src_count // 8, 8, LANES)
+            peaks.append(jnp.max(z, axis=0))
+            masses.append(jnp.sum(jnp.exp2(z - peaks[-1]), axis=0))
+        peak = jnp.max(functools.reduce(jnp.maximum, peaks), axis=0, keepdims=True)
+        mass = sum(mass * jnp.exp2(high - peak) for high, mass in zip(peaks, masses))
         mass = jnp.sum(mass, axis=0, keepdims=True)
-        out_ref[group : group + 1, :] = peak + jnp.log(mass)
+        out_ref[group : group + 1, :] = peak * LOG_2 + jnp.log(mass)
 
 
 def pair_kernel(near_ref, far_ref, lse_ref, slope_ref, shift_ref, out_ref, off_ref):
@@ -187,7 +198,7 @@
     far = chips - 1
     groups = tgt_count // LANES
     src_groups = src_count // LANES
-    assert chips > 1 and chips & (chips - 1) == 0 and sets & (sets - 1) == 0
+    assert chips > 1 and sets > 1 and chips & (chips - 1) == 0 and sets & (sets - 1) == 0
 
     def pair(value):
         return lax.ppermute(value, "blk", [(i, i ^ 1) for i in range(slabs)])
@@ -261,15 +272,23 @@
         name="far_rows",
     )(*moved[:far], held, offset, pair_targets, pair_offset, lse, line)
 
+    def mirror(value, chip):
+        return jnp.stack([value[slot ^ chip] for slot in range(chips)])
+
+    joined = lax.ppermute(
+        payload,
+        ("blk", "tsplit"),
+        [(b * sets + z, (b ^ 2) * sets + (z ^ 1)) for b in range(slabs) for z in range(sets)],
+    )
+    beside = along(payload, 1)
     other = across(payload, 1)
     lines = jnp.stack([line, other[chips:]] + moved[far:], axis=1)
-    lse = merge(payload[:chips], jnp.stack([other[slot ^ 1] for slot in range(chips)]))
+    lse = merge(payload[:chips], mirror(joined, 1), beside[:chips], mirror(other, 1))
     chip = 2
     while chip < chips:
-        other = across(lse, chip)
-        lse = merge(lse, jnp.stack([other[slot ^ chip] for slot in range(chips)]))
+        lse = merge(lse, mirror(across(lse, chip), chip))
         chip *= 2
-    step = 1
+    step = 2
     while step < sets:
         lse = merge(lse, along(lse, step))
         step *= 2

time: 25.3 us -> 24.9 us (0.984)
  starting transfers between devices: 11.2 us -> 10.3 us
  waiting for transfers between devices: 5.71 us -> 6.38 us
    ppermute x0 -> x1, starting transfers between devices: none -> 3.37 us  [shards(): lax.ppermute(payload, ('blk', 'tsplit'), [(b * sets + z, (b ^ 2) * sets +...]
    ppermute x2, starting transfers between devices: 5.24 us -> 2.77 us  [along(): return lax.ppermute(value, 'tsplit', [(i, i ^ step) for i in range(sets)])]
    ppermute x2, starting transfers between devices: 4.98 us -> 3.13 us  [across(): return lax.ppermute(value, 'blk', [(i, i ^ 2 * chip) for i in range(slabs)])]
    ppermute x0 -> x1, waiting for transfers between devices: none -> 0.93 us  [shards(): lax.ppermute(payload, ('blk', 'tsplit'), [(b * sets + z, (b ^ 2) * sets +...]
    ppermute x2, waiting for transfers between devices: 3.11 us -> 2.41 us  [along(): return lax.ppermute(value, 'tsplit', [(i, i ^ step) for i in range(sets)])]
    ppermute x2, waiting for transfers between devices: 1.73 us -> 2.16 us  [across(): return lax.ppermute(value, 'blk', [(i, i ^ 2 * chip) for i in range(slabs)])]
  transfers between devices with their start and end apart: 7 -> 8, of which waited for: 5 -> 7; matrix products, arithmetic and copies ran while one was open for 0% -> 0% of each run, Pallas kernels for 20% -> 20%
where the time goes in v10:
time: 24.9 us; the launch traced here: 24.7 us
  starting transfers between devices  10.3 us (41%)
  Pallas kernels  6.67 us (27%)
  waiting for transfers between devices  6.38 us (26%)
  between operations  0.7 us (3%)
  other arithmetic  0.67 us (3%)
    ppermute x1, starting transfers between devices, shards(): lax.ppermute(payload, ('blk', 'tsplit'), [(b * sets + z, (b ^ 2) * sets +...  3.37 us
    ppermute x2, starting transfers between devices, across(): return lax.ppermute(value, 'blk', [(i, i ^ 2 * chip) for i in range(slabs)])  3.13 us
    ppermute x2, starting transfers between devices, along(): return lax.ppermute(value, 'tsplit', [(i, i ^ step) for i in range(sets)])  2.77 us
    ppermute x2, waiting for transfers between devices, along(): return lax.ppermute(value, 'tsplit', [(i, i ^ step) for i in range(sets)])  2.41 us
    pallas_call x2, Pallas kernels, prepare_on(): pl.pallas_call(functools.partial(prepare_kernel, turn), out_shape=(jax.Sh...  2.3 us
    ppermute x2, waiting for transfers between devices, across(): return lax.ppermute(value, 'blk', [(i, i ^ 2 * chip) for i in range(slabs)])  2.16 us
    pallas_call x1, Pallas kernels, shards(): pl.pallas_call(near_kernel, out_shape=(f32(src_count, tgt_count), f32(1,...  1.67 us
    pallas_call x2, Pallas kernels, columns(): pl.pallas_call(kernel, out_shape=outs, in_specs=[VMEM] * (5 + len(more)),...  1.63 us
  transfers between devices with their start and end apart: 8, of which 7 were waited for; matrix products, arithmetic and copies ran while one was open for 0% of the time, Pallas kernels for 20%

profile of v10, /device:TPU:0, one launch (start us, length us, event | category | flops | bytes accessed | tf_op | source)
XLA Modules:
  0.0 24.7 jit_solution(2381038774258606426)
XLA Ops:
  0.6 0.5 %collective-permute-start = (bf16[1024,512]{1,0:T(8,128)(2,1)}, bf16[1024,512]{1,0:T(8,128)(2,1)S(1)}, u32[]{:S(2)}, u32[]{:S(2)}) collective-permute-start(bf16[1024,512]{1,0:T(8,128)(2,1)} %refs_1_.3), channel_id=1, source_target_pairs={{0,4},{4,0},{8,12},{12,8},{1,5},{5,1},{9,13},{13,9},{2,6},{6,2},{1... | collective-permute-start | bytes 3145736 | tf_op jit(solution)/shard_map/ppermute | solution.py:204
  1.1 0.1 prepare_1.1
  1.2 2.6 %collective-permute-start.2 = (bf16[256,512]{1,0:T(8,128)(2,1)}, bf16[256,512]{1,0:T(8,128)(2,1)S(1)}, u32[]{:S(2)}, u32[]{:S(2)}) collective-permute-start(bf16[256,512]{1,0:T(8,128)(2,1)} %rows_ref.1), channel_id=1, source_target_pairs={{0,8},{4,12},{8,0},{12,4},{1,9},{5,13},{9,1},{13,5},{2,10},{6,14},... | collective-permute-start | bytes 786440 | tf_op jit(solution)/shard_map/ppermute | solution.py:207
  3.8 2.3 %prepare_0.1 = (bf16[1024,512]{1,0:T(8,128)(2,1)S(1)}, f32[1,1024]{1,0:T(1,128)S(1)}, f32[256,1024]{1,0:T(8,128)S(1)}, f32[1,256]{1,0:T(1,128)S(1)}, f32[2,256]{1,0:T(2,128)S(1)}, /*index=5*/f32[1,256]{1,0:T(1,128)S(1)}) custom-call(s32[1]{0:T(128)} %bitcast.core_ref, bf16[256,512]{1,0:T(8,128)(2,1)} %rows_ref.1, bf16[1024,512]{1,0:T(8,128)(2,1)} %refs_1_.3, ...), custom_call_target="tpu_custom_call" | custom-call | flops 268435456 | bytes 1048576 | tf_op jit(solution)/shard_map/prepare_0/pallas_call | solution.py:230
  6.1 0.4 %collective-permute-start.1 = (f32[1,1024]{1,0:T(1,128)S(1)}, f32[1,1024]{1,0:T(1,128)S(1)}, u32[]{:S(2)}, u32[]{:S(2)}) collective-permute-start(f32[1,1024]{1,0:T(1,128)S(1)} %get-tuple-element.35.refs_2_), channel_id=1, source_target_pairs={{0,4},{4,0},{8,12},{12,8},{1,5},{5,1},{9,13},{13,9},{2,6},{6,2},{1... | collective-permute-start | bytes 12296 | tf_op jit(solution)/shard_map/ppermute | solution.py:204
  6.5 0.8 %collective-permute-done.1.offset_ref.refs_4_ = f32[1,1024]{1,0:T(1,128)S(1)} collective-permute-done((f32[1,1024]{1,0:T(1,128)S(1)}, f32[1,1024]{1,0:T(1,128)S(1)}, u32[]{:S(2)}, u32[]{:S(2)}) %collective-permute-start.1) | collective-permute-done | bytes 4128 | tf_op jit(solution)/shard_map/ppermute | solution.py:204
  7.3 1.7 %near_rows.1 = (f32[256,1024]{1,0:T(8,128)S(1)}, f32[1,256]{1,0:T(1,128)S(1)}) custom-call(bf16[256,512]{1,0:T(8,128)(2,1)} %rows_ref.1, bf16[1024,512]{1,0:T(8,128)(2,1)S(1)} %collective-permute-done.tgt_ref.refs_3_, f32[1,1024]{1,0:T(1,128)S(1)} %collective-permute-done.1.offset_ref.refs_4_, f32[1,256]{1,0:T(1,128)S(1)} %get-tuple-element.36.held_ref), custom_call_target="tpu_custom_call" | custom-call | flops 268435456 | bytes 1048576 | tf_op jit(solution)/shard_map/near_rows/pallas_call | solution.py:254
  9.0 0.1 collective-permute-done.2.refs_0_
  9.1 1.1 %far_rows.1 = (f32[1,256,1024]{2,1,0:T(8,128)S(1)}, f32[1,256,1024]{2,1,0:T(8,128)S(1)}, f32[4,256]{1,0:T(4,128)S(1)}) custom-call(bf16[256,512]{1,0:T(8,128)(2,1)S(1)} %collective-permute-done.2.refs_0_, bf16[1024,512]{1,0:T(8,128)(2,1)S(1)} %get-tuple-element.40.refs_1_, f32[1,1024]{1,0:T(1,128)S(1)} %get-tuple-element.35.refs_2_, ...), custom_call_target="tpu_custom_call" | custom-call | flops 536870912 | bytes 1048576 | tf_op jit(solution)/shard_map/far_rows/pallas_call | solution.py:265
  10.2 3.4 %collective-permute-start.3 = (f32[4,256]{1,0:T(4,128)S(1)}, f32[4,256]{1,0:T(4,128)S(1)}, u32[]{:S(2)}, u32[]{:S(2)}) collective-permute-start(f32[4,256]{1,0:T(4,128)S(1)} %get-tuple-element.44), channel_id=1, source_target_pairs={{0,9},{1,8},{2,11},{3,10},{4,13},{5,12},{6,15},{7,14},{8,1},{9,0},... | collective-permute-start | bytes 12296 | tf_op jit(solution)/shard_map/ppermute | solution.py:278
  13.6 0.5 %collective-permute-start.5 = (f32[4,256]{1,0:T(4,128)S(1)}, f32[4,256]{1,0:T(4,128)S(1)}, u32[]{:S(2)}, u32[]{:S(2)}) collective-permute-start(f32[4,256]{1,0:T(4,128)S(1)} %get-tuple-element.44), channel_id=1, source_target_pairs={{0,8},{4,12},{8,0},{12,4},{1,9},{5,13},{9,1},{13,5},{2,10},{6,14},... | collective-permute-start | bytes 12296 | tf_op jit(solution)/shard_map/ppermute | solution.py:207
  14.1 0.1 collective-permute-start.4
  14.2 0.9 %collective-permute-done.3 = f32[4,256]{1,0:T(4,128)S(1)} collective-permute-done((f32[4,256]{1,0:T(4,128)S(1)}, f32[4,256]{1,0:T(4,128)S(1)}, u32[]{:S(2)}, u32[]{:S(2)}) %collective-permute-start.3) | collective-permute-done | bytes 4128 | tf_op jit(solution)/shard_map/ppermute | solution.py:278
  15.2 2.0 %collective-permute-done.5 = f32[4,256]{1,0:T(4,128)S(1)} collective-permute-done((f32[4,256]{1,0:T(4,128)S(1)}, f32[4,256]{1,0:T(4,128)S(1)}, u32[]{:S(2)}, u32[]{:S(2)}) %collective-permute-start.5) | collective-permute-done | bytes 4128 | tf_op jit(solution)/shard_map/ppermute | solution.py:207
  17.2 0.5 %collective-permute-done.4 = f32[4,256]{1,0:T(4,128)S(1)} collective-permute-done((f32[4,256]{1,0:T(4,128)S(1)}, f32[4,256]{1,0:T(4,128)S(1)}, u32[]{:S(2)}, u32[]{:S(2)}) %collective-permute-start.4) | collective-permute-done | bytes 4128 | tf_op jit(solution)/shard_map/ppermute | solution.py:210
  17.7 2.6 %collective-permute-start.6 = (f32[2,256]{1,0:T(2,128)S(1)}, f32[2,256]{1,0:T(2,128)S(1)}, u32[]{:S(2)}, u32[]{:S(2)}) collective-permute-start(f32[2,256]{1,0:T(2,128)S(1)} %log_add_fusion.1), channel_id=1, source_target_pairs={{0,2},{1,3},{2,0},{3,1},{4,6},{5,7},{6,4},{7,5},{8,10},{9,11},{10,... | collective-permute-start | bytes 6152 | tf_op jit(solution)/shard_map/ppermute | solution.py:210
  20.4 1.9 %collective-permute-done.6 = f32[2,256]{1,0:T(2,128)S(1)} collective-permute-done((f32[2,256]{1,0:T(2,128)S(1)}, f32[2,256]{1,0:T(2,128)S(1)}, u32[]{:S(2)}, u32[]{:S(2)}) %collective-permute-start.6) | collective-permute-done | bytes 2080 | tf_op jit(solution)/shard_map/ppermute | solution.py:210
  22.3 0.6 %columns.2 = f32[8,128]{1,0:T(8,128)S(1)} custom-call(f32[256,1024]{1,0:T(8,128)S(1)} %get-tuple-element.45.near_ref, f32[1,256,1024]{2,1,0:T(8,128)S(1)} %get-tuple-element.46.far_ref, f32[2,256]{1,0:T(2,128)S(1)} %log_add_fusion.lse_ref, f32[2,256]{1,0:T(2,128)S(1)} %get-tuple-element.53.slope_ref, f32[2,256]{1,0:T(2,128)S(1)} %get-tuple-element.52.shift_ref), custom_call_target="tpu_custom_call" | custom-call | flops 3145728 | bytes 1048576 | tf_op jit(solution)/shard_map/columns/pallas_call | solution.py:298
  22.9 0.1 collective-permute-start.7
  22.9 0.0 copy-start
  23.0 0.0 copy-start.1
  23.0 1.1 %columns.3 = (f32[8,128]{1,0:T(8,128)S(1)}, f32[1,256]{1,0:T(1,128)}) custom-call(f32[256,1024]{1,0:T(8,128)S(1)} %get-tuple-element.34.near_ref, f32[1,256,1024]{2,1,0:T(8,128)S(1)} %get-tuple-element.43.far_ref, f32[2,256]{1,0:T(2,128)S(1)} %log_add_fusion.lse_ref, f32[2,256]{1,0:T(2,128)S(1)} %get-tuple-element.53.slope_ref, ...), custom_call_target="tpu_custom_call" | custom-call | flops 3145728 | bytes 1048576 | tf_op jit(solution)/shard_map/columns/pallas_call | solution.py:298
  24.0 0.1 collective-permute-done.7
  24.1 0.6 %fusion = f32[1024]{0:T(1024)} fusion(f32[1024]{0:T(1024)S(1)} %copy-done.2, f32[8,128]{1,0:T(8,128)S(1)} %collective-permute-done.7, f32[8,128]{1,0:T(8,128)S(1)} %get-tuple-element.50, f32[1024]{0:T(1024)S(1)} %copy-done, f32[1024]{0:T(1024)S(1)} %copy-done.1), kind=kLoop, calls=%fused_computation.3 | loop fusion | flops 9216 | bytes 24576 | tf_op jit(solution)/shard_map/mul | solution.py:318
  (13 shorter events, 0.1 us)
Async XLA Ops:
  0.6 6.7 %collective-permute-start = (bf16[1024,512]{1,0:T(8,128)(2,1)}, bf16[1024,512]{1,0:T(8,128)(2,1)S(1)}, u32[]{:S(2)}, u32[]{:S(2)}) collective-permute-start(bf16[1024,512]{1,0:T(8,128)(2,1)} %refs_1_.3), channel_id=1, source_target_pairs={{0,4},{4,0},{8,12},{12,8},{1,5},{5,1},{9,13},{13,9},{2,6},{6,2},{1... | collective-permute-start | bytes 3145736 | tf_op jit(solution)/shard_map/ppermute | solution.py:204
  1.2 7.9 %collective-permute-start.2 = (bf16[256,512]{1,0:T(8,128)(2,1)}, bf16[256,512]{1,0:T(8,128)(2,1)S(1)}, u32[]{:S(2)}, u32[]{:S(2)}) collective-permute-start(bf16[256,512]{1,0:T(8,128)(2,1)} %rows_ref.1), channel_id=1, source_target_pairs={{0,8},{4,12},{8,0},{12,4},{1,9},{5,13},{9,1},{13,5},{2,10},{6,14},... | collective-permute-start | bytes 786440 | tf_op jit(solution)/shard_map/ppermute | solution.py:207
  6.1 1.2 %collective-permute-start.1 = (f32[1,1024]{1,0:T(1,128)S(1)}, f32[1,1024]{1,0:T(1,128)S(1)}, u32[]{:S(2)}, u32[]{:S(2)}) collective-permute-start(f32[1,1024]{1,0:T(1,128)S(1)} %get-tuple-element.35.refs_2_), channel_id=1, source_target_pairs={{0,4},{4,0},{8,12},{12,8},{1,5},{5,1},{9,13},{13,9},{2,6},{6,2},{1... | collective-permute-start | bytes 12296 | tf_op jit(solution)/shard_map/ppermute | solution.py:204
  10.2 5.0 %collective-permute-start.3 = (f32[4,256]{1,0:T(4,128)S(1)}, f32[4,256]{1,0:T(4,128)S(1)}, u32[]{:S(2)}, u32[]{:S(2)}) collective-permute-start(f32[4,256]{1,0:T(4,128)S(1)} %get-tuple-element.44), channel_id=1, source_target_pairs={{0,9},{1,8},{2,11},{3,10},{4,13},{5,12},{6,15},{7,14},{8,1},{9,0},... | collective-permute-start | bytes 12296 | tf_op jit(solution)/shard_map/ppermute | solution.py:278
  13.6 3.6 %collective-permute-start.5 = (f32[4,256]{1,0:T(4,128)S(1)}, f32[4,256]{1,0:T(4,128)S(1)}, u32[]{:S(2)}, u32[]{:S(2)}) collective-permute-start(f32[4,256]{1,0:T(4,128)S(1)} %get-tuple-element.44), channel_id=1, source_target_pairs={{0,8},{4,12},{8,0},{12,4},{1,9},{5,13},{9,1},{13,5},{2,10},{6,14},... | collective-permute-start | bytes 12296 | tf_op jit(solution)/shard_map/ppermute | solution.py:207
  14.1 3.6 %collective-permute-start.4 = (f32[4,256]{1,0:T(4,128)S(1)}, f32[4,256]{1,0:T(4,128)S(1)}, u32[]{:S(2)}, u32[]{:S(2)}) collective-permute-start(f32[4,256]{1,0:T(4,128)S(1)} %get-tuple-element.44), channel_id=1, source_target_pairs={{0,1},{1,0},{2,3},{3,2},{4,5},{5,4},{6,7},{7,6},{8,9},{9,8},{10,11... | collective-permute-start | bytes 12296 | tf_op jit(solution)/shard_map/ppermute | solution.py:210
  17.7 4.5 %collective-permute-start.6 = (f32[2,256]{1,0:T(2,128)S(1)}, f32[2,256]{1,0:T(2,128)S(1)}, u32[]{:S(2)}, u32[]{:S(2)}) collective-permute-start(f32[2,256]{1,0:T(2,128)S(1)} %log_add_fusion.1), channel_id=1, source_target_pairs={{0,2},{1,3},{2,0},{3,1},{4,6},{5,7},{6,4},{7,5},{8,10},{9,11},{10,... | collective-permute-start | bytes 6152 | tf_op jit(solution)/shard_map/ppermute | solution.py:210
  22.9 1.2 %collective-permute-start.7 = (f32[8,128]{1,0:T(8,128)S(1)}, f32[8,128]{1,0:T(8,128)S(1)}, u32[]{:S(2)}, u32[]{:S(2)}) collective-permute-start(f32[8,128]{1,0:T(8,128)S(1)} %columns.2), channel_id=1, source_target_pairs={{0,4},{4,0},{8,12},{12,8},{1,5},{5,1},{9,13},{13,9},{2,6},{6,2},{1... | collective-permute-start | bytes 12296 | tf_op jit(solution)/shard_map/ppermute | solution.py:204
  22.9 1.2 %copy-start = (f32[1024]{0:T(1024)S(1)}, f32[1024]{0:T(1024)}, u32[]{:S(2)}) copy-start(f32[1024]{0:T(1024)} %param.9) | copy-start | bytes 12292
  23.0 1.1 %copy-start.1 = (f32[1024]{0:T(1024)S(1)}, f32[1024]{0:T(1024)}, u32[]{:S(2)}) copy-start(f32[1024]{0:T(1024)} %param.11) | copy-start | bytes 12292
  23.0 1.1 %copy-start.2 = (f32[1024]{0:T(1024)S(1)}, f32[1024]{0:T(1024)}, u32[]{:S(2)}) copy-start(f32[1024]{0:T(1024)} %param.13) | copy-start | bytes 12292

commit v11 on v10

--- a/solution.py
+++ b/solution.py
@@ -14,6 +14,7 @@
 LOG_2 = math.log(2.0)
 LANES = 128
 CHUNK = 256
+PIECE = 512
 VMEM = pl.BlockSpec(memory_space=pltpu.VMEM)
 SMEM = pl.BlockSpec(memory_space=pltpu.SMEM)
 HBM = pl.BlockSpec(memory_space=pltpu.HBM)
@@ -44,45 +45,55 @@
     return jnp.sum(rows * rows, axis=1, keepdims=True) / EPSILON
 
 
-def row_block(rows, sides, eye):
+def row_sums(rows, sides, z_ref):
     rows = rows * LOGIT_SCALE
-    src_count = rows.shape[0]
-
-    def product(side, at):
-        tgt_ref, offset_ref, z_ref = sides[side]
-        cols = slice(at, at + CHUNK)
-        dots = lax.dot_general(rows, tgt_ref[cols, :], NT_DIMS, preferred_element_type=jnp.float32)
-        z = (dots + offset_ref[:, cols]) * LOG2_E
-        z_ref[:, cols] = z
-        high = z[:, :LANES]
-        for lane in range(LANES, CHUNK, LANES):
-            high = jnp.maximum(high, z[:, lane : lane + LANES])
-        return high
-
-    def raise_to(side, at, peak):
-        z_ref = sides[side][2]
-        return sum(jnp.exp2(z_ref[:, lane : lane + LANES] - peak) for lane in range(at, at + CHUNK, LANES))
-
-    steps = range(0, sides[0][0].shape[0], CHUNK)
-    peaks, masses = [], []
-    for side in range(len(sides) + 1):
-        peak = mass = None
-        for at in steps:
-            if side < len(sides):
-                high = product(side, at)
-                peak = high if peak is None else jnp.maximum(peak, high)
-            if side > 0:
-                term = raise_to(side - 1, at, peaks[-1])
-                mass = term if mass is None else mass + term
-        if side < len(sides):
-            peaks.append(peak)
-        if side > 0:
-            masses.append(mass)
-    peak = jnp.max(functools.reduce(jnp.maximum, peaks), axis=1, keepdims=True)
-    mass = sum(mass * jnp.exp2(high - peak) for high, mass in zip(peaks, masses))
-    mass = jnp.sum(mass, axis=1, keepdims=True)
-    parts = [slice(at, at + LANES) for at in range(0, src_count, LANES)]
-    return jnp.concatenate([to_lanes(peak[p], eye) * LOG_2 + jnp.log(to_lanes(mass[p], eye)) for p in parts], axis=1)
+    pieces = [(side, at) for side, (tgt_ref, _) in enumerate(sides) for at in range(0, tgt_ref.shape[0], PIECE)]
+
+    def product(index):
+        side, at = pieces[index]
+        part = sides[side][0][at : at + PIECE, :]
+        z_ref[index % 2] = lax.dot_general(part, rows, NT_DIMS, preferred_element_type=jnp.float32)
+
+    def absorb(index, state):
+        side, at = pieces[index]
+        for inner in range(0, PIECE, LANES):
+            offset = sides[side][1][at + inner : at + inner + LANES, :]
+            offset = jnp.concatenate([offset] * (rows.shape[0] // LANES), axis=1)
+            z = z_ref[index % 2, inner : inner + LANES, :] * LOG2_E + offset
+            z = z.reshape(LANES // 8, 8, rows.shape[0])
+            high = jnp.max(z, axis=0)
+            peak = high if state is None else jnp.maximum(state[0], high)
+            mass = jnp.sum(jnp.exp2(z - peak), axis=0)
+            if state is not None:
+                mass = mass + state[1] * jnp.exp2(state[0] - peak)
+            state = (peak, mass)
+        return state
+
+    state = None
+    product(0)
+    for index in range(len(pieces)):
+        if index + 1 < len(pieces):
+            product(index + 1)
+        state = absorb(index, state)
+    high, mass = state
+    peak = jnp.max(high, axis=0, keepdims=True)
+    mass = jnp.sum(mass * jnp.exp2(high - peak), axis=0, keepdims=True)
+    return peak * LOG_2 + jnp.log(mass)
+
+
+def put_offsets(offset_ref, column_ref, eye):
+    for at in range(0, offset_ref.shape[1], LANES):
+        column = to_column(offset_ref[:, at : at + LANES] * LOG2_E, eye)
+        column_ref[at : at + LANES, :] = jnp.broadcast_to(column, (LANES, LANES))
+
+
+def logits_kernel(rows_ref, own_ref, own_offset_ref, pair_ref, pair_offset_ref, own_z_ref, pair_z_ref):
+    rows = rows_ref[...] * LOGIT_SCALE
+    for tgt_ref, offset_ref, z_ref in ((own_ref, own_offset_ref, own_z_ref), (pair_ref, pair_offset_ref, pair_z_ref)):
+        for at in range(0, tgt_ref.shape[0], CHUNK):
+            cols = slice(at, at + CHUNK)
+            dots = lax.dot_general(rows, tgt_ref[cols, :], NT_DIMS, preferred_element_type=jnp.float32)
+            z_ref[:, cols] = (dots + offset_ref[:, cols]) * LOG2_E
 
 
 def prepare_kernel(turn, core_ref, *refs):
@@ -104,8 +115,8 @@
 
 def prepare(
     src_hbm, tgt_hbm, pot_hbm, mass_hbm, slope_hbm, logmass_hbm,
-    tgt_ref, offset_ref, z_ref, lse_ref, line_ref, sum_ref,
-    src_ref, pot_ref, mass_ref, slope_ref, logmass_ref, sems,
+    tgt_ref, offset_ref, column_ref, lse_ref, line_ref, sum_ref,
+    src_ref, pot_ref, mass_ref, slope_ref, logmass_ref, z_ref, sems,
 ):
     pairs = (
         (tgt_hbm, tgt_ref), (src_hbm, src_ref), (pot_hbm, pot_ref),
@@ -130,26 +141,27 @@
         at = group * LANES
         base = pot_ref[group : group + 1, :] + mass_ref[group : group + 1, :]
         offset_ref[:, at : at + LANES] = base - to_lanes(squares(tgt_ref, at), eye)
-    lse_ref[...] = row_block(src_ref[...], ((tgt_ref, offset_ref, z_ref),), eye)
-
-
-def near_kernel(rows_ref, tgt_ref, offset_ref, held_ref, z_ref, lse_ref):
-    lse_ref[...] = merge(held_ref[...], row_block(rows_ref[...], ((tgt_ref, offset_ref, z_ref),), diagonal()))
+    put_offsets(offset_ref, column_ref, eye)
+    lse_ref[...] = row_sums(src_ref[...], ((tgt_ref, column_ref),), z_ref)
+
+
+def near_kernel(rows_ref, tgt_ref, offset_ref, held_ref, column_ref, lse_ref, z_ref):
+    put_offsets(offset_ref, column_ref, diagonal())
+    lse_ref[...] = merge(held_ref[...], row_sums(rows_ref[...], ((tgt_ref, column_ref),), z_ref))
 
 
 def far_kernel(count, *refs):
-    eye = diagonal()
-    own_ref, own_offset_ref, pair_ref, pair_offset_ref, held_ref, line_ref = refs[count : count + 6]
-    own_z_ref, pair_z_ref, out_ref = refs[count + 6 :]
+    own_ref, own_column_ref, pair_ref, pair_column_ref, held_ref, line_ref = refs[count : count + 6]
+    out_ref, z_ref = refs[count + 6 :]
     slots = count + 1
     out_ref[0:1, :] = held_ref[...]
     out_ref[slots : slots + 2, :] = line_ref[...]
     for slot in range(count):
-        sides = ((own_ref, own_offset_ref, own_z_ref.at[slot]), (pair_ref, pair_offset_ref, pair_z_ref.at[slot]))
-        out_ref[slot + 1 : slot + 2, :] = row_block(refs[slot][...], sides, eye)
-
-
-def sum_columns(near_ref, far_ref, offset, off_ref, out_ref):
+        sides = ((own_ref, own_column_ref), (pair_ref, pair_column_ref))
+        out_ref[slot + 1 : slot + 2, :] = row_sums(refs[slot][...], sides, z_ref)
+
+
+def sum_columns(z_refs, offset, off_ref, out_ref):
     eye = diagonal()
     slots, src_count = offset.shape
     for slot in range(slots):
@@ -161,8 +173,7 @@
         cols = slice(group * LANES, (group + 1) * LANES)
         peaks, masses = [], []
         for slot in range(slots):
-            z = near_ref[:, cols] if slot == 0 else far_ref[slot - 1, :, cols]
-            z = (z + off_ref[slot]).reshape(src_count // 8, 8, LANES)
+            z = (z_refs[slot][:, cols] + off_ref[slot]).reshape(src_count // 8, 8, LANES)
             peaks.append(jnp.max(z, axis=0))
             masses.append(jnp.sum(jnp.exp2(z - peaks[-1]), axis=0))
         peak = jnp.max(functools.reduce(jnp.maximum, peaks), axis=0, keepdims=True)
@@ -171,14 +182,16 @@
         out_ref[group : group + 1, :] = peak * LOG_2 + jnp.log(mass)
 
 
-def pair_kernel(near_ref, far_ref, lse_ref, slope_ref, shift_ref, out_ref, off_ref):
-    sum_columns(near_ref, far_ref, shift_ref[...] - slope_ref[...] * lse_ref[...], off_ref, out_ref)
-
-
-def own_kernel(near_ref, far_ref, lse_ref, slope_ref, shift_ref, sum_ref, out_ref, potential_ref, off_ref):
+def pair_kernel(slots, *refs):
+    lse_ref, slope_ref, shift_ref, out_ref, off_ref = refs[slots:]
+    sum_columns(refs[:slots], shift_ref[...] - slope_ref[...] * lse_ref[...], off_ref, out_ref)
+
+
+def own_kernel(slots, *refs):
+    lse_ref, slope_ref, shift_ref, sum_ref, out_ref, potential_ref, off_ref = refs[slots:]
     lse, slope = lse_ref[...], slope_ref[...]
     potential_ref[...] = slope[0:1, :] * (sum_ref[...] - lse[0:1, :])
-    sum_columns(near_ref, far_ref, shift_ref[...] - slope * lse, off_ref, out_ref)
+    sum_columns(refs[:slots], shift_ref[...] - slope * lse, off_ref, out_ref)
 
 
 def f32(*shape):
@@ -226,13 +239,15 @@
     )
     inputs = [pltpu.with_memory_space_constraint(x, pltpu.HBM) for x in inputs]
 
+    product_space = pltpu.VMEM((2, PIECE, src_count), jnp.float32)
+
     def prepare_on(turn, *earlier):
         return pl.pallas_call(
             functools.partial(prepare_kernel, turn),
             out_shape=(
                 jax.ShapeDtypeStruct(targets.shape, targets.dtype),
                 f32(1, tgt_count),
-                f32(src_count, tgt_count),
+                f32(tgt_count, LANES),
                 f32(1, src_count),
                 f32(2, src_count),
                 f32(1, src_count),
@@ -240,7 +255,7 @@
             in_specs=[SMEM] + [HBM] * 6 + [VMEM] * len(earlier),
             out_specs=(VMEM,) * 6,
             scratch_shapes=[pltpu.VMEM(x.shape, x.dtype) for x in (inputs[0], *inputs[2:])]
-            + [pltpu.SemaphoreType.DMA((6,))],
+            + [product_space, pltpu.SemaphoreType.DMA((6,))],
             compiler_params=params(12),
             cost_estimate=cost(1),
             name=f"prepare_{turn}",
@@ -249,28 +264,45 @@
     earlier = prepare_on(1)
     first, sent = lax.optimization_barrier((earlier[5], sources))
     far_blocks = [across(sent, chip) for chip in range(1, chips)]
-    held, offset, own_z, lse, line, src_sum = prepare_on(0, *earlier[:5], first)
+    held, offset, column, lse, line, src_sum = prepare_on(0, *earlier[:5], first)
     pair_offset = pair(offset)
-    pair_z, lse = pl.pallas_call(
+    pair_column, lse = pl.pallas_call(
         near_kernel,
-        out_shape=(f32(src_count, tgt_count), f32(1, src_count)),
+        out_shape=(f32(tgt_count, LANES), f32(1, src_count)),
         in_specs=[VMEM] * 4,
         out_specs=(VMEM,) * 2,
+        scratch_shapes=[product_space],
         compiler_params=params(12),
         cost_estimate=cost(1),
         name="near_rows",
     )(sources, pair_targets, pair_offset, lse)
     far_lines = [across(line, chip) for chip in range(2, chips)]
     lse, *moved = lax.optimization_barrier((lse, *far_blocks, *far_lines))
-    own_far_z, pair_far_z, payload = pl.pallas_call(
+    payload = pl.pallas_call(
         functools.partial(far_kernel, far),
-        out_shape=(f32(far, src_count, tgt_count), f32(far, src_count, tgt_count), f32(chips + 2, src_count)),
+        out_shape=f32(chips + 2, src_count),
         in_specs=[VMEM] * (far + 6),
-        out_specs=(VMEM,) * 3,
-        compiler_params=params(8 + 3 * far),
+        out_specs=VMEM,
+        scratch_shapes=[product_space],
+        compiler_params=params(12 + far),
         cost_estimate=cost(2 * far),
         name="far_rows",
-    )(*moved[:far], held, offset, pair_targets, pair_offset, lse, line)
+    )(*moved[:far], held, column, pair_targets, pair_column, lse, line)
+
+    payload, *blocks = lax.optimization_barrier((payload, sources, *moved[:far]))
+    own_zs, pair_zs = [], []
+    for block in blocks:
+        own_z, pair_z = pl.pallas_call(
+            logits_kernel,
+            out_shape=(f32(src_count, tgt_count), f32(src_count, tgt_count)),
+            in_specs=[VMEM] * 5,
+            out_specs=(VMEM,) * 2,
+            compiler_params=params(12),
+            cost_estimate=cost(2),
+            name="logits",
+        )(block, held, offset, pair_targets, pair_offset)
+        own_zs.append(own_z)
+        pair_zs.append(pair_z)
 
     def mirror(value, chip):
         return jnp.stack([value[slot ^ chip] for slot in range(chips)])
@@ -293,12 +325,12 @@
         lse = merge(lse, along(lse, step))
         step *= 2
 
-    def columns(kernel, near_z, far_z, *more):
+    def columns(kernel, zs, *more):
         outs = (f32(groups, LANES), f32(1, src_count))[: 1 + len(more)]
         return pl.pallas_call(
-            kernel,
+            functools.partial(kernel, chips),
             out_shape=outs,
-            in_specs=[VMEM] * (5 + len(more)),
+            in_specs=[VMEM] * (chips + 3 + len(more)),
             out_specs=(VMEM,) * len(outs),
             scratch_shapes=[pltpu.VMEM((chips, src_count, LANES), jnp.float32)],
             compiler_params=params(8 + 2 * chips),
@@ -308,12 +340,12 @@
                 transcendentals=chips * src_count * tgt_count,
             ),
             name="columns",
-        )(near_z, far_z, lse, lines[0], lines[1], *more)
-
-    (pair_part,) = columns(pair_kernel, pair_z, pair_far_z)
+        )(*zs, lse, lines[0], lines[1], *more)
+
+    (pair_part,) = columns(pair_kernel, pair_zs)
     lse, pair_part = lax.optimization_barrier((lse, pair_part))
     home = pair(pair_part)
-    own_part, src_potential = columns(own_kernel, own_z, own_far_z, src_sum)
+    own_part, src_potential = columns(own_kernel, own_zs, src_sum)
     total = merge(own_part, home).reshape(tgt_count)
     tgt_update = tgt_exponent * (2.0 * tgt_logmass + tgt_potential - total)
     return (src_potential.reshape(src_count), tgt_update)

time: 24.9 us -> 24.9 us (level)
  Pallas kernels: 6.67 us -> 8.83 us
  waiting for transfers between devices: 6.38 us -> 4.23 us
    pallas_call x4 -> x6, Pallas kernels: 4.36 us -> 6.62 us  [the longest x2 2.44 us: shards(): pl.pallas_call(logits_kernel, out_shape=(f32(src_count, tgt_count), f32(s...]
    ppermute x2, waiting for transfers between devices: 2.16 us -> 0.92 us  [across(): return lax.ppermute(value, 'blk', [(i, i ^ 2 * chip) for i in range(slabs)])]
    ppermute x1, waiting for transfers between devices: 0.93 us -> 0.01 us  [shards(): lax.ppermute(payload, ('blk', 'tsplit'), [(b * sets + z, (b ^ 2) * sets +...]
  transfers between devices with their start and end apart: 8 -> 8, of which waited for: 7 -> 5; matrix products, arithmetic and copies ran while one was open for 0% -> 0% of each run, Pallas kernels for 20% -> 30%
where the time goes in v11:
time: 24.9 us; the launch traced here: 24.7 us
  starting transfers between devices  10.2 us (41%)
  Pallas kernels  8.83 us (35%)
  waiting for transfers between devices  4.23 us (17%)
  between operations  0.73 us (3%)
  other arithmetic  0.67 us (3%)
    ppermute x1, starting transfers between devices, shards(): lax.ppermute(payload, ('blk', 'tsplit'), [(b * sets + z, (b ^ 2) * sets +...  3.37 us
    ppermute x2, starting transfers between devices, across(): return lax.ppermute(value, 'blk', [(i, i ^ 2 * chip) for i in range(slabs)])  3.11 us
    ppermute x2, starting transfers between devices, along(): return lax.ppermute(value, 'tsplit', [(i, i ^ step) for i in range(sets)])  2.79 us
    pallas_call x2, Pallas kernels, shards(): pl.pallas_call(logits_kernel, out_shape=(f32(src_count, tgt_count), f32(s...  2.44 us
    ppermute x2, waiting for transfers between devices, along(): return lax.ppermute(value, 'tsplit', [(i, i ^ step) for i in range(sets)])  2.4 us
    pallas_call x2, Pallas kernels, prepare_on(): pl.pallas_call(functools.partial(prepare_kernel, turn), out_shape=(jax.Sh...  2.2 us
    pallas_call x2, Pallas kernels, columns(): pl.pallas_call(functools.partial(kernel, chips), out_shape=outs, in_specs...  1.64 us
    pallas_call x1, Pallas kernels, shards(): pl.pallas_call(near_kernel, out_shape=(f32(tgt_count, LANES), f32(1, src_...  1.58 us
  transfers between devices with their start and end apart: 8, of which 5 were waited for; matrix products, arithmetic and copies ran while one was open for 0% of the time, Pallas kernels for 30%

profile of v11, /device:TPU:0, one launch (start us, length us, event | category | flops | bytes accessed | tf_op | source)
XLA Modules:
  0.0 24.7 jit_solution(14414420797000384572)
XLA Ops:
  0.6 0.5 %collective-permute-start = (bf16[1024,512]{1,0:T(8,128)(2,1)}, bf16[1024,512]{1,0:T(8,128)(2,1)S(1)}, u32[]{:S(2)}, u32[]{:S(2)}) collective-permute-start(bf16[1024,512]{1,0:T(8,128)(2,1)} %refs_1_.3), channel_id=1, source_target_pairs={{0,4},{4,0},{8,12},{12,8},{1,5},{5,1},{9,13},{13,9},{2,6},{6,2},{1... | collective-permute-start | bytes 3145736 | tf_op jit(solution)/shard_map/ppermute | solution.py:217
  1.1 0.1 prepare_1.1
  1.2 2.6 %collective-permute-start.2 = (bf16[256,512]{1,0:T(8,128)(2,1)}, bf16[256,512]{1,0:T(8,128)(2,1)S(1)}, u32[]{:S(2)}, u32[]{:S(2)}) collective-permute-start(bf16[256,512]{1,0:T(8,128)(2,1)} %rows_ref.2), channel_id=1, source_target_pairs={{0,8},{4,12},{8,0},{12,4},{1,9},{5,13},{9,1},{13,5},{2,10},{6,14},... | collective-permute-start | bytes 786440 | tf_op jit(solution)/shard_map/ppermute | solution.py:220
  3.8 2.1 %prepare_0.1 = (bf16[1024,512]{1,0:T(8,128)(2,1)S(1)}, f32[1,1024]{1,0:T(1,128)S(1)}, f32[1024,128]{1,0:T(8,128)S(1)}, f32[1,256]{1,0:T(1,128)S(1)}, f32[2,256]{1,0:T(2,128)S(1)}, /*index=5*/f32[1,256]{1,0:T(1,128)S(1)}) custom-call(s32[1]{0:T(128)} %bitcast.core_ref, bf16[256,512]{1,0:T(8,128)(2,1)} %rows_ref.2, bf16[1024,512]{1,0:T(8,128)(2,1)} %refs_1_.3, ...), custom_call_target="tpu_custom_call" | custom-call | flops 268435456 | bytes 1048576 | tf_op jit(solution)/shard_map/prepare_0/pallas_call | solution.py:245
  6.0 0.4 %collective-permute-start.1 = (f32[1,1024]{1,0:T(1,128)S(1)}, f32[1,1024]{1,0:T(1,128)S(1)}, u32[]{:S(2)}, u32[]{:S(2)}) collective-permute-start(f32[1,1024]{1,0:T(1,128)S(1)} %get-tuple-element.38.own_offset_ref), channel_id=1, source_target_pairs={{0,4},{4,0},{8,12},{12,8},{1,5},{5,1},{9,13},{13,9},{2,6},{6,2},{1... | collective-permute-start | bytes 12296 | tf_op jit(solution)/shard_map/ppermute | solution.py:217
  6.3 0.9 %collective-permute-done.1.offset_ref.pair_offset_ref = f32[1,1024]{1,0:T(1,128)S(1)} collective-permute-done((f32[1,1024]{1,0:T(1,128)S(1)}, f32[1,1024]{1,0:T(1,128)S(1)}, u32[]{:S(2)}, u32[]{:S(2)}) %collective-permute-start.1) | collective-permute-done | bytes 4128 | tf_op jit(solution)/shard_map/ppermute | solution.py:217
  7.2 1.6 %near_rows.1 = (f32[1024,128]{1,0:T(8,128)S(1)}, f32[1,256]{1,0:T(1,128)S(1)}) custom-call(bf16[256,512]{1,0:T(8,128)(2,1)} %rows_ref.2, bf16[1024,512]{1,0:T(8,128)(2,1)S(1)} %collective-permute-done.tgt_ref.refs_3_.pair_ref, f32[1,1024]{1,0:T(1,128)S(1)} %collective-permute-done.1.offset_ref.pair_offset_ref, f32[1,256]{1,0:T(1,128)S(1)} %get-tuple-element.39.held_ref), custom_call_target="tpu_custom_call" | custom-call | flops 268435456 | bytes 1048576 | tf_op jit(solution)/shard_map/near_rows/pallas_call | solution.py:269
  8.8 0.4 %collective-permute-done.2.refs_0_.rows_ref = bf16[256,512]{1,0:T(8,128)(2,1)S(1)} collective-permute-done((bf16[256,512]{1,0:T(8,128)(2,1)}, bf16[256,512]{1,0:T(8,128)(2,1)S(1)}, u32[]{:S(2)}, u32[]{:S(2)}) %collective-permute-start.2) | collective-permute-done | bytes 262176 | tf_op jit(solution)/shard_map/ppermute | solution.py:220
  9.2 1.0 %far_rows.1 = f32[4,256]{1,0:T(4,128)S(1)} custom-call(bf16[256,512]{1,0:T(8,128)(2,1)S(1)} %collective-permute-done.2.refs_0_.rows_ref, bf16[1024,512]{1,0:T(8,128)(2,1)S(1)} %get-tuple-element.43.refs_1_.own_ref, f32[1024,128]{1,0:T(8,128)S(1)} %get-tuple-element.44.refs_2_, bf16[1024,512]{1,0:T(8,128)(2,1)S(1)} %collective-permute-done.tgt_ref.refs_3_.pair_ref, ...), custom_call_target="tpu_custom_call" | custom-call | flops 536870912 | bytes 1048576 | tf_op jit(solution)/shard_map/far_rows/pallas_call | solution.py:281
  10.2 3.4 %collective-permute-start.3 = (f32[4,256]{1,0:T(4,128)S(1)}, f32[4,256]{1,0:T(4,128)S(1)}, u32[]{:S(2)}, u32[]{:S(2)}) collective-permute-start(f32[4,256]{1,0:T(4,128)S(1)} %far_rows.1), channel_id=1, source_target_pairs={{0,9},{1,8},{2,11},{3,10},{4,13},{5,12},{6,15},{7,14},{8,1},{9,0},... | collective-permute-start | bytes 12296 | tf_op jit(solution)/shard_map/ppermute | solution.py:310
  13.6 0.5 %collective-permute-start.5 = (f32[4,256]{1,0:T(4,128)S(1)}, f32[4,256]{1,0:T(4,128)S(1)}, u32[]{:S(2)}, u32[]{:S(2)}) collective-permute-start(f32[4,256]{1,0:T(4,128)S(1)} %far_rows.1), channel_id=1, source_target_pairs={{0,8},{4,12},{8,0},{12,4},{1,9},{5,13},{9,1},{13,5},{2,10},{6,14},... | collective-permute-start | bytes 12296 | tf_op jit(solution)/shard_map/ppermute | solution.py:220
  14.1 0.1 collective-permute-start.4
  14.2 0.7 %logits.3 = (f32[256,1024]{1,0:T(8,128)S(1)}, f32[256,1024]{1,0:T(8,128)S(1)}) custom-call(bf16[256,512]{1,0:T(8,128)(2,1)S(1)} %collective-permute-done.2.refs_0_.rows_ref, bf16[1024,512]{1,0:T(8,128)(2,1)S(1)} %get-tuple-element.43.refs_1_.own_ref, f32[1,1024]{1,0:T(1,128)S(1)} %get-tuple-element.38.own_offset_ref, ...), custom_call_target="tpu_custom_call" | custom-call | flops 536870912 | bytes 1048576 | tf_op jit(solution)/shard_map/logits/pallas_call | solution.py:295
  15.0 1.7 %logits.2 = (f32[256,1024]{1,0:T(8,128)S(1)}, f32[256,1024]{1,0:T(8,128)S(1)}) custom-call(bf16[256,512]{1,0:T(8,128)(2,1)} %rows_ref.2, bf16[1024,512]{1,0:T(8,128)(2,1)S(1)} %get-tuple-element.43.refs_1_.own_ref, f32[1,1024]{1,0:T(1,128)S(1)} %get-tuple-element.38.own_offset_ref, bf16[1024,512]{1,0:T(8,128)(2,1)S(1)} %collective-permute-done.tgt_ref.refs_3_.pair_ref, ...), custom_call_target="tpu_custom_call" | custom-call | flops 536870912 | bytes 1048576 | tf_op jit(solution)/shard_map/logits/pallas_call | solution.py:295
  16.7 0.5 %collective-permute-done.5 = f32[4,256]{1,0:T(4,128)S(1)} collective-permute-done((f32[4,256]{1,0:T(4,128)S(1)}, f32[4,256]{1,0:T(4,128)S(1)}, u32[]{:S(2)}, u32[]{:S(2)}) %collective-permute-start.5) | collective-permute-done | bytes 4128 | tf_op jit(solution)/shard_map/ppermute | solution.py:220
  17.2 0.5 %collective-permute-done.4 = f32[4,256]{1,0:T(4,128)S(1)} collective-permute-done((f32[4,256]{1,0:T(4,128)S(1)}, f32[4,256]{1,0:T(4,128)S(1)}, u32[]{:S(2)}, u32[]{:S(2)}) %collective-permute-start.4) | collective-permute-done | bytes 4128 | tf_op jit(solution)/shard_map/ppermute | solution.py:223
  17.7 2.6 %collective-permute-start.6 = (f32[2,256]{1,0:T(2,128)S(1)}, f32[2,256]{1,0:T(2,128)S(1)}, u32[]{:S(2)}, u32[]{:S(2)}) collective-permute-start(f32[2,256]{1,0:T(2,128)S(1)} %log_add_fusion.1), channel_id=1, source_target_pairs={{0,2},{1,3},{2,0},{3,1},{4,6},{5,7},{6,4},{7,5},{8,10},{9,11},{10,... | collective-permute-start | bytes 6152 | tf_op jit(solution)/shard_map/ppermute | solution.py:223
  20.4 1.9 %collective-permute-done.6 = f32[2,256]{1,0:T(2,128)S(1)} collective-permute-done((f32[2,256]{1,0:T(2,128)S(1)}, f32[2,256]{1,0:T(2,128)S(1)}, u32[]{:S(2)}, u32[]{:S(2)}) %collective-permute-start.6) | collective-permute-done | bytes 2080 | tf_op jit(solution)/shard_map/ppermute | solution.py:223
  22.3 0.6 %columns.2 = f32[8,128]{1,0:T(8,128)S(1)} custom-call(f32[256,1024]{1,0:T(8,128)S(1)} %get-tuple-element.53.refs_0_, f32[256,1024]{1,0:T(8,128)S(1)} %get-tuple-element.54.refs_1_, f32[2,256]{1,0:T(2,128)S(1)} %log_add_fusion.refs_2_, f32[2,256]{1,0:T(2,128)S(1)} %get-tuple-element.61.refs_3_, f32[2,256]{1,0:T(2,128)S(1)} %get-tuple-element.60.refs_4_), custom_call_target="tpu_custom_call" | custom-call | flops 3145728 | bytes 1048576 | tf_op jit(solution)/shard_map/columns/pallas_call | solution.py:330
  22.9 0.1 collective-permute-start.7
  23.0 0.0 copy-start.1
  23.0 1.1 %columns.3 = (f32[8,128]{1,0:T(8,128)S(1)}, f32[1,256]{1,0:T(1,128)}) custom-call(f32[256,1024]{1,0:T(8,128)S(1)} %get-tuple-element.49.refs_0_, f32[256,1024]{1,0:T(8,128)S(1)} %get-tuple-element.51.refs_1_, f32[2,256]{1,0:T(2,128)S(1)} %log_add_fusion.refs_2_, f32[2,256]{1,0:T(2,128)S(1)} %get-tuple-element.61.refs_3_, ...), custom_call_target="tpu_custom_call" | custom-call | flops 3145728 | bytes 1048576 | tf_op jit(solution)/shard_map/columns/pallas_call | solution.py:330
  24.1 0.0 collective-permute-done.7
  24.1 0.6 %fusion = f32[1024]{0:T(1024)} fusion(f32[1024]{0:T(1024)S(1)} %copy-done.2, f32[8,128]{1,0:T(8,128)S(1)} %collective-permute-done.7, f32[8,128]{1,0:T(8,128)S(1)} %get-tuple-element.58, f32[1024]{0:T(1024)S(1)} %copy-done, f32[1024]{0:T(1024)S(1)} %copy-done.1), kind=kLoop, calls=%fused_computation.3 | loop fusion | flops 9216 | bytes 24576 | tf_op jit(solution)/shard_map/mul | solution.py:350
  (15 shorter events, 0.1 us)
Async XLA Ops:
  0.6 6.6 %collective-permute-start = (bf16[1024,512]{1,0:T(8,128)(2,1)}, bf16[1024,512]{1,0:T(8,128)(2,1)S(1)}, u32[]{:S(2)}, u32[]{:S(2)}) collective-permute-start(bf16[1024,512]{1,0:T(8,128)(2,1)} %refs_1_.3), channel_id=1, source_target_pairs={{0,4},{4,0},{8,12},{12,8},{1,5},{5,1},{9,13},{13,9},{2,6},{6,2},{1... | collective-permute-start | bytes 3145736 | tf_op jit(solution)/shard_map/ppermute | solution.py:217
  1.2 8.0 %collective-permute-start.2 = (bf16[256,512]{1,0:T(8,128)(2,1)}, bf16[256,512]{1,0:T(8,128)(2,1)S(1)}, u32[]{:S(2)}, u32[]{:S(2)}) collective-permute-start(bf16[256,512]{1,0:T(8,128)(2,1)} %rows_ref.2), channel_id=1, source_target_pairs={{0,8},{4,12},{8,0},{12,4},{1,9},{5,13},{9,1},{13,5},{2,10},{6,14},... | collective-permute-start | bytes 786440 | tf_op jit(solution)/shard_map/ppermute | solution.py:220
  6.0 1.2 %collective-permute-start.1 = (f32[1,1024]{1,0:T(1,128)S(1)}, f32[1,1024]{1,0:T(1,128)S(1)}, u32[]{:S(2)}, u32[]{:S(2)}) collective-permute-start(f32[1,1024]{1,0:T(1,128)S(1)} %get-tuple-element.38.own_offset_ref), channel_id=1, source_target_pairs={{0,4},{4,0},{8,12},{12,8},{1,5},{5,1},{9,13},{13,9},{2,6},{6,2},{1... | collective-permute-start | bytes 12296 | tf_op jit(solution)/shard_map/ppermute | solution.py:217
  10.2 6.5 %collective-permute-start.3 = (f32[4,256]{1,0:T(4,128)S(1)}, f32[4,256]{1,0:T(4,128)S(1)}, u32[]{:S(2)}, u32[]{:S(2)}) collective-permute-start(f32[4,256]{1,0:T(4,128)S(1)} %far_rows.1), channel_id=1, source_target_pairs={{0,9},{1,8},{2,11},{3,10},{4,13},{5,12},{6,15},{7,14},{8,1},{9,0},... | collective-permute-start | bytes 12296 | tf_op jit(solution)/shard_map/ppermute | solution.py:310
  13.6 3.6 %collective-permute-start.5 = (f32[4,256]{1,0:T(4,128)S(1)}, f32[4,256]{1,0:T(4,128)S(1)}, u32[]{:S(2)}, u32[]{:S(2)}) collective-permute-start(f32[4,256]{1,0:T(4,128)S(1)} %far_rows.1), channel_id=1, source_target_pairs={{0,8},{4,12},{8,0},{12,4},{1,9},{5,13},{9,1},{13,5},{2,10},{6,14},... | collective-permute-start | bytes 12296 | tf_op jit(solution)/shard_map/ppermute | solution.py:220
  14.1 3.6 %collective-permute-start.4 = (f32[4,256]{1,0:T(4,128)S(1)}, f32[4,256]{1,0:T(4,128)S(1)}, u32[]{:S(2)}, u32[]{:S(2)}) collective-permute-start(f32[4,256]{1,0:T(4,128)S(1)} %far_rows.1), channel_id=1, source_target_pairs={{0,1},{1,0},{2,3},{3,2},{4,5},{5,4},{6,7},{7,6},{8,9},{9,8},{10,11... | collective-permute-start | bytes 12296 | tf_op jit(solution)/shard_map/ppermute | solution.py:223
  17.7 4.5 %collective-permute-start.6 = (f32[2,256]{1,0:T(2,128)S(1)}, f32[2,256]{1,0:T(2,128)S(1)}, u32[]{:S(2)}, u32[]{:S(2)}) collective-permute-start(f32[2,256]{1,0:T(2,128)S(1)} %log_add_fusion.1), channel_id=1, source_target_pairs={{0,2},{1,3},{2,0},{3,1},{4,6},{5,7},{6,4},{7,5},{8,10},{9,11},{10,... | collective-permute-start | bytes 6152 | tf_op jit(solution)/shard_map/ppermute | solution.py:223
  22.9 1.2 %collective-permute-start.7 = (f32[8,128]{1,0:T(8,128)S(1)}, f32[8,128]{1,0:T(8,128)S(1)}, u32[]{:S(2)}, u32[]{:S(2)}) collective-permute-start(f32[8,128]{1,0:T(8,128)S(1)} %columns.2), channel_id=1, source_target_pairs={{0,4},{4,0},{8,12},{12,8},{1,5},{5,1},{9,13},{13,9},{2,6},{6,2},{1... | collective-permute-start | bytes 12296 | tf_op jit(solution)/shard_map/ppermute | solution.py:217
  22.9 1.2 %copy-start = (f32[1024]{0:T(1024)S(1)}, f32[1024]{0:T(1024)}, u32[]{:S(2)}) copy-start(f32[1024]{0:T(1024)} %param.9) | copy-start | bytes 12292
  23.0 1.1 %copy-start.1 = (f32[1024]{0:T(1024)S(1)}, f32[1024]{0:T(1024)}, u32[]{:S(2)}) copy-start(f32[1024]{0:T(1024)} %param.11) | copy-start | bytes 12292
  23.0 1.1 %copy-start.2 = (f32[1024]{0:T(1024)S(1)}, f32[1024]{0:T(1024)}, u32[]{:S(2)}) copy-start(f32[1024]{0:T(1024)} %param.13) | copy-start | bytes 12292

commit v12 on v11

--- a/solution.py
+++ b/solution.py
@@ -145,20 +145,26 @@
     lse_ref[...] = row_sums(src_ref[...], ((tgt_ref, column_ref),), z_ref)
 
 
-def near_kernel(rows_ref, tgt_ref, offset_ref, held_ref, column_ref, lse_ref, z_ref):
+def far_kernel(count, *refs):
+    own_ref, column_ref, out_ref, z_ref = refs[count:]
+    for slot in range(count):
+        out_ref[slot : slot + 1, :] = row_sums(refs[slot][...], ((own_ref, column_ref),), z_ref)
+
+
+def pair_rows_kernel(count, *refs):
+    blocks, refs = refs[:count], refs[count:]
+    src_hbm, tgt_ref, offset_ref, near_ref, far_ref, line_ref, out_ref, src_ref, column_ref, z_ref, sem = refs
+    copy = pltpu.make_async_copy(src_hbm, src_ref, sem)
+    copy.start()
     put_offsets(offset_ref, column_ref, diagonal())
-    lse_ref[...] = merge(held_ref[...], row_sums(rows_ref[...], ((tgt_ref, column_ref),), z_ref))
-
-
-def far_kernel(count, *refs):
-    own_ref, own_column_ref, pair_ref, pair_column_ref, held_ref, line_ref = refs[count : count + 6]
-    out_ref, z_ref = refs[count + 6 :]
     slots = count + 1
-    out_ref[0:1, :] = held_ref[...]
     out_ref[slots : slots + 2, :] = line_ref[...]
+    sides = ((tgt_ref, column_ref),)
     for slot in range(count):
-        sides = ((own_ref, own_column_ref), (pair_ref, pair_column_ref))
-        out_ref[slot + 1 : slot + 2, :] = row_sums(refs[slot][...], sides, z_ref)
+        held = far_ref[slot : slot + 1, :]
+        out_ref[slot + 1 : slot + 2, :] = merge(held, row_sums(blocks[slot][...], sides, z_ref))
+    copy.wait()
+    out_ref[0:1, :] = merge(near_ref[...], row_sums(src_ref[...], sides, z_ref))
 
 
 def sum_columns(z_refs, offset, off_ref, out_ref):
@@ -228,7 +234,6 @@
 
     core = lax.axis_index("blk") & 1
     core_word = core.astype(jnp.int32).reshape(1)
-    pair_targets = pair(targets)
     inputs = (
         sources,
         targets,
@@ -266,30 +271,31 @@
     far_blocks = [across(sent, chip) for chip in range(1, chips)]
     held, offset, column, lse, line, src_sum = prepare_on(0, *earlier[:5], first)
     pair_offset = pair(offset)
-    pair_column, lse = pl.pallas_call(
-        near_kernel,
-        out_shape=(f32(tgt_count, LANES), f32(1, src_count)),
-        in_specs=[VMEM] * 4,
-        out_specs=(VMEM,) * 2,
-        scratch_shapes=[product_space],
-        compiler_params=params(12),
-        cost_estimate=cost(1),
-        name="near_rows",
-    )(sources, pair_targets, pair_offset, lse)
+    pair_targets = pair(held)
     far_lines = [across(line, chip) for chip in range(2, chips)]
-    lse, *moved = lax.optimization_barrier((lse, *far_blocks, *far_lines))
-    payload = pl.pallas_call(
+    far_own = pl.pallas_call(
         functools.partial(far_kernel, far),
-        out_shape=f32(chips + 2, src_count),
-        in_specs=[VMEM] * (far + 6),
+        out_shape=f32(far, src_count),
+        in_specs=[VMEM] * (far + 2),
         out_specs=VMEM,
         scratch_shapes=[product_space],
         compiler_params=params(12 + far),
-        cost_estimate=cost(2 * far),
-        name="far_rows",
-    )(*moved[:far], held, column, pair_targets, pair_column, lse, line)
-
-    payload, *blocks = lax.optimization_barrier((payload, sources, *moved[:far]))
+        cost_estimate=cost(100 * far),
+        name="far_own_rows",
+    )(*far_blocks, held, column)
+    far_own, pair_targets, pair_offset = lax.optimization_barrier((far_own, pair_targets, pair_offset))
+    payload, held_sources = pl.pallas_call(
+        functools.partial(pair_rows_kernel, far),
+        out_shape=(f32(chips + 2, src_count), jax.ShapeDtypeStruct(sources.shape, sources.dtype)),
+        in_specs=[VMEM] * far + [HBM] + [VMEM] * 5,
+        out_specs=(VMEM,) * 2,
+        scratch_shapes=[pltpu.VMEM((tgt_count, LANES), jnp.float32), product_space, pltpu.SemaphoreType.DMA(())],
+        compiler_params=params(12 + far),
+        cost_estimate=cost(chips),
+        name="pair_rows",
+    )(*far_blocks, inputs[0], pair_targets, pair_offset, lse, far_own, line)
+
+    payload, *blocks = lax.optimization_barrier((payload, held_sources, *far_blocks))
     own_zs, pair_zs = [], []
     for block in blocks:
         own_z, pair_z = pl.pallas_call(
@@ -314,7 +320,7 @@
     )
     beside = along(payload, 1)
     other = across(payload, 1)
-    lines = jnp.stack([line, other[chips:]] + moved[far:], axis=1)
+    lines = jnp.stack([line, other[chips:]] + far_lines, axis=1)
     lse = merge(payload[:chips], mirror(joined, 1), beside[:chips], mirror(other, 1))
     chip = 2
     while chip < chips:

time: 24.9 us -> 29.2 us (1.17)
  waiting for transfers between devices: 4.23 us -> 8.92 us
  Pallas kernels: 8.83 us -> 7.55 us
  local copies, waits for them, and re-layouts: 0.04 us -> 0.91 us
    ppermute x1, starting transfers between devices: 3.37 us -> 0.01 us  [shards(): lax.ppermute(payload, ('blk', 'tsplit'), [(b * sets + z, (b ^ 2) * sets +...]
    ppermute x2, waiting for transfers between devices: 0.92 us -> 4.01 us  [across(): return lax.ppermute(value, 'blk', [(i, i ^ 2 * chip) for i in range(slabs)])]
    ppermute x1, waiting for transfers between devices: 0.01 us -> 2.98 us  [shards(): lax.ppermute(payload, ('blk', 'tsplit'), [(b * sets + z, (b ^ 2) * sets +...]
    ppermute x2, starting transfers between devices: 3.11 us -> 5.27 us  [across(): return lax.ppermute(value, 'blk', [(i, i ^ 2 * chip) for i in range(slabs)])]
    ppermute x2, starting transfers between devices: 2.79 us -> 4.23 us  [along(): return lax.ppermute(value, 'tsplit', [(i, i ^ step) for i in range(sets)])]
    pallas_call x2, Pallas kernels: 2.44 us -> 1.48 us  [shards(): pl.pallas_call(logits_kernel, out_shape=(f32(src_count, tgt_count), f32(s...]
    unnamed x6 -> x8, local copies, waits for them, and re-layouts: 0.02 us -> 0.89 us
    ppermute x3, waiting for transfers between devices: 0.9 us -> 0.05 us  [pair(): return lax.ppermute(value, 'blk', [(i, i ^ 1) for i in range(slabs)])]
  transfers between devices with their start and end apart: 8 -> 8, of which waited for: 5 -> 3; matrix products, arithmetic and copies ran while one was open for 0% -> 0% of each run, Pallas kernels for 30% -> 18%
where the time goes in v12:
time: 29.2 us; the launch traced here: 29 us
  starting transfers between devices  10.1 us (35%)
  waiting for transfers between devices  8.92 us (31%)
  Pallas kernels  7.55 us (26%)
  local copies, waits for them, and re-layouts  0.91 us (3%)
  between operations  0.78 us (3%)
  other arithmetic  0.67 us (2%)
    ppermute x2, starting transfers between devices, across(): return lax.ppermute(value, 'blk', [(i, i ^ 2 * chip) for i in range(slabs)])  5.27 us
    ppermute x2, starting transfers between devices, along(): return lax.ppermute(value, 'tsplit', [(i, i ^ step) for i in range(sets)])  4.23 us
    ppermute x2, waiting for transfers between devices, across(): return lax.ppermute(value, 'blk', [(i, i ^ 2 * chip) for i in range(slabs)])  4.01 us
    ppermute x1, waiting for transfers between devices, shards(): lax.ppermute(payload, ('blk', 'tsplit'), [(b * sets + z, (b ^ 2) * sets +...  2.98 us
    pallas_call x2, Pallas kernels, prepare_on(): pl.pallas_call(functools.partial(prepare_kernel, turn), out_shape=(jax.Sh...  2.21 us
    ppermute x2, waiting for transfers between devices, along(): return lax.ppermute(value, 'tsplit', [(i, i ^ step) for i in range(sets)])  1.89 us
    pallas_call x2, Pallas kernels, columns(): pl.pallas_call(functools.partial(kernel, chips), out_shape=outs, in_specs...  1.64 us
    pallas_call x1, Pallas kernels, shards(): pl.pallas_call(functools.partial(pair_rows_kernel, far), out_shape=(f32(c...  1.6 us
  transfers between devices with their start and end apart: 8, of which 3 were waited for; matrix products, arithmetic and copies ran while one was open for 0% of the time, Pallas kernels for 18%

profile of v12, /device:TPU:0, one launch (start us, length us, event | category | flops | bytes accessed | tf_op | source)
XLA Modules:
  0.0 29.0 jit_solution(8756274411284338971)
XLA Ops:
  0.6 0.0 copy-start
  0.6 0.1 prepare_1.1
  0.7 0.9 %copy-done = bf16[256,512]{1,0:T(8,128)(2,1)S(1)} copy-done((bf16[256,512]{1,0:T(8,128)(2,1)S(1)}, bf16[256,512]{1,0:T(8,128)(2,1)}, u32[]{:S(2)}) %copy-start) | copy-done | bytes 262168
  1.6 3.0 %collective-permute-start = (bf16[256,512]{1,0:T(8,128)(2,1)S(1)}, bf16[256,512]{1,0:T(8,128)(2,1)S(1)}, u32[]{:S(2)}, u32[]{:S(2)}) collective-permute-start(bf16[256,512]{1,0:T(8,128)(2,1)S(1)} %copy-done), channel_id=1, source_target_pairs={{0,8},{4,12},{8,0},{12,4},{1,9},{5,13},{9,1},{13,5},{2,10},{6,14},... | collective-permute-start | bytes 786440 | tf_op jit(solution)/shard_map/ppermute | solution.py:226
  4.6 2.1 %prepare_0.1 = (bf16[1024,512]{1,0:T(8,128)(2,1)S(1)}, f32[1,1024]{1,0:T(1,128)S(1)}, f32[1024,128]{1,0:T(8,128)S(1)}, f32[1,256]{1,0:T(1,128)S(1)}, f32[2,256]{1,0:T(2,128)S(1)}, /*index=5*/f32[1,256]{1,0:T(1,128)S(1)}) custom-call(s32[1]{0:T(128)} %bitcast.core_ref, bf16[256,512]{1,0:T(8,128)(2,1)} %refs_1_.5, bf16[1024,512]{1,0:T(8,128)(2,1)} %refs_1_.4, ...), custom_call_target="tpu_custom_call" | custom-call | flops 268435456 | bytes 1048576 | tf_op jit(solution)/shard_map/prepare_0/pallas_call | solution.py:250
  6.7 0.1 collective-permute-start.2
  6.8 0.5 %collective-permute-start.1 = (bf16[1024,512]{1,0:T(8,128)(2,1)S(1)}, bf16[1024,512]{1,0:T(8,128)(2,1)S(1)}, u32[]{:S(2)}, u32[]{:S(2)}) collective-permute-start(bf16[1024,512]{1,0:T(8,128)(2,1)S(1)} %get-tuple-element.40.refs_1_.own_ref), channel_id=1, source_target_pairs={{0,4},{4,0},{8,12},{12,8},{1,5},{5,1},{9,13},{13,9},{2,6},{6,2},{1... | collective-permute-start | bytes 3145736 | tf_op jit(solution)/shard_map/ppermute | solution.py:223
  7.3 4.0 %collective-permute-done.refs_0_.rows_ref = bf16[256,512]{1,0:T(8,128)(2,1)S(1)} collective-permute-done((bf16[256,512]{1,0:T(8,128)(2,1)S(1)}, bf16[256,512]{1,0:T(8,128)(2,1)S(1)}, u32[]{:S(2)}, u32[]{:S(2)}) %collective-permute-start) | collective-permute-done | bytes 262176 | tf_op jit(solution)/shard_map/ppermute | solution.py:226
  11.3 0.6 %far_own_rows.1.refs_5_ = f32[1,256]{1,0:T(1,128)S(1)} custom-call(bf16[256,512]{1,0:T(8,128)(2,1)S(1)} %collective-permute-done.refs_0_.rows_ref, bf16[1024,512]{1,0:T(8,128)(2,1)S(1)} %get-tuple-element.40.refs_1_.own_ref, f32[1024,128]{1,0:T(8,128)S(1)} %get-tuple-element.41.refs_2_), custom_call_target="tpu_custom_call" | custom-call | flops 26843545600 | bytes 1048576 | tf_op jit(solution)/shard_map/far_own_rows/pallas_call | solution.py:276
  11.9 1.6 %pair_rows.1 = (f32[4,256]{1,0:T(4,128)S(1)}, bf16[256,512]{1,0:T(8,128)(2,1)S(1)}) custom-call(bf16[256,512]{1,0:T(8,128)(2,1)S(1)} %collective-permute-done.refs_0_.rows_ref, bf16[256,512]{1,0:T(8,128)(2,1)} %refs_1_.5, bf16[1024,512]{1,0:T(8,128)(2,1)S(1)} %collective-permute-done.1.refs_2_.pair_ref, ...), custom_call_target="tpu_custom_call" | custom-call | flops 536870912 | bytes 1048576 | tf_op jit(solution)/shard_map/pair_rows/pallas_call | solution.py:287
  13.5 2.3 %collective-permute-start.5 = (f32[4,256]{1,0:T(4,128)S(1)}, f32[4,256]{1,0:T(4,128)S(1)}, u32[]{:S(2)}, u32[]{:S(2)}) collective-permute-start(f32[4,256]{1,0:T(4,128)S(1)} %get-tuple-element.54), channel_id=1, source_target_pairs={{0,8},{4,12},{8,0},{12,4},{1,9},{5,13},{9,1},{13,5},{2,10},{6,14},... | collective-permute-start | bytes 12296 | tf_op jit(solution)/shard_map/ppermute | solution.py:226
  15.8 1.6 %collective-permute-start.4 = (f32[4,256]{1,0:T(4,128)S(1)}, f32[4,256]{1,0:T(4,128)S(1)}, u32[]{:S(2)}, u32[]{:S(2)}) collective-permute-start(f32[4,256]{1,0:T(4,128)S(1)} %get-tuple-element.54), channel_id=1, source_target_pairs={{0,1},{1,0},{2,3},{3,2},{4,5},{5,4},{6,7},{7,6},{8,9},{9,8},{10,11... | collective-permute-start | bytes 12296 | tf_op jit(solution)/shard_map/ppermute | solution.py:229
  17.4 0.7 %logits.2 = (f32[256,1024]{1,0:T(8,128)S(1)}, f32[256,1024]{1,0:T(8,128)S(1)}) custom-call(bf16[256,512]{1,0:T(8,128)(2,1)S(1)} %get-tuple-element.50.rows_ref, bf16[1024,512]{1,0:T(8,128)(2,1)S(1)} %get-tuple-element.40.refs_1_.own_ref, f32[1,1024]{1,0:T(1,128)S(1)} %get-tuple-element.42.own_offset_ref, ...), custom_call_target="tpu_custom_call" | custom-call | flops 536870912 | bytes 1048576 | tf_op jit(solution)/shard_map/logits/pallas_call | solution.py:301
  18.2 0.7 %logits.3 = (f32[256,1024]{1,0:T(8,128)S(1)}, f32[256,1024]{1,0:T(8,128)S(1)}) custom-call(bf16[256,512]{1,0:T(8,128)(2,1)S(1)} %collective-permute-done.refs_0_.rows_ref, bf16[1024,512]{1,0:T(8,128)(2,1)S(1)} %get-tuple-element.40.refs_1_.own_ref, f32[1,1024]{1,0:T(1,128)S(1)} %get-tuple-element.42.own_offset_ref, ...), custom_call_target="tpu_custom_call" | custom-call | flops 536870912 | bytes 1048576 | tf_op jit(solution)/shard_map/logits/pallas_call | solution.py:301
  18.9 3.0 %collective-permute-done.3 = f32[4,256]{1,0:T(4,128)S(1)} collective-permute-done((f32[4,256]{1,0:T(4,128)S(1)}, f32[4,256]{1,0:T(4,128)S(1)}, u32[]{:S(2)}, u32[]{:S(2)}) %collective-permute-start.3) | collective-permute-done | bytes 4128 | tf_op jit(solution)/shard_map/ppermute | solution.py:316
  22.0 2.7 %collective-permute-start.6 = (f32[2,256]{1,0:T(2,128)S(1)}, f32[2,256]{1,0:T(2,128)S(1)}, u32[]{:S(2)}, u32[]{:S(2)}) collective-permute-start(f32[2,256]{1,0:T(2,128)S(1)} %log_add_fusion.1), channel_id=1, source_target_pairs={{0,2},{1,3},{2,0},{3,1},{4,6},{5,7},{6,4},{7,5},{8,10},{9,11},{10,... | collective-permute-start | bytes 6152 | tf_op jit(solution)/shard_map/ppermute | solution.py:229
  24.6 1.9 %collective-permute-done.6 = f32[2,256]{1,0:T(2,128)S(1)} collective-permute-done((f32[2,256]{1,0:T(2,128)S(1)}, f32[2,256]{1,0:T(2,128)S(1)}, u32[]{:S(2)}, u32[]{:S(2)}) %collective-permute-start.6) | collective-permute-done | bytes 2080 | tf_op jit(solution)/shard_map/ppermute | solution.py:229
  26.5 0.6 %columns.2 = f32[8,128]{1,0:T(8,128)S(1)} custom-call(f32[256,1024]{1,0:T(8,128)S(1)} %get-tuple-element.55.refs_0_, f32[256,1024]{1,0:T(8,128)S(1)} %get-tuple-element.56.refs_1_, f32[2,256]{1,0:T(2,128)S(1)} %log_add_fusion.refs_2_, f32[2,256]{1,0:T(2,128)S(1)} %get-tuple-element.63.refs_3_, f32[2,256]{1,0:T(2,128)S(1)} %get-tuple-element.62.refs_4_), custom_call_target="tpu_custom_call" | custom-call | flops 3145728 | bytes 1048576 | tf_op jit(solution)/shard_map/columns/pallas_call | solution.py:336
  27.1 0.1 collective-permute-start.7
  27.2 0.0 copy-start.1
  27.2 0.0 copy-start.2
  27.2 1.1 %columns.3 = (f32[8,128]{1,0:T(8,128)S(1)}, f32[1,256]{1,0:T(1,128)}) custom-call(f32[256,1024]{1,0:T(8,128)S(1)} %get-tuple-element.51.refs_0_, f32[256,1024]{1,0:T(8,128)S(1)} %get-tuple-element.53.refs_1_, f32[2,256]{1,0:T(2,128)S(1)} %log_add_fusion.refs_2_, f32[2,256]{1,0:T(2,128)S(1)} %get-tuple-element.63.refs_3_, ...), custom_call_target="tpu_custom_call" | custom-call | flops 3145728 | bytes 1048576 | tf_op jit(solution)/shard_map/columns/pallas_call | solution.py:336
  28.3 0.0 collective-permute-done.7
  28.4 0.6 %fusion = f32[1024]{0:T(1024)} fusion(f32[1024]{0:T(1024)S(1)} %copy-done.3, f32[8,128]{1,0:T(8,128)S(1)} %collective-permute-done.7, f32[8,128]{1,0:T(8,128)S(1)} %get-tuple-element.60, f32[1024]{0:T(1024)S(1)} %copy-done.1, f32[1024]{0:T(1024)S(1)} %copy-done.2), kind=kLoop, calls=%fused_computation.3 | loop fusion | flops 9216 | bytes 24576 | tf_op jit(solution)/shard_map/mul | solution.py:356
  (17 shorter events, 0.1 us)
Async XLA Ops:
  0.6 1.0 %copy-start = (bf16[256,512]{1,0:T(8,128)(2,1)S(1)}, bf16[256,512]{1,0:T(8,128)(2,1)}, u32[]{:S(2)}) copy-start(bf16[256,512]{1,0:T(8,128)(2,1)} %refs_1_.5) | copy-start | bytes 786436
  1.6 9.7 %collective-permute-start = (bf16[256,512]{1,0:T(8,128)(2,1)S(1)}, bf16[256,512]{1,0:T(8,128)(2,1)S(1)}, u32[]{:S(2)}, u32[]{:S(2)}) collective-permute-start(bf16[256,512]{1,0:T(8,128)(2,1)S(1)} %copy-done), channel_id=1, source_target_pairs={{0,8},{4,12},{8,0},{12,4},{1,9},{5,13},{9,1},{13,5},{2,10},{6,14},... | collective-permute-start | bytes 786440 | tf_op jit(solution)/shard_map/ppermute | solution.py:226
  6.7 5.2 %collective-permute-start.2 = (f32[1,1024]{1,0:T(1,128)S(1)}, f32[1,1024]{1,0:T(1,128)S(1)}, u32[]{:S(2)}, u32[]{:S(2)}) collective-permute-start(f32[1,1024]{1,0:T(1,128)S(1)} %get-tuple-element.42.own_offset_ref), channel_id=1, source_target_pairs={{0,4},{4,0},{8,12},{12,8},{1,5},{5,1},{9,13},{13,9},{2,6},{6,2},{1... | collective-permute-start | bytes 12296 | tf_op jit(solution)/shard_map/ppermute | solution.py:223
  6.8 5.1 %collective-permute-start.1 = (bf16[1024,512]{1,0:T(8,128)(2,1)S(1)}, bf16[1024,512]{1,0:T(8,128)(2,1)S(1)}, u32[]{:S(2)}, u32[]{:S(2)}) collective-permute-start(bf16[1024,512]{1,0:T(8,128)(2,1)S(1)} %get-tuple-element.40.refs_1_.own_ref), channel_id=1, source_target_pairs={{0,4},{4,0},{8,12},{12,8},{1,5},{5,1},{9,13},{13,9},{2,6},{6,2},{1... | collective-permute-start | bytes 3145736 | tf_op jit(solution)/shard_map/ppermute | solution.py:223
  13.5 5.4 %collective-permute-start.5 = (f32[4,256]{1,0:T(4,128)S(1)}, f32[4,256]{1,0:T(4,128)S(1)}, u32[]{:S(2)}, u32[]{:S(2)}) collective-permute-start(f32[4,256]{1,0:T(4,128)S(1)} %get-tuple-element.54), channel_id=1, source_target_pairs={{0,8},{4,12},{8,0},{12,4},{1,9},{5,13},{9,1},{13,5},{2,10},{6,14},... | collective-permute-start | bytes 12296 | tf_op jit(solution)/shard_map/ppermute | solution.py:226
  15.8 6.1 %collective-permute-start.4 = (f32[4,256]{1,0:T(4,128)S(1)}, f32[4,256]{1,0:T(4,128)S(1)}, u32[]{:S(2)}, u32[]{:S(2)}) collective-permute-start(f32[4,256]{1,0:T(4,128)S(1)} %get-tuple-element.54), channel_id=1, source_target_pairs={{0,1},{1,0},{2,3},{3,2},{4,5},{5,4},{6,7},{7,6},{8,9},{9,8},{10,11... | collective-permute-start | bytes 12296 | tf_op jit(solution)/shard_map/ppermute | solution.py:229
  17.4 4.5 %collective-permute-start.3 = (f32[4,256]{1,0:T(4,128)S(1)}, f32[4,256]{1,0:T(4,128)S(1)}, u32[]{:S(2)}, u32[]{:S(2)}) collective-permute-start(f32[4,256]{1,0:T(4,128)S(1)} %get-tuple-element.54), channel_id=1, source_target_pairs={{0,9},{1,8},{2,11},{3,10},{4,13},{5,12},{6,15},{7,14},{8,1},{9,0},... | collective-permute-start | bytes 12296 | tf_op jit(solution)/shard_map/ppermute | solution.py:316
  22.0 4.5 %collective-permute-start.6 = (f32[2,256]{1,0:T(2,128)S(1)}, f32[2,256]{1,0:T(2,128)S(1)}, u32[]{:S(2)}, u32[]{:S(2)}) collective-permute-start(f32[2,256]{1,0:T(2,128)S(1)} %log_add_fusion.1), channel_id=1, source_target_pairs={{0,2},{1,3},{2,0},{3,1},{4,6},{5,7},{6,4},{7,5},{8,10},{9,11},{10,... | collective-permute-start | bytes 6152 | tf_op jit(solution)/shard_map/ppermute | solution.py:229
  27.1 1.2 %collective-permute-start.7 = (f32[8,128]{1,0:T(8,128)S(1)}, f32[8,128]{1,0:T(8,128)S(1)}, u32[]{:S(2)}, u32[]{:S(2)}) collective-permute-start(f32[8,128]{1,0:T(8,128)S(1)} %columns.2), channel_id=1, source_target_pairs={{0,4},{4,0},{8,12},{12,8},{1,5},{5,1},{9,13},{13,9},{2,6},{6,2},{1... | collective-permute-start | bytes 12296 | tf_op jit(solution)/shard_map/ppermute | solution.py:223
  27.2 1.2 %copy-start.1 = (f32[1024]{0:T(1024)S(1)}, f32[1024]{0:T(1024)}, u32[]{:S(2)}) copy-start(f32[1024]{0:T(1024)} %param.9) | copy-start | bytes 12292
  27.2 1.1 %copy-start.2 = (f32[1024]{0:T(1024)S(1)}, f32[1024]{0:T(1024)}, u32[]{:S(2)}) copy-start(f32[1024]{0:T(1024)} %param.11) | copy-start | bytes 12292
  27.2 1.1 %copy-start.3 = (f32[1024]{0:T(1024)S(1)}, f32[1024]{0:T(1024)}, u32[]{:S(2)}) copy-start(f32[1024]{0:T(1024)} %param.13) | copy-start | bytes 12292

commit v13 on v11

--- a/solution.py
+++ b/solution.py
@@ -87,19 +87,23 @@
         column_ref[at : at + LANES, :] = jnp.broadcast_to(column, (LANES, LANES))
 
 
-def logits_kernel(rows_ref, own_ref, own_offset_ref, pair_ref, pair_offset_ref, own_z_ref, pair_z_ref):
-    rows = rows_ref[...] * LOGIT_SCALE
-    for tgt_ref, offset_ref, z_ref in ((own_ref, own_offset_ref, own_z_ref), (pair_ref, pair_offset_ref, pair_z_ref)):
-        for at in range(0, tgt_ref.shape[0], CHUNK):
-            cols = slice(at, at + CHUNK)
-            dots = lax.dot_general(rows, tgt_ref[cols, :], NT_DIMS, preferred_element_type=jnp.float32)
-            z_ref[:, cols] = (dots + offset_ref[:, cols]) * LOG2_E
+def make_logits(rows, tgt_ref, offset_ref, z_ref):
+    rows = rows * LOGIT_SCALE
+    for at in range(0, tgt_ref.shape[0], CHUNK):
+        cols = slice(at, at + CHUNK)
+        dots = lax.dot_general(rows, tgt_ref[cols, :], NT_DIMS, preferred_element_type=jnp.float32)
+        z_ref[:, cols] = (dots + offset_ref[:, cols]) * LOG2_E
+
+
+def logits_kernel(sides, rows_ref, *refs):
+    for side in range(sides):
+        make_logits(rows_ref[...], refs[2 * side], refs[2 * side + 1], refs[2 * sides + side])
 
 
 def prepare_kernel(turn, core_ref, *refs):
     inputs, refs = refs[:6], refs[6:]
-    earlier, refs = refs[: 6 * (1 - turn)], refs[6 * (1 - turn) :]
-    outs, scratch = refs[:6], refs[6:]
+    earlier, refs = refs[: 7 * (1 - turn)], refs[7 * (1 - turn) :]
+    outs, scratch = refs[:7], refs[7:]
 
     @pl.when(core_ref[0] == turn)
     def work():
@@ -115,7 +119,7 @@
 
 def prepare(
     src_hbm, tgt_hbm, pot_hbm, mass_hbm, slope_hbm, logmass_hbm,
-    tgt_ref, offset_ref, column_ref, lse_ref, line_ref, sum_ref,
+    tgt_ref, offset_ref, column_ref, own_z_ref, lse_ref, line_ref, sum_ref,
     src_ref, pot_ref, mass_ref, slope_ref, logmass_ref, z_ref, sems,
 ):
     pairs = (
@@ -143,6 +147,7 @@
         offset_ref[:, at : at + LANES] = base - to_lanes(squares(tgt_ref, at), eye)
     put_offsets(offset_ref, column_ref, eye)
     lse_ref[...] = row_sums(src_ref[...], ((tgt_ref, column_ref),), z_ref)
+    make_logits(src_ref[...], tgt_ref, offset_ref, own_z_ref)
 
 
 def near_kernel(rows_ref, tgt_ref, offset_ref, held_ref, column_ref, lse_ref, z_ref):
@@ -248,12 +253,13 @@
                 jax.ShapeDtypeStruct(targets.shape, targets.dtype),
                 f32(1, tgt_count),
                 f32(tgt_count, LANES),
+                f32(src_count, tgt_count),
                 f32(1, src_count),
                 f32(2, src_count),
                 f32(1, src_count),
             ),
             in_specs=[SMEM] + [HBM] * 6 + [VMEM] * len(earlier),
-            out_specs=(VMEM,) * 6,
+            out_specs=(VMEM,) * 7,
             scratch_shapes=[pltpu.VMEM(x.shape, x.dtype) for x in (inputs[0], *inputs[2:])]
             + [product_space, pltpu.SemaphoreType.DMA((6,))],
             compiler_params=params(12),
@@ -262,9 +268,9 @@
         )(core_word, *inputs, *earlier)
 
     earlier = prepare_on(1)
-    first, sent = lax.optimization_barrier((earlier[5], sources))
+    first, sent = lax.optimization_barrier((earlier[6], sources))
     far_blocks = [across(sent, chip) for chip in range(1, chips)]
-    held, offset, column, lse, line, src_sum = prepare_on(0, *earlier[:5], first)
+    held, offset, column, own_z, lse, line, src_sum = prepare_on(0, *earlier[:6], first)
     pair_offset = pair(offset)
     pair_column, lse = pl.pallas_call(
         near_kernel,
@@ -290,32 +296,35 @@
     )(*moved[:far], held, column, pair_targets, pair_column, lse, line)
 
     payload, *blocks = lax.optimization_barrier((payload, sources, *moved[:far]))
-    own_zs, pair_zs = [], []
-    for block in blocks:
-        own_z, pair_z = pl.pallas_call(
-            logits_kernel,
-            out_shape=(f32(src_count, tgt_count), f32(src_count, tgt_count)),
-            in_specs=[VMEM] * 5,
-            out_specs=(VMEM,) * 2,
+    def logits(block, *sides):
+        return pl.pallas_call(
+            functools.partial(logits_kernel, len(sides) // 2),
+            out_shape=(f32(src_count, tgt_count),) * (len(sides) // 2),
+            in_specs=[VMEM] * (1 + len(sides)),
+            out_specs=(VMEM,) * (len(sides) // 2),
             compiler_params=params(12),
-            cost_estimate=cost(2),
+            cost_estimate=cost(len(sides) // 2),
             name="logits",
-        )(block, held, offset, pair_targets, pair_offset)
+        )(block, *sides)
+
+    own_zs, pair_zs = [own_z], list(logits(blocks[0], pair_targets, pair_offset))
+    for block in blocks[1:]:
+        own_z, pair_z = logits(block, held, offset, pair_targets, pair_offset)
         own_zs.append(own_z)
         pair_zs.append(pair_z)
 
     def mirror(value, chip):
         return jnp.stack([value[slot ^ chip] for slot in range(chips)])
 
+    other = across(payload, 1)
+    beside = along(payload, 1)
     joined = lax.ppermute(
         payload,
         ("blk", "tsplit"),
         [(b * sets + z, (b ^ 2) * sets + (z ^ 1)) for b in range(slabs) for z in range(sets)],
     )
-    beside = along(payload, 1)
-    other = across(payload, 1)
     lines = jnp.stack([line, other[chips:]] + moved[far:], axis=1)
-    lse = merge(payload[:chips], mirror(joined, 1), beside[:chips], mirror(other, 1))
+    lse = merge(payload[:chips], mirror(other, 1), beside[:chips], mirror(joined, 1))
     chip = 2
     while chip < chips:
         lse = merge(lse, mirror(across(lse, chip), chip))

time: 24.9 us -> 24.6 us (0.988)
  waiting for transfers between devices: 4.23 us -> 3.96 us
    ppermute x2, waiting for transfers between devices: 2.4 us -> 1.88 us  [along(): return lax.ppermute(value, 'tsplit', [(i, i ^ step) for i in range(sets)])]
    ppermute x2, starting transfers between devices: 2.79 us -> 3.1 us  [along(): return lax.ppermute(value, 'tsplit', [(i, i ^ step) for i in range(sets)])]
    ppermute x2, starting transfers between devices: 3.11 us -> 2.8 us  [across(): return lax.ppermute(value, 'blk', [(i, i ^ 2 * chip) for i in range(slabs)])]
    pallas_call x2, Pallas kernels: 2.2 us -> 2.49 us  [prepare_on(): pl.pallas_call(functools.partial(prepare_kernel, turn), out_shape=(jax.Sh...]
    ppermute x2, waiting for transfers between devices: 0.92 us -> 1.2 us  [across(): return lax.ppermute(value, 'blk', [(i, i ^ 2 * chip) for i in range(slabs)])]
    pallas_call x2, Pallas kernels: 2.44 us -> 2.18 us  [logits(): pl.pallas_call(functools.partial(logits_kernel, len(sides) // 2), out_sha...]
  transfers between devices with their start and end apart: 8 -> 8, of which waited for: 5 -> 4; matrix products, arithmetic and copies ran while one was open for 0% -> 0% of each run, Pallas kernels for 30% -> 30%
where the time goes in v13:
time: 24.6 us; the launch traced here: 24.4 us
  starting transfers between devices  10.1 us (41%)
  Pallas kernels  8.86 us (36%)
  waiting for transfers between devices  3.96 us (16%)
  between operations  0.74 us (3%)
  other arithmetic  0.67 us (3%)
    ppermute x1, starting transfers between devices, shards(): lax.ppermute(payload, ('blk', 'tsplit'), [(b * sets + z, (b ^ 2) * sets +...  3.18 us
    ppermute x2, starting transfers between devices, along(): return lax.ppermute(value, 'tsplit', [(i, i ^ step) for i in range(sets)])  3.1 us
    ppermute x2, starting transfers between devices, across(): return lax.ppermute(value, 'blk', [(i, i ^ 2 * chip) for i in range(slabs)])  2.8 us
    pallas_call x2, Pallas kernels, prepare_on(): pl.pallas_call(functools.partial(prepare_kernel, turn), out_shape=(jax.Sh...  2.49 us
    pallas_call x2, Pallas kernels, logits(): pl.pallas_call(functools.partial(logits_kernel, len(sides) // 2), out_sha...  2.18 us
    ppermute x2, waiting for transfers between devices, along(): return lax.ppermute(value, 'tsplit', [(i, i ^ step) for i in range(sets)])  1.88 us
    pallas_call x2, Pallas kernels, columns(): pl.pallas_call(functools.partial(kernel, chips), out_shape=outs, in_specs...  1.63 us
    pallas_call x1, Pallas kernels, shards(): pl.pallas_call(near_kernel, out_shape=(f32(tgt_count, LANES), f32(1, src_...  1.59 us
  transfers between devices with their start and end apart: 8, of which 4 were waited for; matrix products, arithmetic and copies ran while one was open for 0% of the time, Pallas kernels for 30%

profile of v13, /device:TPU:0, one launch (start us, length us, event | category | flops | bytes accessed | tf_op | source)
XLA Modules:
  0.0 24.4 jit_solution(995312390793629288)
XLA Ops:
  0.6 0.5 %collective-permute-start = (bf16[1024,512]{1,0:T(8,128)(2,1)}, bf16[1024,512]{1,0:T(8,128)(2,1)S(1)}, u32[]{:S(2)}, u32[]{:S(2)}) collective-permute-start(bf16[1024,512]{1,0:T(8,128)(2,1)} %refs_1_.3), channel_id=1, source_target_pairs={{0,4},{4,0},{8,12},{12,8},{1,5},{5,1},{9,13},{13,9},{2,6},{6,2},{1... | collective-permute-start | bytes 3145736 | tf_op jit(solution)/shard_map/ppermute | solution.py:222
  1.1 0.1 prepare_1.1
  1.2 2.6 %collective-permute-start.2 = (bf16[256,512]{1,0:T(8,128)(2,1)}, bf16[256,512]{1,0:T(8,128)(2,1)S(1)}, u32[]{:S(2)}, u32[]{:S(2)}) collective-permute-start(bf16[256,512]{1,0:T(8,128)(2,1)} %rows_ref.2), channel_id=1, source_target_pairs={{0,8},{4,12},{8,0},{12,4},{1,9},{5,13},{9,1},{13,5},{2,10},{6,14},... | collective-permute-start | bytes 786440 | tf_op jit(solution)/shard_map/ppermute | solution.py:225
  3.8 2.4 %prepare_0.1 = (bf16[1024,512]{1,0:T(8,128)(2,1)S(1)}, f32[1,1024]{1,0:T(1,128)S(1)}, f32[1024,128]{1,0:T(8,128)S(1)}, f32[256,1024]{1,0:T(8,128)S(1)}, f32[1,25...) custom-call(s32[1]{0:T(128)} %bitcast.core_ref, bf16[256,512]{1,0:T(8,128)(2,1)} %rows_ref.2, ...), custom_call_target="tpu_custom_call" | custom-call | flops 268435456 | bytes 1048576 | tf_op jit(solution)/shard_map/prepare_0/pallas_call | solution.py:250
  6.3 0.4 %collective-permute-start.1 = (f32[1,1024]{1,0:T(1,128)S(1)}, f32[1,1024]{1,0:T(1,128)S(1)}, u32[]{:S(2)}, u32[]{:S(2)}) collective-permute-start(f32[1,1024]{1,0:T(1,128)S(1)} %get-tuple-element.40.refs_1_), channel_id=1, source_target_pairs={{0,4},{4,0},{8,12},{12,8},{1,5},{5,1},{9,13},{13,9},{2,6},{6,2},{1... | collective-permute-start | bytes 12296 | tf_op jit(solution)/shard_map/ppermute | solution.py:222
  6.7 0.8 %collective-permute-done.1.offset_ref.refs_3_.refs_1_ = f32[1,1024]{1,0:T(1,128)S(1)} collective-permute-done((f32[1,1024]{1,0:T(1,128)S(1)}, f32[1,1024]{1,0:T(1,128)S(1)}, u32[]{:S(2)}, u32[]{:S(2)}) %collective-permute-start.1) | collective-permute-done | bytes 4128 | tf_op jit(solution)/shard_map/ppermute | solution.py:222
  7.5 1.6 %near_rows.1 = (f32[1024,128]{1,0:T(8,128)S(1)}, f32[1,256]{1,0:T(1,128)S(1)}) custom-call(bf16[256,512]{1,0:T(8,128)(2,1)} %rows_ref.2, bf16[1024,512]{1,0:T(8,128)(2,1)S(1)} %collective-permute-done.tgt_ref.refs_3_.refs_2_.refs_0_, f32[1,1024]{1,0:T(1,128)S(1)} %collective-permute-done.1.offset_ref.refs_3_.refs_1_, f32[1,256]{1,0:T(1,128)S(1)} %get-tuple-element.41.held_ref), custom_call_target="tpu_custom_call" | custom-call | flops 268435456 | bytes 1048576 | tf_op jit(solution)/shard_map/near_rows/pallas_call | solution.py:275
  9.1 1.0 %far_rows.1 = f32[4,256]{1,0:T(4,128)S(1)} custom-call(bf16[256,512]{1,0:T(8,128)(2,1)S(1)} %collective-permute-done.2.refs_0_.rows_ref, bf16[1024,512]{1,0:T(8,128)(2,1)S(1)} %get-tuple-element.45.refs_1_.refs_0_, f32[1024,128]{1,0:T(8,128)S(1)} %get-tuple-element.46.refs_2_, bf16[1024,512]{1,0:T(8,128)(2,1)S(1)} %collective-permute-done.tgt_ref.refs_3_.refs_2_.refs_0_, ...), custom_call_target="tpu_custom_call" | custom-call | flops 536870912 | bytes 1048576 | tf_op jit(solution)/shard_map/far_rows/pallas_call | solution.py:287
  10.1 3.2 %collective-permute-start.5 = (f32[4,256]{1,0:T(4,128)S(1)}, f32[4,256]{1,0:T(4,128)S(1)}, u32[]{:S(2)}, u32[]{:S(2)}) collective-permute-start(f32[4,256]{1,0:T(4,128)S(1)} %far_rows.1), channel_id=1, source_target_pairs={{0,9},{1,8},{2,11},{3,10},{4,13},{5,12},{6,15},{7,14},{8,1},{9,0},... | collective-permute-start | bytes 12296 | tf_op jit(solution)/shard_map/ppermute | solution.py:321
  13.3 0.5 %collective-permute-start.4 = (f32[4,256]{1,0:T(4,128)S(1)}, f32[4,256]{1,0:T(4,128)S(1)}, u32[]{:S(2)}, u32[]{:S(2)}) collective-permute-start(f32[4,256]{1,0:T(4,128)S(1)} %far_rows.1), channel_id=1, source_target_pairs={{0,1},{1,0},{2,3},{3,2},{4,5},{5,4},{6,7},{7,6},{8,9},{9,8},{10,11... | collective-permute-start | bytes 12296 | tf_op jit(solution)/shard_map/ppermute | solution.py:228
  13.7 0.2 collective-permute-start.3
  13.9 0.8 %logits.2 = (f32[256,1024]{1,0:T(8,128)S(1)}, f32[256,1024]{1,0:T(8,128)S(1)}) custom-call(bf16[256,512]{1,0:T(8,128)(2,1)S(1)} %collective-permute-done.2.refs_0_.rows_ref, bf16[1024,512]{1,0:T(8,128)(2,1)S(1)} %get-tuple-element.45.refs_1_.refs_0_, f32[1,1024]{1,0:T(1,128)S(1)} %get-tuple-element.40.refs_1_, ...), custom_call_target="tpu_custom_call" | custom-call | flops 536870912 | bytes 1048576 | tf_op jit(solution)/shard_map/logits/pallas_call | solution.py:300
  14.7 1.4 %logits.3.refs_0_ = f32[256,1024]{1,0:T(8,128)S(1)} custom-call(bf16[256,512]{1,0:T(8,128)(2,1)} %rows_ref.2, bf16[1024,512]{1,0:T(8,128)(2,1)S(1)} %collective-permute-done.tgt_ref.refs_3_.refs_2_.refs_0_, f32[1,1024]{1,0:T(1,128)S(1)} %collective-permute-done.1.offset_ref.refs_3_.refs_1_), custom_call_target="tpu_custom_call" | custom-call | flops 268435456 | bytes 1048576 | tf_op jit(solution)/shard_map/logits/pallas_call | solution.py:300
  16.1 1.2 %collective-permute-done.3 = f32[4,256]{1,0:T(4,128)S(1)} collective-permute-done((f32[4,256]{1,0:T(4,128)S(1)}, f32[4,256]{1,0:T(4,128)S(1)}, u32[]{:S(2)}, u32[]{:S(2)}) %collective-permute-start.3) | collective-permute-done | bytes 4128 | tf_op jit(solution)/shard_map/ppermute | solution.py:225
  17.4 2.7 %collective-permute-start.6 = (f32[2,256]{1,0:T(2,128)S(1)}, f32[2,256]{1,0:T(2,128)S(1)}, u32[]{:S(2)}, u32[]{:S(2)}) collective-permute-start(f32[2,256]{1,0:T(2,128)S(1)} %log_add_fusion.1), channel_id=1, source_target_pairs={{0,2},{1,3},{2,0},{3,1},{4,6},{5,7},{6,4},{7,5},{8,10},{9,11},{10,... | collective-permute-start | bytes 6152 | tf_op jit(solution)/shard_map/ppermute | solution.py:228
  20.1 1.9 %collective-permute-done.6 = f32[2,256]{1,0:T(2,128)S(1)} collective-permute-done((f32[2,256]{1,0:T(2,128)S(1)}, f32[2,256]{1,0:T(2,128)S(1)}, u32[]{:S(2)}, u32[]{:S(2)}) %collective-permute-start.6) | collective-permute-done | bytes 2080 | tf_op jit(solution)/shard_map/ppermute | solution.py:228
  22.0 0.6 %columns.2 = f32[8,128]{1,0:T(8,128)S(1)} custom-call(f32[256,1024]{1,0:T(8,128)S(1)} %logits.3.refs_0_, f32[256,1024]{1,0:T(8,128)S(1)} %get-tuple-element.54.refs_1_, f32[2,256]{1,0:T(2,128)S(1)} %log_add_fusion.refs_2_, f32[2,256]{1,0:T(2,128)S(1)} %get-tuple-element.61.refs_3_, f32[2,256]{1,0:T(2,128)S(1)} %get-tuple-element.60.refs_4_), custom_call_target="tpu_custom_call" | custom-call | flops 3145728 | bytes 1048576 | tf_op jit(solution)/shard_map/columns/pallas_call | solution.py:339
  22.5 0.1 collective-permute-start.7
  22.6 0.0 copy-start
  22.6 0.0 copy-start.1
  22.6 0.0 copy-start.2
  22.6 1.1 %columns.3 = (f32[8,128]{1,0:T(8,128)S(1)}, f32[1,256]{1,0:T(1,128)}) custom-call(f32[256,1024]{1,0:T(8,128)S(1)} %get-tuple-element.39.refs_0_, f32[256,1024]{1,0:T(8,128)S(1)} %get-tuple-element.51.refs_1_, f32[2,256]{1,0:T(2,128)S(1)} %log_add_fusion.refs_2_, f32[2,256]{1,0:T(2,128)S(1)} %get-tuple-element.61.refs_3_, ...), custom_call_target="tpu_custom_call" | custom-call | flops 3145728 | bytes 1048576 | tf_op jit(solution)/shard_map/columns/pallas_call | solution.py:339
  23.7 0.1 collective-permute-done.7
  23.8 0.6 %fusion = f32[1024]{0:T(1024)} fusion(f32[1024]{0:T(1024)S(1)} %copy-done.2, f32[8,128]{1,0:T(8,128)S(1)} %collective-permute-done.7, f32[8,128]{1,0:T(8,128)S(1)} %get-tuple-element.58, f32[1024]{0:T(1024)S(1)} %copy-done, f32[1024]{0:T(1024)S(1)} %copy-done.1), kind=kLoop, calls=%fused_computation.3 | loop fusion | flops 9216 | bytes 24576 | tf_op jit(solution)/shard_map/mul | solution.py:359
  (15 shorter events, 0.1 us)
Async XLA Ops:
  0.6 6.9 %collective-permute-start = (bf16[1024,512]{1,0:T(8,128)(2,1)}, bf16[1024,512]{1,0:T(8,128)(2,1)S(1)}, u32[]{:S(2)}, u32[]{:S(2)}) collective-permute-start(bf16[1024,512]{1,0:T(8,128)(2,1)} %refs_1_.3), channel_id=1, source_target_pairs={{0,4},{4,0},{8,12},{12,8},{1,5},{5,1},{9,13},{13,9},{2,6},{6,2},{1... | collective-permute-start | bytes 3145736 | tf_op jit(solution)/shard_map/ppermute | solution.py:222
  1.2 7.9 %collective-permute-start.2 = (bf16[256,512]{1,0:T(8,128)(2,1)}, bf16[256,512]{1,0:T(8,128)(2,1)S(1)}, u32[]{:S(2)}, u32[]{:S(2)}) collective-permute-start(bf16[256,512]{1,0:T(8,128)(2,1)} %rows_ref.2), channel_id=1, source_target_pairs={{0,8},{4,12},{8,0},{12,4},{1,9},{5,13},{9,1},{13,5},{2,10},{6,14},... | collective-permute-start | bytes 786440 | tf_op jit(solution)/shard_map/ppermute | solution.py:225
  6.3 1.3 %collective-permute-start.1 = (f32[1,1024]{1,0:T(1,128)S(1)}, f32[1,1024]{1,0:T(1,128)S(1)}, u32[]{:S(2)}, u32[]{:S(2)}) collective-permute-start(f32[1,1024]{1,0:T(1,128)S(1)} %get-tuple-element.40.refs_1_), channel_id=1, source_target_pairs={{0,4},{4,0},{8,12},{12,8},{1,5},{5,1},{9,13},{13,9},{2,6},{6,2},{1... | collective-permute-start | bytes 12296 | tf_op jit(solution)/shard_map/ppermute | solution.py:222
  10.1 6.0 %collective-permute-start.5 = (f32[4,256]{1,0:T(4,128)S(1)}, f32[4,256]{1,0:T(4,128)S(1)}, u32[]{:S(2)}, u32[]{:S(2)}) collective-permute-start(f32[4,256]{1,0:T(4,128)S(1)} %far_rows.1), channel_id=1, source_target_pairs={{0,9},{1,8},{2,11},{3,10},{4,13},{5,12},{6,15},{7,14},{8,1},{9,0},... | collective-permute-start | bytes 12296 | tf_op jit(solution)/shard_map/ppermute | solution.py:321
  13.3 4.1 %collective-permute-start.4 = (f32[4,256]{1,0:T(4,128)S(1)}, f32[4,256]{1,0:T(4,128)S(1)}, u32[]{:S(2)}, u32[]{:S(2)}) collective-permute-start(f32[4,256]{1,0:T(4,128)S(1)} %far_rows.1), channel_id=1, source_target_pairs={{0,1},{1,0},{2,3},{3,2},{4,5},{5,4},{6,7},{7,6},{8,9},{9,8},{10,11... | collective-permute-start | bytes 12296 | tf_op jit(solution)/shard_map/ppermute | solution.py:228
  13.7 3.6 %collective-permute-start.3 = (f32[4,256]{1,0:T(4,128)S(1)}, f32[4,256]{1,0:T(4,128)S(1)}, u32[]{:S(2)}, u32[]{:S(2)}) collective-permute-start(f32[4,256]{1,0:T(4,128)S(1)} %far_rows.1), channel_id=1, source_target_pairs={{0,8},{4,12},{8,0},{12,4},{1,9},{5,13},{9,1},{13,5},{2,10},{6,14},... | collective-permute-start | bytes 12296 | tf_op jit(solution)/shard_map/ppermute | solution.py:225
  17.4 4.5 %collective-permute-start.6 = (f32[2,256]{1,0:T(2,128)S(1)}, f32[2,256]{1,0:T(2,128)S(1)}, u32[]{:S(2)}, u32[]{:S(2)}) collective-permute-start(f32[2,256]{1,0:T(2,128)S(1)} %log_add_fusion.1), channel_id=1, source_target_pairs={{0,2},{1,3},{2,0},{3,1},{4,6},{5,7},{6,4},{7,5},{8,10},{9,11},{10,... | collective-permute-start | bytes 6152 | tf_op jit(solution)/shard_map/ppermute | solution.py:228
  22.5 1.2 %collective-permute-start.7 = (f32[8,128]{1,0:T(8,128)S(1)}, f32[8,128]{1,0:T(8,128)S(1)}, u32[]{:S(2)}, u32[]{:S(2)}) collective-permute-start(f32[8,128]{1,0:T(8,128)S(1)} %columns.2), channel_id=1, source_target_pairs={{0,4},{4,0},{8,12},{12,8},{1,5},{5,1},{9,13},{13,9},{2,6},{6,2},{1... | collective-permute-start | bytes 12296 | tf_op jit(solution)/shard_map/ppermute | solution.py:222
  22.6 1.2 %copy-start = (f32[1024]{0:T(1024)S(1)}, f32[1024]{0:T(1024)}, u32[]{:S(2)}) copy-start(f32[1024]{0:T(1024)} %param.9) | copy-start | bytes 12292
  22.6 1.1 %copy-start.1 = (f32[1024]{0:T(1024)S(1)}, f32[1024]{0:T(1024)}, u32[]{:S(2)}) copy-start(f32[1024]{0:T(1024)} %param.11) | copy-start | bytes 12292
  22.6 1.1 %copy-start.2 = (f32[1024]{0:T(1024)S(1)}, f32[1024]{0:T(1024)}, u32[]{:S(2)}) copy-start(f32[1024]{0:T(1024)} %param.13) | copy-start | bytes 12292

commit v14 on v13

--- a/solution.py
+++ b/solution.py
@@ -100,18 +100,18 @@
         make_logits(rows_ref[...], refs[2 * side], refs[2 * side + 1], refs[2 * sides + side])
 
 
-def prepare_kernel(turn, core_ref, *refs):
+def prepare_kernel(turn, word_ref, *refs):
     inputs, refs = refs[:6], refs[6:]
     earlier, refs = refs[: 7 * (1 - turn)], refs[7 * (1 - turn) :]
     outs, scratch = refs[:7], refs[7:]
 
-    @pl.when(core_ref[0] == turn)
+    @pl.when(word_ref[0] == turn)
     def work():
         prepare(*inputs, *outs, *scratch)
 
     if earlier:
 
-        @pl.when(core_ref[0] != turn)
+        @pl.when(word_ref[0] != turn)
         def hand_on():
             for source, target in zip(earlier, outs):
                 target[...] = source[...]
@@ -150,20 +150,32 @@
     make_logits(src_ref[...], tgt_ref, offset_ref, own_z_ref)
 
 
-def near_kernel(rows_ref, tgt_ref, offset_ref, held_ref, column_ref, lse_ref, z_ref):
+def near_kernel(rows_ref, tgt_ref, offset_ref, held_ref, line_ref, column_ref, out_ref, z_ref):
     put_offsets(offset_ref, column_ref, diagonal())
-    lse_ref[...] = merge(held_ref[...], row_sums(rows_ref[...], ((tgt_ref, column_ref),), z_ref))
+    out_ref[0:1, :] = merge(held_ref[...], row_sums(rows_ref[...], ((tgt_ref, column_ref),), z_ref))
+    out_ref[1:3, :] = line_ref[...]
 
 
 def far_kernel(count, *refs):
-    own_ref, own_column_ref, pair_ref, pair_column_ref, held_ref, line_ref = refs[count : count + 6]
-    out_ref, z_ref = refs[count + 6 :]
-    slots = count + 1
-    out_ref[0:1, :] = held_ref[...]
-    out_ref[slots : slots + 2, :] = line_ref[...]
+    own_ref, own_column_ref, pair_ref, pair_column_ref, out_ref, z_ref = refs[count:]
     for slot in range(count):
         sides = ((own_ref, own_column_ref), (pair_ref, pair_column_ref))
-        out_ref[slot + 1 : slot + 2, :] = row_sums(refs[slot][...], sides, z_ref)
+        out_ref[slot : slot + 1, :] = row_sums(refs[slot][...], sides, z_ref)
+
+
+def near_logits_kernel(
+    word_ref, own_rows_ref, pair_rows_ref, held_ref, own_ref, own_offset_ref, pair_ref, pair_offset_ref,
+    own_z_ref, pair_z_ref,
+):
+    @pl.when(word_ref[1] == 0)
+    def straight():
+        own_z_ref[...] = held_ref[...]
+        make_logits(own_rows_ref[...], pair_ref, pair_offset_ref, pair_z_ref)
+
+    @pl.when(word_ref[1] != 0)
+    def flipped():
+        make_logits(pair_rows_ref[...], own_ref, own_offset_ref, own_z_ref)
+        make_logits(pair_rows_ref[...], pair_ref, pair_offset_ref, pair_z_ref)
 
 
 def sum_columns(z_refs, offset, off_ref, out_ref):
@@ -189,14 +201,27 @@
 
 def pair_kernel(slots, *refs):
     lse_ref, slope_ref, shift_ref, out_ref, off_ref = refs[slots:]
+    groups = refs[0].shape[1] // LANES
+    sum_columns(refs[:slots], shift_ref[...] - slope_ref[...] * lse_ref[...], off_ref, out_ref.at[:groups])
+    for at in range(0, lse_ref.shape[1], LANES):
+        row = groups + at // LANES
+        out_ref[row : row + 1, :] = lse_ref[0:1, at : at + LANES]
+
+
+def own_kernel(slots, *refs):
+    lse_ref, slope_ref, shift_ref, out_ref, off_ref = refs[slots:]
     sum_columns(refs[:slots], shift_ref[...] - slope_ref[...] * lse_ref[...], off_ref, out_ref)
 
 
-def own_kernel(slots, *refs):
-    lse_ref, slope_ref, shift_ref, sum_ref, out_ref, potential_ref, off_ref = refs[slots:]
-    lse, slope = lse_ref[...], slope_ref[...]
-    potential_ref[...] = slope[0:1, :] * (sum_ref[...] - lse[0:1, :])
-    sum_columns(refs[:slots], shift_ref[...] - slope * lse, off_ref, out_ref)
+def final_kernel(
+    word_ref, own_ref, home_ref, lse_ref, line_ref, sum_ref, pot_ref, mass_ref, expo_ref, update_ref, potential_ref
+):
+    groups = own_ref.shape[0]
+    total = merge(own_ref[...], home_ref[:groups, :])
+    update_ref[...] = expo_ref[...] * (2.0 * mass_ref[...] + pot_ref[...] - total)
+    away = jnp.concatenate([home_ref[row : row + 1, :] for row in range(groups, home_ref.shape[0])], axis=1)
+    lse = jnp.where(word_ref[1] == 0, lse_ref[0:1, :], away)
+    potential_ref[...] = line_ref[0:1, :] * (sum_ref[...] - lse)
 
 
 def f32(*shape):
@@ -216,7 +241,7 @@
     far = chips - 1
     groups = tgt_count // LANES
     src_groups = src_count // LANES
-    assert chips > 1 and sets > 1 and chips & (chips - 1) == 0 and sets & (sets - 1) == 0
+    assert chips > 1 and sets > 2 and chips & (chips - 1) == 0 and sets & (sets - 1) == 0
 
     def pair(value):
         return lax.ppermute(value, "blk", [(i, i ^ 1) for i in range(slabs)])
@@ -231,14 +256,29 @@
         pairs = blocks * src_count * tgt_count
         return pl.CostEstimate(flops=2 * pairs * width, bytes_accessed=2**20, transcendentals=pairs)
 
+    half = sets // 2
     core = lax.axis_index("blk") & 1
-    core_word = core.astype(jnp.int32).reshape(1)
+    flip = lax.axis_index("tsplit") // half
+    word = jnp.stack([core ^ flip, flip]).astype(jnp.int32)
+
+    def crossed(value, chip, core_flip, step):
+        ways = [
+            (b * sets + z, (b ^ (2 * chip) ^ core_flip(z)) * sets + (z ^ step))
+            for b in range(slabs)
+            for z in range(sets)
+        ]
+        return lax.ppermute(value, ("blk", "tsplit"), ways)
+
     pair_targets = pair(targets)
+    pair_sources = pair(sources)
+    potential = tgt_potential.reshape(groups, LANES)
+    logmass = tgt_logmass.reshape(groups, LANES)
+    exponent = tgt_exponent.reshape(groups, LANES)
     inputs = (
         sources,
         targets,
-        tgt_potential.reshape(groups, LANES),
-        tgt_logmass.reshape(groups, LANES),
+        potential,
+        logmass,
         src_exponent.reshape(src_groups, LANES),
         src_logmass.reshape(src_groups, LANES),
     )
@@ -265,37 +305,39 @@
             compiler_params=params(12),
             cost_estimate=cost(1),
             name=f"prepare_{turn}",
-        )(core_word, *inputs, *earlier)
+        )(word, *inputs, *earlier)
 
     earlier = prepare_on(1)
     first, sent = lax.optimization_barrier((earlier[6], sources))
-    far_blocks = [across(sent, chip) for chip in range(1, chips)]
+    far_blocks = [crossed(sent, chip, lambda z: z // half, 0) for chip in range(1, chips)]
     held, offset, column, own_z, lse, line, src_sum = prepare_on(0, *earlier[:6], first)
     pair_offset = pair(offset)
-    pair_column, lse = pl.pallas_call(
+    pair_column, near = pl.pallas_call(
         near_kernel,
-        out_shape=(f32(tgt_count, LANES), f32(1, src_count)),
-        in_specs=[VMEM] * 4,
+        out_shape=(f32(tgt_count, LANES), f32(3, src_count)),
+        in_specs=[VMEM] * 5,
         out_specs=(VMEM,) * 2,
         scratch_shapes=[product_space],
         compiler_params=params(12),
         cost_estimate=cost(1),
         name="near_rows",
-    )(sources, pair_targets, pair_offset, lse)
-    far_lines = [across(line, chip) for chip in range(2, chips)]
-    lse, *moved = lax.optimization_barrier((lse, *far_blocks, *far_lines))
-    payload = pl.pallas_call(
+    )(sources, pair_targets, pair_offset, lse, line)
+    near_away = pair(near)
+    near, *far_blocks = lax.optimization_barrier((near, *far_blocks))
+    far_lse = pl.pallas_call(
         functools.partial(far_kernel, far),
-        out_shape=f32(chips + 2, src_count),
-        in_specs=[VMEM] * (far + 6),
+        out_shape=f32(far, src_count),
+        in_specs=[VMEM] * (far + 4),
         out_specs=VMEM,
         scratch_shapes=[product_space],
         compiler_params=params(12 + far),
         cost_estimate=cost(2 * far),
         name="far_rows",
-    )(*moved[:far], held, column, pair_targets, pair_column, lse, line)
-
-    payload, *blocks = lax.optimization_barrier((payload, sources, *moved[:far]))
+    )(*far_blocks, held, column, pair_targets, pair_column)
+    near = jnp.where(flip == 0, near, near_away)
+    payload = jnp.concatenate([near[:1], far_lse, near[1:]])
+
+    payload, pair_sources, *far_blocks = lax.optimization_barrier((payload, pair_sources, *far_blocks))
     def logits(block, *sides):
         return pl.pallas_call(
             functools.partial(logits_kernel, len(sides) // 2),
@@ -307,40 +349,43 @@
             name="logits",
         )(block, *sides)
 
-    own_zs, pair_zs = [own_z], list(logits(blocks[0], pair_targets, pair_offset))
-    for block in blocks[1:]:
-        own_z, pair_z = logits(block, held, offset, pair_targets, pair_offset)
-        own_zs.append(own_z)
-        pair_zs.append(pair_z)
+    zs = [logits(block, held, offset, pair_targets, pair_offset) for block in far_blocks]
+    near_zs = pl.pallas_call(
+        near_logits_kernel,
+        out_shape=(f32(src_count, tgt_count),) * 2,
+        in_specs=[SMEM] + [VMEM] * 7,
+        out_specs=(VMEM,) * 2,
+        compiler_params=params(12),
+        cost_estimate=cost(2),
+        name="near_logits",
+    )(word, sources, pair_sources, own_z, held, offset, pair_targets, pair_offset)
+    own_zs, pair_zs = zip(near_zs, *zs)
 
     def mirror(value, chip):
         return jnp.stack([value[slot ^ chip] for slot in range(chips)])
 
     other = across(payload, 1)
     beside = along(payload, 1)
-    joined = lax.ppermute(
-        payload,
-        ("blk", "tsplit"),
-        [(b * sets + z, (b ^ 2) * sets + (z ^ 1)) for b in range(slabs) for z in range(sets)],
-    )
-    lines = jnp.stack([line, other[chips:]] + moved[far:], axis=1)
+    joined = crossed(payload, 1, lambda z: 0, 1)
+    far_lines = [across(near[1:], chip) for chip in range(2, chips)]
+    lines = jnp.stack([near[1:], other[chips:]] + far_lines, axis=1)
     lse = merge(payload[:chips], mirror(other, 1), beside[:chips], mirror(joined, 1))
     chip = 2
     while chip < chips:
         lse = merge(lse, mirror(across(lse, chip), chip))
         chip *= 2
     step = 2
-    while step < sets:
+    while step < half:
         lse = merge(lse, along(lse, step))
         step *= 2
-
-    def columns(kernel, zs, *more):
-        outs = (f32(groups, LANES), f32(1, src_count))[: 1 + len(more)]
+    lse = merge(lse, crossed(lse, 0, lambda z: 1, half))
+
+    def columns(kernel, zs, rows):
         return pl.pallas_call(
             functools.partial(kernel, chips),
-            out_shape=outs,
-            in_specs=[VMEM] * (chips + 3 + len(more)),
-            out_specs=(VMEM,) * len(outs),
+            out_shape=f32(rows, LANES),
+            in_specs=[VMEM] * (chips + 3),
+            out_specs=VMEM,
             scratch_shapes=[pltpu.VMEM((chips, src_count, LANES), jnp.float32)],
             compiler_params=params(8 + 2 * chips),
             cost_estimate=pl.CostEstimate(
@@ -349,15 +394,21 @@
                 transcendentals=chips * src_count * tgt_count,
             ),
             name="columns",
-        )(*zs, lse, lines[0], lines[1], *more)
-
-    (pair_part,) = columns(pair_kernel, pair_zs)
+        )(*zs, lse, lines[0], lines[1])
+
+    pair_part = columns(pair_kernel, pair_zs, groups + src_groups)
     lse, pair_part = lax.optimization_barrier((lse, pair_part))
     home = pair(pair_part)
-    own_part, src_potential = columns(own_kernel, own_zs, src_sum)
-    total = merge(own_part, home).reshape(tgt_count)
-    tgt_update = tgt_exponent * (2.0 * tgt_logmass + tgt_potential - total)
-    return (src_potential.reshape(src_count), tgt_update)
+    own_part = columns(own_kernel, own_zs, groups)
+    tgt_update, src_potential = pl.pallas_call(
+        final_kernel,
+        out_shape=(f32(groups, LANES), f32(1, src_count)),
+        in_specs=[SMEM] + [VMEM] * 8,
+        out_specs=(VMEM,) * 2,
+        compiler_params=params(8),
+        name="results",
+    )(word, own_part, home, lse, line, src_sum, potential, logmass, exponent)
+    return (src_potential.reshape(src_count), tgt_update.reshape(tgt_count))
 
 
 def solution(mesh):

time: 24.6 us -> 28.2 us (1.15)
  starting transfers between devices: 10.1 us -> 13.1 us
  Pallas kernels: 8.86 us -> 10.8 us
  waiting for transfers between devices: 3.96 us -> 2.27 us
  local copies, waits for them, and re-layouts: 0.04 us -> 0.84 us
  other arithmetic: 0.67 us -> 0.15 us
    ppermute x1 -> x3, starting transfers between devices: 3.18 us -> 8.47 us  [crossed(): return lax.ppermute(value, ('blk', 'tsplit'), ways)]
    ppermute x2 -> x1, starting transfers between devices: 3.1 us -> 0.32 us  [along(): return lax.ppermute(value, 'tsplit', [(i, i ^ step) for i in range(sets)])]
    pallas_call x4 -> x6, Pallas kernels: 4.19 us -> 6.48 us  [the longest x1 1.65 us: shards(): pl.pallas_call(near_kernel, out_shape=(f32(tgt_count, LANES), f32(3, src_...]
    ppermute x2 -> x1, waiting for transfers between devices: 1.88 us -> 0.01 us  [along(): return lax.ppermute(value, 'tsplit', [(i, i ^ step) for i in range(sets)])]
    ppermute x3 -> x5, starting transfers between devices: 1.03 us -> 2.7 us  [pair(): return lax.ppermute(value, 'blk', [(i, i ^ 1) for i in range(slabs)])]
    pallas_call x2 -> x1, Pallas kernels: 2.18 us -> 0.74 us  [logits(): pl.pallas_call(functools.partial(logits_kernel, len(sides) // 2), out_sha...]
    ppermute x1 -> x3, waiting for transfers between devices: 0.01 us -> 1.29 us  [crossed(): return lax.ppermute(value, ('blk', 'tsplit'), ways)]
    ppermute x2 -> x1, waiting for transfers between devices: 1.2 us -> 0.01 us  [across(): return lax.ppermute(value, 'blk', [(i, i ^ 2 * chip) for i in range(slabs)])]
  transfers between devices with their start and end apart: 8 -> 10, of which waited for: 4 -> 3; matrix products, arithmetic and copies ran while one was open for 0% -> 0% of each run, Pallas kernels for 30% -> 32%
where the time goes in v14:
time: 28.2 us; the launch traced here: 28 us
  starting transfers between devices  13.1 us (46%)
  Pallas kernels  10.8 us (38%)
  waiting for transfers between devices  2.27 us (8%)
  local copies, waits for them, and re-layouts  0.84 us (3%)
  between operations  0.78 us (3%)
    ppermute x3, starting transfers between devices, crossed(): return lax.ppermute(value, ('blk', 'tsplit'), ways)  8.47 us
    pallas_call x2, Pallas kernels, prepare_on(): pl.pallas_call(functools.partial(prepare_kernel, turn), out_shape=(jax.Sh...  3.56 us
    ppermute x5, starting transfers between devices, pair(): return lax.ppermute(value, 'blk', [(i, i ^ 1) for i in range(slabs)])  2.7 us
    ppermute x1, starting transfers between devices, across(): return lax.ppermute(value, 'blk', [(i, i ^ 2 * chip) for i in range(slabs)])  1.65 us
    pallas_call x1, Pallas kernels, shards(): pl.pallas_call(near_kernel, out_shape=(f32(tgt_count, LANES), f32(3, src_...  1.65 us
    pallas_call x1, Pallas kernels, shards(): pl.pallas_call(near_logits_kernel, out_shape=(f32(src_count, tgt_count),)...  1.59 us
    ppermute x3, waiting for transfers between devices, crossed(): return lax.ppermute(value, ('blk', 'tsplit'), ways)  1.29 us
    pallas_call x1, Pallas kernels, shards(): pl.pallas_call(final_kernel, out_shape=(f32(groups, LANES), f32(1, src_co...  1.16 us
  transfers between devices with their start and end apart: 10, of which 3 were waited for; matrix products, arithmetic and copies ran while one was open for 0% of the time, Pallas kernels for 32%

profile of v14, /device:TPU:0, one launch (start us, length us, event | category | flops | bytes accessed | tf_op | source)
XLA Modules:
  0.0 28.0 jit_solution(15740922981899673621)
XLA Ops:
  0.6 0.5 %collective-permute-start = (bf16[1024,512]{1,0:T(8,128)(2,1)}, bf16[1024,512]{1,0:T(8,128)(2,1)S(1)}, u32[]{:S(2)}, u32[]{:S(2)}) collective-permute-start(bf16[1024,512]{1,0:T(8,128)(2,1)} %refs_1_.3), channel_id=1, source_target_pairs={{0,4},{4,0},{8,12},{12,8},{1,5},{5,1},{9,13},{13,9},{2,6},{6,2},{1... | collective-permute-start | bytes 3145736 | tf_op jit(solution)/shard_map/ppermute | solution.py:247
  1.1 0.1 pad_add_fusion.word_ref
  1.2 0.6 %prepare_1.1 = (bf16[1024,512]{1,0:T(8,128)(2,1)S(1)}, f32[1,1024]{1,0:T(1,128)S(1)}, f32[1024,128]{1,0:T(8,128)S(1)}, f32[256,1024]{1,0:T(8,128)S(1)}, f32[1,25...) custom-call(s32[2]{0:T(128)S(1)} %pad_add_fusion.word_ref, bf16[256,512]{1,0:T(8,128)(2,1)} %own_rows_ref.1, ...), custom_call_target="tpu_custom_call" | custom-call | flops 268435456 | bytes 1048576 | tf_op jit(solution)/shard_map/prepare_1/pallas_call | solution.py:290
  1.8 2.6 %collective-permute-start.2 = (bf16[256,512]{1,0:T(8,128)(2,1)}, bf16[256,512]{1,0:T(8,128)(2,1)S(1)}, u32[]{:S(2)}, u32[]{:S(2)}) collective-permute-start(bf16[256,512]{1,0:T(8,128)(2,1)} %own_rows_ref.1), channel_id=1, source_target_pairs={{0,8},{1,9},{2,14},{3,15},{4,12},{5,13},{6,10},{7,11},{8,0},{9,1},... | collective-permute-start | bytes 786440 | tf_op jit(solution)/shard_map/ppermute | solution.py:270
  4.4 3.0 %prepare_0.1 = (bf16[1024,512]{1,0:T(8,128)(2,1)S(1)}, f32[1,1024]{1,0:T(1,128)S(1)}, f32[1024,128]{1,0:T(8,128)S(1)}, f32[256,1024]{1,0:T(8,128)S(1)}, f32[1,25...) custom-call(s32[2]{0:T(128)S(1)} %pad_add_fusion.word_ref, bf16[256,512]{1,0:T(8,128)(2,1)} %own_rows_ref.1, ...), custom_call_target="tpu_custom_call" | custom-call | flops 268435456 | bytes 1048576 | tf_op jit(solution)/shard_map/prepare_0/pallas_call | solution.py:290
  7.4 0.8 %copy-done = f32[1024,128]{1,0:T(8,128)} copy-done((f32[1024,128]{1,0:T(8,128)}, f32[1024,128]{1,0:T(8,128)S(1)}, u32[]{:S(2)}) %copy-start) | copy-done | bytes 524312
  8.2 0.4 %collective-permute-start.1 = (f32[1,1024]{1,0:T(1,128)S(1)}, f32[1,1024]{1,0:T(1,128)S(1)}, u32[]{:S(2)}, u32[]{:S(2)}) collective-permute-start(f32[1,1024]{1,0:T(1,128)S(1)} %get-tuple-element.41.own_offset_ref.refs_1_), channel_id=1, source_target_pairs={{0,4},{4,0},{8,12},{12,8},{1,5},{5,1},{9,13},{13,9},{2,6},{6,2},{1... | collective-permute-start | bytes 12296 | tf_op jit(solution)/shard_map/ppermute | solution.py:247
  8.6 0.1 collective-permute-start.4
  8.7 0.7 %collective-permute-done.1.offset_ref.pair_offset_ref.refs_3_ = f32[1,1024]{1,0:T(1,128)S(1)} collective-permute-done((f32[1,1024]{1,0:T(1,128)S(1)}, f32[1,1024]{1,0:T(1,128)S(1)}, u32[]{:S(2)}, u32[]{:S(2)}) %collective-permute-start.1) | collective-permute-done | bytes 4128 | tf_op jit(solution)/shard_map/ppermute | solution.py:247
  9.4 1.7 %near_rows.1 = (f32[1024,128]{1,0:T(8,128)S(1)}, f32[3,256]{1,0:T(4,128)S(1)}) custom-call(bf16[256,512]{1,0:T(8,128)(2,1)} %own_rows_ref.1, bf16[1024,512]{1,0:T(8,128)(2,1)S(1)} %collective-permute-done.tgt_ref.refs_3_.pair_ref.refs_2_, f32[1,1024]{1,0:T(1,128)S(1)} %collective-permute-done.1.offset_ref.pair_offset_ref.refs_3_, ...), custom_call_target="tpu_custom_call" | custom-call | flops 268435456 | bytes 1048576 | tf_op jit(solution)/shard_map/near_rows/pallas_call | solution.py:315
  11.1 0.4 %collective-permute-start.3 = (f32[3,256]{1,0:T(4,128)S(1)}, f32[3,256]{1,0:T(4,128)S(1)}, u32[]{:S(2)}, u32[]{:S(2)}) collective-permute-start(f32[3,256]{1,0:T(4,128)S(1)} %get-tuple-element.46), channel_id=1, source_target_pairs={{0,4},{4,0},{8,12},{12,8},{1,5},{5,1},{9,13},{13,9},{2,6},{6,2},{1... | collective-permute-start | bytes 9224 | tf_op jit(solution)/shard_map/ppermute | solution.py:247
  11.5 1.0 %far_rows.1 = f32[1,256]{1,0:T(1,128)S(1)} custom-call(bf16[256,512]{1,0:T(8,128)(2,1)S(1)} %collective-permute-done.2.refs_0_.rows_ref, bf16[1024,512]{1,0:T(8,128)(2,1)S(1)} %get-tuple-element.48.refs_1_.own_ref.refs_0_, f32[1024,128]{1,0:T(8,128)S(1)} %copy-done.1, bf16[1024,512]{1,0:T(8,128)(2,1)S(1)} %collective-permute-done.tgt_ref.refs_3_.pair_ref.refs_2_, ...), custom_call_target="tpu_custom_call" | custom-call | flops 536870912 | bytes 1048576 | tf_op jit(solution)/shard_map/far_rows/pallas_call | solution.py:327
  12.5 1.6 %collective-permute-start.7 = (f32[4,256]{1,0:T(4,128)S(1)}, f32[4,256]{1,0:T(4,128)S(1)}, u32[]{:S(2)}, u32[]{:S(2)}) collective-permute-start(f32[4,256]{1,0:T(4,128)S(1)} %pad_maximum_fusion), channel_id=1, source_target_pairs={{0,9},{1,8},{2,11},{3,10},{4,13},{5,12},{6,15},{7,14},{8,1},{9,0},... | collective-permute-start | bytes 12296 | tf_op jit(solution)/shard_map/ppermute | solution.py:270
  14.1 0.3 %collective-permute-start.6 = (f32[4,256]{1,0:T(4,128)S(1)}, f32[4,256]{1,0:T(4,128)S(1)}, u32[]{:S(2)}, u32[]{:S(2)}) collective-permute-start(f32[4,256]{1,0:T(4,128)S(1)} %pad_maximum_fusion), channel_id=1, source_target_pairs={{0,1},{1,0},{2,3},{3,2},{4,5},{5,4},{6,7},{7,6},{8,9},{9,8},{10,11... | collective-permute-start | bytes 12296 | tf_op jit(solution)/shard_map/ppermute | solution.py:253
  14.4 1.7 %collective-permute-start.5 = (f32[4,256]{1,0:T(4,128)S(1)}, f32[4,256]{1,0:T(4,128)S(1)}, u32[]{:S(2)}, u32[]{:S(2)}) collective-permute-start(f32[4,256]{1,0:T(4,128)S(1)} %pad_maximum_fusion), channel_id=1, source_target_pairs={{0,8},{4,12},{8,0},{12,4},{1,9},{5,13},{9,1},{13,5},{2,10},{6,14},... | collective-permute-start | bytes 12296 | tf_op jit(solution)/shard_map/ppermute | solution.py:250
  16.1 0.7 %logits.1 = (f32[256,1024]{1,0:T(8,128)S(1)}, f32[256,1024]{1,0:T(8,128)S(1)}) custom-call(bf16[256,512]{1,0:T(8,128)(2,1)S(1)} %collective-permute-done.2.refs_0_.rows_ref, bf16[1024,512]{1,0:T(8,128)(2,1)S(1)} %get-tuple-element.48.refs_1_.own_ref.refs_0_, f32[1,1024]{1,0:T(1,128)S(1)} %get-tuple-element.41.own_offset_ref.refs_1_, ...), custom_call_target="tpu_custom_call" | custom-call | flops 536870912 | bytes 1048576 | tf_op jit(solution)/shard_map/logits/pallas_call | solution.py:342
  16.8 1.6 %near_logits.1 = (f32[256,1024]{1,0:T(8,128)S(1)}, f32[256,1024]{1,0:T(8,128)S(1)}) custom-call(s32[2]{0:T(128)S(1)} %pad_add_fusion.word_ref, bf16[256,512]{1,0:T(8,128)(2,1)} %own_rows_ref.1, bf16[256,512]{1,0:T(8,128)(2,1)} %collective-permute-done.4.pair_rows_ref, f32[256,1024]{1,0:T(8,128)S(1)} %get-tuple-element.52.held_ref, ...), custom_call_target="tpu_custom_call" | custom-call | flops 536870912 | bytes 1048576 | tf_op jit(solution)/shard_map/near_logits/pallas_call | solution.py:353
  18.5 4.3 %collective-permute-start.8 = (f32[2,256]{1,0:T(2,128)S(1)}, f32[2,256]{1,0:T(2,128)S(1)}, u32[]{:S(2)}, u32[]{:S(2)}) collective-permute-start(f32[2,256]{1,0:T(2,128)S(1)} %log_add_fusion.1), channel_id=1, source_target_pairs={{0,6},{1,7},{2,4},{3,5},{4,2},{5,3},{6,0},{7,1},{8,14},{9,15},{10,... | collective-permute-start | bytes 6152 | tf_op jit(solution)/shard_map/ppermute | solution.py:270
  22.8 1.3 %collective-permute-done.8 = f32[2,256]{1,0:T(2,128)S(1)} collective-permute-done((f32[2,256]{1,0:T(2,128)S(1)}, f32[2,256]{1,0:T(2,128)S(1)}, u32[]{:S(2)}, u32[]{:S(2)}) %collective-permute-start.8) | collective-permute-done | bytes 2080 | tf_op jit(solution)/shard_map/ppermute | solution.py:270
  24.1 0.6 %columns.2 = f32[10,128]{1,0:T(8,128)S(1)} custom-call(f32[256,1024]{1,0:T(8,128)S(1)} %get-tuple-element.57.refs_0_, f32[256,1024]{1,0:T(8,128)S(1)} %get-tuple-element.58.refs_1_, f32[2,256]{1,0:T(2,128)S(1)} %log_add_fusion.refs_2_.lse_ref, f32[2,256]{1,0:T(2,128)S(1)} %get-tuple-element.73.refs_3_, f32[2,256]{1,0:T(2,128)S(1)} %get-tuple-element.72.refs_4_), custom_call_target="tpu_custom_call" | custom-call | flops 3145728 | bytes 1048576 | tf_op jit(solution)/shard_map/columns/pallas_call | solution.py:384
  24.7 1.3 %collective-permute-start.9 = (f32[10,128]{1,0:T(8,128)S(1)}, f32[10,128]{1,0:T(8,128)S(1)}, u32[]{:S(2)}, u32[]{:S(2)}) collective-permute-start(f32[10,128]{1,0:T(8,128)S(1)} %columns.2), channel_id=1, source_target_pairs={{0,4},{4,0},{8,12},{12,8},{1,5},{5,1},{9,13},{13,9},{2,6},{6,2},{1... | collective-permute-start | bytes 15368 | tf_op jit(solution)/shard_map/ppermute | solution.py:247
  26.0 0.6 %columns.3.own_ref = f32[8,128]{1,0:T(8,128)S(1)} custom-call(f32[256,1024]{1,0:T(8,128)S(1)} %get-tuple-element.53.refs_0_, f32[256,1024]{1,0:T(8,128)S(1)} %get-tuple-element.55.refs_1_, f32[2,256]{1,0:T(2,128)S(1)} %log_add_fusion.refs_2_.lse_ref, f32[2,256]{1,0:T(2,128)S(1)} %get-tuple-element.73.refs_3_, f32[2,256]{1,0:T(2,128)S(1)} %get-tuple-element.72.refs_4_), custom_call_target="tpu_custom_call" | custom-call | flops 3145728 | bytes 1048576 | tf_op jit(solution)/shard_map/columns/pallas_call | solution.py:384
  26.5 0.3 collective-permute-done.9.home_ref
  26.8 1.2 %results.1 = (f32[8,128]{1,0:T(8,128)}, f32[1,256]{1,0:T(1,128)}) custom-call(s32[2]{0:T(128)S(1)} %pad_add_fusion.word_ref, f32[8,128]{1,0:T(8,128)S(1)} %columns.3.own_ref, f32[10,128]{1,0:T(8,128)S(1)} %collective-permute-done.9.home_ref, f32[2,256]{1,0:T(2,128)S(1)} %log_add_fusion.refs_2_.lse_ref, f32[2,256]{1,0:T(2,128)S(1)} %get-tuple-element.43.line_ref, ...), custom_call_target="tpu_custom_call" | custom-call | tf_op jit(solution)/shard_map/results/pallas_call | solution.py:403
  (27 shorter events, 0.1 us)
Async XLA Ops:
  0.6 8.8 %collective-permute-start = (bf16[1024,512]{1,0:T(8,128)(2,1)}, bf16[1024,512]{1,0:T(8,128)(2,1)S(1)}, u32[]{:S(2)}, u32[]{:S(2)}) collective-permute-start(bf16[1024,512]{1,0:T(8,128)(2,1)} %refs_1_.3), channel_id=1, source_target_pairs={{0,4},{4,0},{8,12},{12,8},{1,5},{5,1},{9,13},{13,9},{2,6},{6,2},{1... | collective-permute-start | bytes 3145736 | tf_op jit(solution)/shard_map/ppermute | solution.py:247
  1.8 9.7 %collective-permute-start.2 = (bf16[256,512]{1,0:T(8,128)(2,1)}, bf16[256,512]{1,0:T(8,128)(2,1)S(1)}, u32[]{:S(2)}, u32[]{:S(2)}) collective-permute-start(bf16[256,512]{1,0:T(8,128)(2,1)} %own_rows_ref.1), channel_id=1, source_target_pairs={{0,8},{1,9},{2,14},{3,15},{4,12},{5,13},{6,10},{7,11},{8,0},{9,1},... | collective-permute-start | bytes 786440 | tf_op jit(solution)/shard_map/ppermute | solution.py:270
  7.4 0.8 %copy-start = (f32[1024,128]{1,0:T(8,128)}, f32[1024,128]{1,0:T(8,128)S(1)}, u32[]{:S(2)}) copy-start(f32[1024,128]{1,0:T(8,128)S(1)} %get-tuple-element.49.refs_2_) | copy-start | bytes 1572868
  8.2 1.2 %collective-permute-start.1 = (f32[1,1024]{1,0:T(1,128)S(1)}, f32[1,1024]{1,0:T(1,128)S(1)}, u32[]{:S(2)}, u32[]{:S(2)}) collective-permute-start(f32[1,1024]{1,0:T(1,128)S(1)} %get-tuple-element.41.own_offset_ref.refs_1_), channel_id=1, source_target_pairs={{0,4},{4,0},{8,12},{12,8},{1,5},{5,1},{9,13},{13,9},{2,6},{6,2},{1... | collective-permute-start | bytes 12296 | tf_op jit(solution)/shard_map/ppermute | solution.py:247
  8.6 3.9 %collective-permute-start.4 = (bf16[256,512]{1,0:T(8,128)(2,1)}, bf16[256,512]{1,0:T(8,128)(2,1)}, u32[]{:S(2)}, u32[]{:S(2)}) collective-permute-start(bf16[256,512]{1,0:T(8,128)(2,1)} %own_rows_ref.1), channel_id=1, source_target_pairs={{0,4},{4,0},{8,12},{12,8},{1,5},{5,1},{9,13},{13,9},{2,6},{6,2},{1... | collective-permute-start | bytes 786440 | tf_op jit(solution)/shard_map/ppermute | solution.py:247
  9.4 2.1 %copy-start.1 = (f32[1024,128]{1,0:T(8,128)S(1)}, f32[1024,128]{1,0:T(8,128)}, u32[]{:S(2)}) copy-start(f32[1024,128]{1,0:T(8,128)} %copy-done) | copy-start | bytes 1572868
  11.1 1.4 %collective-permute-start.3 = (f32[3,256]{1,0:T(4,128)S(1)}, f32[3,256]{1,0:T(4,128)S(1)}, u32[]{:S(2)}, u32[]{:S(2)}) collective-permute-start(f32[3,256]{1,0:T(4,128)S(1)} %get-tuple-element.46), channel_id=1, source_target_pairs={{0,4},{4,0},{8,12},{12,8},{1,5},{5,1},{9,13},{13,9},{2,6},{6,2},{1... | collective-permute-start | bytes 9224 | tf_op jit(solution)/shard_map/ppermute | solution.py:247
  12.5 5.9 %collective-permute-start.7 = (f32[4,256]{1,0:T(4,128)S(1)}, f32[4,256]{1,0:T(4,128)S(1)}, u32[]{:S(2)}, u32[]{:S(2)}) collective-permute-start(f32[4,256]{1,0:T(4,128)S(1)} %pad_maximum_fusion), channel_id=1, source_target_pairs={{0,9},{1,8},{2,11},{3,10},{4,13},{5,12},{6,15},{7,14},{8,1},{9,0},... | collective-permute-start | bytes 12296 | tf_op jit(solution)/shard_map/ppermute | solution.py:270
  14.1 4.4 %collective-permute-start.6 = (f32[4,256]{1,0:T(4,128)S(1)}, f32[4,256]{1,0:T(4,128)S(1)}, u32[]{:S(2)}, u32[]{:S(2)}) collective-permute-start(f32[4,256]{1,0:T(4,128)S(1)} %pad_maximum_fusion), channel_id=1, source_target_pairs={{0,1},{1,0},{2,3},{3,2},{4,5},{5,4},{6,7},{7,6},{8,9},{9,8},{10,11... | collective-permute-start | bytes 12296 | tf_op jit(solution)/shard_map/ppermute | solution.py:253
  14.4 4.0 %collective-permute-start.5 = (f32[4,256]{1,0:T(4,128)S(1)}, f32[4,256]{1,0:T(4,128)S(1)}, u32[]{:S(2)}, u32[]{:S(2)}) collective-permute-start(f32[4,256]{1,0:T(4,128)S(1)} %pad_maximum_fusion), channel_id=1, source_target_pairs={{0,8},{4,12},{8,0},{12,4},{1,9},{5,13},{9,1},{13,5},{2,10},{6,14},... | collective-permute-start | bytes 12296 | tf_op jit(solution)/shard_map/ppermute | solution.py:250
  18.5 5.6 %collective-permute-start.8 = (f32[2,256]{1,0:T(2,128)S(1)}, f32[2,256]{1,0:T(2,128)S(1)}, u32[]{:S(2)}, u32[]{:S(2)}) collective-permute-start(f32[2,256]{1,0:T(2,128)S(1)} %log_add_fusion.1), channel_id=1, source_target_pairs={{0,6},{1,7},{2,4},{3,5},{4,2},{5,3},{6,0},{7,1},{8,14},{9,15},{10,... | collective-permute-start | bytes 6152 | tf_op jit(solution)/shard_map/ppermute | solution.py:270
  24.7 2.1 %collective-permute-start.9 = (f32[10,128]{1,0:T(8,128)S(1)}, f32[10,128]{1,0:T(8,128)S(1)}, u32[]{:S(2)}, u32[]{:S(2)}) collective-permute-start(f32[10,128]{1,0:T(8,128)S(1)} %columns.2), channel_id=1, source_target_pairs={{0,4},{4,0},{8,12},{12,8},{1,5},{5,1},{9,13},{13,9},{2,6},{6,2},{1... | collective-permute-start | bytes 15368 | tf_op jit(solution)/shard_map/ppermute | solution.py:247
  26.0 0.8 %copy-start.2 = (f32[1024]{0:T(1024)S(1)}, f32[1024]{0:T(1024)}, u32[]{:S(2)}) copy-start(f32[1024]{0:T(1024)} %param.9) | copy-start | bytes 12292
  26.0 0.8 %copy-start.3 = (f32[1024]{0:T(1024)S(1)}, f32[1024]{0:T(1024)}, u32[]{:S(2)}) copy-start(f32[1024]{0:T(1024)} %param.11) | copy-start | bytes 12292
  26.0 0.8 %copy-start.4 = (f32[1024]{0:T(1024)S(1)}, f32[1024]{0:T(1024)}, u32[]{:S(2)}) copy-start(f32[1024]{0:T(1024)} %param.13) | copy-start | bytes 12292

commit v15 on v13

--- a/solution.py
+++ b/solution.py
@@ -54,31 +54,26 @@
         part = sides[side][0][at : at + PIECE, :]
         z_ref[index % 2] = lax.dot_general(part, rows, NT_DIMS, preferred_element_type=jnp.float32)
 
-    def absorb(index, state):
+    peaks, masses = [], []
+
+    def absorb(index):
         side, at = pieces[index]
         for inner in range(0, PIECE, LANES):
             offset = sides[side][1][at + inner : at + inner + LANES, :]
             offset = jnp.concatenate([offset] * (rows.shape[0] // LANES), axis=1)
             z = z_ref[index % 2, inner : inner + LANES, :] * LOG2_E + offset
             z = z.reshape(LANES // 8, 8, rows.shape[0])
-            high = jnp.max(z, axis=0)
-            peak = high if state is None else jnp.maximum(state[0], high)
-            mass = jnp.sum(jnp.exp2(z - peak), axis=0)
-            if state is not None:
-                mass = mass + state[1] * jnp.exp2(state[0] - peak)
-            state = (peak, mass)
-        return state
-
-    state = None
+            peaks.append(jnp.max(z, axis=0))
+            masses.append(jnp.sum(jnp.exp2(z - peaks[-1]), axis=0))
+
     product(0)
     for index in range(len(pieces)):
         if index + 1 < len(pieces):
             product(index + 1)
-        state = absorb(index, state)
-    high, mass = state
-    peak = jnp.max(high, axis=0, keepdims=True)
-    mass = jnp.sum(mass * jnp.exp2(high - peak), axis=0, keepdims=True)
-    return peak * LOG_2 + jnp.log(mass)
+        absorb(index)
+    peak = jnp.max(functools.reduce(jnp.maximum, peaks), axis=0, keepdims=True)
+    mass = sum(mass * jnp.exp2(high - peak) for high, mass in zip(peaks, masses))
+    return peak * LOG_2 + jnp.log(jnp.sum(mass, axis=0, keepdims=True))
 
 
 def put_offsets(offset_ref, column_ref, eye):
@@ -157,16 +152,21 @@
 
 def far_kernel(count, *refs):
     own_ref, own_column_ref, pair_ref, pair_column_ref, held_ref, line_ref = refs[count : count + 6]
-    out_ref, z_ref = refs[count + 6 :]
+    out_ref, mirrored_ref, z_ref = refs[count + 6 :]
     slots = count + 1
-    out_ref[0:1, :] = held_ref[...]
-    out_ref[slots : slots + 2, :] = line_ref[...]
-    for slot in range(count):
-        sides = ((own_ref, own_column_ref), (pair_ref, pair_column_ref))
-        out_ref[slot + 1 : slot + 2, :] = row_sums(refs[slot][...], sides, z_ref)
-
-
-def sum_columns(z_refs, offset, off_ref, out_ref):
+    for ref in (out_ref, mirrored_ref):
+        ref[slots : slots + 2, :] = line_ref[...]
+    for slot in range(slots):
+        if slot == 0:
+            lse = held_ref[...]
+        else:
+            sides = ((own_ref, own_column_ref), (pair_ref, pair_column_ref))
+            lse = row_sums(refs[slot - 1][...], sides, z_ref)
+        out_ref[slot : slot + 1, :] = lse
+        mirrored_ref[slot ^ 1 : (slot ^ 1) + 1, :] = lse
+
+
+def sum_columns(z_refs, offset, out_ref, off_ref, peak_ref, mass_ref):
     eye = diagonal()
     slots, src_count = offset.shape
     for slot in range(slots):
@@ -176,27 +176,40 @@
 
     for group in range(out_ref.shape[0]):
         cols = slice(group * LANES, (group + 1) * LANES)
-        peaks, masses = [], []
         for slot in range(slots):
             z = (z_refs[slot][:, cols] + off_ref[slot]).reshape(src_count // 8, 8, LANES)
-            peaks.append(jnp.max(z, axis=0))
-            masses.append(jnp.sum(jnp.exp2(z - peaks[-1]), axis=0))
-        peak = jnp.max(functools.reduce(jnp.maximum, peaks), axis=0, keepdims=True)
-        mass = sum(mass * jnp.exp2(high - peak) for high, mass in zip(peaks, masses))
-        mass = jnp.sum(mass, axis=0, keepdims=True)
-        out_ref[group : group + 1, :] = peak * LOG_2 + jnp.log(mass)
+            peak = jnp.max(z, axis=0)
+            peak_ref[slot, :, cols] = peak
+            mass_ref[slot, :, cols] = jnp.sum(jnp.exp2(z - peak), axis=0)
+    peak = jnp.max(functools.reduce(jnp.maximum, [peak_ref[slot] for slot in range(slots)]), axis=0, keepdims=True)
+    mass = sum(mass_ref[slot] * jnp.exp2(peak_ref[slot] - peak) for slot in range(slots))
+    total = peak * LOG_2 + jnp.log(jnp.sum(mass, axis=0, keepdims=True))
+    for group in range(out_ref.shape[0]):
+        out_ref[group : group + 1, :] = total[:, group * LANES : (group + 1) * LANES]
 
 
 def pair_kernel(slots, *refs):
-    lse_ref, slope_ref, shift_ref, out_ref, off_ref = refs[slots:]
-    sum_columns(refs[:slots], shift_ref[...] - slope_ref[...] * lse_ref[...], off_ref, out_ref)
-
-
-def own_kernel(slots, *refs):
-    lse_ref, slope_ref, shift_ref, sum_ref, out_ref, potential_ref, off_ref = refs[slots:]
-    lse, slope = lse_ref[...], slope_ref[...]
-    potential_ref[...] = slope[0:1, :] * (sum_ref[...] - lse[0:1, :])
-    sum_columns(refs[:slots], shift_ref[...] - slope * lse, off_ref, out_ref)
+    lse_ref, slope_ref, shift_ref, out_ref, *scratch = refs[slots:]
+    sum_columns(refs[:slots], shift_ref[...] - slope_ref[...] * lse_ref[...], out_ref, *scratch)
+
+
+def own_kernel(turn, slots, *refs):
+    z_refs, (lse_ref, slope_ref, shift_ref, core_ref), refs = refs[:slots], refs[slots : slots + 4], refs[slots + 4 :]
+    if turn == 0:
+        sum_ref, earlier_ref, out_ref, potential_ref, *scratch = refs
+        potential_ref[...] = slope_ref[0:1, :] * (sum_ref[...] - lse_ref[0:1, :])
+    else:
+        out_ref, *scratch = refs
+
+    @pl.when(core_ref[0] == turn)
+    def work():
+        sum_columns(z_refs, shift_ref[...] - slope_ref[...] * lse_ref[...], out_ref, *scratch)
+
+    if turn == 0:
+
+        @pl.when(core_ref[0] != turn)
+        def hand_on():
+            out_ref[...] = earlier_ref[...]
 
 
 def f32(*shape):
@@ -284,18 +297,18 @@
     )(sources, pair_targets, pair_offset, lse)
     far_lines = [across(line, chip) for chip in range(2, chips)]
     lse, *moved = lax.optimization_barrier((lse, *far_blocks, *far_lines))
-    payload = pl.pallas_call(
+    payload, mirrored = pl.pallas_call(
         functools.partial(far_kernel, far),
-        out_shape=f32(chips + 2, src_count),
+        out_shape=(f32(chips + 2, src_count),) * 2,
         in_specs=[VMEM] * (far + 6),
-        out_specs=VMEM,
+        out_specs=(VMEM,) * 2,
         scratch_shapes=[product_space],
         compiler_params=params(12 + far),
         cost_estimate=cost(2 * far),
         name="far_rows",
     )(*moved[:far], held, column, pair_targets, pair_column, lse, line)
 
-    payload, *blocks = lax.optimization_barrier((payload, sources, *moved[:far]))
+    payload, mirrored, *blocks = lax.optimization_barrier((payload, mirrored, sources, *moved[:far]))
     def logits(block, *sides):
         return pl.pallas_call(
             functools.partial(logits_kernel, len(sides) // 2),
@@ -313,35 +326,36 @@
         own_zs.append(own_z)
         pair_zs.append(pair_z)
 
-    def mirror(value, chip):
-        return jnp.stack([value[slot ^ chip] for slot in range(chips)])
-
-    other = across(payload, 1)
-    beside = along(payload, 1)
     joined = lax.ppermute(
-        payload,
+        mirrored,
         ("blk", "tsplit"),
         [(b * sets + z, (b ^ 2) * sets + (z ^ 1)) for b in range(slabs) for z in range(sets)],
     )
-    lines = jnp.stack([line, other[chips:]] + moved[far:], axis=1)
-    lse = merge(payload[:chips], mirror(other, 1), beside[:chips], mirror(joined, 1))
+    other = across(mirrored, 1)
+    beside = along(payload, 1)
+    lines = jnp.stack([line, joined[chips:]] + moved[far:], axis=1)
+    lse = merge(payload[:chips], other[:chips], beside[:chips], joined[:chips])
     chip = 2
     while chip < chips:
-        lse = merge(lse, mirror(across(lse, chip), chip))
+        there = across(lse, chip)
+        lse = merge(lse, jnp.stack([there[slot ^ chip] for slot in range(chips)]))
         chip *= 2
     step = 2
     while step < sets:
         lse = merge(lse, along(lse, step))
         step *= 2
 
-    def columns(kernel, zs, *more):
-        outs = (f32(groups, LANES), f32(1, src_count))[: 1 + len(more)]
+    def columns(kernel, zs, *more, outs=(f32(groups, LANES),)):
         return pl.pallas_call(
-            functools.partial(kernel, chips),
+            kernel,
             out_shape=outs,
-            in_specs=[VMEM] * (chips + 3 + len(more)),
+            in_specs=[VMEM] * (chips + 3) + [SMEM] * min(1, len(more)) + [VMEM] * (len(more) - 1),
             out_specs=(VMEM,) * len(outs),
-            scratch_shapes=[pltpu.VMEM((chips, src_count, LANES), jnp.float32)],
+            scratch_shapes=[
+                pltpu.VMEM((chips, src_count, LANES), jnp.float32),
+                pltpu.VMEM((chips, 8, tgt_count), jnp.float32),
+                pltpu.VMEM((chips, 8, tgt_count), jnp.float32),
+            ],
             compiler_params=params(8 + 2 * chips),
             cost_estimate=pl.CostEstimate(
                 flops=6 * chips * src_count * tgt_count,
@@ -351,10 +365,18 @@
             name="columns",
         )(*zs, lse, lines[0], lines[1], *more)
 
-    (pair_part,) = columns(pair_kernel, pair_zs)
-    lse, pair_part = lax.optimization_barrier((lse, pair_part))
+    (pair_part,) = columns(functools.partial(pair_kernel, chips), pair_zs)
+    (early_part,) = columns(functools.partial(own_kernel, 1, chips), own_zs, core_word)
+    lse, pair_part, early_part = lax.optimization_barrier((lse, pair_part, early_part))
     home = pair(pair_part)
-    own_part, src_potential = columns(own_kernel, own_zs, src_sum)
+    own_part, src_potential = columns(
+        functools.partial(own_kernel, 0, chips),
+        own_zs,
+        core_word,
+        src_sum,
+        early_part,
+        outs=(f32(groups, LANES), f32(1, src_count)),
+    )
     total = merge(own_part, home).reshape(tgt_count)
     tgt_update = tgt_exponent * (2.0 * tgt_logmass + tgt_potential - total)
     return (src_potential.reshape(src_count), tgt_update)

time: 24.6 us -> 24.6 us (level)
    ppermute x2, starting transfers between devices: 2.8 us -> 4.77 us  [across(): return lax.ppermute(value, 'blk', [(i, i ^ 2 * chip) for i in range(slabs)])]
    ppermute x1, starting transfers between devices: 3.18 us -> 1.51 us  [shards(): lax.ppermute(mirrored, ('blk', 'tsplit'), [(b * sets + z, (b ^ 2) * sets...]
    ppermute x2, waiting for transfers between devices: 1.88 us -> 3.24 us  [along(): return lax.ppermute(value, 'tsplit', [(i, i ^ step) for i in range(sets)])]
    ppermute x2, waiting for transfers between devices: 1.2 us -> 0.01 us  [across(): return lax.ppermute(value, 'blk', [(i, i ^ 2 * chip) for i in range(slabs)])]
    ppermute x2, starting transfers between devices: 3.1 us -> 2.71 us  [along(): return lax.ppermute(value, 'tsplit', [(i, i ^ step) for i in range(sets)])]
    pallas_call x3 -> x4, Pallas kernels: 2.6 us -> 2.64 us  [the longest x3 1.66 us: columns(): pl.pallas_call(kernel, out_shape=outs, in_specs=[VMEM] * (chips + 3) + [S...]
  transfers between devices with their start and end apart: 8 -> 8, of which waited for: 4 -> 3; matrix products, arithmetic and copies ran while one was open for 0% -> 0% of each run, Pallas kernels for 30% -> 30%
where the time goes in v15:
time: 24.6 us; the launch traced here: 24.4 us
  starting transfers between devices  10 us (41%)
  Pallas kernels  8.89 us (36%)
  waiting for transfers between devices  4.07 us (17%)
  between operations  0.76 us (3%)
  other arithmetic  0.66 us (3%)
    ppermute x2, starting transfers between devices, across(): return lax.ppermute(value, 'blk', [(i, i ^ 2 * chip) for i in range(slabs)])  4.77 us
    ppermute x2, waiting for transfers between devices, along(): return lax.ppermute(value, 'tsplit', [(i, i ^ step) for i in range(sets)])  3.24 us
    ppermute x2, starting transfers between devices, along(): return lax.ppermute(value, 'tsplit', [(i, i ^ step) for i in range(sets)])  2.71 us
    pallas_call x2, Pallas kernels, prepare_on(): pl.pallas_call(functools.partial(prepare_kernel, turn), out_shape=(jax.Sh...  2.49 us
    pallas_call x2, Pallas kernels, logits(): pl.pallas_call(functools.partial(logits_kernel, len(sides) // 2), out_sha...  2.17 us
    pallas_call x3, Pallas kernels, columns(): pl.pallas_call(kernel, out_shape=outs, in_specs=[VMEM] * (chips + 3) + [S...  1.66 us
    pallas_call x1, Pallas kernels, shards(): pl.pallas_call(near_kernel, out_shape=(f32(tgt_count, LANES), f32(1, src_...  1.59 us
    ppermute x1, starting transfers between devices, shards(): lax.ppermute(mirrored, ('blk', 'tsplit'), [(b * sets + z, (b ^ 2) * sets...  1.51 us
  transfers between devices with their start and end apart: 8, of which 3 were waited for; matrix products, arithmetic and copies ran while one was open for 0% of the time, Pallas kernels for 30%

profile of v15, /device:TPU:0, one launch (start us, length us, event | category | flops | bytes accessed | tf_op | source)
XLA Modules:
  0.0 24.4 jit_solution(15192201326065835595)
XLA Ops:
  0.6 0.5 %collective-permute-start = (bf16[1024,512]{1,0:T(8,128)(2,1)}, bf16[1024,512]{1,0:T(8,128)(2,1)S(1)}, u32[]{:S(2)}, u32[]{:S(2)}) collective-permute-start(bf16[1024,512]{1,0:T(8,128)(2,1)} %refs_1_.3), channel_id=1, source_target_pairs={{0,4},{4,0},{8,12},{12,8},{1,5},{5,1},{9,13},{13,9},{2,6},{6,2},{1... | collective-permute-start | bytes 3145736 | tf_op jit(solution)/shard_map/ppermute | solution.py:235
  1.1 0.1 prepare_1.1
  1.2 2.6 %collective-permute-start.2 = (bf16[256,512]{1,0:T(8,128)(2,1)}, bf16[256,512]{1,0:T(8,128)(2,1)S(1)}, u32[]{:S(2)}, u32[]{:S(2)}) collective-permute-start(bf16[256,512]{1,0:T(8,128)(2,1)} %rows_ref.2), channel_id=1, source_target_pairs={{0,8},{4,12},{8,0},{12,4},{1,9},{5,13},{9,1},{13,5},{2,10},{6,14},... | collective-permute-start | bytes 786440 | tf_op jit(solution)/shard_map/ppermute | solution.py:238
  3.8 2.4 %prepare_0.1 = (bf16[1024,512]{1,0:T(8,128)(2,1)S(1)}, f32[1,1024]{1,0:T(1,128)S(1)}, f32[1024,128]{1,0:T(8,128)S(1)}, f32[256,1024]{1,0:T(8,128)S(1)}, f32[1,25...) custom-call(s32[1]{0:T(128)} %bitcast.core_ref.refs_5_, bf16[256,512]{1,0:T(8,128)(2,1)} %rows_ref.2, ...), custom_call_target="tpu_custom_call" | custom-call | flops 268435456 | bytes 1048576 | tf_op jit(solution)/shard_map/prepare_0/pallas_call | solution.py:263
  6.3 0.4 %collective-permute-start.1 = (f32[1,1024]{1,0:T(1,128)S(1)}, f32[1,1024]{1,0:T(1,128)S(1)}, u32[]{:S(2)}, u32[]{:S(2)}) collective-permute-start(f32[1,1024]{1,0:T(1,128)S(1)} %get-tuple-element.44.refs_1_), channel_id=1, source_target_pairs={{0,4},{4,0},{8,12},{12,8},{1,5},{5,1},{9,13},{13,9},{2,6},{6,2},{1... | collective-permute-start | bytes 12296 | tf_op jit(solution)/shard_map/ppermute | solution.py:235
  6.7 0.8 %collective-permute-done.1.offset_ref.refs_3_.refs_1_ = f32[1,1024]{1,0:T(1,128)S(1)} collective-permute-done((f32[1,1024]{1,0:T(1,128)S(1)}, f32[1,1024]{1,0:T(1,128)S(1)}, u32[]{:S(2)}, u32[]{:S(2)}) %collective-permute-start.1) | collective-permute-done | bytes 4128 | tf_op jit(solution)/shard_map/ppermute | solution.py:235
  7.5 0.0 collective-permute-done.tgt_ref.refs_3_.refs_2_.refs_0_
  7.5 1.6 %near_rows.1 = (f32[1024,128]{1,0:T(8,128)S(1)}, f32[1,256]{1,0:T(1,128)S(1)}) custom-call(bf16[256,512]{1,0:T(8,128)(2,1)} %rows_ref.2, bf16[1024,512]{1,0:T(8,128)(2,1)S(1)} %collective-permute-done.tgt_ref.refs_3_.refs_2_.refs_0_, f32[1,1024]{1,0:T(1,128)S(1)} %collective-permute-done.1.offset_ref.refs_3_.refs_1_, f32[1,256]{1,0:T(1,128)S(1)} %get-tuple-element.45.held_ref), custom_call_target="tpu_custom_call" | custom-call | flops 268435456 | bytes 1048576 | tf_op jit(solution)/shard_map/near_rows/pallas_call | solution.py:288
  9.1 1.0 %far_rows.1 = (f32[4,256]{1,0:T(4,128)S(1)}, f32[4,256]{1,0:T(4,128)S(1)}) custom-call(bf16[256,512]{1,0:T(8,128)(2,1)S(1)} %collective-permute-done.2.refs_0_.rows_ref, bf16[1024,512]{1,0:T(8,128)(2,1)S(1)} %get-tuple-element.49.refs_1_.refs_0_, f32[1024,128]{1,0:T(8,128)S(1)} %get-tuple-element.50.refs_2_, ...), custom_call_target="tpu_custom_call" | custom-call | flops 536870912 | bytes 1048576 | tf_op jit(solution)/shard_map/far_rows/pallas_call | solution.py:300
  10.1 2.2 %collective-permute-start.3 = (f32[4,256]{1,0:T(4,128)S(1)}, f32[4,256]{1,0:T(4,128)S(1)}, u32[]{:S(2)}, u32[]{:S(2)}) collective-permute-start(f32[4,256]{1,0:T(4,128)S(1)} %get-tuple-element.59), channel_id=1, source_target_pairs={{0,8},{4,12},{8,0},{12,4},{1,9},{5,13},{9,1},{13,5},{2,10},{6,14},... | collective-permute-start | bytes 12296 | tf_op jit(solution)/shard_map/ppermute | solution.py:238
  12.3 1.5 %collective-permute-start.5 = (f32[4,256]{1,0:T(4,128)S(1)}, f32[4,256]{1,0:T(4,128)S(1)}, u32[]{:S(2)}, u32[]{:S(2)}) collective-permute-start(f32[4,256]{1,0:T(4,128)S(1)} %get-tuple-element.59), channel_id=1, source_target_pairs={{0,9},{1,8},{2,11},{3,10},{4,13},{5,12},{6,15},{7,14},{8,1},{9,0},... | collective-permute-start | bytes 12296 | tf_op jit(solution)/shard_map/ppermute | solution.py:329
  13.8 0.1 collective-permute-start.4
  13.9 0.7 %logits.2 = (f32[256,1024]{1,0:T(8,128)S(1)}, f32[256,1024]{1,0:T(8,128)S(1)}) custom-call(bf16[256,512]{1,0:T(8,128)(2,1)S(1)} %collective-permute-done.2.refs_0_.rows_ref, bf16[1024,512]{1,0:T(8,128)(2,1)S(1)} %get-tuple-element.49.refs_1_.refs_0_, f32[1,1024]{1,0:T(1,128)S(1)} %get-tuple-element.44.refs_1_, ...), custom_call_target="tpu_custom_call" | custom-call | flops 536870912 | bytes 1048576 | tf_op jit(solution)/shard_map/logits/pallas_call | solution.py:313
  14.6 1.4 %logits.3.refs_0_ = f32[256,1024]{1,0:T(8,128)S(1)} custom-call(bf16[256,512]{1,0:T(8,128)(2,1)} %rows_ref.2, bf16[1024,512]{1,0:T(8,128)(2,1)S(1)} %collective-permute-done.tgt_ref.refs_3_.refs_2_.refs_0_, f32[1,1024]{1,0:T(1,128)S(1)} %collective-permute-done.1.offset_ref.refs_3_.refs_1_), custom_call_target="tpu_custom_call" | custom-call | flops 268435456 | bytes 1048576 | tf_op jit(solution)/shard_map/logits/pallas_call | solution.py:313
  16.1 1.3 %collective-permute-done.4 = f32[4,256]{1,0:T(4,128)S(1)} collective-permute-done((f32[4,256]{1,0:T(4,128)S(1)}, f32[4,256]{1,0:T(4,128)S(1)}, u32[]{:S(2)}, u32[]{:S(2)}) %collective-permute-start.4) | collective-permute-done | bytes 4128 | tf_op jit(solution)/shard_map/ppermute | solution.py:241
  17.4 2.6 %collective-permute-start.6 = (f32[2,256]{1,0:T(2,128)S(1)}, f32[2,256]{1,0:T(2,128)S(1)}, u32[]{:S(2)}, u32[]{:S(2)}) collective-permute-start(f32[2,256]{1,0:T(2,128)S(1)} %get-tuple-element.71), channel_id=1, source_target_pairs={{0,2},{1,3},{2,0},{3,1},{4,6},{5,7},{6,4},{7,5},{8,10},{9,11},{10,... | collective-permute-start | bytes 6152 | tf_op jit(solution)/shard_map/ppermute | solution.py:241
  20.1 1.9 %collective-permute-done.6 = f32[2,256]{1,0:T(2,128)S(1)} collective-permute-done((f32[2,256]{1,0:T(2,128)S(1)}, f32[2,256]{1,0:T(2,128)S(1)}, u32[]{:S(2)}, u32[]{:S(2)}) %collective-permute-start.6) | collective-permute-done | bytes 2080 | tf_op jit(solution)/shard_map/ppermute | solution.py:241
  22.0 0.5 %columns.3 = f32[8,128]{1,0:T(8,128)S(1)} custom-call(f32[256,1024]{1,0:T(8,128)S(1)} %logits.3.refs_0_, f32[256,1024]{1,0:T(8,128)S(1)} %get-tuple-element.61.refs_1_, f32[2,256]{1,0:T(2,128)S(1)} %log_add_fusion.refs_2_, f32[2,256]{1,0:T(2,128)S(1)} %get-tuple-element.69.refs_3_, f32[2,256]{1,0:T(2,128)S(1)} %get-tuple-element.68.refs_4_), custom_call_target="tpu_custom_call" | custom-call | flops 3145728 | bytes 1048576 | tf_op jit(solution)/shard_map/columns/pallas_call | solution.py:349
  22.6 0.1 collective-permute-start.7
  22.6 0.0 copy-start
  22.7 0.0 copy-start.1
  22.7 0.0 copy-start.2
  22.7 1.1 %columns.5 = (f32[8,128]{1,0:T(8,128)S(1)}, f32[1,256]{1,0:T(1,128)}) custom-call(f32[256,1024]{1,0:T(8,128)S(1)} %get-tuple-element.43.refs_0_, f32[256,1024]{1,0:T(8,128)S(1)} %get-tuple-element.57.refs_1_, f32[2,256]{1,0:T(2,128)S(1)} %log_add_fusion.refs_2_, f32[2,256]{1,0:T(2,128)S(1)} %get-tuple-element.69.refs_3_, ...), custom_call_target="tpu_custom_call" | custom-call | flops 3145728 | bytes 1048576 | tf_op jit(solution)/shard_map/columns/pallas_call | solution.py:349
  23.8 0.6 %fusion = f32[1024]{0:T(1024)} fusion(f32[1024]{0:T(1024)S(1)} %copy-done.2, f32[8,128]{1,0:T(8,128)S(1)} %collective-permute-done.7, f32[8,128]{1,0:T(8,128)S(1)} %get-tuple-element.66, f32[1024]{0:T(1024)S(1)} %copy-done, f32[1024]{0:T(1024)S(1)} %copy-done.1), kind=kLoop, calls=%fused_computation.3 | loop fusion | flops 9216 | bytes 24576 | tf_op jit(solution)/shard_map/mul | solution.py:381
  (13 shorter events, 0.1 us)
Async XLA Ops:
  0.6 6.9 %collective-permute-start = (bf16[1024,512]{1,0:T(8,128)(2,1)}, bf16[1024,512]{1,0:T(8,128)(2,1)S(1)}, u32[]{:S(2)}, u32[]{:S(2)}) collective-permute-start(bf16[1024,512]{1,0:T(8,128)(2,1)} %refs_1_.3), channel_id=1, source_target_pairs={{0,4},{4,0},{8,12},{12,8},{1,5},{5,1},{9,13},{13,9},{2,6},{6,2},{1... | collective-permute-start | bytes 3145736 | tf_op jit(solution)/shard_map/ppermute | solution.py:235
  1.2 7.9 %collective-permute-start.2 = (bf16[256,512]{1,0:T(8,128)(2,1)}, bf16[256,512]{1,0:T(8,128)(2,1)S(1)}, u32[]{:S(2)}, u32[]{:S(2)}) collective-permute-start(bf16[256,512]{1,0:T(8,128)(2,1)} %rows_ref.2), channel_id=1, source_target_pairs={{0,8},{4,12},{8,0},{12,4},{1,9},{5,13},{9,1},{13,5},{2,10},{6,14},... | collective-permute-start | bytes 786440 | tf_op jit(solution)/shard_map/ppermute | solution.py:238
  6.3 1.3 %collective-permute-start.1 = (f32[1,1024]{1,0:T(1,128)S(1)}, f32[1,1024]{1,0:T(1,128)S(1)}, u32[]{:S(2)}, u32[]{:S(2)}) collective-permute-start(f32[1,1024]{1,0:T(1,128)S(1)} %get-tuple-element.44.refs_1_), channel_id=1, source_target_pairs={{0,4},{4,0},{8,12},{12,8},{1,5},{5,1},{9,13},{13,9},{2,6},{6,2},{1... | collective-permute-start | bytes 12296 | tf_op jit(solution)/shard_map/ppermute | solution.py:235
  10.1 5.9 %collective-permute-start.3 = (f32[4,256]{1,0:T(4,128)S(1)}, f32[4,256]{1,0:T(4,128)S(1)}, u32[]{:S(2)}, u32[]{:S(2)}) collective-permute-start(f32[4,256]{1,0:T(4,128)S(1)} %get-tuple-element.59), channel_id=1, source_target_pairs={{0,8},{4,12},{8,0},{12,4},{1,9},{5,13},{9,1},{13,5},{2,10},{6,14},... | collective-permute-start | bytes 12296 | tf_op jit(solution)/shard_map/ppermute | solution.py:238
  12.3 5.1 %collective-permute-start.5 = (f32[4,256]{1,0:T(4,128)S(1)}, f32[4,256]{1,0:T(4,128)S(1)}, u32[]{:S(2)}, u32[]{:S(2)}) collective-permute-start(f32[4,256]{1,0:T(4,128)S(1)} %get-tuple-element.59), channel_id=1, source_target_pairs={{0,9},{1,8},{2,11},{3,10},{4,13},{5,12},{6,15},{7,14},{8,1},{9,0},... | collective-permute-start | bytes 12296 | tf_op jit(solution)/shard_map/ppermute | solution.py:329
  13.8 3.6 %collective-permute-start.4 = (f32[4,256]{1,0:T(4,128)S(1)}, f32[4,256]{1,0:T(4,128)S(1)}, u32[]{:S(2)}, u32[]{:S(2)}) collective-permute-start(f32[4,256]{1,0:T(4,128)S(1)} %get-tuple-element.58), channel_id=1, source_target_pairs={{0,1},{1,0},{2,3},{3,2},{4,5},{5,4},{6,7},{7,6},{8,9},{9,8},{10,11... | collective-permute-start | bytes 12296 | tf_op jit(solution)/shard_map/ppermute | solution.py:241
  17.4 4.5 %collective-permute-start.6 = (f32[2,256]{1,0:T(2,128)S(1)}, f32[2,256]{1,0:T(2,128)S(1)}, u32[]{:S(2)}, u32[]{:S(2)}) collective-permute-start(f32[2,256]{1,0:T(2,128)S(1)} %get-tuple-element.71), channel_id=1, source_target_pairs={{0,2},{1,3},{2,0},{3,1},{4,6},{5,7},{6,4},{7,5},{8,10},{9,11},{10,... | collective-permute-start | bytes 6152 | tf_op jit(solution)/shard_map/ppermute | solution.py:241
  22.6 1.2 %collective-permute-start.7 = (f32[8,128]{1,0:T(8,128)S(1)}, f32[8,128]{1,0:T(8,128)S(1)}, u32[]{:S(2)}, u32[]{:S(2)}) collective-permute-start(f32[8,128]{1,0:T(8,128)S(1)} %columns.3), channel_id=1, source_target_pairs={{0,4},{4,0},{8,12},{12,8},{1,5},{5,1},{9,13},{13,9},{2,6},{6,2},{1... | collective-permute-start | bytes 12296 | tf_op jit(solution)/shard_map/ppermute | solution.py:235
  22.6 1.2 %copy-start = (f32[1024]{0:T(1024)S(1)}, f32[1024]{0:T(1024)}, u32[]{:S(2)}) copy-start(f32[1024]{0:T(1024)} %param.9) | copy-start | bytes 12292
  22.7 1.2 %copy-start.1 = (f32[1024]{0:T(1024)S(1)}, f32[1024]{0:T(1024)}, u32[]{:S(2)}) copy-start(f32[1024]{0:T(1024)} %param.11) | copy-start | bytes 12292
  22.7 1.2 %copy-start.2 = (f32[1024]{0:T(1024)S(1)}, f32[1024]{0:T(1024)}, u32[]{:S(2)}) copy-start(f32[1024]{0:T(1024)} %param.13) | copy-start | bytes 12292

commit v16 on v13

--- a/solution.py
+++ b/solution.py
@@ -14,7 +14,7 @@
 LOG_2 = math.log(2.0)
 LANES = 128
 CHUNK = 256
-PIECE = 512
+PIECE = 1024
 VMEM = pl.BlockSpec(memory_space=pltpu.VMEM)
 SMEM = pl.BlockSpec(memory_space=pltpu.SMEM)
 HBM = pl.BlockSpec(memory_space=pltpu.HBM)
@@ -54,31 +54,26 @@
         part = sides[side][0][at : at + PIECE, :]
         z_ref[index % 2] = lax.dot_general(part, rows, NT_DIMS, preferred_element_type=jnp.float32)
 
-    def absorb(index, state):
+    peaks, masses = [], []
+
+    def absorb(index):
         side, at = pieces[index]
         for inner in range(0, PIECE, LANES):
             offset = sides[side][1][at + inner : at + inner + LANES, :]
             offset = jnp.concatenate([offset] * (rows.shape[0] // LANES), axis=1)
             z = z_ref[index % 2, inner : inner + LANES, :] * LOG2_E + offset
             z = z.reshape(LANES // 8, 8, rows.shape[0])
-            high = jnp.max(z, axis=0)
-            peak = high if state is None else jnp.maximum(state[0], high)
-            mass = jnp.sum(jnp.exp2(z - peak), axis=0)
-            if state is not None:
-                mass = mass + state[1] * jnp.exp2(state[0] - peak)
-            state = (peak, mass)
-        return state
-
-    state = None
+            peaks.append(jnp.max(z, axis=0))
+            masses.append(jnp.sum(jnp.exp2(z - peaks[-1]), axis=0))
+
     product(0)
     for index in range(len(pieces)):
         if index + 1 < len(pieces):
             product(index + 1)
-        state = absorb(index, state)
-    high, mass = state
-    peak = jnp.max(high, axis=0, keepdims=True)
-    mass = jnp.sum(mass * jnp.exp2(high - peak), axis=0, keepdims=True)
-    return peak * LOG_2 + jnp.log(mass)
+        absorb(index)
+    peak = jnp.max(functools.reduce(jnp.maximum, peaks), axis=0, keepdims=True)
+    mass = sum(mass * jnp.exp2(high - peak) for high, mass in zip(peaks, masses))
+    return peak * LOG_2 + jnp.log(jnp.sum(mass, axis=0, keepdims=True))
 
 
 def put_offsets(offset_ref, column_ref, eye):
@@ -166,7 +161,7 @@
         out_ref[slot + 1 : slot + 2, :] = row_sums(refs[slot][...], sides, z_ref)
 
 
-def sum_columns(z_refs, offset, off_ref, out_ref):
+def sum_columns(z_refs, offset, out_ref, off_ref, peak_ref, mass_ref):
     eye = diagonal()
     slots, src_count = offset.shape
     for slot in range(slots):
@@ -176,27 +171,28 @@
 
     for group in range(out_ref.shape[0]):
         cols = slice(group * LANES, (group + 1) * LANES)
-        peaks, masses = [], []
         for slot in range(slots):
             z = (z_refs[slot][:, cols] + off_ref[slot]).reshape(src_count // 8, 8, LANES)
-            peaks.append(jnp.max(z, axis=0))
-            masses.append(jnp.sum(jnp.exp2(z - peaks[-1]), axis=0))
-        peak = jnp.max(functools.reduce(jnp.maximum, peaks), axis=0, keepdims=True)
-        mass = sum(mass * jnp.exp2(high - peak) for high, mass in zip(peaks, masses))
-        mass = jnp.sum(mass, axis=0, keepdims=True)
-        out_ref[group : group + 1, :] = peak * LOG_2 + jnp.log(mass)
+            peak = jnp.max(z, axis=0)
+            peak_ref[slot, :, cols] = peak
+            mass_ref[slot, :, cols] = jnp.sum(jnp.exp2(z - peak), axis=0)
+    peak = jnp.max(functools.reduce(jnp.maximum, [peak_ref[slot] for slot in range(slots)]), axis=0, keepdims=True)
+    mass = sum(mass_ref[slot] * jnp.exp2(peak_ref[slot] - peak) for slot in range(slots))
+    total = peak * LOG_2 + jnp.log(jnp.sum(mass, axis=0, keepdims=True))
+    for group in range(out_ref.shape[0]):
+        out_ref[group : group + 1, :] = total[:, group * LANES : (group + 1) * LANES]
 
 
 def pair_kernel(slots, *refs):
-    lse_ref, slope_ref, shift_ref, out_ref, off_ref = refs[slots:]
-    sum_columns(refs[:slots], shift_ref[...] - slope_ref[...] * lse_ref[...], off_ref, out_ref)
+    lse_ref, slope_ref, shift_ref, out_ref, *scratch = refs[slots:]
+    sum_columns(refs[:slots], shift_ref[...] - slope_ref[...] * lse_ref[...], out_ref, *scratch)
 
 
 def own_kernel(slots, *refs):
-    lse_ref, slope_ref, shift_ref, sum_ref, out_ref, potential_ref, off_ref = refs[slots:]
+    lse_ref, slope_ref, shift_ref, sum_ref, out_ref, potential_ref, *scratch = refs[slots:]
     lse, slope = lse_ref[...], slope_ref[...]
     potential_ref[...] = slope[0:1, :] * (sum_ref[...] - lse[0:1, :])
-    sum_columns(refs[:slots], shift_ref[...] - slope * lse, off_ref, out_ref)
+    sum_columns(refs[:slots], shift_ref[...] - slope * lse, out_ref, *scratch)
 
 
 def f32(*shape):
@@ -341,7 +337,11 @@
             out_shape=outs,
             in_specs=[VMEM] * (chips + 3 + len(more)),
             out_specs=(VMEM,) * len(outs),
-            scratch_shapes=[pltpu.VMEM((chips, src_count, LANES), jnp.float32)],
+            scratch_shapes=[
+                pltpu.VMEM((chips, src_count, LANES), jnp.float32),
+                pltpu.VMEM((chips, 8, tgt_count), jnp.float32),
+                pltpu.VMEM((chips, 8, tgt_count), jnp.float32),
+            ],
             compiler_params=params(8 + 2 * chips),
             cost_estimate=pl.CostEstimate(
                 flops=6 * chips * src_count * tgt_count,

time: 24.6 us -> 24.7 us (level)
  transfers between devices with their start and end apart: 8 -> 8, of which waited for: 4 -> 5; matrix products, arithmetic and copies ran while one was open for 0% -> 0% of each run, Pallas kernels for 30% -> 29%
where the time goes in v16:
time: 24.7 us; the launch traced here: 24.5 us
  starting transfers between devices  10.3 us (42%)
  Pallas kernels  8.63 us (35%)
  waiting for transfers between devices  4.14 us (17%)
  between operations  0.74 us (3%)
  other arithmetic  0.67 us (3%)
    ppermute x1, starting transfers between devices, shards(): lax.ppermute(payload, ('blk', 'tsplit'), [(b * sets + z, (b ^ 2) * sets +...  3.38 us
    ppermute x2, starting transfers between devices, along(): return lax.ppermute(value, 'tsplit', [(i, i ^ step) for i in range(sets)])  3.09 us
    ppermute x2, starting transfers between devices, across(): return lax.ppermute(value, 'blk', [(i, i ^ 2 * chip) for i in range(slabs)])  2.8 us
    pallas_call x2, Pallas kernels, prepare_on(): pl.pallas_call(functools.partial(prepare_kernel, turn), out_shape=(jax.Sh...  2.37 us
    pallas_call x2, Pallas kernels, logits(): pl.pallas_call(functools.partial(logits_kernel, len(sides) // 2), out_sha...  2.17 us
    ppermute x2, waiting for transfers between devices, along(): return lax.ppermute(value, 'tsplit', [(i, i ^ step) for i in range(sets)])  1.88 us
    pallas_call x2, Pallas kernels, columns(): pl.pallas_call(functools.partial(kernel, chips), out_shape=outs, in_specs...  1.57 us
    pallas_call x1, Pallas kernels, shards(): pl.pallas_call(near_kernel, out_shape=(f32(tgt_count, LANES), f32(1, src_...  1.49 us
  transfers between devices with their start and end apart: 8, of which 5 were waited for; matrix products, arithmetic and copies ran while one was open for 0% of the time, Pallas kernels for 29%

profile of v16, /device:TPU:0, one launch (start us, length us, event | category | flops | bytes accessed | tf_op | source)
XLA Modules:
  0.0 24.5 jit_solution(10898503317650587092)
XLA Ops:
  0.6 0.5 %collective-permute-start = (bf16[1024,512]{1,0:T(8,128)(2,1)}, bf16[1024,512]{1,0:T(8,128)(2,1)S(1)}, u32[]{:S(2)}, u32[]{:S(2)}) collective-permute-start(bf16[1024,512]{1,0:T(8,128)(2,1)} %refs_1_.3), channel_id=1, source_target_pairs={{0,4},{4,0},{8,12},{12,8},{1,5},{5,1},{9,13},{13,9},{2,6},{6,2},{1... | collective-permute-start | bytes 3145736 | tf_op jit(solution)/shard_map/ppermute | solution.py:218
  1.1 0.1 prepare_1.1
  1.2 2.6 %collective-permute-start.2 = (bf16[256,512]{1,0:T(8,128)(2,1)}, bf16[256,512]{1,0:T(8,128)(2,1)S(1)}, u32[]{:S(2)}, u32[]{:S(2)}) collective-permute-start(bf16[256,512]{1,0:T(8,128)(2,1)} %rows_ref.2), channel_id=1, source_target_pairs={{0,8},{4,12},{8,0},{12,4},{1,9},{5,13},{9,1},{13,5},{2,10},{6,14},... | collective-permute-start | bytes 786440 | tf_op jit(solution)/shard_map/ppermute | solution.py:221
  3.8 2.3 %prepare_0.1 = (bf16[1024,512]{1,0:T(8,128)(2,1)S(1)}, f32[1,1024]{1,0:T(1,128)S(1)}, f32[1024,128]{1,0:T(8,128)S(1)}, f32[256,1024]{1,0:T(8,128)S(1)}, f32[1,25...) custom-call(s32[1]{0:T(128)} %bitcast.core_ref, bf16[256,512]{1,0:T(8,128)(2,1)} %rows_ref.2, ...), custom_call_target="tpu_custom_call" | custom-call | flops 268435456 | bytes 1048576 | tf_op jit(solution)/shard_map/prepare_0/pallas_call | solution.py:246
  6.1 0.4 %collective-permute-start.1 = (f32[1,1024]{1,0:T(1,128)S(1)}, f32[1,1024]{1,0:T(1,128)S(1)}, u32[]{:S(2)}, u32[]{:S(2)}) collective-permute-start(f32[1,1024]{1,0:T(1,128)S(1)} %get-tuple-element.40.refs_1_), channel_id=1, source_target_pairs={{0,4},{4,0},{8,12},{12,8},{1,5},{5,1},{9,13},{13,9},{2,6},{6,2},{1... | collective-permute-start | bytes 12296 | tf_op jit(solution)/shard_map/ppermute | solution.py:218
  6.6 0.8 %collective-permute-done.1.offset_ref.refs_3_.refs_1_ = f32[1,1024]{1,0:T(1,128)S(1)} collective-permute-done((f32[1,1024]{1,0:T(1,128)S(1)}, f32[1,1024]{1,0:T(1,128)S(1)}, u32[]{:S(2)}, u32[]{:S(2)}) %collective-permute-start.1) | collective-permute-done | bytes 4128 | tf_op jit(solution)/shard_map/ppermute | solution.py:218
  7.4 1.5 %near_rows.1 = (f32[1024,128]{1,0:T(8,128)S(1)}, f32[1,256]{1,0:T(1,128)S(1)}) custom-call(bf16[256,512]{1,0:T(8,128)(2,1)} %rows_ref.2, bf16[1024,512]{1,0:T(8,128)(2,1)S(1)} %collective-permute-done.tgt_ref.refs_3_.refs_2_.refs_0_, f32[1,1024]{1,0:T(1,128)S(1)} %collective-permute-done.1.offset_ref.refs_3_.refs_1_, f32[1,256]{1,0:T(1,128)S(1)} %get-tuple-element.41.held_ref), custom_call_target="tpu_custom_call" | custom-call | flops 268435456 | bytes 1048576 | tf_op jit(solution)/shard_map/near_rows/pallas_call | solution.py:271
  8.9 0.2 collective-permute-done.2.refs_0_.rows_ref
  9.1 1.0 %far_rows.1 = f32[4,256]{1,0:T(4,128)S(1)} custom-call(bf16[256,512]{1,0:T(8,128)(2,1)S(1)} %collective-permute-done.2.refs_0_.rows_ref, bf16[1024,512]{1,0:T(8,128)(2,1)S(1)} %get-tuple-element.45.refs_1_.refs_0_, f32[1024,128]{1,0:T(8,128)S(1)} %get-tuple-element.46.refs_2_, bf16[1024,512]{1,0:T(8,128)(2,1)S(1)} %collective-permute-done.tgt_ref.refs_3_.refs_2_.refs_0_, ...), custom_call_target="tpu_custom_call" | custom-call | flops 536870912 | bytes 1048576 | tf_op jit(solution)/shard_map/far_rows/pallas_call | solution.py:283
  10.1 3.4 %collective-permute-start.5 = (f32[4,256]{1,0:T(4,128)S(1)}, f32[4,256]{1,0:T(4,128)S(1)}, u32[]{:S(2)}, u32[]{:S(2)}) collective-permute-start(f32[4,256]{1,0:T(4,128)S(1)} %far_rows.1), channel_id=1, source_target_pairs={{0,9},{1,8},{2,11},{3,10},{4,13},{5,12},{6,15},{7,14},{8,1},{9,0},... | collective-permute-start | bytes 12296 | tf_op jit(solution)/shard_map/ppermute | solution.py:317
  13.5 0.4 %collective-permute-start.4 = (f32[4,256]{1,0:T(4,128)S(1)}, f32[4,256]{1,0:T(4,128)S(1)}, u32[]{:S(2)}, u32[]{:S(2)}) collective-permute-start(f32[4,256]{1,0:T(4,128)S(1)} %far_rows.1), channel_id=1, source_target_pairs={{0,1},{1,0},{2,3},{3,2},{4,5},{5,4},{6,7},{7,6},{8,9},{9,8},{10,11... | collective-permute-start | bytes 12296 | tf_op jit(solution)/shard_map/ppermute | solution.py:224
  13.9 0.2 collective-permute-start.3
  14.1 0.8 %logits.2 = (f32[256,1024]{1,0:T(8,128)S(1)}, f32[256,1024]{1,0:T(8,128)S(1)}) custom-call(bf16[256,512]{1,0:T(8,128)(2,1)S(1)} %collective-permute-done.2.refs_0_.rows_ref, bf16[1024,512]{1,0:T(8,128)(2,1)S(1)} %get-tuple-element.45.refs_1_.refs_0_, f32[1,1024]{1,0:T(1,128)S(1)} %get-tuple-element.40.refs_1_, ...), custom_call_target="tpu_custom_call" | custom-call | flops 536870912 | bytes 1048576 | tf_op jit(solution)/shard_map/logits/pallas_call | solution.py:296
  14.9 1.4 %logits.3.refs_0_ = f32[256,1024]{1,0:T(8,128)S(1)} custom-call(bf16[256,512]{1,0:T(8,128)(2,1)} %rows_ref.2, bf16[1024,512]{1,0:T(8,128)(2,1)S(1)} %collective-permute-done.tgt_ref.refs_3_.refs_2_.refs_0_, f32[1,1024]{1,0:T(1,128)S(1)} %collective-permute-done.1.offset_ref.refs_3_.refs_1_), custom_call_target="tpu_custom_call" | custom-call | flops 268435456 | bytes 1048576 | tf_op jit(solution)/shard_map/logits/pallas_call | solution.py:296
  16.3 1.2 %collective-permute-done.3 = f32[4,256]{1,0:T(4,128)S(1)} collective-permute-done((f32[4,256]{1,0:T(4,128)S(1)}, f32[4,256]{1,0:T(4,128)S(1)}, u32[]{:S(2)}, u32[]{:S(2)}) %collective-permute-start.3) | collective-permute-done | bytes 4128 | tf_op jit(solution)/shard_map/ppermute | solution.py:221
  17.6 2.6 %collective-permute-start.6 = (f32[2,256]{1,0:T(2,128)S(1)}, f32[2,256]{1,0:T(2,128)S(1)}, u32[]{:S(2)}, u32[]{:S(2)}) collective-permute-start(f32[2,256]{1,0:T(2,128)S(1)} %log_add_fusion.1), channel_id=1, source_target_pairs={{0,2},{1,3},{2,0},{3,1},{4,6},{5,7},{6,4},{7,5},{8,10},{9,11},{10,... | collective-permute-start | bytes 6152 | tf_op jit(solution)/shard_map/ppermute | solution.py:224
  20.2 1.9 %collective-permute-done.6 = f32[2,256]{1,0:T(2,128)S(1)} collective-permute-done((f32[2,256]{1,0:T(2,128)S(1)}, f32[2,256]{1,0:T(2,128)S(1)}, u32[]{:S(2)}, u32[]{:S(2)}) %collective-permute-start.6) | collective-permute-done | bytes 2080 | tf_op jit(solution)/shard_map/ppermute | solution.py:224
  22.1 0.5 %columns.2 = f32[8,128]{1,0:T(8,128)S(1)} custom-call(f32[256,1024]{1,0:T(8,128)S(1)} %logits.3.refs_0_, f32[256,1024]{1,0:T(8,128)S(1)} %get-tuple-element.54.refs_1_, f32[2,256]{1,0:T(2,128)S(1)} %log_add_fusion.refs_2_, f32[2,256]{1,0:T(2,128)S(1)} %get-tuple-element.61.refs_3_, f32[2,256]{1,0:T(2,128)S(1)} %get-tuple-element.60.refs_4_), custom_call_target="tpu_custom_call" | custom-call | flops 3145728 | bytes 1048576 | tf_op jit(solution)/shard_map/columns/pallas_call | solution.py:335
  22.7 0.1 collective-permute-start.7
  22.8 0.0 copy-start
  22.8 0.0 copy-start.2
  22.8 1.0 %columns.3 = (f32[8,128]{1,0:T(8,128)S(1)}, f32[1,256]{1,0:T(1,128)}) custom-call(f32[256,1024]{1,0:T(8,128)S(1)} %get-tuple-element.39.refs_0_, f32[256,1024]{1,0:T(8,128)S(1)} %get-tuple-element.51.refs_1_, f32[2,256]{1,0:T(2,128)S(1)} %log_add_fusion.refs_2_, f32[2,256]{1,0:T(2,128)S(1)} %get-tuple-element.61.refs_3_, ...), custom_call_target="tpu_custom_call" | custom-call | flops 3145728 | bytes 1048576 | tf_op jit(solution)/shard_map/columns/pallas_call | solution.py:335
  23.8 0.1 collective-permute-done.7
  23.9 0.6 %fusion = f32[1024]{0:T(1024)} fusion(f32[1024]{0:T(1024)S(1)} %copy-done.2, f32[8,128]{1,0:T(8,128)S(1)} %collective-permute-done.7, f32[8,128]{1,0:T(8,128)S(1)} %get-tuple-element.58, f32[1024]{0:T(1024)S(1)} %copy-done, f32[1024]{0:T(1024)S(1)} %copy-done.1), kind=kLoop, calls=%fused_computation.3 | loop fusion | flops 9216 | bytes 24576 | tf_op jit(solution)/shard_map/mul | solution.py:359
  (15 shorter events, 0.1 us)
Async XLA Ops:
  0.6 6.8 %collective-permute-start = (bf16[1024,512]{1,0:T(8,128)(2,1)}, bf16[1024,512]{1,0:T(8,128)(2,1)S(1)}, u32[]{:S(2)}, u32[]{:S(2)}) collective-permute-start(bf16[1024,512]{1,0:T(8,128)(2,1)} %refs_1_.3), channel_id=1, source_target_pairs={{0,4},{4,0},{8,12},{12,8},{1,5},{5,1},{9,13},{13,9},{2,6},{6,2},{1... | collective-permute-start | bytes 3145736 | tf_op jit(solution)/shard_map/ppermute | solution.py:218
  1.2 7.9 %collective-permute-start.2 = (bf16[256,512]{1,0:T(8,128)(2,1)}, bf16[256,512]{1,0:T(8,128)(2,1)S(1)}, u32[]{:S(2)}, u32[]{:S(2)}) collective-permute-start(bf16[256,512]{1,0:T(8,128)(2,1)} %rows_ref.2), channel_id=1, source_target_pairs={{0,8},{4,12},{8,0},{12,4},{1,9},{5,13},{9,1},{13,5},{2,10},{6,14},... | collective-permute-start | bytes 786440 | tf_op jit(solution)/shard_map/ppermute | solution.py:221
  6.1 1.3 %collective-permute-start.1 = (f32[1,1024]{1,0:T(1,128)S(1)}, f32[1,1024]{1,0:T(1,128)S(1)}, u32[]{:S(2)}, u32[]{:S(2)}) collective-permute-start(f32[1,1024]{1,0:T(1,128)S(1)} %get-tuple-element.40.refs_1_), channel_id=1, source_target_pairs={{0,4},{4,0},{8,12},{12,8},{1,5},{5,1},{9,13},{13,9},{2,6},{6,2},{1... | collective-permute-start | bytes 12296 | tf_op jit(solution)/shard_map/ppermute | solution.py:218
  10.1 6.2 %collective-permute-start.5 = (f32[4,256]{1,0:T(4,128)S(1)}, f32[4,256]{1,0:T(4,128)S(1)}, u32[]{:S(2)}, u32[]{:S(2)}) collective-permute-start(f32[4,256]{1,0:T(4,128)S(1)} %far_rows.1), channel_id=1, source_target_pairs={{0,9},{1,8},{2,11},{3,10},{4,13},{5,12},{6,15},{7,14},{8,1},{9,0},... | collective-permute-start | bytes 12296 | tf_op jit(solution)/shard_map/ppermute | solution.py:317
  13.5 4.1 %collective-permute-start.4 = (f32[4,256]{1,0:T(4,128)S(1)}, f32[4,256]{1,0:T(4,128)S(1)}, u32[]{:S(2)}, u32[]{:S(2)}) collective-permute-start(f32[4,256]{1,0:T(4,128)S(1)} %far_rows.1), channel_id=1, source_target_pairs={{0,1},{1,0},{2,3},{3,2},{4,5},{5,4},{6,7},{7,6},{8,9},{9,8},{10,11... | collective-permute-start | bytes 12296 | tf_op jit(solution)/shard_map/ppermute | solution.py:224
  13.9 3.6 %collective-permute-start.3 = (f32[4,256]{1,0:T(4,128)S(1)}, f32[4,256]{1,0:T(4,128)S(1)}, u32[]{:S(2)}, u32[]{:S(2)}) collective-permute-start(f32[4,256]{1,0:T(4,128)S(1)} %far_rows.1), channel_id=1, source_target_pairs={{0,8},{4,12},{8,0},{12,4},{1,9},{5,13},{9,1},{13,5},{2,10},{6,14},... | collective-permute-start | bytes 12296 | tf_op jit(solution)/shard_map/ppermute | solution.py:221
  17.6 4.5 %collective-permute-start.6 = (f32[2,256]{1,0:T(2,128)S(1)}, f32[2,256]{1,0:T(2,128)S(1)}, u32[]{:S(2)}, u32[]{:S(2)}) collective-permute-start(f32[2,256]{1,0:T(2,128)S(1)} %log_add_fusion.1), channel_id=1, source_target_pairs={{0,2},{1,3},{2,0},{3,1},{4,6},{5,7},{6,4},{7,5},{8,10},{9,11},{10,... | collective-permute-start | bytes 6152 | tf_op jit(solution)/shard_map/ppermute | solution.py:224
  22.7 1.2 %collective-permute-start.7 = (f32[8,128]{1,0:T(8,128)S(1)}, f32[8,128]{1,0:T(8,128)S(1)}, u32[]{:S(2)}, u32[]{:S(2)}) collective-permute-start(f32[8,128]{1,0:T(8,128)S(1)} %columns.2), channel_id=1, source_target_pairs={{0,4},{4,0},{8,12},{12,8},{1,5},{5,1},{9,13},{13,9},{2,6},{6,2},{1... | collective-permute-start | bytes 12296 | tf_op jit(solution)/shard_map/ppermute | solution.py:218
  22.8 1.2 %copy-start = (f32[1024]{0:T(1024)S(1)}, f32[1024]{0:T(1024)}, u32[]{:S(2)}) copy-start(f32[1024]{0:T(1024)} %param.9) | copy-start | bytes 12292
  22.8 1.1 %copy-start.1 = (f32[1024]{0:T(1024)S(1)}, f32[1024]{0:T(1024)}, u32[]{:S(2)}) copy-start(f32[1024]{0:T(1024)} %param.11) | copy-start | bytes 12292
  22.8 1.1 %copy-start.2 = (f32[1024]{0:T(1024)S(1)}, f32[1024]{0:T(1024)}, u32[]{:S(2)}) copy-start(f32[1024]{0:T(1024)} %param.13) | copy-start | bytes 12292

commit v17 on v16

--- a/solution.py
+++ b/solution.py
@@ -14,7 +14,7 @@
 LOG_2 = math.log(2.0)
 LANES = 128
 CHUNK = 256
-PIECE = 1024
+PIECE = 256
 VMEM = pl.BlockSpec(memory_space=pltpu.VMEM)
 SMEM = pl.BlockSpec(memory_space=pltpu.SMEM)
 HBM = pl.BlockSpec(memory_space=pltpu.HBM)

time: 24.7 us -> 24.4 us (0.988)
    ppermute x1, starting transfers between devices: 3.38 us -> 3.13 us  [shards(): lax.ppermute(payload, ('blk', 'tsplit'), [(b * sets + z, (b ^ 2) * sets +...]
  transfers between devices with their start and end apart: 8 -> 8, of which waited for: 5 -> 4; matrix products, arithmetic and copies ran while one was open for 0% -> 0% of each run, Pallas kernels for 29% -> 30%
where the time goes in v17:
time: 24.4 us; the launch traced here: 24.2 us
  starting transfers between devices  10.1 us (41%)
  Pallas kernels  8.72 us (36%)
  waiting for transfers between devices  3.98 us (16%)
  between operations  0.75 us (3%)
  other arithmetic  0.67 us (3%)
    ppermute x1, starting transfers between devices, shards(): lax.ppermute(payload, ('blk', 'tsplit'), [(b * sets + z, (b ^ 2) * sets +...  3.13 us
    ppermute x2, starting transfers between devices, along(): return lax.ppermute(value, 'tsplit', [(i, i ^ step) for i in range(sets)])  3.09 us
    ppermute x2, starting transfers between devices, across(): return lax.ppermute(value, 'blk', [(i, i ^ 2 * chip) for i in range(slabs)])  2.81 us
    pallas_call x2, Pallas kernels, prepare_on(): pl.pallas_call(functools.partial(prepare_kernel, turn), out_shape=(jax.Sh...  2.54 us
    pallas_call x2, Pallas kernels, logits(): pl.pallas_call(functools.partial(logits_kernel, len(sides) // 2), out_sha...  2.17 us
    ppermute x2, waiting for transfers between devices, along(): return lax.ppermute(value, 'tsplit', [(i, i ^ step) for i in range(sets)])  1.88 us
    pallas_call x2, Pallas kernels, columns(): pl.pallas_call(functools.partial(kernel, chips), out_shape=outs, in_specs...  1.57 us
    pallas_call x1, Pallas kernels, shards(): pl.pallas_call(near_kernel, out_shape=(f32(tgt_count, LANES), f32(1, src_...  1.54 us
  transfers between devices with their start and end apart: 8, of which 4 were waited for; matrix products, arithmetic and copies ran while one was open for 0% of the time, Pallas kernels for 30%

profile of v17, /device:TPU:0, one launch (start us, length us, event | category | flops | bytes accessed | tf_op | source)
XLA Modules:
  0.0 24.2 jit_solution(16559207087389428445)
XLA Ops:
  0.6 0.5 %collective-permute-start = (bf16[1024,512]{1,0:T(8,128)(2,1)}, bf16[1024,512]{1,0:T(8,128)(2,1)S(1)}, u32[]{:S(2)}, u32[]{:S(2)}) collective-permute-start(bf16[1024,512]{1,0:T(8,128)(2,1)} %refs_1_.3), channel_id=1, source_target_pairs={{0,4},{4,0},{8,12},{12,8},{1,5},{5,1},{9,13},{13,9},{2,6},{6,2},{1... | collective-permute-start | bytes 3145736 | tf_op jit(solution)/shard_map/ppermute | solution.py:218
  1.1 0.1 prepare_1.1
  1.2 2.6 %collective-permute-start.2 = (bf16[256,512]{1,0:T(8,128)(2,1)}, bf16[256,512]{1,0:T(8,128)(2,1)S(1)}, u32[]{:S(2)}, u32[]{:S(2)}) collective-permute-start(bf16[256,512]{1,0:T(8,128)(2,1)} %rows_ref.2), channel_id=1, source_target_pairs={{0,8},{4,12},{8,0},{12,4},{1,9},{5,13},{9,1},{13,5},{2,10},{6,14},... | collective-permute-start | bytes 786440 | tf_op jit(solution)/shard_map/ppermute | solution.py:221
  3.8 2.5 %prepare_0.1 = (bf16[1024,512]{1,0:T(8,128)(2,1)S(1)}, f32[1,1024]{1,0:T(1,128)S(1)}, f32[1024,128]{1,0:T(8,128)S(1)}, f32[256,1024]{1,0:T(8,128)S(1)}, f32[1,25...) custom-call(s32[1]{0:T(128)} %bitcast.core_ref, bf16[256,512]{1,0:T(8,128)(2,1)} %rows_ref.2, ...), custom_call_target="tpu_custom_call" | custom-call | flops 268435456 | bytes 1048576 | tf_op jit(solution)/shard_map/prepare_0/pallas_call | solution.py:246
  6.3 0.4 %collective-permute-start.1 = (f32[1,1024]{1,0:T(1,128)S(1)}, f32[1,1024]{1,0:T(1,128)S(1)}, u32[]{:S(2)}, u32[]{:S(2)}) collective-permute-start(f32[1,1024]{1,0:T(1,128)S(1)} %get-tuple-element.40.refs_1_), channel_id=1, source_target_pairs={{0,4},{4,0},{8,12},{12,8},{1,5},{5,1},{9,13},{13,9},{2,6},{6,2},{1... | collective-permute-start | bytes 12296 | tf_op jit(solution)/shard_map/ppermute | solution.py:218
  6.8 0.8 %collective-permute-done.1.offset_ref.refs_3_.refs_1_ = f32[1,1024]{1,0:T(1,128)S(1)} collective-permute-done((f32[1,1024]{1,0:T(1,128)S(1)}, f32[1,1024]{1,0:T(1,128)S(1)}, u32[]{:S(2)}, u32[]{:S(2)}) %collective-permute-start.1) | collective-permute-done | bytes 4128 | tf_op jit(solution)/shard_map/ppermute | solution.py:218
  7.6 1.5 %near_rows.1 = (f32[1024,128]{1,0:T(8,128)S(1)}, f32[1,256]{1,0:T(1,128)S(1)}) custom-call(bf16[256,512]{1,0:T(8,128)(2,1)} %rows_ref.2, bf16[1024,512]{1,0:T(8,128)(2,1)S(1)} %collective-permute-done.tgt_ref.refs_3_.refs_2_.refs_0_, f32[1,1024]{1,0:T(1,128)S(1)} %collective-permute-done.1.offset_ref.refs_3_.refs_1_, f32[1,256]{1,0:T(1,128)S(1)} %get-tuple-element.41.held_ref), custom_call_target="tpu_custom_call" | custom-call | flops 268435456 | bytes 1048576 | tf_op jit(solution)/shard_map/near_rows/pallas_call | solution.py:271
  9.1 0.9 %far_rows.1 = f32[4,256]{1,0:T(4,128)S(1)} custom-call(bf16[256,512]{1,0:T(8,128)(2,1)S(1)} %collective-permute-done.2.refs_0_.rows_ref, bf16[1024,512]{1,0:T(8,128)(2,1)S(1)} %get-tuple-element.45.refs_1_.refs_0_, f32[1024,128]{1,0:T(8,128)S(1)} %get-tuple-element.46.refs_2_, bf16[1024,512]{1,0:T(8,128)(2,1)S(1)} %collective-permute-done.tgt_ref.refs_3_.refs_2_.refs_0_, ...), custom_call_target="tpu_custom_call" | custom-call | flops 536870912 | bytes 1048576 | tf_op jit(solution)/shard_map/far_rows/pallas_call | solution.py:283
  10.0 3.1 %collective-permute-start.5 = (f32[4,256]{1,0:T(4,128)S(1)}, f32[4,256]{1,0:T(4,128)S(1)}, u32[]{:S(2)}, u32[]{:S(2)}) collective-permute-start(f32[4,256]{1,0:T(4,128)S(1)} %far_rows.1), channel_id=1, source_target_pairs={{0,9},{1,8},{2,11},{3,10},{4,13},{5,12},{6,15},{7,14},{8,1},{9,0},... | collective-permute-start | bytes 12296 | tf_op jit(solution)/shard_map/ppermute | solution.py:317
  13.2 0.4 %collective-permute-start.4 = (f32[4,256]{1,0:T(4,128)S(1)}, f32[4,256]{1,0:T(4,128)S(1)}, u32[]{:S(2)}, u32[]{:S(2)}) collective-permute-start(f32[4,256]{1,0:T(4,128)S(1)} %far_rows.1), channel_id=1, source_target_pairs={{0,1},{1,0},{2,3},{3,2},{4,5},{5,4},{6,7},{7,6},{8,9},{9,8},{10,11... | collective-permute-start | bytes 12296 | tf_op jit(solution)/shard_map/ppermute | solution.py:224
  13.6 0.2 collective-permute-start.3
  13.8 0.8 %logits.2 = (f32[256,1024]{1,0:T(8,128)S(1)}, f32[256,1024]{1,0:T(8,128)S(1)}) custom-call(bf16[256,512]{1,0:T(8,128)(2,1)S(1)} %collective-permute-done.2.refs_0_.rows_ref, bf16[1024,512]{1,0:T(8,128)(2,1)S(1)} %get-tuple-element.45.refs_1_.refs_0_, f32[1,1024]{1,0:T(1,128)S(1)} %get-tuple-element.40.refs_1_, ...), custom_call_target="tpu_custom_call" | custom-call | flops 536870912 | bytes 1048576 | tf_op jit(solution)/shard_map/logits/pallas_call | solution.py:296
  14.6 1.4 %logits.3.refs_0_ = f32[256,1024]{1,0:T(8,128)S(1)} custom-call(bf16[256,512]{1,0:T(8,128)(2,1)} %rows_ref.2, bf16[1024,512]{1,0:T(8,128)(2,1)S(1)} %collective-permute-done.tgt_ref.refs_3_.refs_2_.refs_0_, f32[1,1024]{1,0:T(1,128)S(1)} %collective-permute-done.1.offset_ref.refs_3_.refs_1_), custom_call_target="tpu_custom_call" | custom-call | flops 268435456 | bytes 1048576 | tf_op jit(solution)/shard_map/logits/pallas_call | solution.py:296
  16.0 1.2 %collective-permute-done.3 = f32[4,256]{1,0:T(4,128)S(1)} collective-permute-done((f32[4,256]{1,0:T(4,128)S(1)}, f32[4,256]{1,0:T(4,128)S(1)}, u32[]{:S(2)}, u32[]{:S(2)}) %collective-permute-start.3) | collective-permute-done | bytes 4128 | tf_op jit(solution)/shard_map/ppermute | solution.py:221
  17.3 2.6 %collective-permute-start.6 = (f32[2,256]{1,0:T(2,128)S(1)}, f32[2,256]{1,0:T(2,128)S(1)}, u32[]{:S(2)}, u32[]{:S(2)}) collective-permute-start(f32[2,256]{1,0:T(2,128)S(1)} %log_add_fusion.1), channel_id=1, source_target_pairs={{0,2},{1,3},{2,0},{3,1},{4,6},{5,7},{6,4},{7,5},{8,10},{9,11},{10,... | collective-permute-start | bytes 6152 | tf_op jit(solution)/shard_map/ppermute | solution.py:224
  19.9 1.9 %collective-permute-done.6 = f32[2,256]{1,0:T(2,128)S(1)} collective-permute-done((f32[2,256]{1,0:T(2,128)S(1)}, f32[2,256]{1,0:T(2,128)S(1)}, u32[]{:S(2)}, u32[]{:S(2)}) %collective-permute-start.6) | collective-permute-done | bytes 2080 | tf_op jit(solution)/shard_map/ppermute | solution.py:224
  21.8 0.5 %columns.2 = f32[8,128]{1,0:T(8,128)S(1)} custom-call(f32[256,1024]{1,0:T(8,128)S(1)} %logits.3.refs_0_, f32[256,1024]{1,0:T(8,128)S(1)} %get-tuple-element.54.refs_1_, f32[2,256]{1,0:T(2,128)S(1)} %log_add_fusion.refs_2_, f32[2,256]{1,0:T(2,128)S(1)} %get-tuple-element.61.refs_3_, f32[2,256]{1,0:T(2,128)S(1)} %get-tuple-element.60.refs_4_), custom_call_target="tpu_custom_call" | custom-call | flops 3145728 | bytes 1048576 | tf_op jit(solution)/shard_map/columns/pallas_call | solution.py:335
  22.4 0.1 collective-permute-start.7
  22.4 0.0 copy-start
  22.4 0.0 copy-start.1
  22.5 0.0 copy-start.2
  22.5 1.0 %columns.3 = (f32[8,128]{1,0:T(8,128)S(1)}, f32[1,256]{1,0:T(1,128)}) custom-call(f32[256,1024]{1,0:T(8,128)S(1)} %get-tuple-element.39.refs_0_, f32[256,1024]{1,0:T(8,128)S(1)} %get-tuple-element.51.refs_1_, f32[2,256]{1,0:T(2,128)S(1)} %log_add_fusion.refs_2_, f32[2,256]{1,0:T(2,128)S(1)} %get-tuple-element.61.refs_3_, ...), custom_call_target="tpu_custom_call" | custom-call | flops 3145728 | bytes 1048576 | tf_op jit(solution)/shard_map/columns/pallas_call | solution.py:335
  23.5 0.1 collective-permute-done.7
  23.6 0.6 %fusion = f32[1024]{0:T(1024)} fusion(f32[1024]{0:T(1024)S(1)} %copy-done.2, f32[8,128]{1,0:T(8,128)S(1)} %collective-permute-done.7, f32[8,128]{1,0:T(8,128)S(1)} %get-tuple-element.58, f32[1024]{0:T(1024)S(1)} %copy-done, f32[1024]{0:T(1024)S(1)} %copy-done.1), kind=kLoop, calls=%fused_computation.3 | loop fusion | flops 9216 | bytes 24576 | tf_op jit(solution)/shard_map/mul | solution.py:359
  (15 shorter events, 0.1 us)
Async XLA Ops:
  0.6 7.0 %collective-permute-start = (bf16[1024,512]{1,0:T(8,128)(2,1)}, bf16[1024,512]{1,0:T(8,128)(2,1)S(1)}, u32[]{:S(2)}, u32[]{:S(2)}) collective-permute-start(bf16[1024,512]{1,0:T(8,128)(2,1)} %refs_1_.3), channel_id=1, source_target_pairs={{0,4},{4,0},{8,12},{12,8},{1,5},{5,1},{9,13},{13,9},{2,6},{6,2},{1... | collective-permute-start | bytes 3145736 | tf_op jit(solution)/shard_map/ppermute | solution.py:218
  1.2 7.9 %collective-permute-start.2 = (bf16[256,512]{1,0:T(8,128)(2,1)}, bf16[256,512]{1,0:T(8,128)(2,1)S(1)}, u32[]{:S(2)}, u32[]{:S(2)}) collective-permute-start(bf16[256,512]{1,0:T(8,128)(2,1)} %rows_ref.2), channel_id=1, source_target_pairs={{0,8},{4,12},{8,0},{12,4},{1,9},{5,13},{9,1},{13,5},{2,10},{6,14},... | collective-permute-start | bytes 786440 | tf_op jit(solution)/shard_map/ppermute | solution.py:221
  6.3 1.3 %collective-permute-start.1 = (f32[1,1024]{1,0:T(1,128)S(1)}, f32[1,1024]{1,0:T(1,128)S(1)}, u32[]{:S(2)}, u32[]{:S(2)}) collective-permute-start(f32[1,1024]{1,0:T(1,128)S(1)} %get-tuple-element.40.refs_1_), channel_id=1, source_target_pairs={{0,4},{4,0},{8,12},{12,8},{1,5},{5,1},{9,13},{13,9},{2,6},{6,2},{1... | collective-permute-start | bytes 12296 | tf_op jit(solution)/shard_map/ppermute | solution.py:218
  10.0 6.0 %collective-permute-start.5 = (f32[4,256]{1,0:T(4,128)S(1)}, f32[4,256]{1,0:T(4,128)S(1)}, u32[]{:S(2)}, u32[]{:S(2)}) collective-permute-start(f32[4,256]{1,0:T(4,128)S(1)} %far_rows.1), channel_id=1, source_target_pairs={{0,9},{1,8},{2,11},{3,10},{4,13},{5,12},{6,15},{7,14},{8,1},{9,0},... | collective-permute-start | bytes 12296 | tf_op jit(solution)/shard_map/ppermute | solution.py:317
  13.2 4.1 %collective-permute-start.4 = (f32[4,256]{1,0:T(4,128)S(1)}, f32[4,256]{1,0:T(4,128)S(1)}, u32[]{:S(2)}, u32[]{:S(2)}) collective-permute-start(f32[4,256]{1,0:T(4,128)S(1)} %far_rows.1), channel_id=1, source_target_pairs={{0,1},{1,0},{2,3},{3,2},{4,5},{5,4},{6,7},{7,6},{8,9},{9,8},{10,11... | collective-permute-start | bytes 12296 | tf_op jit(solution)/shard_map/ppermute | solution.py:224
  13.6 3.6 %collective-permute-start.3 = (f32[4,256]{1,0:T(4,128)S(1)}, f32[4,256]{1,0:T(4,128)S(1)}, u32[]{:S(2)}, u32[]{:S(2)}) collective-permute-start(f32[4,256]{1,0:T(4,128)S(1)} %far_rows.1), channel_id=1, source_target_pairs={{0,8},{4,12},{8,0},{12,4},{1,9},{5,13},{9,1},{13,5},{2,10},{6,14},... | collective-permute-start | bytes 12296 | tf_op jit(solution)/shard_map/ppermute | solution.py:221
  17.3 4.5 %collective-permute-start.6 = (f32[2,256]{1,0:T(2,128)S(1)}, f32[2,256]{1,0:T(2,128)S(1)}, u32[]{:S(2)}, u32[]{:S(2)}) collective-permute-start(f32[2,256]{1,0:T(2,128)S(1)} %log_add_fusion.1), channel_id=1, source_target_pairs={{0,2},{1,3},{2,0},{3,1},{4,6},{5,7},{6,4},{7,5},{8,10},{9,11},{10,... | collective-permute-start | bytes 6152 | tf_op jit(solution)/shard_map/ppermute | solution.py:224
  22.4 1.2 %collective-permute-start.7 = (f32[8,128]{1,0:T(8,128)S(1)}, f32[8,128]{1,0:T(8,128)S(1)}, u32[]{:S(2)}, u32[]{:S(2)}) collective-permute-start(f32[8,128]{1,0:T(8,128)S(1)} %columns.2), channel_id=1, source_target_pairs={{0,4},{4,0},{8,12},{12,8},{1,5},{5,1},{9,13},{13,9},{2,6},{6,2},{1... | collective-permute-start | bytes 12296 | tf_op jit(solution)/shard_map/ppermute | solution.py:218
  22.4 1.2 %copy-start = (f32[1024]{0:T(1024)S(1)}, f32[1024]{0:T(1024)}, u32[]{:S(2)}) copy-start(f32[1024]{0:T(1024)} %param.9) | copy-start | bytes 12292
  22.4 1.1 %copy-start.1 = (f32[1024]{0:T(1024)S(1)}, f32[1024]{0:T(1024)}, u32[]{:S(2)}) copy-start(f32[1024]{0:T(1024)} %param.11) | copy-start | bytes 12292
  22.5 1.1 %copy-start.2 = (f32[1024]{0:T(1024)S(1)}, f32[1024]{0:T(1024)}, u32[]{:S(2)}) copy-start(f32[1024]{0:T(1024)} %param.13) | copy-start | bytes 12292

commit v18 on v17

--- a/solution.py
+++ b/solution.py
@@ -90,9 +90,17 @@
         z_ref[:, cols] = (dots + offset_ref[:, cols]) * LOG2_E
 
 
-def logits_kernel(sides, rows_ref, *refs):
-    for side in range(sides):
-        make_logits(rows_ref[...], refs[2 * side], refs[2 * side + 1], refs[2 * sides + side])
+def logits_kernel(sides, core_ref, rows_ref, *refs):
+    for side, needed in enumerate(sides):
+        args = (rows_ref, refs[2 * side], refs[2 * side + 1], refs[2 * len(sides) + side])
+        if needed is None:
+            make_logits(args[0][...], *args[1:])
+        else:
+            pl.when(core_ref[0] == needed)(functools.partial(make_logits_of, *args))
+
+
+def make_logits_of(rows_ref, *refs):
+    make_logits(rows_ref[...], *refs)
 
 
 def prepare_kernel(turn, core_ref, *refs):
@@ -183,9 +191,37 @@
         out_ref[group : group + 1, :] = total[:, group * LANES : (group + 1) * LANES]
 
 
-def pair_kernel(slots, *refs):
+def pair_kernel(slots, core_ref, *refs):
     lse_ref, slope_ref, shift_ref, out_ref, *scratch = refs[slots:]
-    sum_columns(refs[:slots], shift_ref[...] - slope_ref[...] * lse_ref[...], out_ref, *scratch)
+    offset = shift_ref[...] - slope_ref[...] * lse_ref[...]
+    rows = offset.shape[1] // LANES
+
+    @pl.when(core_ref[0] == 1)
+    def work():
+        sum_columns(refs[:slots], offset, out_ref.at[: refs[0].shape[1] // LANES], *scratch)
+
+    @pl.when(core_ref[0] == 0)
+    def send():
+        for row in range(slots * rows):
+            at = row % rows * LANES
+            out_ref[row : row + 1, :] = offset[row // rows : row // rows + 1, at : at + LANES]
+
+
+def away_kernel(slots, core_ref, *refs):
+    home_ref, out_ref, *scratch = refs[slots:]
+    rows = refs[0].shape[0] // LANES
+
+    @pl.when(core_ref[0] == 1)
+    def work():
+        lines = [
+            jnp.concatenate([home_ref[at : at + 1, :] for at in range(slot * rows, (slot + 1) * rows)], axis=1)
+            for slot in range(slots)
+        ]
+        sum_columns(refs[:slots], jnp.concatenate(lines, axis=0), out_ref, *scratch)
+
+    @pl.when(core_ref[0] == 0)
+    def take():
+        out_ref[...] = home_ref[: out_ref.shape[0], :]
 
 
 def own_kernel(slots, *refs):
@@ -268,6 +304,8 @@
     far_blocks = [across(sent, chip) for chip in range(1, chips)]
     held, offset, column, own_z, lse, line, src_sum = prepare_on(0, *earlier[:6], first)
     pair_offset = pair(offset)
+    offset, late_sources = lax.optimization_barrier((offset, sources))
+    pair_sources = pair(late_sources)
     pair_column, lse = pl.pallas_call(
         near_kernel,
         out_shape=(f32(tgt_count, LANES), f32(1, src_count)),
@@ -291,23 +329,24 @@
         name="far_rows",
     )(*moved[:far], held, column, pair_targets, pair_column, lse, line)
 
-    payload, *blocks = lax.optimization_barrier((payload, sources, *moved[:far]))
+    payload, pair_sources, *blocks = lax.optimization_barrier((payload, pair_sources, sources, *moved[:far]))
     def logits(block, *sides):
         return pl.pallas_call(
-            functools.partial(logits_kernel, len(sides) // 2),
-            out_shape=(f32(src_count, tgt_count),) * (len(sides) // 2),
-            in_specs=[VMEM] * (1 + len(sides)),
-            out_specs=(VMEM,) * (len(sides) // 2),
+            functools.partial(logits_kernel, [side[0] for side in sides]),
+            out_shape=(f32(src_count, tgt_count),) * len(sides),
+            in_specs=[SMEM] + [VMEM] * (1 + 2 * len(sides)),
+            out_specs=(VMEM,) * len(sides),
             compiler_params=params(12),
-            cost_estimate=cost(len(sides) // 2),
+            cost_estimate=cost(len(sides)),
             name="logits",
-        )(block, *sides)
-
-    own_zs, pair_zs = [own_z], list(logits(blocks[0], pair_targets, pair_offset))
+        )(core_word, block, *[array for side in sides for array in side[1:]])
+
+    own_zs, pair_zs = [own_z], list(logits(blocks[0], (1, pair_targets, pair_offset)))
     for block in blocks[1:]:
-        own_z, pair_z = logits(block, held, offset, pair_targets, pair_offset)
+        own_z, pair_z = logits(block, (None, held, offset), (1, pair_targets, pair_offset))
         own_zs.append(own_z)
         pair_zs.append(pair_z)
+    away_zs = [logits(block, (1, held, offset))[0] for block in [pair_sources] + [pair(block) for block in blocks[1:]]]
 
     def mirror(value, chip):
         return jnp.stack([value[slot ^ chip] for slot in range(chips)])
@@ -319,7 +358,7 @@
         ("blk", "tsplit"),
         [(b * sets + z, (b ^ 2) * sets + (z ^ 1)) for b in range(slabs) for z in range(sets)],
     )
-    lines = jnp.stack([line, other[chips:]] + moved[far:], axis=1)
+    lines = jnp.stack([line, joined[chips:]] + moved[far:], axis=1)
     lse = merge(payload[:chips], mirror(other, 1), beside[:chips], mirror(joined, 1))
     chip = 2
     while chip < chips:
@@ -330,12 +369,13 @@
         lse = merge(lse, along(lse, step))
         step *= 2
 
-    def columns(kernel, zs, *more):
-        outs = (f32(groups, LANES), f32(1, src_count))[: 1 + len(more)]
+    rows = max(groups, chips * src_groups)
+
+    def columns(kernel, words, vectors, outs):
         return pl.pallas_call(
             functools.partial(kernel, chips),
             out_shape=outs,
-            in_specs=[VMEM] * (chips + 3 + len(more)),
+            in_specs=[SMEM] * len(words) + [VMEM] * len(vectors),
             out_specs=(VMEM,) * len(outs),
             scratch_shapes=[
                 pltpu.VMEM((chips, src_count, LANES), jnp.float32),
@@ -349,13 +389,18 @@
                 transcendentals=chips * src_count * tgt_count,
             ),
             name="columns",
-        )(*zs, lse, lines[0], lines[1], *more)
-
-    (pair_part,) = columns(pair_kernel, pair_zs)
-    lse, pair_part = lax.optimization_barrier((lse, pair_part))
-    home = pair(pair_part)
-    own_part, src_potential = columns(own_kernel, own_zs, src_sum)
-    total = merge(own_part, home).reshape(tgt_count)
+        )(*words, *vectors)
+
+    found = (lse, lines[0], lines[1])
+    (sent_part,) = columns(pair_kernel, (core_word,), (*pair_zs, *found), (f32(rows, LANES),))
+    lse, sent_part = lax.optimization_barrier((lse, sent_part))
+    home = pair(sent_part)
+    own_part, src_potential = columns(
+        own_kernel, (), (*own_zs, lse, lines[0], lines[1], src_sum), (f32(groups, LANES), f32(1, src_count))
+    )
+    own_part, home = lax.optimization_barrier((own_part, home))
+    (away_part,) = columns(away_kernel, (core_word,), (*away_zs, home), (f32(groups, LANES),))
+    total = merge(own_part, away_part).reshape(tgt_count)
     tgt_update = tgt_exponent * (2.0 * tgt_logmass + tgt_potential - total)
     return (src_potential.reshape(src_count), tgt_update)
 

time: 24.4 us -> 25.6 us (1.049)
  the two profiles are of different devices: /device:TPU:0 before, /device:TPU:1 now
where the time goes in v18:
time: 25.6 us; the launch traced here: 25.4 us
  Pallas kernels  10.6 us (41%)
  starting transfers between devices  9.97 us (39%)
  waiting for transfers between devices  3.19 us (12%)
  between operations  0.8 us (3%)
  other arithmetic  0.67 us (3%)
    pallas_call x4, Pallas kernels, logits(): pl.pallas_call(functools.partial(logits_kernel, [side[0] for side in side...  3.29 us
    ppermute x2, starting transfers between devices, across(): return lax.ppermute(value, 'blk', [(i, i ^ 2 * chip) for i in range(slabs)])  2.98 us
    ppermute x1, starting transfers between devices, shards(): lax.ppermute(payload, ('blk', 'tsplit'), [(b * sets + z, (b ^ 2) * sets +...  2.81 us
    pallas_call x2, Pallas kernels, prepare_on(): pl.pallas_call(functools.partial(prepare_kernel, turn), out_shape=(jax.Sh...  2.72 us
    ppermute x2, starting transfers between devices, along(): return lax.ppermute(value, 'tsplit', [(i, i ^ step) for i in range(sets)])  2.55 us
    pallas_call x3, Pallas kernels, columns(): pl.pallas_call(functools.partial(kernel, chips), out_shape=outs, in_specs...  2.13 us
    ppermute x5, starting transfers between devices, pair(): return lax.ppermute(value, 'blk', [(i, i ^ 1) for i in range(slabs)])  1.63 us
    pallas_call x1, Pallas kernels, shards(): pl.pallas_call(near_kernel, out_shape=(f32(tgt_count, LANES), f32(1, src_...  1.54 us
  transfers between devices with their start and end apart: 10, of which 3 were waited for; matrix products, arithmetic and copies ran while one was open for 0% of the time, Pallas kernels for 38%

profile of v18, /device:TPU:1, one launch (start us, length us, event | category | flops | bytes accessed | tf_op | source)
XLA Modules:
  0.0 25.4 jit_solution(17291515729706328293)
XLA Ops:
  0.6 0.1 collective-permute-start
  0.8 2.5 %prepare_1.1 = (bf16[1024,512]{1,0:T(8,128)(2,1)S(1)}, f32[1,1024]{1,0:T(1,128)S(1)}, f32[1024,128]{1,0:T(8,128)S(1)}, f32[256,1024]{1,0:T(8,128)S(1)}, f32[1,25...) custom-call(s32[1]{0:T(128)} %bitcast.core_ref, bf16[256,512]{1,0:T(8,128)(2,1)} %rows_ref.2, ...), custom_call_target="tpu_custom_call" | custom-call | flops 268435456 | bytes 1048576 | tf_op jit(solution)/shard_map/prepare_1/pallas_call | solution.py:282
  3.3 2.8 %collective-permute-start.2 = (bf16[256,512]{1,0:T(8,128)(2,1)}, bf16[256,512]{1,0:T(8,128)(2,1)S(1)}, u32[]{:S(2)}, u32[]{:S(2)}) collective-permute-start(bf16[256,512]{1,0:T(8,128)(2,1)} %rows_ref.2), channel_id=1, source_target_pairs={{0,8},{4,12},{8,0},{12,4},{1,9},{5,13},{9,1},{13,5},{2,10},{6,14},... | collective-permute-start | bytes 786440 | tf_op jit(solution)/shard_map/ppermute | solution.py:257
  6.0 0.2 prepare_0.1
  6.2 0.2 collective-permute-start.3
  6.4 0.4 %collective-permute-start.1 = (f32[1,1024]{1,0:T(1,128)S(1)}, f32[1,1024]{1,0:T(1,128)S(1)}, u32[]{:S(2)}, u32[]{:S(2)}) collective-permute-start(f32[1,1024]{1,0:T(1,128)S(1)} %get-tuple-element.57.refs_1_), channel_id=1, source_target_pairs={{0,4},{4,0},{8,12},{12,8},{1,5},{5,1},{9,13},{13,9},{2,6},{6,2},{1... | collective-permute-start | bytes 12296 | tf_op jit(solution)/shard_map/ppermute | solution.py:254
  6.8 1.0 %collective-permute-done.1.offset_ref.refs_3_.refs_1_ = f32[1,1024]{1,0:T(1,128)S(1)} collective-permute-done((f32[1,1024]{1,0:T(1,128)S(1)}, f32[1,1024]{1,0:T(1,128)S(1)}, u32[]{:S(2)}, u32[]{:S(2)}) %collective-permute-start.1) | collective-permute-done | bytes 4128 | tf_op jit(solution)/shard_map/ppermute | solution.py:254
  7.8 1.5 %near_rows.1 = (f32[1024,128]{1,0:T(8,128)S(1)}, f32[1,256]{1,0:T(1,128)S(1)}) custom-call(bf16[256,512]{1,0:T(8,128)(2,1)} %rows_ref.2, bf16[1024,512]{1,0:T(8,128)(2,1)S(1)} %collective-permute-done.tgt_ref.refs_3_.refs_2_.refs_0_, f32[1,1024]{1,0:T(1,128)S(1)} %collective-permute-done.1.offset_ref.refs_3_.refs_1_, f32[1,256]{1,0:T(1,128)S(1)} %get-tuple-element.46.held_ref), custom_call_target="tpu_custom_call" | custom-call | flops 268435456 | bytes 1048576 | tf_op jit(solution)/shard_map/near_rows/pallas_call | solution.py:309
  9.4 1.2 %collective-permute-done.2.refs_0_.rows_ref = bf16[256,512]{1,0:T(8,128)(2,1)S(1)} collective-permute-done((bf16[256,512]{1,0:T(8,128)(2,1)}, bf16[256,512]{1,0:T(8,128)(2,1)S(1)}, u32[]{:S(2)}, u32[]{:S(2)}) %collective-permute-start.2) | collective-permute-done | bytes 262176 | tf_op jit(solution)/shard_map/ppermute | solution.py:257
  10.6 0.9 %far_rows.1 = f32[4,256]{1,0:T(4,128)S(1)} custom-call(bf16[256,512]{1,0:T(8,128)(2,1)S(1)} %collective-permute-done.2.refs_0_.rows_ref, bf16[1024,512]{1,0:T(8,128)(2,1)S(1)} %get-tuple-element.50.refs_1_.refs_0_, f32[1024,128]{1,0:T(8,128)S(1)} %get-tuple-element.51.refs_2_, bf16[1024,512]{1,0:T(8,128)(2,1)S(1)} %collective-permute-done.tgt_ref.refs_3_.refs_2_.refs_0_, ...), custom_call_target="tpu_custom_call" | custom-call | flops 536870912 | bytes 1048576 | tf_op jit(solution)/shard_map/far_rows/pallas_call | solution.py:321
  11.5 2.8 %collective-permute-start.6 = (f32[4,256]{1,0:T(4,128)S(1)}, f32[4,256]{1,0:T(4,128)S(1)}, u32[]{:S(2)}, u32[]{:S(2)}) collective-permute-start(f32[4,256]{1,0:T(4,128)S(1)} %far_rows.1), channel_id=1, source_target_pairs={{0,9},{1,8},{2,11},{3,10},{4,13},{5,12},{6,15},{7,14},{8,1},{9,0},... | collective-permute-start | bytes 12296 | tf_op jit(solution)/shard_map/ppermute | solution.py:356
  14.3 0.2 collective-permute-start.4
  14.5 0.1 collective-permute-start.5
  14.6 0.9 %logits.4 = (f32[256,1024]{1,0:T(8,128)S(1)}, f32[256,1024]{1,0:T(8,128)S(1)}) custom-call(s32[1]{0:T(128)} %bitcast.core_ref, bf16[256,512]{1,0:T(8,128)(2,1)S(1)} %collective-permute-done.2.refs_0_.rows_ref, bf16[1024,512]{1,0:T(8,128)(2,1)S(1)} %get-tuple-element.50.refs_1_.refs_0_, f32[1,1024]{1,0:T(1,128)S(1)} %get-tuple-element.57.refs_1_, ...), custom_call_target="tpu_custom_call" | custom-call | flops 536870912 | bytes 1048576 | tf_op jit(solution)/shard_map/logits/pallas_call | solution.py:334
  15.6 1.4 %logits.5.refs_0_ = f32[256,1024]{1,0:T(8,128)S(1)} custom-call(s32[1]{0:T(128)} %bitcast.core_ref, bf16[256,512]{1,0:T(8,128)(2,1)} %rows_ref.2, bf16[1024,512]{1,0:T(8,128)(2,1)S(1)} %collective-permute-done.tgt_ref.refs_3_.refs_2_.refs_0_, f32[1,1024]{1,0:T(1,128)S(1)} %collective-permute-done.1.offset_ref.refs_3_.refs_1_), custom_call_target="tpu_custom_call" | custom-call | flops 268435456 | bytes 1048576 | tf_op jit(solution)/shard_map/logits/pallas_call | solution.py:334
  17.1 2.4 %collective-permute-start.7 = (f32[2,256]{1,0:T(2,128)S(1)}, f32[2,256]{1,0:T(2,128)S(1)}, u32[]{:S(2)}, u32[]{:S(2)}) collective-permute-start(f32[2,256]{1,0:T(2,128)S(1)} %log_add_fusion.1), channel_id=1, source_target_pairs={{0,2},{1,3},{2,0},{3,1},{4,6},{5,7},{6,4},{7,5},{8,10},{9,11},{10,... | collective-permute-start | bytes 6152 | tf_op jit(solution)/shard_map/ppermute | solution.py:260
  19.5 1.0 %collective-permute-done.7 = f32[2,256]{1,0:T(2,128)S(1)} collective-permute-done((f32[2,256]{1,0:T(2,128)S(1)}, f32[2,256]{1,0:T(2,128)S(1)}, u32[]{:S(2)}, u32[]{:S(2)}) %collective-permute-start.7) | collective-permute-done | bytes 2080 | tf_op jit(solution)/shard_map/ppermute | solution.py:260
  20.5 0.5 %columns.3 = f32[8,128]{1,0:T(8,128)S(1)} custom-call(s32[1]{0:T(128)} %bitcast.core_ref, f32[256,1024]{1,0:T(8,128)S(1)} %logits.5.refs_0_, f32[256,1024]{1,0:T(8,128)S(1)} %get-tuple-element.61.refs_1_, f32[2,256]{1,0:T(2,128)S(1)} %log_add_fusion.refs_2_, f32[2,256]{1,0:T(2,128)S(1)} %get-tuple-element.71.refs_3_, f32[2,256]{1,0:T(2,128)S(1)} %get-tuple-element.70.refs_4_), custom_call_target="tpu_custom_call" | custom-call | flops 3145728 | bytes 1048576 | tf_op jit(solution)/shard_map/columns/pallas_call | solution.py:375
  21.1 0.9 %collective-permute-start.8 = (f32[8,128]{1,0:T(8,128)S(1)}, f32[8,128]{1,0:T(8,128)S(1)}, u32[]{:S(2)}, u32[]{:S(2)}) collective-permute-start(f32[8,128]{1,0:T(8,128)S(1)} %columns.3), channel_id=1, source_target_pairs={{0,4},{4,0},{8,12},{12,8},{1,5},{5,1},{9,13},{13,9},{2,6},{6,2},{1... | collective-permute-start | bytes 12296 | tf_op jit(solution)/shard_map/ppermute | solution.py:254
  22.0 0.5 %logits.6.refs_0_ = f32[256,1024]{1,0:T(8,128)S(1)} custom-call(s32[1]{0:T(128)} %bitcast.core_ref, bf16[256,512]{1,0:T(8,128)(2,1)S(1)} %collective-permute-done.3.rows_ref, bf16[1024,512]{1,0:T(8,128)(2,1)S(1)} %get-tuple-element.50.refs_1_.refs_0_, f32[1,1024]{1,0:T(1,128)S(1)} %get-tuple-element.57.refs_1_), custom_call_target="tpu_custom_call" | custom-call | flops 268435456 | bytes 1048576 | tf_op jit(solution)/shard_map/logits/pallas_call | solution.py:334
  22.5 1.0 %columns.4 = (f32[8,128]{1,0:T(8,128)S(1)}, f32[1,256]{1,0:T(1,128)}) custom-call(f32[256,1024]{1,0:T(8,128)S(1)} %get-tuple-element.44.refs_0_, f32[256,1024]{1,0:T(8,128)S(1)} %get-tuple-element.58.refs_1_, f32[2,256]{1,0:T(2,128)S(1)} %log_add_fusion.refs_2_, f32[2,256]{1,0:T(2,128)S(1)} %get-tuple-element.71.refs_3_, ...), custom_call_target="tpu_custom_call" | custom-call | flops 3145728 | bytes 1048576 | tf_op jit(solution)/shard_map/columns/pallas_call | solution.py:375
  23.5 0.5 %logits.7.refs_1_ = f32[256,1024]{1,0:T(8,128)S(1)} custom-call(s32[1]{0:T(128)} %bitcast.core_ref, bf16[256,512]{1,0:T(8,128)(2,1)S(1)} %collective-permute-done.9.rows_ref, bf16[1024,512]{1,0:T(8,128)(2,1)S(1)} %get-tuple-element.50.refs_1_.refs_0_, f32[1,1024]{1,0:T(1,128)S(1)} %get-tuple-element.57.refs_1_), custom_call_target="tpu_custom_call" | custom-call | flops 268435456 | bytes 1048576 | tf_op jit(solution)/shard_map/logits/pallas_call | solution.py:334
  24.1 0.5 %columns.5 = f32[8,128]{1,0:T(8,128)S(1)} custom-call(s32[1]{0:T(128)} %bitcast.core_ref, f32[256,1024]{1,0:T(8,128)S(1)} %logits.6.refs_0_, f32[256,1024]{1,0:T(8,128)S(1)} %logits.7.refs_1_, f32[8,128]{1,0:T(8,128)S(1)} %collective-permute-done.8.refs_2_), custom_call_target="tpu_custom_call" | custom-call | flops 3145728 | bytes 1048576 | tf_op jit(solution)/shard_map/columns/pallas_call | solution.py:375
  24.7 0.6 %fusion = f32[1024]{0:T(1024)} fusion(f32[1024]{0:T(1024)S(1)} %copy-done.2, f32[8,128]{1,0:T(8,128)S(1)} %columns.5, f32[8,128]{1,0:T(8,128)S(1)} %get-tuple-element.67, f32[1024]{0:T(1024)S(1)} %copy-done, f32[1024]{0:T(1024)S(1)} %copy-done.1), kind=kLoop, calls=%fused_computation.3 | loop fusion | flops 9216 | bytes 24576 | tf_op jit(solution)/shard_map/mul | solution.py:404
  (22 shorter events, 0.2 us)
Async XLA Ops:
  0.6 7.2 %collective-permute-start = (bf16[1024,512]{1,0:T(8,128)(2,1)}, bf16[1024,512]{1,0:T(8,128)(2,1)S(1)}, u32[]{:S(2)}, u32[]{:S(2)}) collective-permute-start(bf16[1024,512]{1,0:T(8,128)(2,1)} %refs_1_.3), channel_id=1, source_target_pairs={{0,4},{4,0},{8,12},{12,8},{1,5},{5,1},{9,13},{13,9},{2,6},{6,2},{1... | collective-permute-start | bytes 3145736 | tf_op jit(solution)/shard_map/ppermute | solution.py:254
  3.3 7.3 %collective-permute-start.2 = (bf16[256,512]{1,0:T(8,128)(2,1)}, bf16[256,512]{1,0:T(8,128)(2,1)S(1)}, u32[]{:S(2)}, u32[]{:S(2)}) collective-permute-start(bf16[256,512]{1,0:T(8,128)(2,1)} %rows_ref.2), channel_id=1, source_target_pairs={{0,8},{4,12},{8,0},{12,4},{1,9},{5,13},{9,1},{13,5},{2,10},{6,14},... | collective-permute-start | bytes 786440 | tf_op jit(solution)/shard_map/ppermute | solution.py:257
  6.2 5.2 %collective-permute-start.3 = (bf16[256,512]{1,0:T(8,128)(2,1)}, bf16[256,512]{1,0:T(8,128)(2,1)S(1)}, u32[]{:S(2)}, u32[]{:S(2)}) collective-permute-start(bf16[256,512]{1,0:T(8,128)(2,1)} %rows_ref.2), channel_id=1, source_target_pairs={{0,4},{4,0},{8,12},{12,8},{1,5},{5,1},{9,13},{13,9},{2,6},{6,2},{1... | collective-permute-start | bytes 786440 | tf_op jit(solution)/shard_map/ppermute | solution.py:254
  6.4 1.4 %collective-permute-start.1 = (f32[1,1024]{1,0:T(1,128)S(1)}, f32[1,1024]{1,0:T(1,128)S(1)}, u32[]{:S(2)}, u32[]{:S(2)}) collective-permute-start(f32[1,1024]{1,0:T(1,128)S(1)} %get-tuple-element.57.refs_1_), channel_id=1, source_target_pairs={{0,4},{4,0},{8,12},{12,8},{1,5},{5,1},{9,13},{13,9},{2,6},{6,2},{1... | collective-permute-start | bytes 12296 | tf_op jit(solution)/shard_map/ppermute | solution.py:254
  11.5 5.6 %collective-permute-start.6 = (f32[4,256]{1,0:T(4,128)S(1)}, f32[4,256]{1,0:T(4,128)S(1)}, u32[]{:S(2)}, u32[]{:S(2)}) collective-permute-start(f32[4,256]{1,0:T(4,128)S(1)} %far_rows.1), channel_id=1, source_target_pairs={{0,9},{1,8},{2,11},{3,10},{4,13},{5,12},{6,15},{7,14},{8,1},{9,0},... | collective-permute-start | bytes 12296 | tf_op jit(solution)/shard_map/ppermute | solution.py:356
  14.3 2.7 %collective-permute-start.4 = (f32[4,256]{1,0:T(4,128)S(1)}, f32[4,256]{1,0:T(4,128)S(1)}, u32[]{:S(2)}, u32[]{:S(2)}) collective-permute-start(f32[4,256]{1,0:T(4,128)S(1)} %far_rows.1), channel_id=1, source_target_pairs={{0,8},{4,12},{8,0},{12,4},{1,9},{5,13},{9,1},{13,5},{2,10},{6,14},... | collective-permute-start | bytes 12296 | tf_op jit(solution)/shard_map/ppermute | solution.py:257
  14.5 2.6 %collective-permute-start.5 = (f32[4,256]{1,0:T(4,128)S(1)}, f32[4,256]{1,0:T(4,128)S(1)}, u32[]{:S(2)}, u32[]{:S(2)}) collective-permute-start(f32[4,256]{1,0:T(4,128)S(1)} %far_rows.1), channel_id=1, source_target_pairs={{0,1},{1,0},{2,3},{3,2},{4,5},{5,4},{6,7},{7,6},{8,9},{9,8},{10,11... | collective-permute-start | bytes 12296 | tf_op jit(solution)/shard_map/ppermute | solution.py:260
  14.6 8.9 %collective-permute-start.9 = (bf16[256,512]{1,0:T(8,128)(2,1)S(1)}, bf16[256,512]{1,0:T(8,128)(2,1)S(1)}, u32[]{:S(2)}, u32[]{:S(2)}) collective-permute-start(bf16[256,512]{1,0:T(8,128)(2,1)S(1)} %collective-permute-done.2.refs_0_.rows_ref), channel_id=1, source_target_pairs={{0,4},{4,0},{8,12},{12,8},{1,5},{5,1},{9,13},{13,9},{2,6},{6,2},{1... | collective-permute-start | bytes 786440 | tf_op jit(solution)/shard_map/ppermute | solution.py:254
  17.1 3.4 %collective-permute-start.7 = (f32[2,256]{1,0:T(2,128)S(1)}, f32[2,256]{1,0:T(2,128)S(1)}, u32[]{:S(2)}, u32[]{:S(2)}) collective-permute-start(f32[2,256]{1,0:T(2,128)S(1)} %log_add_fusion.1), channel_id=1, source_target_pairs={{0,2},{1,3},{2,0},{3,1},{4,6},{5,7},{6,4},{7,5},{8,10},{9,11},{10,... | collective-permute-start | bytes 6152 | tf_op jit(solution)/shard_map/ppermute | solution.py:260
  21.1 2.4 %collective-permute-start.8 = (f32[8,128]{1,0:T(8,128)S(1)}, f32[8,128]{1,0:T(8,128)S(1)}, u32[]{:S(2)}, u32[]{:S(2)}) collective-permute-start(f32[8,128]{1,0:T(8,128)S(1)} %columns.3), channel_id=1, source_target_pairs={{0,4},{4,0},{8,12},{12,8},{1,5},{5,1},{9,13},{13,9},{2,6},{6,2},{1... | collective-permute-start | bytes 12296 | tf_op jit(solution)/shard_map/ppermute | solution.py:254
  24.0 0.7 %copy-start = (f32[1024]{0:T(1024)S(1)}, f32[1024]{0:T(1024)}, u32[]{:S(2)}) copy-start(f32[1024]{0:T(1024)} %param.9) | copy-start | bytes 12292
  24.0 0.7 %copy-start.1 = (f32[1024]{0:T(1024)S(1)}, f32[1024]{0:T(1024)}, u32[]{:S(2)}) copy-start(f32[1024]{0:T(1024)} %param.11) | copy-start | bytes 12292
  24.0 0.7 %copy-start.2 = (f32[1024]{0:T(1024)S(1)}, f32[1024]{0:T(1024)}, u32[]{:S(2)}) copy-start(f32[1024]{0:T(1024)} %param.13) | copy-start | bytes 12292

commit v19 on v17

--- a/solution.py
+++ b/solution.py
@@ -184,15 +184,29 @@
 
 
 def pair_kernel(slots, *refs):
-    lse_ref, slope_ref, shift_ref, out_ref, *scratch = refs[slots:]
-    sum_columns(refs[:slots], shift_ref[...] - slope_ref[...] * lse_ref[...], out_ref, *scratch)
-
-
-def own_kernel(slots, *refs):
-    lse_ref, slope_ref, shift_ref, sum_ref, out_ref, potential_ref, *scratch = refs[slots:]
-    lse, slope = lse_ref[...], slope_ref[...]
-    potential_ref[...] = slope[0:1, :] * (sum_ref[...] - lse[0:1, :])
-    sum_columns(refs[:slots], shift_ref[...] - slope * lse, out_ref, *scratch)
+    lse_ref, there_ref, slope_ref, shift_ref, out_ref, *scratch = refs[slots:]
+    lse = merge(lse_ref[...], there_ref[...])
+    sum_columns(refs[:slots], shift_ref[...] - slope_ref[...] * lse, out_ref, *scratch)
+
+
+def own_kernel(turn, slots, *refs):
+    z_refs, (lse_ref, there_ref, slope_ref, shift_ref, core_ref), refs = refs[:slots], refs[slots : slots + 5], refs[slots + 5 :]
+    lse = merge(lse_ref[...], there_ref[...])
+    if turn == 0:
+        sum_ref, earlier_ref, out_ref, potential_ref, *scratch = refs
+        potential_ref[...] = slope_ref[0:1, :] * (sum_ref[...] - lse[0:1, :])
+    else:
+        out_ref, *scratch = refs
+
+    @pl.when(core_ref[0] == turn)
+    def work():
+        sum_columns(z_refs, shift_ref[...] - slope_ref[...] * lse, out_ref, *scratch)
+
+    if turn == 0:
+
+        @pl.when(core_ref[0] != turn)
+        def hand_on():
+            out_ref[...] = earlier_ref[...]
 
 
 def f32(*shape):
@@ -212,7 +226,7 @@
     far = chips - 1
     groups = tgt_count // LANES
     src_groups = src_count // LANES
-    assert chips > 1 and sets > 1 and chips & (chips - 1) == 0 and sets & (sets - 1) == 0
+    assert chips > 1 and sets > 2 and chips & (chips - 1) == 0 and sets & (sets - 1) == 0
 
     def pair(value):
         return lax.ppermute(value, "blk", [(i, i ^ 1) for i in range(slabs)])
@@ -326,16 +340,16 @@
         lse = merge(lse, mirror(across(lse, chip), chip))
         chip *= 2
     step = 2
-    while step < sets:
+    while 2 * step < sets:
         lse = merge(lse, along(lse, step))
         step *= 2
-
-    def columns(kernel, zs, *more):
-        outs = (f32(groups, LANES), f32(1, src_count))[: 1 + len(more)]
+    there = along(lse, step)
+
+    def columns(kernel, zs, *more, outs=(f32(groups, LANES),)):
         return pl.pallas_call(
-            functools.partial(kernel, chips),
+            kernel,
             out_shape=outs,
-            in_specs=[VMEM] * (chips + 3 + len(more)),
+            in_specs=[VMEM] * (chips + 4) + [SMEM] * min(1, len(more)) + [VMEM] * (len(more) - 1),
             out_specs=(VMEM,) * len(outs),
             scratch_shapes=[
                 pltpu.VMEM((chips, src_count, LANES), jnp.float32),
@@ -349,12 +363,20 @@
                 transcendentals=chips * src_count * tgt_count,
             ),
             name="columns",
-        )(*zs, lse, lines[0], lines[1], *more)
-
-    (pair_part,) = columns(pair_kernel, pair_zs)
-    lse, pair_part = lax.optimization_barrier((lse, pair_part))
+        )(*zs, lse, there, lines[0], lines[1], *more)
+
+    (pair_part,) = columns(functools.partial(pair_kernel, chips), pair_zs)
+    (early_part,) = columns(functools.partial(own_kernel, 1, chips), own_zs, core_word)
+    there, pair_part, early_part = lax.optimization_barrier((there, pair_part, early_part))
     home = pair(pair_part)
-    own_part, src_potential = columns(own_kernel, own_zs, src_sum)
+    own_part, src_potential = columns(
+        functools.partial(own_kernel, 0, chips),
+        own_zs,
+        core_word,
+        src_sum,
+        early_part,
+        outs=(f32(groups, LANES), f32(1, src_count)),
+    )
     total = merge(own_part, home).reshape(tgt_count)
     tgt_update = tgt_exponent * (2.0 * tgt_logmass + tgt_potential - total)
     return (src_potential.reshape(src_count), tgt_update)

time: 24.4 us -> 24.5 us (level)
    pallas_call x2 -> x3, Pallas kernels: 1.57 us -> 1.7 us  [columns(): pl.pallas_call(kernel, out_shape=outs, in_specs=[VMEM] * (chips + 4) + [S...]
  transfers between devices with their start and end apart: 8 -> 8, of which waited for: 4 -> 3; matrix products, arithmetic and copies ran while one was open for 0% -> 0% of each run, Pallas kernels for 30% -> 30%
where the time goes in v19:
time: 24.5 us; the launch traced here: 24.3 us
  starting transfers between devices  10.1 us (41%)
  Pallas kernels  8.85 us (36%)
  waiting for transfers between devices  3.92 us (16%)
  between operations  0.76 us (3%)
  other arithmetic  0.66 us (3%)
    ppermute x1, starting transfers between devices, shards(): lax.ppermute(payload, ('blk', 'tsplit'), [(b * sets + z, (b ^ 2) * sets +...  3.13 us
    ppermute x2, starting transfers between devices, along(): return lax.ppermute(value, 'tsplit', [(i, i ^ step) for i in range(sets)])  3.1 us
    ppermute x2, starting transfers between devices, across(): return lax.ppermute(value, 'blk', [(i, i ^ 2 * chip) for i in range(slabs)])  2.8 us
    pallas_call x2, Pallas kernels, prepare_on(): pl.pallas_call(functools.partial(prepare_kernel, turn), out_shape=(jax.Sh...  2.55 us
    pallas_call x2, Pallas kernels, logits(): pl.pallas_call(functools.partial(logits_kernel, len(sides) // 2), out_sha...  2.16 us
    ppermute x2, waiting for transfers between devices, along(): return lax.ppermute(value, 'tsplit', [(i, i ^ step) for i in range(sets)])  1.88 us
    pallas_call x3, Pallas kernels, columns(): pl.pallas_call(kernel, out_shape=outs, in_specs=[VMEM] * (chips + 4) + [S...  1.7 us
    pallas_call x1, Pallas kernels, shards(): pl.pallas_call(near_kernel, out_shape=(f32(tgt_count, LANES), f32(1, src_...  1.54 us
  transfers between devices with their start and end apart: 8, of which 3 were waited for; matrix products, arithmetic and copies ran while one was open for 0% of the time, Pallas kernels for 30%

profile of v19, /device:TPU:0, one launch (start us, length us, event | category | flops | bytes accessed | tf_op | source)
XLA Modules:
  0.0 24.3 jit_solution(11465007340069269466)
XLA Ops:
  0.6 0.5 %collective-permute-start = (bf16[1024,512]{1,0:T(8,128)(2,1)}, bf16[1024,512]{1,0:T(8,128)(2,1)S(1)}, u32[]{:S(2)}, u32[]{:S(2)}) collective-permute-start(bf16[1024,512]{1,0:T(8,128)(2,1)} %refs_1_.3), channel_id=1, source_target_pairs={{0,4},{4,0},{8,12},{12,8},{1,5},{5,1},{9,13},{13,9},{2,6},{6,2},{1... | collective-permute-start | bytes 3145736 | tf_op jit(solution)/shard_map/ppermute | solution.py:232
  1.1 0.1 prepare_1.1
  1.2 2.6 %collective-permute-start.2 = (bf16[256,512]{1,0:T(8,128)(2,1)}, bf16[256,512]{1,0:T(8,128)(2,1)S(1)}, u32[]{:S(2)}, u32[]{:S(2)}) collective-permute-start(bf16[256,512]{1,0:T(8,128)(2,1)} %rows_ref.2), channel_id=1, source_target_pairs={{0,8},{4,12},{8,0},{12,4},{1,9},{5,13},{9,1},{13,5},{2,10},{6,14},... | collective-permute-start | bytes 786440 | tf_op jit(solution)/shard_map/ppermute | solution.py:235
  3.8 2.5 %prepare_0.1 = (bf16[1024,512]{1,0:T(8,128)(2,1)S(1)}, f32[1,1024]{1,0:T(1,128)S(1)}, f32[1024,128]{1,0:T(8,128)S(1)}, f32[256,1024]{1,0:T(8,128)S(1)}, f32[1,25...) custom-call(s32[1]{0:T(128)} %bitcast.core_ref.refs_6_, bf16[256,512]{1,0:T(8,128)(2,1)} %rows_ref.2, ...), custom_call_target="tpu_custom_call" | custom-call | flops 268435456 | bytes 1048576 | tf_op jit(solution)/shard_map/prepare_0/pallas_call | solution.py:260
  6.3 0.4 %collective-permute-start.1 = (f32[1,1024]{1,0:T(1,128)S(1)}, f32[1,1024]{1,0:T(1,128)S(1)}, u32[]{:S(2)}, u32[]{:S(2)}) collective-permute-start(f32[1,1024]{1,0:T(1,128)S(1)} %get-tuple-element.41.refs_1_), channel_id=1, source_target_pairs={{0,4},{4,0},{8,12},{12,8},{1,5},{5,1},{9,13},{13,9},{2,6},{6,2},{1... | collective-permute-start | bytes 12296 | tf_op jit(solution)/shard_map/ppermute | solution.py:232
  6.8 0.8 %collective-permute-done.1.offset_ref.refs_3_.refs_1_ = f32[1,1024]{1,0:T(1,128)S(1)} collective-permute-done((f32[1,1024]{1,0:T(1,128)S(1)}, f32[1,1024]{1,0:T(1,128)S(1)}, u32[]{:S(2)}, u32[]{:S(2)}) %collective-permute-start.1) | collective-permute-done | bytes 4128 | tf_op jit(solution)/shard_map/ppermute | solution.py:232
  7.6 0.0 collective-permute-done.tgt_ref.refs_3_.refs_2_.refs_0_
  7.6 1.5 %near_rows.1 = (f32[1024,128]{1,0:T(8,128)S(1)}, f32[1,256]{1,0:T(1,128)S(1)}) custom-call(bf16[256,512]{1,0:T(8,128)(2,1)} %rows_ref.2, bf16[1024,512]{1,0:T(8,128)(2,1)S(1)} %collective-permute-done.tgt_ref.refs_3_.refs_2_.refs_0_, f32[1,1024]{1,0:T(1,128)S(1)} %collective-permute-done.1.offset_ref.refs_3_.refs_1_, f32[1,256]{1,0:T(1,128)S(1)} %get-tuple-element.42.held_ref), custom_call_target="tpu_custom_call" | custom-call | flops 268435456 | bytes 1048576 | tf_op jit(solution)/shard_map/near_rows/pallas_call | solution.py:285
  9.1 0.9 %far_rows.1 = f32[4,256]{1,0:T(4,128)S(1)} custom-call(bf16[256,512]{1,0:T(8,128)(2,1)S(1)} %collective-permute-done.2.refs_0_.rows_ref, bf16[1024,512]{1,0:T(8,128)(2,1)S(1)} %get-tuple-element.46.refs_1_.refs_0_, f32[1024,128]{1,0:T(8,128)S(1)} %get-tuple-element.47.refs_2_, bf16[1024,512]{1,0:T(8,128)(2,1)S(1)} %collective-permute-done.tgt_ref.refs_3_.refs_2_.refs_0_, ...), custom_call_target="tpu_custom_call" | custom-call | flops 536870912 | bytes 1048576 | tf_op jit(solution)/shard_map/far_rows/pallas_call | solution.py:297
  10.0 3.1 %collective-permute-start.5 = (f32[4,256]{1,0:T(4,128)S(1)}, f32[4,256]{1,0:T(4,128)S(1)}, u32[]{:S(2)}, u32[]{:S(2)}) collective-permute-start(f32[4,256]{1,0:T(4,128)S(1)} %far_rows.1), channel_id=1, source_target_pairs={{0,9},{1,8},{2,11},{3,10},{4,13},{5,12},{6,15},{7,14},{8,1},{9,0},... | collective-permute-start | bytes 12296 | tf_op jit(solution)/shard_map/ppermute | solution.py:331
  13.2 0.4 %collective-permute-start.4 = (f32[4,256]{1,0:T(4,128)S(1)}, f32[4,256]{1,0:T(4,128)S(1)}, u32[]{:S(2)}, u32[]{:S(2)}) collective-permute-start(f32[4,256]{1,0:T(4,128)S(1)} %far_rows.1), channel_id=1, source_target_pairs={{0,1},{1,0},{2,3},{3,2},{4,5},{5,4},{6,7},{7,6},{8,9},{9,8},{10,11... | collective-permute-start | bytes 12296 | tf_op jit(solution)/shard_map/ppermute | solution.py:238
  13.6 0.2 collective-permute-start.3
  13.8 0.7 %logits.2 = (f32[256,1024]{1,0:T(8,128)S(1)}, f32[256,1024]{1,0:T(8,128)S(1)}) custom-call(bf16[256,512]{1,0:T(8,128)(2,1)S(1)} %collective-permute-done.2.refs_0_.rows_ref, bf16[1024,512]{1,0:T(8,128)(2,1)S(1)} %get-tuple-element.46.refs_1_.refs_0_, f32[1,1024]{1,0:T(1,128)S(1)} %get-tuple-element.41.refs_1_, ...), custom_call_target="tpu_custom_call" | custom-call | flops 536870912 | bytes 1048576 | tf_op jit(solution)/shard_map/logits/pallas_call | solution.py:310
  14.6 1.4 %logits.3.refs_0_ = f32[256,1024]{1,0:T(8,128)S(1)} custom-call(bf16[256,512]{1,0:T(8,128)(2,1)} %rows_ref.2, bf16[1024,512]{1,0:T(8,128)(2,1)S(1)} %collective-permute-done.tgt_ref.refs_3_.refs_2_.refs_0_, f32[1,1024]{1,0:T(1,128)S(1)} %collective-permute-done.1.offset_ref.refs_3_.refs_1_), custom_call_target="tpu_custom_call" | custom-call | flops 268435456 | bytes 1048576 | tf_op jit(solution)/shard_map/logits/pallas_call | solution.py:310
  16.0 1.2 %collective-permute-done.3 = f32[4,256]{1,0:T(4,128)S(1)} collective-permute-done((f32[4,256]{1,0:T(4,128)S(1)}, f32[4,256]{1,0:T(4,128)S(1)}, u32[]{:S(2)}, u32[]{:S(2)}) %collective-permute-start.3) | collective-permute-done | bytes 4128 | tf_op jit(solution)/shard_map/ppermute | solution.py:235
  17.3 2.7 %collective-permute-start.6 = (f32[2,256]{1,0:T(2,128)S(1)}, f32[2,256]{1,0:T(2,128)S(1)}, u32[]{:S(2)}, u32[]{:S(2)}) collective-permute-start(f32[2,256]{1,0:T(2,128)S(1)} %log_add_fusion.refs_2_), channel_id=1, source_target_pairs={{0,2},{1,3},{2,0},{3,1},{4,6},{5,7},{6,4},{7,5},{8,10},{9,11},{10,... | collective-permute-start | bytes 6152 | tf_op jit(solution)/shard_map/ppermute | solution.py:238
  19.9 1.9 %collective-permute-done.6.refs_3_ = f32[2,256]{1,0:T(2,128)S(1)} collective-permute-done((f32[2,256]{1,0:T(2,128)S(1)}, f32[2,256]{1,0:T(2,128)S(1)}, u32[]{:S(2)}, u32[]{:S(2)}) %collective-permute-start.6) | collective-permute-done | bytes 2080 | tf_op jit(solution)/shard_map/ppermute | solution.py:238
  21.8 0.5 %columns.3 = f32[8,128]{1,0:T(8,128)S(1)} custom-call(f32[256,1024]{1,0:T(8,128)S(1)} %logits.3.refs_0_, f32[256,1024]{1,0:T(8,128)S(1)} %get-tuple-element.55.refs_1_, f32[2,256]{1,0:T(2,128)S(1)} %log_add_fusion.refs_2_, f32[2,256]{1,0:T(2,128)S(1)} %collective-permute-done.6.refs_3_, f32[2,256]{1,0:T(2,128)S(1)} %get-tuple-element.63.refs_4_, ...), custom_call_target="tpu_custom_call" | custom-call | flops 3145728 | bytes 1048576 | tf_op jit(solution)/shard_map/columns/pallas_call | solution.py:349
  22.4 0.1 collective-permute-start.7
  22.5 0.0 copy-start
  22.5 0.0 copy-start.1
  22.5 0.0 copy-start.2
  22.5 1.1 %columns.5 = (f32[8,128]{1,0:T(8,128)S(1)}, f32[1,256]{1,0:T(1,128)}) custom-call(f32[256,1024]{1,0:T(8,128)S(1)} %get-tuple-element.40.refs_0_, f32[256,1024]{1,0:T(8,128)S(1)} %get-tuple-element.52.refs_1_, f32[2,256]{1,0:T(2,128)S(1)} %log_add_fusion.refs_2_, f32[2,256]{1,0:T(2,128)S(1)} %collective-permute-done.6.refs_3_, ...), custom_call_target="tpu_custom_call" | custom-call | flops 3145728 | bytes 1048576 | tf_op jit(solution)/shard_map/columns/pallas_call | solution.py:349
  23.7 0.6 %fusion = f32[1024]{0:T(1024)} fusion(f32[1024]{0:T(1024)S(1)} %copy-done.2, f32[8,128]{1,0:T(8,128)S(1)} %collective-permute-done.7, f32[8,128]{1,0:T(8,128)S(1)} %get-tuple-element.60, f32[1024]{0:T(1024)S(1)} %copy-done, f32[1024]{0:T(1024)S(1)} %copy-done.1), kind=kLoop, calls=%fused_computation.3 | loop fusion | flops 9216 | bytes 24576 | tf_op jit(solution)/shard_map/mul | solution.py:381
  (15 shorter events, 0.1 us)
Async XLA Ops:
  0.6 7.0 %collective-permute-start = (bf16[1024,512]{1,0:T(8,128)(2,1)}, bf16[1024,512]{1,0:T(8,128)(2,1)S(1)}, u32[]{:S(2)}, u32[]{:S(2)}) collective-permute-start(bf16[1024,512]{1,0:T(8,128)(2,1)} %refs_1_.3), channel_id=1, source_target_pairs={{0,4},{4,0},{8,12},{12,8},{1,5},{5,1},{9,13},{13,9},{2,6},{6,2},{1... | collective-permute-start | bytes 3145736 | tf_op jit(solution)/shard_map/ppermute | solution.py:232
  1.2 7.9 %collective-permute-start.2 = (bf16[256,512]{1,0:T(8,128)(2,1)}, bf16[256,512]{1,0:T(8,128)(2,1)S(1)}, u32[]{:S(2)}, u32[]{:S(2)}) collective-permute-start(bf16[256,512]{1,0:T(8,128)(2,1)} %rows_ref.2), channel_id=1, source_target_pairs={{0,8},{4,12},{8,0},{12,4},{1,9},{5,13},{9,1},{13,5},{2,10},{6,14},... | collective-permute-start | bytes 786440 | tf_op jit(solution)/shard_map/ppermute | solution.py:235
  6.3 1.3 %collective-permute-start.1 = (f32[1,1024]{1,0:T(1,128)S(1)}, f32[1,1024]{1,0:T(1,128)S(1)}, u32[]{:S(2)}, u32[]{:S(2)}) collective-permute-start(f32[1,1024]{1,0:T(1,128)S(1)} %get-tuple-element.41.refs_1_), channel_id=1, source_target_pairs={{0,4},{4,0},{8,12},{12,8},{1,5},{5,1},{9,13},{13,9},{2,6},{6,2},{1... | collective-permute-start | bytes 12296 | tf_op jit(solution)/shard_map/ppermute | solution.py:232
  10.0 5.9 %collective-permute-start.5 = (f32[4,256]{1,0:T(4,128)S(1)}, f32[4,256]{1,0:T(4,128)S(1)}, u32[]{:S(2)}, u32[]{:S(2)}) collective-permute-start(f32[4,256]{1,0:T(4,128)S(1)} %far_rows.1), channel_id=1, source_target_pairs={{0,9},{1,8},{2,11},{3,10},{4,13},{5,12},{6,15},{7,14},{8,1},{9,0},... | collective-permute-start | bytes 12296 | tf_op jit(solution)/shard_map/ppermute | solution.py:331
  13.2 4.1 %collective-permute-start.4 = (f32[4,256]{1,0:T(4,128)S(1)}, f32[4,256]{1,0:T(4,128)S(1)}, u32[]{:S(2)}, u32[]{:S(2)}) collective-permute-start(f32[4,256]{1,0:T(4,128)S(1)} %far_rows.1), channel_id=1, source_target_pairs={{0,1},{1,0},{2,3},{3,2},{4,5},{5,4},{6,7},{7,6},{8,9},{9,8},{10,11... | collective-permute-start | bytes 12296 | tf_op jit(solution)/shard_map/ppermute | solution.py:238
  13.6 3.6 %collective-permute-start.3 = (f32[4,256]{1,0:T(4,128)S(1)}, f32[4,256]{1,0:T(4,128)S(1)}, u32[]{:S(2)}, u32[]{:S(2)}) collective-permute-start(f32[4,256]{1,0:T(4,128)S(1)} %far_rows.1), channel_id=1, source_target_pairs={{0,8},{4,12},{8,0},{12,4},{1,9},{5,13},{9,1},{13,5},{2,10},{6,14},... | collective-permute-start | bytes 12296 | tf_op jit(solution)/shard_map/ppermute | solution.py:235
  17.3 4.5 %collective-permute-start.6 = (f32[2,256]{1,0:T(2,128)S(1)}, f32[2,256]{1,0:T(2,128)S(1)}, u32[]{:S(2)}, u32[]{:S(2)}) collective-permute-start(f32[2,256]{1,0:T(2,128)S(1)} %log_add_fusion.refs_2_), channel_id=1, source_target_pairs={{0,2},{1,3},{2,0},{3,1},{4,6},{5,7},{6,4},{7,5},{8,10},{9,11},{10,... | collective-permute-start | bytes 6152 | tf_op jit(solution)/shard_map/ppermute | solution.py:238
  22.4 1.3 %collective-permute-start.7 = (f32[8,128]{1,0:T(8,128)S(1)}, f32[8,128]{1,0:T(8,128)S(1)}, u32[]{:S(2)}, u32[]{:S(2)}) collective-permute-start(f32[8,128]{1,0:T(8,128)S(1)} %columns.3), channel_id=1, source_target_pairs={{0,4},{4,0},{8,12},{12,8},{1,5},{5,1},{9,13},{13,9},{2,6},{6,2},{1... | collective-permute-start | bytes 12296 | tf_op jit(solution)/shard_map/ppermute | solution.py:232
  22.5 1.2 %copy-start = (f32[1024]{0:T(1024)S(1)}, f32[1024]{0:T(1024)}, u32[]{:S(2)}) copy-start(f32[1024]{0:T(1024)} %param.9) | copy-start | bytes 12292
  22.5 1.2 %copy-start.1 = (f32[1024]{0:T(1024)S(1)}, f32[1024]{0:T(1024)}, u32[]{:S(2)}) copy-start(f32[1024]{0:T(1024)} %param.11) | copy-start | bytes 12292
  22.5 1.2 %copy-start.2 = (f32[1024]{0:T(1024)S(1)}, f32[1024]{0:T(1024)}, u32[]{:S(2)}) copy-start(f32[1024]{0:T(1024)} %param.13) | copy-start | bytes 12292

commit v20 on v19

--- a/solution.py
+++ b/solution.py
@@ -14,7 +14,7 @@
 LOG_2 = math.log(2.0)
 LANES = 128
 CHUNK = 256
-PIECE = 256
+PIECE = 128
 VMEM = pl.BlockSpec(memory_space=pltpu.VMEM)
 SMEM = pl.BlockSpec(memory_space=pltpu.SMEM)
 HBM = pl.BlockSpec(memory_space=pltpu.HBM)

time: 24.5 us -> 25 us (1.020)
  Pallas kernels: 8.85 us -> 10.1 us
  waiting for transfers between devices: 3.92 us -> 3.35 us
  starting transfers between devices: 10.1 us -> 9.85 us
    ppermute x1, starting transfers between devices: 3.13 us -> 2.34 us  [shards(): lax.ppermute(payload, ('blk', 'tsplit'), [(b * sets + z, (b ^ 2) * sets +...]
    pallas_call x1, Pallas kernels: 0.9 us -> 1.61 us  [shards(): pl.pallas_call(functools.partial(far_kernel, far), out_shape=f32(chips +...]
    ppermute x2, waiting for transfers between devices: 1.22 us -> 0.65 us  [across(): return lax.ppermute(value, 'blk', [(i, i ^ 2 * chip) for i in range(slabs)])]
    ppermute x2, starting transfers between devices: 2.8 us -> 3.37 us  [across(): return lax.ppermute(value, 'blk', [(i, i ^ 2 * chip) for i in range(slabs)])]
    pallas_call x1, Pallas kernels: 1.54 us -> 1.85 us  [shards(): pl.pallas_call(near_kernel, out_shape=(f32(tgt_count, LANES), f32(1, src_...]
  transfers between devices with their start and end apart: 8 -> 8, of which waited for: 3 -> 3; matrix products, arithmetic and copies ran while one was open for 0% -> 0% of each run, Pallas kernels for 30% -> 32%
where the time goes in v20:
time: 25 us; the launch traced here: 24.8 us
  Pallas kernels  10.1 us (40%)
  starting transfers between devices  9.85 us (39%)
  waiting for transfers between devices  3.35 us (13%)
  between operations  0.76 us (3%)
  other arithmetic  0.66 us (3%)
    ppermute x2, starting transfers between devices, across(): return lax.ppermute(value, 'blk', [(i, i ^ 2 * chip) for i in range(slabs)])  3.37 us
    ppermute x2, starting transfers between devices, along(): return lax.ppermute(value, 'tsplit', [(i, i ^ step) for i in range(sets)])  3.12 us
    pallas_call x2, Pallas kernels, prepare_on(): pl.pallas_call(functools.partial(prepare_kernel, turn), out_shape=(jax.Sh...  2.79 us
    ppermute x1, starting transfers between devices, shards(): lax.ppermute(payload, ('blk', 'tsplit'), [(b * sets + z, (b ^ 2) * sets +...  2.34 us
    pallas_call x2, Pallas kernels, logits(): pl.pallas_call(functools.partial(logits_kernel, len(sides) // 2), out_sha...  2.16 us
    ppermute x2, waiting for transfers between devices, along(): return lax.ppermute(value, 'tsplit', [(i, i ^ step) for i in range(sets)])  1.88 us
    pallas_call x1, Pallas kernels, shards(): pl.pallas_call(near_kernel, out_shape=(f32(tgt_count, LANES), f32(1, src_...  1.85 us
    pallas_call x3, Pallas kernels, columns(): pl.pallas_call(kernel, out_shape=outs, in_specs=[VMEM] * (chips + 4) + [S...  1.7 us
  transfers between devices with their start and end apart: 8, of which 3 were waited for; matrix products, arithmetic and copies ran while one was open for 0% of the time, Pallas kernels for 32%

profile of v20, /device:TPU:0, one launch (start us, length us, event | category | flops | bytes accessed | tf_op | source)
XLA Modules:
  0.0 24.8 jit_solution(17749257341858275839)
XLA Ops:
  0.6 0.5 %collective-permute-start = (bf16[1024,512]{1,0:T(8,128)(2,1)}, bf16[1024,512]{1,0:T(8,128)(2,1)S(1)}, u32[]{:S(2)}, u32[]{:S(2)}) collective-permute-start(bf16[1024,512]{1,0:T(8,128)(2,1)} %refs_1_.3), channel_id=1, source_target_pairs={{0,4},{4,0},{8,12},{12,8},{1,5},{5,1},{9,13},{13,9},{2,6},{6,2},{1... | collective-permute-start | bytes 3145736 | tf_op jit(solution)/shard_map/ppermute | solution.py:232
  1.1 0.1 prepare_1.1
  1.2 2.6 %collective-permute-start.2 = (bf16[256,512]{1,0:T(8,128)(2,1)}, bf16[256,512]{1,0:T(8,128)(2,1)S(1)}, u32[]{:S(2)}, u32[]{:S(2)}) collective-permute-start(bf16[256,512]{1,0:T(8,128)(2,1)} %rows_ref.2), channel_id=1, source_target_pairs={{0,8},{4,12},{8,0},{12,4},{1,9},{5,13},{9,1},{13,5},{2,10},{6,14},... | collective-permute-start | bytes 786440 | tf_op jit(solution)/shard_map/ppermute | solution.py:235
  3.8 2.7 %prepare_0.1 = (bf16[1024,512]{1,0:T(8,128)(2,1)S(1)}, f32[1,1024]{1,0:T(1,128)S(1)}, f32[1024,128]{1,0:T(8,128)S(1)}, f32[256,1024]{1,0:T(8,128)S(1)}, f32[1,25...) custom-call(s32[1]{0:T(128)} %bitcast.core_ref.refs_6_, bf16[256,512]{1,0:T(8,128)(2,1)} %rows_ref.2, ...), custom_call_target="tpu_custom_call" | custom-call | flops 268435456 | bytes 1048576 | tf_op jit(solution)/shard_map/prepare_0/pallas_call | solution.py:260
  6.6 0.4 %collective-permute-start.1 = (f32[1,1024]{1,0:T(1,128)S(1)}, f32[1,1024]{1,0:T(1,128)S(1)}, u32[]{:S(2)}, u32[]{:S(2)}) collective-permute-start(f32[1,1024]{1,0:T(1,128)S(1)} %get-tuple-element.41.refs_1_), channel_id=1, source_target_pairs={{0,4},{4,0},{8,12},{12,8},{1,5},{5,1},{9,13},{13,9},{2,6},{6,2},{1... | collective-permute-start | bytes 12296 | tf_op jit(solution)/shard_map/ppermute | solution.py:232
  7.0 0.8 %collective-permute-done.1.offset_ref.refs_3_.refs_1_ = f32[1,1024]{1,0:T(1,128)S(1)} collective-permute-done((f32[1,1024]{1,0:T(1,128)S(1)}, f32[1,1024]{1,0:T(1,128)S(1)}, u32[]{:S(2)}, u32[]{:S(2)}) %collective-permute-start.1) | collective-permute-done | bytes 4128 | tf_op jit(solution)/shard_map/ppermute | solution.py:232
  7.8 0.0 collective-permute-done.tgt_ref.refs_3_.refs_2_.refs_0_
  7.8 1.9 %near_rows.1 = (f32[1024,128]{1,0:T(8,128)S(1)}, f32[1,256]{1,0:T(1,128)S(1)}) custom-call(bf16[256,512]{1,0:T(8,128)(2,1)} %rows_ref.2, bf16[1024,512]{1,0:T(8,128)(2,1)S(1)} %collective-permute-done.tgt_ref.refs_3_.refs_2_.refs_0_, f32[1,1024]{1,0:T(1,128)S(1)} %collective-permute-done.1.offset_ref.refs_3_.refs_1_, f32[1,256]{1,0:T(1,128)S(1)} %get-tuple-element.42.held_ref), custom_call_target="tpu_custom_call" | custom-call | flops 268435456 | bytes 1048576 | tf_op jit(solution)/shard_map/near_rows/pallas_call | solution.py:285
  9.7 1.6 %far_rows.1 = f32[4,256]{1,0:T(4,128)S(1)} custom-call(bf16[256,512]{1,0:T(8,128)(2,1)S(1)} %collective-permute-done.2.refs_0_.rows_ref, bf16[1024,512]{1,0:T(8,128)(2,1)S(1)} %get-tuple-element.46.refs_1_.refs_0_, f32[1024,128]{1,0:T(8,128)S(1)} %get-tuple-element.47.refs_2_, bf16[1024,512]{1,0:T(8,128)(2,1)S(1)} %collective-permute-done.tgt_ref.refs_3_.refs_2_.refs_0_, ...), custom_call_target="tpu_custom_call" | custom-call | flops 536870912 | bytes 1048576 | tf_op jit(solution)/shard_map/far_rows/pallas_call | solution.py:297
  11.3 2.3 %collective-permute-start.5 = (f32[4,256]{1,0:T(4,128)S(1)}, f32[4,256]{1,0:T(4,128)S(1)}, u32[]{:S(2)}, u32[]{:S(2)}) collective-permute-start(f32[4,256]{1,0:T(4,128)S(1)} %far_rows.1), channel_id=1, source_target_pairs={{0,9},{1,8},{2,11},{3,10},{4,13},{5,12},{6,15},{7,14},{8,1},{9,0},... | collective-permute-start | bytes 12296 | tf_op jit(solution)/shard_map/ppermute | solution.py:331
  13.6 0.5 %collective-permute-start.4 = (f32[4,256]{1,0:T(4,128)S(1)}, f32[4,256]{1,0:T(4,128)S(1)}, u32[]{:S(2)}, u32[]{:S(2)}) collective-permute-start(f32[4,256]{1,0:T(4,128)S(1)} %far_rows.1), channel_id=1, source_target_pairs={{0,1},{1,0},{2,3},{3,2},{4,5},{5,4},{6,7},{7,6},{8,9},{9,8},{10,11... | collective-permute-start | bytes 12296 | tf_op jit(solution)/shard_map/ppermute | solution.py:238
  14.1 0.8 %collective-permute-start.3 = (f32[4,256]{1,0:T(4,128)S(1)}, f32[4,256]{1,0:T(4,128)S(1)}, u32[]{:S(2)}, u32[]{:S(2)}) collective-permute-start(f32[4,256]{1,0:T(4,128)S(1)} %far_rows.1), channel_id=1, source_target_pairs={{0,8},{4,12},{8,0},{12,4},{1,9},{5,13},{9,1},{13,5},{2,10},{6,14},... | collective-permute-start | bytes 12296 | tf_op jit(solution)/shard_map/ppermute | solution.py:235
  14.9 0.7 %logits.2 = (f32[256,1024]{1,0:T(8,128)S(1)}, f32[256,1024]{1,0:T(8,128)S(1)}) custom-call(bf16[256,512]{1,0:T(8,128)(2,1)S(1)} %collective-permute-done.2.refs_0_.rows_ref, bf16[1024,512]{1,0:T(8,128)(2,1)S(1)} %get-tuple-element.46.refs_1_.refs_0_, f32[1,1024]{1,0:T(1,128)S(1)} %get-tuple-element.41.refs_1_, ...), custom_call_target="tpu_custom_call" | custom-call | flops 536870912 | bytes 1048576 | tf_op jit(solution)/shard_map/logits/pallas_call | solution.py:310
  15.6 1.4 %logits.3.refs_0_ = f32[256,1024]{1,0:T(8,128)S(1)} custom-call(bf16[256,512]{1,0:T(8,128)(2,1)} %rows_ref.2, bf16[1024,512]{1,0:T(8,128)(2,1)S(1)} %collective-permute-done.tgt_ref.refs_3_.refs_2_.refs_0_, f32[1,1024]{1,0:T(1,128)S(1)} %collective-permute-done.1.offset_ref.refs_3_.refs_1_), custom_call_target="tpu_custom_call" | custom-call | flops 268435456 | bytes 1048576 | tf_op jit(solution)/shard_map/logits/pallas_call | solution.py:310
  17.1 0.6 %collective-permute-done.3 = f32[4,256]{1,0:T(4,128)S(1)} collective-permute-done((f32[4,256]{1,0:T(4,128)S(1)}, f32[4,256]{1,0:T(4,128)S(1)}, u32[]{:S(2)}, u32[]{:S(2)}) %collective-permute-start.3) | collective-permute-done | bytes 4128 | tf_op jit(solution)/shard_map/ppermute | solution.py:235
  17.7 2.7 %collective-permute-start.6 = (f32[2,256]{1,0:T(2,128)S(1)}, f32[2,256]{1,0:T(2,128)S(1)}, u32[]{:S(2)}, u32[]{:S(2)}) collective-permute-start(f32[2,256]{1,0:T(2,128)S(1)} %log_add_fusion.refs_2_), channel_id=1, source_target_pairs={{0,2},{1,3},{2,0},{3,1},{4,6},{5,7},{6,4},{7,5},{8,10},{9,11},{10,... | collective-permute-start | bytes 6152 | tf_op jit(solution)/shard_map/ppermute | solution.py:238
  20.4 1.9 %collective-permute-done.6.refs_3_ = f32[2,256]{1,0:T(2,128)S(1)} collective-permute-done((f32[2,256]{1,0:T(2,128)S(1)}, f32[2,256]{1,0:T(2,128)S(1)}, u32[]{:S(2)}, u32[]{:S(2)}) %collective-permute-start.6) | collective-permute-done | bytes 2080 | tf_op jit(solution)/shard_map/ppermute | solution.py:238
  22.3 0.5 %columns.3 = f32[8,128]{1,0:T(8,128)S(1)} custom-call(f32[256,1024]{1,0:T(8,128)S(1)} %logits.3.refs_0_, f32[256,1024]{1,0:T(8,128)S(1)} %get-tuple-element.55.refs_1_, f32[2,256]{1,0:T(2,128)S(1)} %log_add_fusion.refs_2_, f32[2,256]{1,0:T(2,128)S(1)} %collective-permute-done.6.refs_3_, f32[2,256]{1,0:T(2,128)S(1)} %get-tuple-element.63.refs_4_, ...), custom_call_target="tpu_custom_call" | custom-call | flops 3145728 | bytes 1048576 | tf_op jit(solution)/shard_map/columns/pallas_call | solution.py:349
  22.9 0.1 collective-permute-start.7
  23.0 0.0 copy-start
  23.0 0.0 copy-start.1
  23.0 0.0 copy-start.2
  23.0 1.1 %columns.5 = (f32[8,128]{1,0:T(8,128)S(1)}, f32[1,256]{1,0:T(1,128)}) custom-call(f32[256,1024]{1,0:T(8,128)S(1)} %get-tuple-element.40.refs_0_, f32[256,1024]{1,0:T(8,128)S(1)} %get-tuple-element.52.refs_1_, f32[2,256]{1,0:T(2,128)S(1)} %log_add_fusion.refs_2_, f32[2,256]{1,0:T(2,128)S(1)} %collective-permute-done.6.refs_3_, ...), custom_call_target="tpu_custom_call" | custom-call | flops 3145728 | bytes 1048576 | tf_op jit(solution)/shard_map/columns/pallas_call | solution.py:349
  24.2 0.6 %fusion = f32[1024]{0:T(1024)} fusion(f32[1024]{0:T(1024)S(1)} %copy-done.2, f32[8,128]{1,0:T(8,128)S(1)} %collective-permute-done.7, f32[8,128]{1,0:T(8,128)S(1)} %get-tuple-element.60, f32[1024]{0:T(1024)S(1)} %copy-done, f32[1024]{0:T(1024)S(1)} %copy-done.1), kind=kLoop, calls=%fused_computation.3 | loop fusion | flops 9216 | bytes 24576 | tf_op jit(solution)/shard_map/mul | solution.py:381
  (15 shorter events, 0.1 us)
Async XLA Ops:
  0.6 7.2 %collective-permute-start = (bf16[1024,512]{1,0:T(8,128)(2,1)}, bf16[1024,512]{1,0:T(8,128)(2,1)S(1)}, u32[]{:S(2)}, u32[]{:S(2)}) collective-permute-start(bf16[1024,512]{1,0:T(8,128)(2,1)} %refs_1_.3), channel_id=1, source_target_pairs={{0,4},{4,0},{8,12},{12,8},{1,5},{5,1},{9,13},{13,9},{2,6},{6,2},{1... | collective-permute-start | bytes 3145736 | tf_op jit(solution)/shard_map/ppermute | solution.py:232
  1.2 8.5 %collective-permute-start.2 = (bf16[256,512]{1,0:T(8,128)(2,1)}, bf16[256,512]{1,0:T(8,128)(2,1)S(1)}, u32[]{:S(2)}, u32[]{:S(2)}) collective-permute-start(bf16[256,512]{1,0:T(8,128)(2,1)} %rows_ref.2), channel_id=1, source_target_pairs={{0,8},{4,12},{8,0},{12,4},{1,9},{5,13},{9,1},{13,5},{2,10},{6,14},... | collective-permute-start | bytes 786440 | tf_op jit(solution)/shard_map/ppermute | solution.py:235
  6.6 1.3 %collective-permute-start.1 = (f32[1,1024]{1,0:T(1,128)S(1)}, f32[1,1024]{1,0:T(1,128)S(1)}, u32[]{:S(2)}, u32[]{:S(2)}) collective-permute-start(f32[1,1024]{1,0:T(1,128)S(1)} %get-tuple-element.41.refs_1_), channel_id=1, source_target_pairs={{0,4},{4,0},{8,12},{12,8},{1,5},{5,1},{9,13},{13,9},{2,6},{6,2},{1... | collective-permute-start | bytes 12296 | tf_op jit(solution)/shard_map/ppermute | solution.py:232
  11.3 5.7 %collective-permute-start.5 = (f32[4,256]{1,0:T(4,128)S(1)}, f32[4,256]{1,0:T(4,128)S(1)}, u32[]{:S(2)}, u32[]{:S(2)}) collective-permute-start(f32[4,256]{1,0:T(4,128)S(1)} %far_rows.1), channel_id=1, source_target_pairs={{0,9},{1,8},{2,11},{3,10},{4,13},{5,12},{6,15},{7,14},{8,1},{9,0},... | collective-permute-start | bytes 12296 | tf_op jit(solution)/shard_map/ppermute | solution.py:331
  13.6 4.1 %collective-permute-start.4 = (f32[4,256]{1,0:T(4,128)S(1)}, f32[4,256]{1,0:T(4,128)S(1)}, u32[]{:S(2)}, u32[]{:S(2)}) collective-permute-start(f32[4,256]{1,0:T(4,128)S(1)} %far_rows.1), channel_id=1, source_target_pairs={{0,1},{1,0},{2,3},{3,2},{4,5},{5,4},{6,7},{7,6},{8,9},{9,8},{10,11... | collective-permute-start | bytes 12296 | tf_op jit(solution)/shard_map/ppermute | solution.py:238
  14.1 3.6 %collective-permute-start.3 = (f32[4,256]{1,0:T(4,128)S(1)}, f32[4,256]{1,0:T(4,128)S(1)}, u32[]{:S(2)}, u32[]{:S(2)}) collective-permute-start(f32[4,256]{1,0:T(4,128)S(1)} %far_rows.1), channel_id=1, source_target_pairs={{0,8},{4,12},{8,0},{12,4},{1,9},{5,13},{9,1},{13,5},{2,10},{6,14},... | collective-permute-start | bytes 12296 | tf_op jit(solution)/shard_map/ppermute | solution.py:235
  17.7 4.6 %collective-permute-start.6 = (f32[2,256]{1,0:T(2,128)S(1)}, f32[2,256]{1,0:T(2,128)S(1)}, u32[]{:S(2)}, u32[]{:S(2)}) collective-permute-start(f32[2,256]{1,0:T(2,128)S(1)} %log_add_fusion.refs_2_), channel_id=1, source_target_pairs={{0,2},{1,3},{2,0},{3,1},{4,6},{5,7},{6,4},{7,5},{8,10},{9,11},{10,... | collective-permute-start | bytes 6152 | tf_op jit(solution)/shard_map/ppermute | solution.py:238
  22.9 1.3 %collective-permute-start.7 = (f32[8,128]{1,0:T(8,128)S(1)}, f32[8,128]{1,0:T(8,128)S(1)}, u32[]{:S(2)}, u32[]{:S(2)}) collective-permute-start(f32[8,128]{1,0:T(8,128)S(1)} %columns.3), channel_id=1, source_target_pairs={{0,4},{4,0},{8,12},{12,8},{1,5},{5,1},{9,13},{13,9},{2,6},{6,2},{1... | collective-permute-start | bytes 12296 | tf_op jit(solution)/shard_map/ppermute | solution.py:232
  23.0 1.2 %copy-start = (f32[1024]{0:T(1024)S(1)}, f32[1024]{0:T(1024)}, u32[]{:S(2)}) copy-start(f32[1024]{0:T(1024)} %param.9) | copy-start | bytes 12292
  23.0 1.2 %copy-start.1 = (f32[1024]{0:T(1024)S(1)}, f32[1024]{0:T(1024)}, u32[]{:S(2)}) copy-start(f32[1024]{0:T(1024)} %param.11) | copy-start | bytes 12292
  23.0 1.2 %copy-start.2 = (f32[1024]{0:T(1024)S(1)}, f32[1024]{0:T(1024)}, u32[]{:S(2)}) copy-start(f32[1024]{0:T(1024)} %param.13) | copy-start | bytes 12292

commit v21 on v19

--- a/solution.py
+++ b/solution.py
@@ -326,6 +326,18 @@
     def mirror(value, chip):
         return jnp.stack([value[slot ^ chip] for slot in range(chips)])
 
+    lse = merge(payload[:chips], along(payload, sets // 2)[:chips])
+    step = 2
+    while 2 * step < sets:
+        lse = merge(lse, along(lse, step))
+        step *= 2
+    chip = 2
+    while chip < chips:
+        lse = merge(lse, mirror(across(lse, chip), chip))
+        chip *= 2
+    payload = jnp.concatenate([lse, line])
+    payload, *zs = lax.optimization_barrier((payload, *own_zs, *pair_zs))
+    own_zs, pair_zs = zs[:chips], zs[chips:]
     other = across(payload, 1)
     beside = along(payload, 1)
     joined = lax.ppermute(
@@ -333,17 +345,9 @@
         ("blk", "tsplit"),
         [(b * sets + z, (b ^ 2) * sets + (z ^ 1)) for b in range(slabs) for z in range(sets)],
     )
-    lines = jnp.stack([line, other[chips:]] + moved[far:], axis=1)
-    lse = merge(payload[:chips], mirror(other, 1), beside[:chips], mirror(joined, 1))
-    chip = 2
-    while chip < chips:
-        lse = merge(lse, mirror(across(lse, chip), chip))
-        chip *= 2
-    step = 2
-    while 2 * step < sets:
-        lse = merge(lse, along(lse, step))
-        step *= 2
-    there = along(lse, step)
+    lines = jnp.stack([line, joined[chips:]] + moved[far:], axis=1)
+    lse = merge(lse, beside[:chips], mirror(joined, 1))
+    there = mirror(other, 1)
 
     def columns(kernel, zs, *more, outs=(f32(groups, LANES),)):
         return pl.pallas_call(

time: 24.5 us -> 25.5 us (1.041)
  starting transfers between devices: 10.1 us -> 11 us
    ppermute x2, waiting for transfers between devices: 1.88 us -> 0.01 us  [along(): return lax.ppermute(value, 'tsplit', [(i, i ^ step) for i in range(sets)])]
    ppermute x1, waiting for transfers between devices: 0.01 us -> 1.01 us  [shards(): lax.ppermute(payload, ('blk', 'tsplit'), [(b * sets + z, (b ^ 2) * sets +...]
    ppermute x2, waiting for transfers between devices: 1.22 us -> 2.07 us  [across(): return lax.ppermute(value, 'blk', [(i, i ^ 2 * chip) for i in range(slabs)])]
    ppermute x3, starting transfers between devices: 1.02 us -> 1.67 us  [pair(): return lax.ppermute(value, 'blk', [(i, i ^ 1) for i in range(slabs)])]
    ppermute x2, starting transfers between devices: 3.1 us -> 3.63 us  [along(): return lax.ppermute(value, 'tsplit', [(i, i ^ step) for i in range(sets)])]
    ppermute x1, starting transfers between devices: 3.13 us -> 2.6 us  [shards(): lax.ppermute(payload, ('blk', 'tsplit'), [(b * sets + z, (b ^ 2) * sets +...]
    ppermute x2, starting transfers between devices: 2.8 us -> 3.12 us  [across(): return lax.ppermute(value, 'blk', [(i, i ^ 2 * chip) for i in range(slabs)])]
  transfers between devices with their start and end apart: 8 -> 8, of which waited for: 3 -> 3; matrix products, arithmetic and copies ran while one was open for 0% -> 0% of each run, Pallas kernels for 30% -> 29%
where the time goes in v21:
time: 25.5 us; the launch traced here: 25.3 us
  starting transfers between devices  11 us (43%)
  Pallas kernels  8.85 us (35%)
  waiting for transfers between devices  3.92 us (15%)
  between operations  0.75 us (3%)
  other arithmetic  0.69 us (3%)
    ppermute x2, starting transfers between devices, along(): return lax.ppermute(value, 'tsplit', [(i, i ^ step) for i in range(sets)])  3.63 us
    ppermute x2, starting transfers between devices, across(): return lax.ppermute(value, 'blk', [(i, i ^ 2 * chip) for i in range(slabs)])  3.12 us
    ppermute x1, starting transfers between devices, shards(): lax.ppermute(payload, ('blk', 'tsplit'), [(b * sets + z, (b ^ 2) * sets +...  2.6 us
    pallas_call x2, Pallas kernels, prepare_on(): pl.pallas_call(functools.partial(prepare_kernel, turn), out_shape=(jax.Sh...  2.55 us
    pallas_call x2, Pallas kernels, logits(): pl.pallas_call(functools.partial(logits_kernel, len(sides) // 2), out_sha...  2.16 us
    ppermute x2, waiting for transfers between devices, across(): return lax.ppermute(value, 'blk', [(i, i ^ 2 * chip) for i in range(slabs)])  2.07 us
    pallas_call x3, Pallas kernels, columns(): pl.pallas_call(kernel, out_shape=outs, in_specs=[VMEM] * (chips + 4) + [S...  1.7 us
    ppermute x3, starting transfers between devices, pair(): return lax.ppermute(value, 'blk', [(i, i ^ 1) for i in range(slabs)])  1.67 us
  transfers between devices with their start and end apart: 8, of which 3 were waited for; matrix products, arithmetic and copies ran while one was open for 0% of the time, Pallas kernels for 29%

profile of v21, /device:TPU:0, one launch (start us, length us, event | category | flops | bytes accessed | tf_op | source)
XLA Modules:
  0.0 25.3 jit_solution(13691916123279537606)
XLA Ops:
  0.6 0.5 %collective-permute-start = (bf16[1024,512]{1,0:T(8,128)(2,1)}, bf16[1024,512]{1,0:T(8,128)(2,1)S(1)}, u32[]{:S(2)}, u32[]{:S(2)}) collective-permute-start(bf16[1024,512]{1,0:T(8,128)(2,1)} %refs_1_.3), channel_id=1, source_target_pairs={{0,4},{4,0},{8,12},{12,8},{1,5},{5,1},{9,13},{13,9},{2,6},{6,2},{1... | collective-permute-start | bytes 3145736 | tf_op jit(solution)/shard_map/ppermute | solution.py:232
  1.1 0.1 prepare_1.1
  1.2 2.6 %collective-permute-start.2 = (bf16[256,512]{1,0:T(8,128)(2,1)}, bf16[256,512]{1,0:T(8,128)(2,1)S(1)}, u32[]{:S(2)}, u32[]{:S(2)}) collective-permute-start(bf16[256,512]{1,0:T(8,128)(2,1)} %rows_ref.2), channel_id=1, source_target_pairs={{0,8},{4,12},{8,0},{12,4},{1,9},{5,13},{9,1},{13,5},{2,10},{6,14},... | collective-permute-start | bytes 786440 | tf_op jit(solution)/shard_map/ppermute | solution.py:235
  3.8 2.5 %prepare_0.1 = (bf16[1024,512]{1,0:T(8,128)(2,1)S(1)}, f32[1,1024]{1,0:T(1,128)S(1)}, f32[1024,128]{1,0:T(8,128)S(1)}, f32[256,1024]{1,0:T(8,128)S(1)}, f32[1,25...) custom-call(s32[1]{0:T(128)} %bitcast.core_ref.refs_6_, bf16[256,512]{1,0:T(8,128)(2,1)} %rows_ref.2, ...), custom_call_target="tpu_custom_call" | custom-call | flops 268435456 | bytes 1048576 | tf_op jit(solution)/shard_map/prepare_0/pallas_call | solution.py:260
  6.3 0.4 %collective-permute-start.1 = (f32[1,1024]{1,0:T(1,128)S(1)}, f32[1,1024]{1,0:T(1,128)S(1)}, u32[]{:S(2)}, u32[]{:S(2)}) collective-permute-start(f32[1,1024]{1,0:T(1,128)S(1)} %get-tuple-element.45.refs_1_), channel_id=1, source_target_pairs={{0,4},{4,0},{8,12},{12,8},{1,5},{5,1},{9,13},{13,9},{2,6},{6,2},{1... | collective-permute-start | bytes 12296 | tf_op jit(solution)/shard_map/ppermute | solution.py:232
  6.8 0.8 %collective-permute-done.1.offset_ref.refs_3_.refs_1_ = f32[1,1024]{1,0:T(1,128)S(1)} collective-permute-done((f32[1,1024]{1,0:T(1,128)S(1)}, f32[1,1024]{1,0:T(1,128)S(1)}, u32[]{:S(2)}, u32[]{:S(2)}) %collective-permute-start.1) | collective-permute-done | bytes 4128 | tf_op jit(solution)/shard_map/ppermute | solution.py:232
  7.6 0.0 collective-permute-done.tgt_ref.refs_3_.refs_2_.refs_0_
  7.6 1.5 %near_rows.1 = (f32[1024,128]{1,0:T(8,128)S(1)}, f32[1,256]{1,0:T(1,128)S(1)}) custom-call(bf16[256,512]{1,0:T(8,128)(2,1)} %rows_ref.2, bf16[1024,512]{1,0:T(8,128)(2,1)S(1)} %collective-permute-done.tgt_ref.refs_3_.refs_2_.refs_0_, f32[1,1024]{1,0:T(1,128)S(1)} %collective-permute-done.1.offset_ref.refs_3_.refs_1_, f32[1,256]{1,0:T(1,128)S(1)} %get-tuple-element.46.held_ref), custom_call_target="tpu_custom_call" | custom-call | flops 268435456 | bytes 1048576 | tf_op jit(solution)/shard_map/near_rows/pallas_call | solution.py:285
  9.1 0.0 collective-permute-done.2.refs_0_.rows_ref
  9.1 0.9 %far_rows.1 = f32[4,256]{1,0:T(4,128)S(1)} custom-call(bf16[256,512]{1,0:T(8,128)(2,1)S(1)} %collective-permute-done.2.refs_0_.rows_ref, bf16[1024,512]{1,0:T(8,128)(2,1)S(1)} %get-tuple-element.50.refs_1_.refs_0_, f32[1024,128]{1,0:T(8,128)S(1)} %get-tuple-element.51.refs_2_, bf16[1024,512]{1,0:T(8,128)(2,1)S(1)} %collective-permute-done.tgt_ref.refs_3_.refs_2_.refs_0_, ...), custom_call_target="tpu_custom_call" | custom-call | flops 536870912 | bytes 1048576 | tf_op jit(solution)/shard_map/far_rows/pallas_call | solution.py:297
  10.0 3.2 %collective-permute-start.3 = (f32[4,256]{1,0:T(4,128)S(1)}, f32[4,256]{1,0:T(4,128)S(1)}, u32[]{:S(2)}, u32[]{:S(2)}) collective-permute-start(f32[4,256]{1,0:T(4,128)S(1)} %far_rows.1), channel_id=1, source_target_pairs={{0,2},{1,3},{2,0},{3,1},{4,6},{5,7},{6,4},{7,5},{8,10},{9,11},{10,... | collective-permute-start | bytes 12296 | tf_op jit(solution)/shard_map/ppermute | solution.py:238
  13.2 0.7 %logits.2 = (f32[256,1024]{1,0:T(8,128)S(1)}, f32[256,1024]{1,0:T(8,128)S(1)}) custom-call(bf16[256,512]{1,0:T(8,128)(2,1)S(1)} %collective-permute-done.2.refs_0_.rows_ref, bf16[1024,512]{1,0:T(8,128)(2,1)S(1)} %get-tuple-element.50.refs_1_.refs_0_, f32[1,1024]{1,0:T(1,128)S(1)} %get-tuple-element.45.refs_1_, ...), custom_call_target="tpu_custom_call" | custom-call | flops 536870912 | bytes 1048576 | tf_op jit(solution)/shard_map/logits/pallas_call | solution.py:310
  14.0 1.4 %logits.3.refs_0_ = f32[256,1024]{1,0:T(8,128)S(1)} custom-call(bf16[256,512]{1,0:T(8,128)(2,1)} %rows_ref.2, bf16[1024,512]{1,0:T(8,128)(2,1)S(1)} %collective-permute-done.tgt_ref.refs_3_.refs_2_.refs_0_, f32[1,1024]{1,0:T(1,128)S(1)} %collective-permute-done.1.offset_ref.refs_3_.refs_1_), custom_call_target="tpu_custom_call" | custom-call | flops 268435456 | bytes 1048576 | tf_op jit(solution)/shard_map/logits/pallas_call | solution.py:310
  15.4 2.6 %collective-permute-start.5 = (f32[4,256]{1,0:T(4,128)S(1)}, f32[4,256]{1,0:T(4,128)S(1)}, u32[]{:S(2)}, u32[]{:S(2)}) collective-permute-start(f32[4,256]{1,0:T(4,128)S(1)} %pad_maximum_fusion), channel_id=1, source_target_pairs={{0,9},{1,8},{2,11},{3,10},{4,13},{5,12},{6,15},{7,14},{8,1},{9,0},... | collective-permute-start | bytes 12296 | tf_op jit(solution)/shard_map/ppermute | solution.py:343
  18.0 0.4 %collective-permute-start.4 = (f32[4,256]{1,0:T(4,128)S(1)}, f32[4,256]{1,0:T(4,128)S(1)}, u32[]{:S(2)}, u32[]{:S(2)}) collective-permute-start(f32[4,256]{1,0:T(4,128)S(1)} %pad_maximum_fusion), channel_id=1, source_target_pairs={{0,1},{1,0},{2,3},{3,2},{4,5},{5,4},{6,7},{7,6},{8,9},{9,8},{10,11... | collective-permute-start | bytes 12296 | tf_op jit(solution)/shard_map/ppermute | solution.py:238
  18.5 0.5 %collective-permute-start.6 = (f32[4,256]{1,0:T(4,128)S(1)}, f32[4,256]{1,0:T(4,128)S(1)}, u32[]{:S(2)}, u32[]{:S(2)}) collective-permute-start(f32[4,256]{1,0:T(4,128)S(1)} %pad_maximum_fusion), channel_id=1, source_target_pairs={{0,8},{4,12},{8,0},{12,4},{1,9},{5,13},{9,1},{13,5},{2,10},{6,14},... | collective-permute-start | bytes 12296 | tf_op jit(solution)/shard_map/ppermute | solution.py:235
  19.0 1.0 %collective-permute-done.5 = f32[4,256]{1,0:T(4,128)S(1)} collective-permute-done((f32[4,256]{1,0:T(4,128)S(1)}, f32[4,256]{1,0:T(4,128)S(1)}, u32[]{:S(2)}, u32[]{:S(2)}) %collective-permute-start.5) | collective-permute-done | bytes 4128 | tf_op jit(solution)/shard_map/ppermute | solution.py:343
  20.0 2.1 %collective-permute-done.6 = f32[4,256]{1,0:T(4,128)S(1)} collective-permute-done((f32[4,256]{1,0:T(4,128)S(1)}, f32[4,256]{1,0:T(4,128)S(1)}, u32[]{:S(2)}, u32[]{:S(2)}) %collective-permute-start.6) | collective-permute-done | bytes 4128 | tf_op jit(solution)/shard_map/ppermute | solution.py:235
  22.1 0.0 collective-permute-done.4
  22.2 0.5 %columns.3 = f32[8,128]{1,0:T(8,128)S(1)} custom-call(f32[256,1024]{1,0:T(8,128)S(1)} %logits.3.refs_0_, f32[256,1024]{1,0:T(8,128)S(1)} %get-tuple-element.65.refs_1_, f32[2,256]{1,0:T(2,128)S(1)} %log_add_fusion.refs_2_, f32[2,256]{1,0:T(2,128)S(1)} %pad_maximum_fusion.3.refs_3_, f32[2,256]{1,0:T(2,128)S(1)} %get-tuple-element.73.refs_4_, ...), custom_call_target="tpu_custom_call" | custom-call | flops 3145728 | bytes 1048576 | tf_op jit(solution)/shard_map/columns/pallas_call | solution.py:353
  22.8 0.7 %collective-permute-start.7 = (f32[8,128]{1,0:T(8,128)S(1)}, f32[8,128]{1,0:T(8,128)S(1)}, u32[]{:S(2)}, u32[]{:S(2)}) collective-permute-start(f32[8,128]{1,0:T(8,128)S(1)} %columns.3), channel_id=1, source_target_pairs={{0,4},{4,0},{8,12},{12,8},{1,5},{5,1},{9,13},{13,9},{2,6},{6,2},{1... | collective-permute-start | bytes 12296 | tf_op jit(solution)/shard_map/ppermute | solution.py:232
  23.5 1.1 %columns.5 = (f32[8,128]{1,0:T(8,128)S(1)}, f32[1,256]{1,0:T(1,128)}) custom-call(f32[256,1024]{1,0:T(8,128)S(1)} %get-tuple-element.61.refs_0_, f32[256,1024]{1,0:T(8,128)S(1)} %get-tuple-element.62.refs_1_, f32[2,256]{1,0:T(2,128)S(1)} %log_add_fusion.refs_2_, f32[2,256]{1,0:T(2,128)S(1)} %pad_maximum_fusion.3.refs_3_, ...), custom_call_target="tpu_custom_call" | custom-call | flops 3145728 | bytes 1048576 | tf_op jit(solution)/shard_map/columns/pallas_call | solution.py:353
  24.6 0.0 collective-permute-done.7
  24.6 0.6 %fusion = f32[1024]{0:T(1024)} fusion(f32[1024]{0:T(1024)S(1)} %copy-done.2, f32[8,128]{1,0:T(8,128)S(1)} %collective-permute-done.7, f32[8,128]{1,0:T(8,128)S(1)} %get-tuple-element.70, f32[1024]{0:T(1024)S(1)} %copy-done, f32[1024]{0:T(1024)S(1)} %copy-done.1), kind=kLoop, calls=%fused_computation.4 | loop fusion | flops 9216 | bytes 24576 | tf_op jit(solution)/shard_map/mul | solution.py:385
  (18 shorter events, 0.1 us)
Async XLA Ops:
  0.6 7.0 %collective-permute-start = (bf16[1024,512]{1,0:T(8,128)(2,1)}, bf16[1024,512]{1,0:T(8,128)(2,1)S(1)}, u32[]{:S(2)}, u32[]{:S(2)}) collective-permute-start(bf16[1024,512]{1,0:T(8,128)(2,1)} %refs_1_.3), channel_id=1, source_target_pairs={{0,4},{4,0},{8,12},{12,8},{1,5},{5,1},{9,13},{13,9},{2,6},{6,2},{1... | collective-permute-start | bytes 3145736 | tf_op jit(solution)/shard_map/ppermute | solution.py:232
  1.2 7.9 %collective-permute-start.2 = (bf16[256,512]{1,0:T(8,128)(2,1)}, bf16[256,512]{1,0:T(8,128)(2,1)S(1)}, u32[]{:S(2)}, u32[]{:S(2)}) collective-permute-start(bf16[256,512]{1,0:T(8,128)(2,1)} %rows_ref.2), channel_id=1, source_target_pairs={{0,8},{4,12},{8,0},{12,4},{1,9},{5,13},{9,1},{13,5},{2,10},{6,14},... | collective-permute-start | bytes 786440 | tf_op jit(solution)/shard_map/ppermute | solution.py:235
  6.3 1.3 %collective-permute-start.1 = (f32[1,1024]{1,0:T(1,128)S(1)}, f32[1,1024]{1,0:T(1,128)S(1)}, u32[]{:S(2)}, u32[]{:S(2)}) collective-permute-start(f32[1,1024]{1,0:T(1,128)S(1)} %get-tuple-element.45.refs_1_), channel_id=1, source_target_pairs={{0,4},{4,0},{8,12},{12,8},{1,5},{5,1},{9,13},{13,9},{2,6},{6,2},{1... | collective-permute-start | bytes 12296 | tf_op jit(solution)/shard_map/ppermute | solution.py:232
  10.0 5.4 %collective-permute-start.3 = (f32[4,256]{1,0:T(4,128)S(1)}, f32[4,256]{1,0:T(4,128)S(1)}, u32[]{:S(2)}, u32[]{:S(2)}) collective-permute-start(f32[4,256]{1,0:T(4,128)S(1)} %far_rows.1), channel_id=1, source_target_pairs={{0,2},{1,3},{2,0},{3,1},{4,6},{5,7},{6,4},{7,5},{8,10},{9,11},{10,... | collective-permute-start | bytes 12296 | tf_op jit(solution)/shard_map/ppermute | solution.py:238
  15.4 4.6 %collective-permute-start.5 = (f32[4,256]{1,0:T(4,128)S(1)}, f32[4,256]{1,0:T(4,128)S(1)}, u32[]{:S(2)}, u32[]{:S(2)}) collective-permute-start(f32[4,256]{1,0:T(4,128)S(1)} %pad_maximum_fusion), channel_id=1, source_target_pairs={{0,9},{1,8},{2,11},{3,10},{4,13},{5,12},{6,15},{7,14},{8,1},{9,0},... | collective-permute-start | bytes 12296 | tf_op jit(solution)/shard_map/ppermute | solution.py:343
  18.0 4.1 %collective-permute-start.4 = (f32[4,256]{1,0:T(4,128)S(1)}, f32[4,256]{1,0:T(4,128)S(1)}, u32[]{:S(2)}, u32[]{:S(2)}) collective-permute-start(f32[4,256]{1,0:T(4,128)S(1)} %pad_maximum_fusion), channel_id=1, source_target_pairs={{0,1},{1,0},{2,3},{3,2},{4,5},{5,4},{6,7},{7,6},{8,9},{9,8},{10,11... | collective-permute-start | bytes 12296 | tf_op jit(solution)/shard_map/ppermute | solution.py:238
  18.5 3.6 %collective-permute-start.6 = (f32[4,256]{1,0:T(4,128)S(1)}, f32[4,256]{1,0:T(4,128)S(1)}, u32[]{:S(2)}, u32[]{:S(2)}) collective-permute-start(f32[4,256]{1,0:T(4,128)S(1)} %pad_maximum_fusion), channel_id=1, source_target_pairs={{0,8},{4,12},{8,0},{12,4},{1,9},{5,13},{9,1},{13,5},{2,10},{6,14},... | collective-permute-start | bytes 12296 | tf_op jit(solution)/shard_map/ppermute | solution.py:235
  22.8 1.9 %collective-permute-start.7 = (f32[8,128]{1,0:T(8,128)S(1)}, f32[8,128]{1,0:T(8,128)S(1)}, u32[]{:S(2)}, u32[]{:S(2)}) collective-permute-start(f32[8,128]{1,0:T(8,128)S(1)} %columns.3), channel_id=1, source_target_pairs={{0,4},{4,0},{8,12},{12,8},{1,5},{5,1},{9,13},{13,9},{2,6},{6,2},{1... | collective-permute-start | bytes 12296 | tf_op jit(solution)/shard_map/ppermute | solution.py:232
  23.5 1.1 %copy-start = (f32[1024]{0:T(1024)S(1)}, f32[1024]{0:T(1024)}, u32[]{:S(2)}) copy-start(f32[1024]{0:T(1024)} %param.9) | copy-start | bytes 12292
  23.5 1.2 %copy-start.1 = (f32[1024]{0:T(1024)S(1)}, f32[1024]{0:T(1024)}, u32[]{:S(2)}) copy-start(f32[1024]{0:T(1024)} %param.11) | copy-start | bytes 12292
  23.5 1.2 %copy-start.2 = (f32[1024]{0:T(1024)S(1)}, f32[1024]{0:T(1024)}, u32[]{:S(2)}) copy-start(f32[1024]{0:T(1024)} %param.13) | copy-start | bytes 12292

commit v22 on v19

--- a/solution.py
+++ b/solution.py
@@ -152,13 +152,18 @@
 
 def far_kernel(count, *refs):
     own_ref, own_column_ref, pair_ref, pair_column_ref, held_ref, line_ref = refs[count : count + 6]
-    out_ref, z_ref = refs[count + 6 :]
+    out_ref, mirrored_ref, z_ref = refs[count + 6 :]
     slots = count + 1
-    out_ref[0:1, :] = held_ref[...]
-    out_ref[slots : slots + 2, :] = line_ref[...]
-    for slot in range(count):
-        sides = ((own_ref, own_column_ref), (pair_ref, pair_column_ref))
-        out_ref[slot + 1 : slot + 2, :] = row_sums(refs[slot][...], sides, z_ref)
+    for ref in (out_ref, mirrored_ref):
+        ref[slots : slots + 2, :] = line_ref[...]
+    for slot in range(slots):
+        if slot == 0:
+            lse = held_ref[...]
+        else:
+            sides = ((own_ref, own_column_ref), (pair_ref, pair_column_ref))
+            lse = row_sums(refs[slot - 1][...], sides, z_ref)
+        out_ref[slot : slot + 1, :] = lse
+        mirrored_ref[slot ^ 1 : (slot ^ 1) + 1, :] = lse
 
 
 def sum_columns(z_refs, offset, out_ref, off_ref, peak_ref, mass_ref):
@@ -294,18 +299,18 @@
     )(sources, pair_targets, pair_offset, lse)
     far_lines = [across(line, chip) for chip in range(2, chips)]
     lse, *moved = lax.optimization_barrier((lse, *far_blocks, *far_lines))
-    payload = pl.pallas_call(
+    payload, mirrored = pl.pallas_call(
         functools.partial(far_kernel, far),
-        out_shape=f32(chips + 2, src_count),
+        out_shape=(f32(chips + 2, src_count),) * 2,
         in_specs=[VMEM] * (far + 6),
-        out_specs=VMEM,
+        out_specs=(VMEM,) * 2,
         scratch_shapes=[product_space],
         compiler_params=params(12 + far),
         cost_estimate=cost(2 * far),
         name="far_rows",
     )(*moved[:far], held, column, pair_targets, pair_column, lse, line)
 
-    payload, *blocks = lax.optimization_barrier((payload, sources, *moved[:far]))
+    payload, mirrored, *blocks = lax.optimization_barrier((payload, mirrored, sources, *moved[:far]))
     def logits(block, *sides):
         return pl.pallas_call(
             functools.partial(logits_kernel, len(sides) // 2),
@@ -326,15 +331,15 @@
     def mirror(value, chip):
         return jnp.stack([value[slot ^ chip] for slot in range(chips)])
 
-    other = across(payload, 1)
+    other = across(mirrored, 1)
     beside = along(payload, 1)
     joined = lax.ppermute(
         payload,
         ("blk", "tsplit"),
         [(b * sets + z, (b ^ 2) * sets + (z ^ 1)) for b in range(slabs) for z in range(sets)],
     )
-    lines = jnp.stack([line, other[chips:]] + moved[far:], axis=1)
-    lse = merge(payload[:chips], mirror(other, 1), beside[:chips], mirror(joined, 1))
+    lines = jnp.stack([line, joined[chips:]] + moved[far:], axis=1)
+    lse = merge(payload[:chips], other[:chips], beside[:chips], mirror(joined, 1))
     chip = 2
     while chip < chips:
         lse = merge(lse, mirror(across(lse, chip), chip))

time: 24.5 us -> 24.5 us (level)
  no operation moved by 1% of the time
where the time goes in v22:
time: 24.5 us; the launch traced here: 24.3 us
  starting transfers between devices  10.1 us (41%)
  Pallas kernels  8.85 us (36%)
  waiting for transfers between devices  3.91 us (16%)
  between operations  0.77 us (3%)
  other arithmetic  0.65 us (3%)
    ppermute x1, starting transfers between devices, shards(): lax.ppermute(payload, ('blk', 'tsplit'), [(b * sets + z, (b ^ 2) * sets +...  3.13 us
    ppermute x2, starting transfers between devices, along(): return lax.ppermute(value, 'tsplit', [(i, i ^ step) for i in range(sets)])  3.1 us
    ppermute x2, starting transfers between devices, across(): return lax.ppermute(value, 'blk', [(i, i ^ 2 * chip) for i in range(slabs)])  2.8 us
    pallas_call x2, Pallas kernels, prepare_on(): pl.pallas_call(functools.partial(prepare_kernel, turn), out_shape=(jax.Sh...  2.55 us
    pallas_call x2, Pallas kernels, logits(): pl.pallas_call(functools.partial(logits_kernel, len(sides) // 2), out_sha...  2.16 us
    ppermute x2, waiting for transfers between devices, along(): return lax.ppermute(value, 'tsplit', [(i, i ^ step) for i in range(sets)])  1.89 us
    pallas_call x3, Pallas kernels, columns(): pl.pallas_call(kernel, out_shape=outs, in_specs=[VMEM] * (chips + 4) + [S...  1.71 us
    pallas_call x1, Pallas kernels, shards(): pl.pallas_call(near_kernel, out_shape=(f32(tgt_count, LANES), f32(1, src_...  1.54 us
  transfers between devices with their start and end apart: 8, of which 3 were waited for; matrix products, arithmetic and copies ran while one was open for 0% of the time, Pallas kernels for 30%

profile of v22, /device:TPU:0, one launch (start us, length us, event | category | flops | bytes accessed | tf_op | source)
XLA Modules:
  0.0 24.3 jit_solution(70511312087305399)
XLA Ops:
  0.6 0.5 %collective-permute-start = (bf16[1024,512]{1,0:T(8,128)(2,1)}, bf16[1024,512]{1,0:T(8,128)(2,1)S(1)}, u32[]{:S(2)}, u32[]{:S(2)}) collective-permute-start(bf16[1024,512]{1,0:T(8,128)(2,1)} %refs_1_.3), channel_id=1, source_target_pairs={{0,4},{4,0},{8,12},{12,8},{1,5},{5,1},{9,13},{13,9},{2,6},{6,2},{1... | collective-permute-start | bytes 3145736 | tf_op jit(solution)/shard_map/ppermute | solution.py:237
  1.1 0.1 prepare_1.1
  1.2 2.6 %collective-permute-start.2 = (bf16[256,512]{1,0:T(8,128)(2,1)}, bf16[256,512]{1,0:T(8,128)(2,1)S(1)}, u32[]{:S(2)}, u32[]{:S(2)}) collective-permute-start(bf16[256,512]{1,0:T(8,128)(2,1)} %rows_ref.2), channel_id=1, source_target_pairs={{0,8},{4,12},{8,0},{12,4},{1,9},{5,13},{9,1},{13,5},{2,10},{6,14},... | collective-permute-start | bytes 786440 | tf_op jit(solution)/shard_map/ppermute | solution.py:240
  3.8 2.5 %prepare_0.1 = (bf16[1024,512]{1,0:T(8,128)(2,1)S(1)}, f32[1,1024]{1,0:T(1,128)S(1)}, f32[1024,128]{1,0:T(8,128)S(1)}, f32[256,1024]{1,0:T(8,128)S(1)}, f32[1,25...) custom-call(s32[1]{0:T(128)} %bitcast.core_ref.refs_6_, bf16[256,512]{1,0:T(8,128)(2,1)} %rows_ref.2, ...), custom_call_target="tpu_custom_call" | custom-call | flops 268435456 | bytes 1048576 | tf_op jit(solution)/shard_map/prepare_0/pallas_call | solution.py:265
  6.3 0.4 %collective-permute-start.1 = (f32[1,1024]{1,0:T(1,128)S(1)}, f32[1,1024]{1,0:T(1,128)S(1)}, u32[]{:S(2)}, u32[]{:S(2)}) collective-permute-start(f32[1,1024]{1,0:T(1,128)S(1)} %get-tuple-element.44.refs_1_), channel_id=1, source_target_pairs={{0,4},{4,0},{8,12},{12,8},{1,5},{5,1},{9,13},{13,9},{2,6},{6,2},{1... | collective-permute-start | bytes 12296 | tf_op jit(solution)/shard_map/ppermute | solution.py:237
  6.8 0.8 %collective-permute-done.1.offset_ref.refs_3_.refs_1_ = f32[1,1024]{1,0:T(1,128)S(1)} collective-permute-done((f32[1,1024]{1,0:T(1,128)S(1)}, f32[1,1024]{1,0:T(1,128)S(1)}, u32[]{:S(2)}, u32[]{:S(2)}) %collective-permute-start.1) | collective-permute-done | bytes 4128 | tf_op jit(solution)/shard_map/ppermute | solution.py:237
  7.6 1.5 %near_rows.1 = (f32[1024,128]{1,0:T(8,128)S(1)}, f32[1,256]{1,0:T(1,128)S(1)}) custom-call(bf16[256,512]{1,0:T(8,128)(2,1)} %rows_ref.2, bf16[1024,512]{1,0:T(8,128)(2,1)S(1)} %collective-permute-done.tgt_ref.refs_3_.refs_2_.refs_0_, f32[1,1024]{1,0:T(1,128)S(1)} %collective-permute-done.1.offset_ref.refs_3_.refs_1_, f32[1,256]{1,0:T(1,128)S(1)} %get-tuple-element.45.held_ref), custom_call_target="tpu_custom_call" | custom-call | flops 268435456 | bytes 1048576 | tf_op jit(solution)/shard_map/near_rows/pallas_call | solution.py:290
  9.1 0.0 collective-permute-done.2.refs_0_.rows_ref
  9.1 0.9 %far_rows.1 = (f32[4,256]{1,0:T(4,128)S(1)}, f32[4,256]{1,0:T(4,128)S(1)}) custom-call(bf16[256,512]{1,0:T(8,128)(2,1)S(1)} %collective-permute-done.2.refs_0_.rows_ref, bf16[1024,512]{1,0:T(8,128)(2,1)S(1)} %get-tuple-element.49.refs_1_.refs_0_, f32[1024,128]{1,0:T(8,128)S(1)} %get-tuple-element.50.refs_2_, ...), custom_call_target="tpu_custom_call" | custom-call | flops 536870912 | bytes 1048576 | tf_op jit(solution)/shard_map/far_rows/pallas_call | solution.py:302
  10.0 3.1 %collective-permute-start.5 = (f32[4,256]{1,0:T(4,128)S(1)}, f32[4,256]{1,0:T(4,128)S(1)}, u32[]{:S(2)}, u32[]{:S(2)}) collective-permute-start(f32[4,256]{1,0:T(4,128)S(1)} %get-tuple-element.58), channel_id=1, source_target_pairs={{0,9},{1,8},{2,11},{3,10},{4,13},{5,12},{6,15},{7,14},{8,1},{9,0},... | collective-permute-start | bytes 12296 | tf_op jit(solution)/shard_map/ppermute | solution.py:336
  13.2 0.4 %collective-permute-start.4 = (f32[4,256]{1,0:T(4,128)S(1)}, f32[4,256]{1,0:T(4,128)S(1)}, u32[]{:S(2)}, u32[]{:S(2)}) collective-permute-start(f32[4,256]{1,0:T(4,128)S(1)} %get-tuple-element.58), channel_id=1, source_target_pairs={{0,1},{1,0},{2,3},{3,2},{4,5},{5,4},{6,7},{7,6},{8,9},{9,8},{10,11... | collective-permute-start | bytes 12296 | tf_op jit(solution)/shard_map/ppermute | solution.py:243
  13.6 0.2 collective-permute-start.3
  13.8 0.7 %logits.2 = (f32[256,1024]{1,0:T(8,128)S(1)}, f32[256,1024]{1,0:T(8,128)S(1)}) custom-call(bf16[256,512]{1,0:T(8,128)(2,1)S(1)} %collective-permute-done.2.refs_0_.rows_ref, bf16[1024,512]{1,0:T(8,128)(2,1)S(1)} %get-tuple-element.49.refs_1_.refs_0_, f32[1,1024]{1,0:T(1,128)S(1)} %get-tuple-element.44.refs_1_, ...), custom_call_target="tpu_custom_call" | custom-call | flops 536870912 | bytes 1048576 | tf_op jit(solution)/shard_map/logits/pallas_call | solution.py:315
  14.6 1.4 %logits.3.refs_0_ = f32[256,1024]{1,0:T(8,128)S(1)} custom-call(bf16[256,512]{1,0:T(8,128)(2,1)} %rows_ref.2, bf16[1024,512]{1,0:T(8,128)(2,1)S(1)} %collective-permute-done.tgt_ref.refs_3_.refs_2_.refs_0_, f32[1,1024]{1,0:T(1,128)S(1)} %collective-permute-done.1.offset_ref.refs_3_.refs_1_), custom_call_target="tpu_custom_call" | custom-call | flops 268435456 | bytes 1048576 | tf_op jit(solution)/shard_map/logits/pallas_call | solution.py:315
  16.0 1.2 %collective-permute-done.3 = f32[4,256]{1,0:T(4,128)S(1)} collective-permute-done((f32[4,256]{1,0:T(4,128)S(1)}, f32[4,256]{1,0:T(4,128)S(1)}, u32[]{:S(2)}, u32[]{:S(2)}) %collective-permute-start.3) | collective-permute-done | bytes 4128 | tf_op jit(solution)/shard_map/ppermute | solution.py:240
  17.3 2.7 %collective-permute-start.6 = (f32[2,256]{1,0:T(2,128)S(1)}, f32[2,256]{1,0:T(2,128)S(1)}, u32[]{:S(2)}, u32[]{:S(2)}) collective-permute-start(f32[2,256]{1,0:T(2,128)S(1)} %log_add_fusion.refs_2_), channel_id=1, source_target_pairs={{0,2},{1,3},{2,0},{3,1},{4,6},{5,7},{6,4},{7,5},{8,10},{9,11},{10,... | collective-permute-start | bytes 6152 | tf_op jit(solution)/shard_map/ppermute | solution.py:243
  19.9 1.9 %collective-permute-done.6.refs_3_ = f32[2,256]{1,0:T(2,128)S(1)} collective-permute-done((f32[2,256]{1,0:T(2,128)S(1)}, f32[2,256]{1,0:T(2,128)S(1)}, u32[]{:S(2)}, u32[]{:S(2)}) %collective-permute-start.6) | collective-permute-done | bytes 2080 | tf_op jit(solution)/shard_map/ppermute | solution.py:243
  21.8 0.6 %columns.3 = f32[8,128]{1,0:T(8,128)S(1)} custom-call(f32[256,1024]{1,0:T(8,128)S(1)} %logits.3.refs_0_, f32[256,1024]{1,0:T(8,128)S(1)} %get-tuple-element.61.refs_1_, f32[2,256]{1,0:T(2,128)S(1)} %log_add_fusion.refs_2_, f32[2,256]{1,0:T(2,128)S(1)} %collective-permute-done.6.refs_3_, f32[2,256]{1,0:T(2,128)S(1)} %get-tuple-element.69.refs_4_, ...), custom_call_target="tpu_custom_call" | custom-call | flops 3145728 | bytes 1048576 | tf_op jit(solution)/shard_map/columns/pallas_call | solution.py:354
  22.4 0.1 collective-permute-start.7
  22.5 0.0 copy-start
  22.5 0.0 copy-start.1
  22.5 0.0 copy-start.2
  22.5 1.1 %columns.5 = (f32[8,128]{1,0:T(8,128)S(1)}, f32[1,256]{1,0:T(1,128)}) custom-call(f32[256,1024]{1,0:T(8,128)S(1)} %get-tuple-element.43.refs_0_, f32[256,1024]{1,0:T(8,128)S(1)} %get-tuple-element.57.refs_1_, f32[2,256]{1,0:T(2,128)S(1)} %log_add_fusion.refs_2_, f32[2,256]{1,0:T(2,128)S(1)} %collective-permute-done.6.refs_3_, ...), custom_call_target="tpu_custom_call" | custom-call | flops 3145728 | bytes 1048576 | tf_op jit(solution)/shard_map/columns/pallas_call | solution.py:354
  23.7 0.6 %fusion = f32[1024]{0:T(1024)} fusion(f32[1024]{0:T(1024)S(1)} %copy-done.2, f32[8,128]{1,0:T(8,128)S(1)} %collective-permute-done.7, f32[8,128]{1,0:T(8,128)S(1)} %get-tuple-element.66, f32[1024]{0:T(1024)S(1)} %copy-done, f32[1024]{0:T(1024)S(1)} %copy-done.1), kind=kLoop, calls=%fused_computation.3 | loop fusion | flops 9216 | bytes 24576 | tf_op jit(solution)/shard_map/mul | solution.py:386
  (14 shorter events, 0.1 us)
Async XLA Ops:
  0.6 7.0 %collective-permute-start = (bf16[1024,512]{1,0:T(8,128)(2,1)}, bf16[1024,512]{1,0:T(8,128)(2,1)S(1)}, u32[]{:S(2)}, u32[]{:S(2)}) collective-permute-start(bf16[1024,512]{1,0:T(8,128)(2,1)} %refs_1_.3), channel_id=1, source_target_pairs={{0,4},{4,0},{8,12},{12,8},{1,5},{5,1},{9,13},{13,9},{2,6},{6,2},{1... | collective-permute-start | bytes 3145736 | tf_op jit(solution)/shard_map/ppermute | solution.py:237
  1.2 7.9 %collective-permute-start.2 = (bf16[256,512]{1,0:T(8,128)(2,1)}, bf16[256,512]{1,0:T(8,128)(2,1)S(1)}, u32[]{:S(2)}, u32[]{:S(2)}) collective-permute-start(bf16[256,512]{1,0:T(8,128)(2,1)} %rows_ref.2), channel_id=1, source_target_pairs={{0,8},{4,12},{8,0},{12,4},{1,9},{5,13},{9,1},{13,5},{2,10},{6,14},... | collective-permute-start | bytes 786440 | tf_op jit(solution)/shard_map/ppermute | solution.py:240
  6.3 1.3 %collective-permute-start.1 = (f32[1,1024]{1,0:T(1,128)S(1)}, f32[1,1024]{1,0:T(1,128)S(1)}, u32[]{:S(2)}, u32[]{:S(2)}) collective-permute-start(f32[1,1024]{1,0:T(1,128)S(1)} %get-tuple-element.44.refs_1_), channel_id=1, source_target_pairs={{0,4},{4,0},{8,12},{12,8},{1,5},{5,1},{9,13},{13,9},{2,6},{6,2},{1... | collective-permute-start | bytes 12296 | tf_op jit(solution)/shard_map/ppermute | solution.py:237
  10.0 5.9 %collective-permute-start.5 = (f32[4,256]{1,0:T(4,128)S(1)}, f32[4,256]{1,0:T(4,128)S(1)}, u32[]{:S(2)}, u32[]{:S(2)}) collective-permute-start(f32[4,256]{1,0:T(4,128)S(1)} %get-tuple-element.58), channel_id=1, source_target_pairs={{0,9},{1,8},{2,11},{3,10},{4,13},{5,12},{6,15},{7,14},{8,1},{9,0},... | collective-permute-start | bytes 12296 | tf_op jit(solution)/shard_map/ppermute | solution.py:336
  13.2 4.1 %collective-permute-start.4 = (f32[4,256]{1,0:T(4,128)S(1)}, f32[4,256]{1,0:T(4,128)S(1)}, u32[]{:S(2)}, u32[]{:S(2)}) collective-permute-start(f32[4,256]{1,0:T(4,128)S(1)} %get-tuple-element.58), channel_id=1, source_target_pairs={{0,1},{1,0},{2,3},{3,2},{4,5},{5,4},{6,7},{7,6},{8,9},{9,8},{10,11... | collective-permute-start | bytes 12296 | tf_op jit(solution)/shard_map/ppermute | solution.py:243
  13.6 3.6 %collective-permute-start.3 = (f32[4,256]{1,0:T(4,128)S(1)}, f32[4,256]{1,0:T(4,128)S(1)}, u32[]{:S(2)}, u32[]{:S(2)}) collective-permute-start(f32[4,256]{1,0:T(4,128)S(1)} %get-tuple-element.59), channel_id=1, source_target_pairs={{0,8},{4,12},{8,0},{12,4},{1,9},{5,13},{9,1},{13,5},{2,10},{6,14},... | collective-permute-start | bytes 12296 | tf_op jit(solution)/shard_map/ppermute | solution.py:240
  17.3 4.5 %collective-permute-start.6 = (f32[2,256]{1,0:T(2,128)S(1)}, f32[2,256]{1,0:T(2,128)S(1)}, u32[]{:S(2)}, u32[]{:S(2)}) collective-permute-start(f32[2,256]{1,0:T(2,128)S(1)} %log_add_fusion.refs_2_), channel_id=1, source_target_pairs={{0,2},{1,3},{2,0},{3,1},{4,6},{5,7},{6,4},{7,5},{8,10},{9,11},{10,... | collective-permute-start | bytes 6152 | tf_op jit(solution)/shard_map/ppermute | solution.py:243
  22.4 1.3 %collective-permute-start.7 = (f32[8,128]{1,0:T(8,128)S(1)}, f32[8,128]{1,0:T(8,128)S(1)}, u32[]{:S(2)}, u32[]{:S(2)}) collective-permute-start(f32[8,128]{1,0:T(8,128)S(1)} %columns.3), channel_id=1, source_target_pairs={{0,4},{4,0},{8,12},{12,8},{1,5},{5,1},{9,13},{13,9},{2,6},{6,2},{1... | collective-permute-start | bytes 12296 | tf_op jit(solution)/shard_map/ppermute | solution.py:237
  22.5 1.2 %copy-start = (f32[1024]{0:T(1024)S(1)}, f32[1024]{0:T(1024)}, u32[]{:S(2)}) copy-start(f32[1024]{0:T(1024)} %param.9) | copy-start | bytes 12292
  22.5 1.2 %copy-start.1 = (f32[1024]{0:T(1024)S(1)}, f32[1024]{0:T(1024)}, u32[]{:S(2)}) copy-start(f32[1024]{0:T(1024)} %param.11) | copy-start | bytes 12292
  22.5 1.2 %copy-start.2 = (f32[1024]{0:T(1024)S(1)}, f32[1024]{0:T(1024)}, u32[]{:S(2)}) copy-start(f32[1024]{0:T(1024)} %param.13) | copy-start | bytes 12292

commit v23 on v19

--- a/solution.py
+++ b/solution.py
@@ -169,15 +169,19 @@
             column = to_column(offset[slot : slot + 1, at : at + LANES] * LOG2_E, eye)
             off_ref[slot, at : at + LANES, :] = jnp.broadcast_to(column, (LANES, LANES))
 
-    for group in range(out_ref.shape[0]):
-        cols = slice(group * LANES, (group + 1) * LANES)
-        for slot in range(slots):
-            z = (z_refs[slot][:, cols] + off_ref[slot]).reshape(src_count // 8, 8, LANES)
+    parts = [(slot, at) for slot in range(slots) for at in range(0, src_count, LANES)]
+    for left in range(0, z_refs[0].shape[1], CHUNK):
+        cols = slice(left, left + CHUNK)
+        for part, (slot, at) in enumerate(parts):
+            rows = slice(at, at + LANES)
+            offsets = jnp.concatenate([off_ref[slot, rows, :]] * (CHUNK // LANES), axis=1)
+            z = (z_refs[slot][rows, cols] + offsets).reshape(LANES // 8, 8, CHUNK)
             peak = jnp.max(z, axis=0)
-            peak_ref[slot, :, cols] = peak
-            mass_ref[slot, :, cols] = jnp.sum(jnp.exp2(z - peak), axis=0)
-    peak = jnp.max(functools.reduce(jnp.maximum, [peak_ref[slot] for slot in range(slots)]), axis=0, keepdims=True)
-    mass = sum(mass_ref[slot] * jnp.exp2(peak_ref[slot] - peak) for slot in range(slots))
+            peak_ref[part, :, cols] = peak
+            mass_ref[part, :, cols] = jnp.sum(jnp.exp2(z - peak), axis=0)
+    every = range(len(parts))
+    peak = jnp.max(functools.reduce(jnp.maximum, [peak_ref[part] for part in every]), axis=0, keepdims=True)
+    mass = sum(mass_ref[part] * jnp.exp2(peak_ref[part] - peak) for part in every)
     total = peak * LOG_2 + jnp.log(jnp.sum(mass, axis=0, keepdims=True))
     for group in range(out_ref.shape[0]):
         out_ref[group : group + 1, :] = total[:, group * LANES : (group + 1) * LANES]
@@ -353,8 +357,8 @@
             out_specs=(VMEM,) * len(outs),
             scratch_shapes=[
                 pltpu.VMEM((chips, src_count, LANES), jnp.float32),
-                pltpu.VMEM((chips, 8, tgt_count), jnp.float32),
-                pltpu.VMEM((chips, 8, tgt_count), jnp.float32),
+                pltpu.VMEM((chips * src_groups, 8, tgt_count), jnp.float32),
+                pltpu.VMEM((chips * src_groups, 8, tgt_count), jnp.float32),
             ],
             compiler_params=params(8 + 2 * chips),
             cost_estimate=pl.CostEstimate(

time: 24.5 us -> 24.5 us (level)
  no operation moved by 1% of the time
where the time goes in v23:
time: 24.5 us; the launch traced here: 24.3 us
  starting transfers between devices  10.1 us (41%)
  Pallas kernels  8.85 us (36%)
  waiting for transfers between devices  3.92 us (16%)
  between operations  0.76 us (3%)
  other arithmetic  0.66 us (3%)
    ppermute x1, starting transfers between devices, shards(): lax.ppermute(payload, ('blk', 'tsplit'), [(b * sets + z, (b ^ 2) * sets +...  3.13 us
    ppermute x2, starting transfers between devices, along(): return lax.ppermute(value, 'tsplit', [(i, i ^ step) for i in range(sets)])  3.1 us
    ppermute x2, starting transfers between devices, across(): return lax.ppermute(value, 'blk', [(i, i ^ 2 * chip) for i in range(slabs)])  2.8 us
    pallas_call x2, Pallas kernels, prepare_on(): pl.pallas_call(functools.partial(prepare_kernel, turn), out_shape=(jax.Sh...  2.55 us
    pallas_call x2, Pallas kernels, logits(): pl.pallas_call(functools.partial(logits_kernel, len(sides) // 2), out_sha...  2.16 us
    ppermute x2, waiting for transfers between devices, along(): return lax.ppermute(value, 'tsplit', [(i, i ^ step) for i in range(sets)])  1.88 us
    pallas_call x3, Pallas kernels, columns(): pl.pallas_call(kernel, out_shape=outs, in_specs=[VMEM] * (chips + 4) + [S...  1.71 us
    pallas_call x1, Pallas kernels, shards(): pl.pallas_call(near_kernel, out_shape=(f32(tgt_count, LANES), f32(1, src_...  1.54 us
  transfers between devices with their start and end apart: 8, of which 3 were waited for; matrix products, arithmetic and copies ran while one was open for 0% of the time, Pallas kernels for 30%

profile of v23, /device:TPU:0, one launch (start us, length us, event | category | flops | bytes accessed | tf_op | source)
XLA Modules:
  0.0 24.3 jit_solution(6971562424682902722)
XLA Ops:
  0.6 0.5 %collective-permute-start = (bf16[1024,512]{1,0:T(8,128)(2,1)}, bf16[1024,512]{1,0:T(8,128)(2,1)S(1)}, u32[]{:S(2)}, u32[]{:S(2)}) collective-permute-start(bf16[1024,512]{1,0:T(8,128)(2,1)} %refs_1_.3), channel_id=1, source_target_pairs={{0,4},{4,0},{8,12},{12,8},{1,5},{5,1},{9,13},{13,9},{2,6},{6,2},{1... | collective-permute-start | bytes 3145736 | tf_op jit(solution)/shard_map/ppermute | solution.py:236
  1.1 0.1 prepare_1.1
  1.2 2.6 %collective-permute-start.2 = (bf16[256,512]{1,0:T(8,128)(2,1)}, bf16[256,512]{1,0:T(8,128)(2,1)S(1)}, u32[]{:S(2)}, u32[]{:S(2)}) collective-permute-start(bf16[256,512]{1,0:T(8,128)(2,1)} %rows_ref.2), channel_id=1, source_target_pairs={{0,8},{4,12},{8,0},{12,4},{1,9},{5,13},{9,1},{13,5},{2,10},{6,14},... | collective-permute-start | bytes 786440 | tf_op jit(solution)/shard_map/ppermute | solution.py:239
  3.8 2.5 %prepare_0.1 = (bf16[1024,512]{1,0:T(8,128)(2,1)S(1)}, f32[1,1024]{1,0:T(1,128)S(1)}, f32[1024,128]{1,0:T(8,128)S(1)}, f32[256,1024]{1,0:T(8,128)S(1)}, f32[1,25...) custom-call(s32[1]{0:T(128)} %bitcast.core_ref.refs_6_, bf16[256,512]{1,0:T(8,128)(2,1)} %rows_ref.2, ...), custom_call_target="tpu_custom_call" | custom-call | flops 268435456 | bytes 1048576 | tf_op jit(solution)/shard_map/prepare_0/pallas_call | solution.py:264
  6.3 0.4 %collective-permute-start.1 = (f32[1,1024]{1,0:T(1,128)S(1)}, f32[1,1024]{1,0:T(1,128)S(1)}, u32[]{:S(2)}, u32[]{:S(2)}) collective-permute-start(f32[1,1024]{1,0:T(1,128)S(1)} %get-tuple-element.41.refs_1_), channel_id=1, source_target_pairs={{0,4},{4,0},{8,12},{12,8},{1,5},{5,1},{9,13},{13,9},{2,6},{6,2},{1... | collective-permute-start | bytes 12296 | tf_op jit(solution)/shard_map/ppermute | solution.py:236
  6.8 0.8 %collective-permute-done.1.offset_ref.refs_3_.refs_1_ = f32[1,1024]{1,0:T(1,128)S(1)} collective-permute-done((f32[1,1024]{1,0:T(1,128)S(1)}, f32[1,1024]{1,0:T(1,128)S(1)}, u32[]{:S(2)}, u32[]{:S(2)}) %collective-permute-start.1) | collective-permute-done | bytes 4128 | tf_op jit(solution)/shard_map/ppermute | solution.py:236
  7.6 0.0 collective-permute-done.tgt_ref.refs_3_.refs_2_.refs_0_
  7.6 1.5 %near_rows.1 = (f32[1024,128]{1,0:T(8,128)S(1)}, f32[1,256]{1,0:T(1,128)S(1)}) custom-call(bf16[256,512]{1,0:T(8,128)(2,1)} %rows_ref.2, bf16[1024,512]{1,0:T(8,128)(2,1)S(1)} %collective-permute-done.tgt_ref.refs_3_.refs_2_.refs_0_, f32[1,1024]{1,0:T(1,128)S(1)} %collective-permute-done.1.offset_ref.refs_3_.refs_1_, f32[1,256]{1,0:T(1,128)S(1)} %get-tuple-element.42.held_ref), custom_call_target="tpu_custom_call" | custom-call | flops 268435456 | bytes 1048576 | tf_op jit(solution)/shard_map/near_rows/pallas_call | solution.py:289
  9.1 0.9 %far_rows.1 = f32[4,256]{1,0:T(4,128)S(1)} custom-call(bf16[256,512]{1,0:T(8,128)(2,1)S(1)} %collective-permute-done.2.refs_0_.rows_ref, bf16[1024,512]{1,0:T(8,128)(2,1)S(1)} %get-tuple-element.46.refs_1_.refs_0_, f32[1024,128]{1,0:T(8,128)S(1)} %get-tuple-element.47.refs_2_, bf16[1024,512]{1,0:T(8,128)(2,1)S(1)} %collective-permute-done.tgt_ref.refs_3_.refs_2_.refs_0_, ...), custom_call_target="tpu_custom_call" | custom-call | flops 536870912 | bytes 1048576 | tf_op jit(solution)/shard_map/far_rows/pallas_call | solution.py:301
  10.0 3.1 %collective-permute-start.5 = (f32[4,256]{1,0:T(4,128)S(1)}, f32[4,256]{1,0:T(4,128)S(1)}, u32[]{:S(2)}, u32[]{:S(2)}) collective-permute-start(f32[4,256]{1,0:T(4,128)S(1)} %far_rows.1), channel_id=1, source_target_pairs={{0,9},{1,8},{2,11},{3,10},{4,13},{5,12},{6,15},{7,14},{8,1},{9,0},... | collective-permute-start | bytes 12296 | tf_op jit(solution)/shard_map/ppermute | solution.py:335
  13.2 0.4 %collective-permute-start.4 = (f32[4,256]{1,0:T(4,128)S(1)}, f32[4,256]{1,0:T(4,128)S(1)}, u32[]{:S(2)}, u32[]{:S(2)}) collective-permute-start(f32[4,256]{1,0:T(4,128)S(1)} %far_rows.1), channel_id=1, source_target_pairs={{0,1},{1,0},{2,3},{3,2},{4,5},{5,4},{6,7},{7,6},{8,9},{9,8},{10,11... | collective-permute-start | bytes 12296 | tf_op jit(solution)/shard_map/ppermute | solution.py:242
  13.6 0.2 collective-permute-start.3
  13.8 0.7 %logits.2 = (f32[256,1024]{1,0:T(8,128)S(1)}, f32[256,1024]{1,0:T(8,128)S(1)}) custom-call(bf16[256,512]{1,0:T(8,128)(2,1)S(1)} %collective-permute-done.2.refs_0_.rows_ref, bf16[1024,512]{1,0:T(8,128)(2,1)S(1)} %get-tuple-element.46.refs_1_.refs_0_, f32[1,1024]{1,0:T(1,128)S(1)} %get-tuple-element.41.refs_1_, ...), custom_call_target="tpu_custom_call" | custom-call | flops 536870912 | bytes 1048576 | tf_op jit(solution)/shard_map/logits/pallas_call | solution.py:314
  14.6 1.4 %logits.3.refs_0_ = f32[256,1024]{1,0:T(8,128)S(1)} custom-call(bf16[256,512]{1,0:T(8,128)(2,1)} %rows_ref.2, bf16[1024,512]{1,0:T(8,128)(2,1)S(1)} %collective-permute-done.tgt_ref.refs_3_.refs_2_.refs_0_, f32[1,1024]{1,0:T(1,128)S(1)} %collective-permute-done.1.offset_ref.refs_3_.refs_1_), custom_call_target="tpu_custom_call" | custom-call | flops 268435456 | bytes 1048576 | tf_op jit(solution)/shard_map/logits/pallas_call | solution.py:314
  16.0 1.2 %collective-permute-done.3 = f32[4,256]{1,0:T(4,128)S(1)} collective-permute-done((f32[4,256]{1,0:T(4,128)S(1)}, f32[4,256]{1,0:T(4,128)S(1)}, u32[]{:S(2)}, u32[]{:S(2)}) %collective-permute-start.3) | collective-permute-done | bytes 4128 | tf_op jit(solution)/shard_map/ppermute | solution.py:239
  17.3 2.7 %collective-permute-start.6 = (f32[2,256]{1,0:T(2,128)S(1)}, f32[2,256]{1,0:T(2,128)S(1)}, u32[]{:S(2)}, u32[]{:S(2)}) collective-permute-start(f32[2,256]{1,0:T(2,128)S(1)} %log_add_fusion.refs_2_), channel_id=1, source_target_pairs={{0,2},{1,3},{2,0},{3,1},{4,6},{5,7},{6,4},{7,5},{8,10},{9,11},{10,... | collective-permute-start | bytes 6152 | tf_op jit(solution)/shard_map/ppermute | solution.py:242
  19.9 1.9 %collective-permute-done.6.refs_3_ = f32[2,256]{1,0:T(2,128)S(1)} collective-permute-done((f32[2,256]{1,0:T(2,128)S(1)}, f32[2,256]{1,0:T(2,128)S(1)}, u32[]{:S(2)}, u32[]{:S(2)}) %collective-permute-start.6) | collective-permute-done | bytes 2080 | tf_op jit(solution)/shard_map/ppermute | solution.py:242
  21.8 0.5 %columns.3 = f32[8,128]{1,0:T(8,128)S(1)} custom-call(f32[256,1024]{1,0:T(8,128)S(1)} %logits.3.refs_0_, f32[256,1024]{1,0:T(8,128)S(1)} %get-tuple-element.55.refs_1_, f32[2,256]{1,0:T(2,128)S(1)} %log_add_fusion.refs_2_, f32[2,256]{1,0:T(2,128)S(1)} %collective-permute-done.6.refs_3_, f32[2,256]{1,0:T(2,128)S(1)} %get-tuple-element.63.refs_4_, ...), custom_call_target="tpu_custom_call" | custom-call | flops 3145728 | bytes 1048576 | tf_op jit(solution)/shard_map/columns/pallas_call | solution.py:353
  22.4 0.1 collective-permute-start.7
  22.5 0.0 copy-start
  22.5 0.0 copy-start.1
  22.5 0.0 copy-start.2
  22.5 1.1 %columns.5 = (f32[8,128]{1,0:T(8,128)S(1)}, f32[1,256]{1,0:T(1,128)}) custom-call(f32[256,1024]{1,0:T(8,128)S(1)} %get-tuple-element.40.refs_0_, f32[256,1024]{1,0:T(8,128)S(1)} %get-tuple-element.52.refs_1_, f32[2,256]{1,0:T(2,128)S(1)} %log_add_fusion.refs_2_, f32[2,256]{1,0:T(2,128)S(1)} %collective-permute-done.6.refs_3_, ...), custom_call_target="tpu_custom_call" | custom-call | flops 3145728 | bytes 1048576 | tf_op jit(solution)/shard_map/columns/pallas_call | solution.py:353
  23.7 0.6 %fusion = f32[1024]{0:T(1024)} fusion(f32[1024]{0:T(1024)S(1)} %copy-done.2, f32[8,128]{1,0:T(8,128)S(1)} %collective-permute-done.7, f32[8,128]{1,0:T(8,128)S(1)} %get-tuple-element.60, f32[1024]{0:T(1024)S(1)} %copy-done, f32[1024]{0:T(1024)S(1)} %copy-done.1), kind=kLoop, calls=%fused_computation.3 | loop fusion | flops 9216 | bytes 24576 | tf_op jit(solution)/shard_map/mul | solution.py:385
  (15 shorter events, 0.1 us)
Async XLA Ops:
  0.6 7.0 %collective-permute-start = (bf16[1024,512]{1,0:T(8,128)(2,1)}, bf16[1024,512]{1,0:T(8,128)(2,1)S(1)}, u32[]{:S(2)}, u32[]{:S(2)}) collective-permute-start(bf16[1024,512]{1,0:T(8,128)(2,1)} %refs_1_.3), channel_id=1, source_target_pairs={{0,4},{4,0},{8,12},{12,8},{1,5},{5,1},{9,13},{13,9},{2,6},{6,2},{1... | collective-permute-start | bytes 3145736 | tf_op jit(solution)/shard_map/ppermute | solution.py:236
  1.2 7.9 %collective-permute-start.2 = (bf16[256,512]{1,0:T(8,128)(2,1)}, bf16[256,512]{1,0:T(8,128)(2,1)S(1)}, u32[]{:S(2)}, u32[]{:S(2)}) collective-permute-start(bf16[256,512]{1,0:T(8,128)(2,1)} %rows_ref.2), channel_id=1, source_target_pairs={{0,8},{4,12},{8,0},{12,4},{1,9},{5,13},{9,1},{13,5},{2,10},{6,14},... | collective-permute-start | bytes 786440 | tf_op jit(solution)/shard_map/ppermute | solution.py:239
  6.3 1.3 %collective-permute-start.1 = (f32[1,1024]{1,0:T(1,128)S(1)}, f32[1,1024]{1,0:T(1,128)S(1)}, u32[]{:S(2)}, u32[]{:S(2)}) collective-permute-start(f32[1,1024]{1,0:T(1,128)S(1)} %get-tuple-element.41.refs_1_), channel_id=1, source_target_pairs={{0,4},{4,0},{8,12},{12,8},{1,5},{5,1},{9,13},{13,9},{2,6},{6,2},{1... | collective-permute-start | bytes 12296 | tf_op jit(solution)/shard_map/ppermute | solution.py:236
  10.0 5.9 %collective-permute-start.5 = (f32[4,256]{1,0:T(4,128)S(1)}, f32[4,256]{1,0:T(4,128)S(1)}, u32[]{:S(2)}, u32[]{:S(2)}) collective-permute-start(f32[4,256]{1,0:T(4,128)S(1)} %far_rows.1), channel_id=1, source_target_pairs={{0,9},{1,8},{2,11},{3,10},{4,13},{5,12},{6,15},{7,14},{8,1},{9,0},... | collective-permute-start | bytes 12296 | tf_op jit(solution)/shard_map/ppermute | solution.py:335
  13.2 4.1 %collective-permute-start.4 = (f32[4,256]{1,0:T(4,128)S(1)}, f32[4,256]{1,0:T(4,128)S(1)}, u32[]{:S(2)}, u32[]{:S(2)}) collective-permute-start(f32[4,256]{1,0:T(4,128)S(1)} %far_rows.1), channel_id=1, source_target_pairs={{0,1},{1,0},{2,3},{3,2},{4,5},{5,4},{6,7},{7,6},{8,9},{9,8},{10,11... | collective-permute-start | bytes 12296 | tf_op jit(solution)/shard_map/ppermute | solution.py:242
  13.6 3.6 %collective-permute-start.3 = (f32[4,256]{1,0:T(4,128)S(1)}, f32[4,256]{1,0:T(4,128)S(1)}, u32[]{:S(2)}, u32[]{:S(2)}) collective-permute-start(f32[4,256]{1,0:T(4,128)S(1)} %far_rows.1), channel_id=1, source_target_pairs={{0,8},{4,12},{8,0},{12,4},{1,9},{5,13},{9,1},{13,5},{2,10},{6,14},... | collective-permute-start | bytes 12296 | tf_op jit(solution)/shard_map/ppermute | solution.py:239
  17.3 4.5 %collective-permute-start.6 = (f32[2,256]{1,0:T(2,128)S(1)}, f32[2,256]{1,0:T(2,128)S(1)}, u32[]{:S(2)}, u32[]{:S(2)}) collective-permute-start(f32[2,256]{1,0:T(2,128)S(1)} %log_add_fusion.refs_2_), channel_id=1, source_target_pairs={{0,2},{1,3},{2,0},{3,1},{4,6},{5,7},{6,4},{7,5},{8,10},{9,11},{10,... | collective-permute-start | bytes 6152 | tf_op jit(solution)/shard_map/ppermute | solution.py:242
  22.4 1.3 %collective-permute-start.7 = (f32[8,128]{1,0:T(8,128)S(1)}, f32[8,128]{1,0:T(8,128)S(1)}, u32[]{:S(2)}, u32[]{:S(2)}) collective-permute-start(f32[8,128]{1,0:T(8,128)S(1)} %columns.3), channel_id=1, source_target_pairs={{0,4},{4,0},{8,12},{12,8},{1,5},{5,1},{9,13},{13,9},{2,6},{6,2},{1... | collective-permute-start | bytes 12296 | tf_op jit(solution)/shard_map/ppermute | solution.py:236
  22.5 1.2 %copy-start = (f32[1024]{0:T(1024)S(1)}, f32[1024]{0:T(1024)}, u32[]{:S(2)}) copy-start(f32[1024]{0:T(1024)} %param.9) | copy-start | bytes 12292
  22.5 1.2 %copy-start.1 = (f32[1024]{0:T(1024)S(1)}, f32[1024]{0:T(1024)}, u32[]{:S(2)}) copy-start(f32[1024]{0:T(1024)} %param.11) | copy-start | bytes 12292
  22.5 1.2 %copy-start.2 = (f32[1024]{0:T(1024)S(1)}, f32[1024]{0:T(1024)}, u32[]{:S(2)}) copy-start(f32[1024]{0:T(1024)} %param.13) | copy-start | bytes 12292

commit v24 on v23

--- a/solution.py
+++ b/solution.py
@@ -162,12 +162,11 @@
 
 
 def sum_columns(z_refs, offset, out_ref, off_ref, peak_ref, mass_ref):
-    eye = diagonal()
     slots, src_count = offset.shape
     for slot in range(slots):
         for at in range(0, src_count, LANES):
-            column = to_column(offset[slot : slot + 1, at : at + LANES] * LOG2_E, eye)
-            off_ref[slot, at : at + LANES, :] = jnp.broadcast_to(column, (LANES, LANES))
+            row = jnp.broadcast_to(offset[slot : slot + 1, at : at + LANES] * LOG2_E, (LANES, LANES))
+            off_ref[slot, at : at + LANES, :] = jnp.transpose(row)
 
     parts = [(slot, at) for slot in range(slots) for at in range(0, src_count, LANES)]
     for left in range(0, z_refs[0].shape[1], CHUNK):

time: 24.5 us -> 24.5 us (level)
  no operation moved by 1% of the time
where the time goes in v24:
time: 24.5 us; the launch traced here: 24.3 us
  starting transfers between devices  10.1 us (41%)
  Pallas kernels  8.83 us (36%)
  waiting for transfers between devices  3.92 us (16%)
  between operations  0.76 us (3%)
  other arithmetic  0.66 us (3%)
    ppermute x1, starting transfers between devices, shards(): lax.ppermute(payload, ('blk', 'tsplit'), [(b * sets + z, (b ^ 2) * sets +...  3.13 us
    ppermute x2, starting transfers between devices, along(): return lax.ppermute(value, 'tsplit', [(i, i ^ step) for i in range(sets)])  3.1 us
    ppermute x2, starting transfers between devices, across(): return lax.ppermute(value, 'blk', [(i, i ^ 2 * chip) for i in range(slabs)])  2.8 us
    pallas_call x2, Pallas kernels, prepare_on(): pl.pallas_call(functools.partial(prepare_kernel, turn), out_shape=(jax.Sh...  2.55 us
    pallas_call x2, Pallas kernels, logits(): pl.pallas_call(functools.partial(logits_kernel, len(sides) // 2), out_sha...  2.16 us
    ppermute x2, waiting for transfers between devices, along(): return lax.ppermute(value, 'tsplit', [(i, i ^ step) for i in range(sets)])  1.88 us
    pallas_call x3, Pallas kernels, columns(): pl.pallas_call(kernel, out_shape=outs, in_specs=[VMEM] * (chips + 4) + [S...  1.68 us
    pallas_call x1, Pallas kernels, shards(): pl.pallas_call(near_kernel, out_shape=(f32(tgt_count, LANES), f32(1, src_...  1.54 us
  transfers between devices with their start and end apart: 8, of which 3 were waited for; matrix products, arithmetic and copies ran while one was open for 0% of the time, Pallas kernels for 30%

profile of v24, /device:TPU:0, one launch (start us, length us, event | category | flops | bytes accessed | tf_op | source)
XLA Modules:
  0.0 24.3 jit_solution(14279947334486138983)
XLA Ops:
  0.6 0.5 %collective-permute-start = (bf16[1024,512]{1,0:T(8,128)(2,1)}, bf16[1024,512]{1,0:T(8,128)(2,1)S(1)}, u32[]{:S(2)}, u32[]{:S(2)}) collective-permute-start(bf16[1024,512]{1,0:T(8,128)(2,1)} %refs_1_.3), channel_id=1, source_target_pairs={{0,4},{4,0},{8,12},{12,8},{1,5},{5,1},{9,13},{13,9},{2,6},{6,2},{1... | collective-permute-start | bytes 3145736 | tf_op jit(solution)/shard_map/ppermute | solution.py:235
  1.1 0.1 prepare_1.1
  1.2 2.6 %collective-permute-start.2 = (bf16[256,512]{1,0:T(8,128)(2,1)}, bf16[256,512]{1,0:T(8,128)(2,1)S(1)}, u32[]{:S(2)}, u32[]{:S(2)}) collective-permute-start(bf16[256,512]{1,0:T(8,128)(2,1)} %rows_ref.2), channel_id=1, source_target_pairs={{0,8},{4,12},{8,0},{12,4},{1,9},{5,13},{9,1},{13,5},{2,10},{6,14},... | collective-permute-start | bytes 786440 | tf_op jit(solution)/shard_map/ppermute | solution.py:238
  3.8 2.5 %prepare_0.1 = (bf16[1024,512]{1,0:T(8,128)(2,1)S(1)}, f32[1,1024]{1,0:T(1,128)S(1)}, f32[1024,128]{1,0:T(8,128)S(1)}, f32[256,1024]{1,0:T(8,128)S(1)}, f32[1,25...) custom-call(s32[1]{0:T(128)} %bitcast.core_ref.refs_6_, bf16[256,512]{1,0:T(8,128)(2,1)} %rows_ref.2, ...), custom_call_target="tpu_custom_call" | custom-call | flops 268435456 | bytes 1048576 | tf_op jit(solution)/shard_map/prepare_0/pallas_call | solution.py:263
  6.3 0.4 %collective-permute-start.1 = (f32[1,1024]{1,0:T(1,128)S(1)}, f32[1,1024]{1,0:T(1,128)S(1)}, u32[]{:S(2)}, u32[]{:S(2)}) collective-permute-start(f32[1,1024]{1,0:T(1,128)S(1)} %get-tuple-element.41.refs_1_), channel_id=1, source_target_pairs={{0,4},{4,0},{8,12},{12,8},{1,5},{5,1},{9,13},{13,9},{2,6},{6,2},{1... | collective-permute-start | bytes 12296 | tf_op jit(solution)/shard_map/ppermute | solution.py:235
  6.8 0.8 %collective-permute-done.1.offset_ref.refs_3_.refs_1_ = f32[1,1024]{1,0:T(1,128)S(1)} collective-permute-done((f32[1,1024]{1,0:T(1,128)S(1)}, f32[1,1024]{1,0:T(1,128)S(1)}, u32[]{:S(2)}, u32[]{:S(2)}) %collective-permute-start.1) | collective-permute-done | bytes 4128 | tf_op jit(solution)/shard_map/ppermute | solution.py:235
  7.6 0.0 collective-permute-done.tgt_ref.refs_3_.refs_2_.refs_0_
  7.6 1.5 %near_rows.1 = (f32[1024,128]{1,0:T(8,128)S(1)}, f32[1,256]{1,0:T(1,128)S(1)}) custom-call(bf16[256,512]{1,0:T(8,128)(2,1)} %rows_ref.2, bf16[1024,512]{1,0:T(8,128)(2,1)S(1)} %collective-permute-done.tgt_ref.refs_3_.refs_2_.refs_0_, f32[1,1024]{1,0:T(1,128)S(1)} %collective-permute-done.1.offset_ref.refs_3_.refs_1_, f32[1,256]{1,0:T(1,128)S(1)} %get-tuple-element.42.held_ref), custom_call_target="tpu_custom_call" | custom-call | flops 268435456 | bytes 1048576 | tf_op jit(solution)/shard_map/near_rows/pallas_call | solution.py:288
  9.1 0.9 %far_rows.1 = f32[4,256]{1,0:T(4,128)S(1)} custom-call(bf16[256,512]{1,0:T(8,128)(2,1)S(1)} %collective-permute-done.2.refs_0_.rows_ref, bf16[1024,512]{1,0:T(8,128)(2,1)S(1)} %get-tuple-element.46.refs_1_.refs_0_, f32[1024,128]{1,0:T(8,128)S(1)} %get-tuple-element.47.refs_2_, bf16[1024,512]{1,0:T(8,128)(2,1)S(1)} %collective-permute-done.tgt_ref.refs_3_.refs_2_.refs_0_, ...), custom_call_target="tpu_custom_call" | custom-call | flops 536870912 | bytes 1048576 | tf_op jit(solution)/shard_map/far_rows/pallas_call | solution.py:300
  10.0 3.1 %collective-permute-start.5 = (f32[4,256]{1,0:T(4,128)S(1)}, f32[4,256]{1,0:T(4,128)S(1)}, u32[]{:S(2)}, u32[]{:S(2)}) collective-permute-start(f32[4,256]{1,0:T(4,128)S(1)} %far_rows.1), channel_id=1, source_target_pairs={{0,9},{1,8},{2,11},{3,10},{4,13},{5,12},{6,15},{7,14},{8,1},{9,0},... | collective-permute-start | bytes 12296 | tf_op jit(solution)/shard_map/ppermute | solution.py:334
  13.2 0.4 %collective-permute-start.4 = (f32[4,256]{1,0:T(4,128)S(1)}, f32[4,256]{1,0:T(4,128)S(1)}, u32[]{:S(2)}, u32[]{:S(2)}) collective-permute-start(f32[4,256]{1,0:T(4,128)S(1)} %far_rows.1), channel_id=1, source_target_pairs={{0,1},{1,0},{2,3},{3,2},{4,5},{5,4},{6,7},{7,6},{8,9},{9,8},{10,11... | collective-permute-start | bytes 12296 | tf_op jit(solution)/shard_map/ppermute | solution.py:241
  13.6 0.2 collective-permute-start.3
  13.8 0.7 %logits.2 = (f32[256,1024]{1,0:T(8,128)S(1)}, f32[256,1024]{1,0:T(8,128)S(1)}) custom-call(bf16[256,512]{1,0:T(8,128)(2,1)S(1)} %collective-permute-done.2.refs_0_.rows_ref, bf16[1024,512]{1,0:T(8,128)(2,1)S(1)} %get-tuple-element.46.refs_1_.refs_0_, f32[1,1024]{1,0:T(1,128)S(1)} %get-tuple-element.41.refs_1_, ...), custom_call_target="tpu_custom_call" | custom-call | flops 536870912 | bytes 1048576 | tf_op jit(solution)/shard_map/logits/pallas_call | solution.py:313
  14.6 1.4 %logits.3.refs_0_ = f32[256,1024]{1,0:T(8,128)S(1)} custom-call(bf16[256,512]{1,0:T(8,128)(2,1)} %rows_ref.2, bf16[1024,512]{1,0:T(8,128)(2,1)S(1)} %collective-permute-done.tgt_ref.refs_3_.refs_2_.refs_0_, f32[1,1024]{1,0:T(1,128)S(1)} %collective-permute-done.1.offset_ref.refs_3_.refs_1_), custom_call_target="tpu_custom_call" | custom-call | flops 268435456 | bytes 1048576 | tf_op jit(solution)/shard_map/logits/pallas_call | solution.py:313
  16.0 1.2 %collective-permute-done.3 = f32[4,256]{1,0:T(4,128)S(1)} collective-permute-done((f32[4,256]{1,0:T(4,128)S(1)}, f32[4,256]{1,0:T(4,128)S(1)}, u32[]{:S(2)}, u32[]{:S(2)}) %collective-permute-start.3) | collective-permute-done | bytes 4128 | tf_op jit(solution)/shard_map/ppermute | solution.py:238
  17.3 2.7 %collective-permute-start.6 = (f32[2,256]{1,0:T(2,128)S(1)}, f32[2,256]{1,0:T(2,128)S(1)}, u32[]{:S(2)}, u32[]{:S(2)}) collective-permute-start(f32[2,256]{1,0:T(2,128)S(1)} %log_add_fusion.refs_2_), channel_id=1, source_target_pairs={{0,2},{1,3},{2,0},{3,1},{4,6},{5,7},{6,4},{7,5},{8,10},{9,11},{10,... | collective-permute-start | bytes 6152 | tf_op jit(solution)/shard_map/ppermute | solution.py:241
  19.9 1.9 %collective-permute-done.6.refs_3_ = f32[2,256]{1,0:T(2,128)S(1)} collective-permute-done((f32[2,256]{1,0:T(2,128)S(1)}, f32[2,256]{1,0:T(2,128)S(1)}, u32[]{:S(2)}, u32[]{:S(2)}) %collective-permute-start.6) | collective-permute-done | bytes 2080 | tf_op jit(solution)/shard_map/ppermute | solution.py:241
  21.8 0.5 %columns.3 = f32[8,128]{1,0:T(8,128)S(1)} custom-call(f32[256,1024]{1,0:T(8,128)S(1)} %logits.3.refs_0_, f32[256,1024]{1,0:T(8,128)S(1)} %get-tuple-element.55.refs_1_, f32[2,256]{1,0:T(2,128)S(1)} %log_add_fusion.refs_2_, f32[2,256]{1,0:T(2,128)S(1)} %collective-permute-done.6.refs_3_, f32[2,256]{1,0:T(2,128)S(1)} %get-tuple-element.63.refs_4_, ...), custom_call_target="tpu_custom_call" | custom-call | flops 3145728 | bytes 1048576 | tf_op jit(solution)/shard_map/columns/pallas_call | solution.py:352
  22.4 0.1 collective-permute-start.7
  22.5 0.0 copy-start
  22.5 0.0 copy-start.1
  22.5 0.0 copy-start.2
  22.5 1.1 %columns.5 = (f32[8,128]{1,0:T(8,128)S(1)}, f32[1,256]{1,0:T(1,128)}) custom-call(f32[256,1024]{1,0:T(8,128)S(1)} %get-tuple-element.40.refs_0_, f32[256,1024]{1,0:T(8,128)S(1)} %get-tuple-element.52.refs_1_, f32[2,256]{1,0:T(2,128)S(1)} %log_add_fusion.refs_2_, f32[2,256]{1,0:T(2,128)S(1)} %collective-permute-done.6.refs_3_, ...), custom_call_target="tpu_custom_call" | custom-call | flops 3145728 | bytes 1048576 | tf_op jit(solution)/shard_map/columns/pallas_call | solution.py:352
  23.6 0.6 %fusion = f32[1024]{0:T(1024)} fusion(f32[1024]{0:T(1024)S(1)} %copy-done.2, f32[8,128]{1,0:T(8,128)S(1)} %collective-permute-done.7, f32[8,128]{1,0:T(8,128)S(1)} %get-tuple-element.60, f32[1024]{0:T(1024)S(1)} %copy-done, f32[1024]{0:T(1024)S(1)} %copy-done.1), kind=kLoop, calls=%fused_computation.3 | loop fusion | flops 9216 | bytes 24576 | tf_op jit(solution)/shard_map/mul | solution.py:384
  (15 shorter events, 0.1 us)
Async XLA Ops:
  0.6 7.0 %collective-permute-start = (bf16[1024,512]{1,0:T(8,128)(2,1)}, bf16[1024,512]{1,0:T(8,128)(2,1)S(1)}, u32[]{:S(2)}, u32[]{:S(2)}) collective-permute-start(bf16[1024,512]{1,0:T(8,128)(2,1)} %refs_1_.3), channel_id=1, source_target_pairs={{0,4},{4,0},{8,12},{12,8},{1,5},{5,1},{9,13},{13,9},{2,6},{6,2},{1... | collective-permute-start | bytes 3145736 | tf_op jit(solution)/shard_map/ppermute | solution.py:235
  1.2 7.9 %collective-permute-start.2 = (bf16[256,512]{1,0:T(8,128)(2,1)}, bf16[256,512]{1,0:T(8,128)(2,1)S(1)}, u32[]{:S(2)}, u32[]{:S(2)}) collective-permute-start(bf16[256,512]{1,0:T(8,128)(2,1)} %rows_ref.2), channel_id=1, source_target_pairs={{0,8},{4,12},{8,0},{12,4},{1,9},{5,13},{9,1},{13,5},{2,10},{6,14},... | collective-permute-start | bytes 786440 | tf_op jit(solution)/shard_map/ppermute | solution.py:238
  6.3 1.3 %collective-permute-start.1 = (f32[1,1024]{1,0:T(1,128)S(1)}, f32[1,1024]{1,0:T(1,128)S(1)}, u32[]{:S(2)}, u32[]{:S(2)}) collective-permute-start(f32[1,1024]{1,0:T(1,128)S(1)} %get-tuple-element.41.refs_1_), channel_id=1, source_target_pairs={{0,4},{4,0},{8,12},{12,8},{1,5},{5,1},{9,13},{13,9},{2,6},{6,2},{1... | collective-permute-start | bytes 12296 | tf_op jit(solution)/shard_map/ppermute | solution.py:235
  10.0 5.9 %collective-permute-start.5 = (f32[4,256]{1,0:T(4,128)S(1)}, f32[4,256]{1,0:T(4,128)S(1)}, u32[]{:S(2)}, u32[]{:S(2)}) collective-permute-start(f32[4,256]{1,0:T(4,128)S(1)} %far_rows.1), channel_id=1, source_target_pairs={{0,9},{1,8},{2,11},{3,10},{4,13},{5,12},{6,15},{7,14},{8,1},{9,0},... | collective-permute-start | bytes 12296 | tf_op jit(solution)/shard_map/ppermute | solution.py:334
  13.2 4.1 %collective-permute-start.4 = (f32[4,256]{1,0:T(4,128)S(1)}, f32[4,256]{1,0:T(4,128)S(1)}, u32[]{:S(2)}, u32[]{:S(2)}) collective-permute-start(f32[4,256]{1,0:T(4,128)S(1)} %far_rows.1), channel_id=1, source_target_pairs={{0,1},{1,0},{2,3},{3,2},{4,5},{5,4},{6,7},{7,6},{8,9},{9,8},{10,11... | collective-permute-start | bytes 12296 | tf_op jit(solution)/shard_map/ppermute | solution.py:241
  13.6 3.6 %collective-permute-start.3 = (f32[4,256]{1,0:T(4,128)S(1)}, f32[4,256]{1,0:T(4,128)S(1)}, u32[]{:S(2)}, u32[]{:S(2)}) collective-permute-start(f32[4,256]{1,0:T(4,128)S(1)} %far_rows.1), channel_id=1, source_target_pairs={{0,8},{4,12},{8,0},{12,4},{1,9},{5,13},{9,1},{13,5},{2,10},{6,14},... | collective-permute-start | bytes 12296 | tf_op jit(solution)/shard_map/ppermute | solution.py:238
  17.3 4.5 %collective-permute-start.6 = (f32[2,256]{1,0:T(2,128)S(1)}, f32[2,256]{1,0:T(2,128)S(1)}, u32[]{:S(2)}, u32[]{:S(2)}) collective-permute-start(f32[2,256]{1,0:T(2,128)S(1)} %log_add_fusion.refs_2_), channel_id=1, source_target_pairs={{0,2},{1,3},{2,0},{3,1},{4,6},{5,7},{6,4},{7,5},{8,10},{9,11},{10,... | collective-permute-start | bytes 6152 | tf_op jit(solution)/shard_map/ppermute | solution.py:241
  22.4 1.2 %collective-permute-start.7 = (f32[8,128]{1,0:T(8,128)S(1)}, f32[8,128]{1,0:T(8,128)S(1)}, u32[]{:S(2)}, u32[]{:S(2)}) collective-permute-start(f32[8,128]{1,0:T(8,128)S(1)} %columns.3), channel_id=1, source_target_pairs={{0,4},{4,0},{8,12},{12,8},{1,5},{5,1},{9,13},{13,9},{2,6},{6,2},{1... | collective-permute-start | bytes 12296 | tf_op jit(solution)/shard_map/ppermute | solution.py:235
  22.5 1.2 %copy-start = (f32[1024]{0:T(1024)S(1)}, f32[1024]{0:T(1024)}, u32[]{:S(2)}) copy-start(f32[1024]{0:T(1024)} %param.9) | copy-start | bytes 12292
  22.5 1.2 %copy-start.1 = (f32[1024]{0:T(1024)S(1)}, f32[1024]{0:T(1024)}, u32[]{:S(2)}) copy-start(f32[1024]{0:T(1024)} %param.11) | copy-start | bytes 12292
  22.5 1.2 %copy-start.2 = (f32[1024]{0:T(1024)S(1)}, f32[1024]{0:T(1024)}, u32[]{:S(2)}) copy-start(f32[1024]{0:T(1024)} %param.13) | copy-start | bytes 12292
